TPU v7x, 256 devices: a whole 4x4x8 slice. The times are simulated.
256 devices in a mesh: dp: 64 (over x, z, core), cache: 4 (over y).
Axes of the slice: x: 4, y: 4, z: 8, core: 2. Of those that a mesh axis runs over, the one named last changes fastest.
Arguments:
- student_feats: bfloat16 [2048, 32, 1024], P('dp'), may hold values from -6 to 6
- head_weight: bfloat16 [1024, 5120], P(None, 'cache'), may hold values from -0.1875 to 0.1875
- teacher_cache: bfloat16 [4096, 32, 5120], P('dp', None, 'cache'), may hold values from -410 to 410, as said below
- holder_index: int32 [2048], replicated, may hold values from 0 to 63, as said below
- valid_count: int32 [2048], P('dp'), may hold values from 1 to 32
- image_embed: bfloat16 [2048, 768], P(('dp', 'cache')), may hold values from -5 to 5
- text_embed: bfloat16 [2048, 768], P(('dp', 'cache')), may hold values from -15 to 15
- pair_ids: int32 [2048], P(('dp', 'cache')), may hold values from 0 to 2047, each once
Outputs:
- head_grad: float32 [1024, 5120], P('dp', 'cache')
- image_loss: float32 [2048], P(('dp', 'cache'))
Inputs may be any that keep to these rules, and one draw needn't show every extreme that they name: `holder_index`: each dp index holds the teacher rows of exactly 64 images or of none, and of at most 1 of the images of one dp index, a count that is reached. `teacher_cache`: along dp index h, slot s holds the teacher rows of the image with the s-th smallest index among those whose holder is h; the other slots belong to no image.
All inputs are finite; a program needn't handle non-finite values.
Results may differ from a plain program's by a relative error of at most 0.00098.
Values may be sent and summed in bfloat16 or wider, within the bound.
No kernel may reach another device: no remote copies, remote signals or barrier semaphores. Data moves between devices by JAX's collectives and lax.ppermute only.
A program may use at most 128 MiB of HBM per device.

v0:
```python
import jax
import jax.numpy as jnp
from jax import lax
from jax.sharding import PartitionSpec as P

eps = 1e-06
loss_scale = 128.0


def row_errors(predicted, teach_wide, full_cols):
    first_sum = jnp.sum(teach_wide, axis=-1)
    square_sum = jnp.sum(teach_wide * teach_wide, axis=-1)
    first_sum, square_sum = lax.psum((first_sum, square_sum), "cache")
    row_mean = first_sum / full_cols
    inv_scale = lax.rsqrt(square_sum / full_cols - row_mean * row_mean + eps)
    residue = predicted - (teach_wide - row_mean[..., None]) * inv_scale[..., None]
    squared = lax.psum(jnp.sum(residue * residue, axis=-1), "cache")
    return (residue, squared)


def local(
    student_feats,
    head_weight,
    teacher_cache,
    holder_index,
    valid_count,
    image_embed,
    text_embed,
    pair_ids,
):
    n_dp = lax.axis_size("dp")
    n_cache = lax.axis_size("cache")
    own_index = lax.axis_index("dp")
    cache_pos = lax.axis_index("cache")
    img_dev, patch_rows, student_width = student_feats.shape
    local_cols = head_weight.shape[1]
    full_cols = local_cols * n_cache
    pair_cap = max(1, 2 * img_dev // n_dp)
    holder_table = holder_index.reshape(n_dp, img_dev)
    is_held = (holder_table == own_index).astype(jnp.int32)
    flat_held = is_held.reshape(-1)
    cache_slot = (jnp.cumsum(flat_held) - flat_held).reshape(n_dp, img_dev)
    position = jnp.cumsum(is_held, axis=1) - is_held
    chosen = is_held[:, :, None] * (
        position[:, :, None] == jnp.arange(pair_cap, dtype=jnp.int32)[None, None, :]
    ).astype(jnp.int32)
    source = jnp.sum(chosen * cache_slot[:, :, None], axis=1)
    outgoing = jnp.take(teacher_cache, source.reshape(-1), axis=0).reshape(
        n_dp, pair_cap, patch_rows, local_cols
    )
    own_holders = lax.dynamic_slice_in_dim(holder_index, own_index * img_dev, img_dev, 0)
    img_order = jnp.arange(img_dev, dtype=jnp.int32)
    earlier = jnp.sum(
        (
            (own_holders[None, :] == own_holders[:, None])
            & (img_order[None, :] < img_order[:, None])
        ).astype(jnp.int32),
        axis=1,
    )
    row_index = jnp.arange(patch_rows, dtype=jnp.int32)
    incoming = lax.all_to_all(outgoing, "dp", split_axis=0, concat_axis=0, tiled=True)
    teacher = jnp.take(
        incoming.reshape(n_dp * pair_cap, patch_rows, local_cols),
        own_holders * pair_cap + earlier,
        axis=0,
    )
    tokens = student_feats.reshape(img_dev * patch_rows, student_width)
    counts_here = valid_count.astype(jnp.float32)
    predicted = jnp.dot(tokens, head_weight, preferred_element_type=jnp.float32).reshape(
        img_dev, patch_rows, local_cols
    )
    teach_wide = teacher.astype(jnp.float32)
    residue, squared = row_errors(predicted, teach_wide, full_cols)
    valid_mask = (row_index[None, :].astype(jnp.float32) < counts_here[:, None]).astype(jnp.float32)
    row_weight = valid_mask / jnp.maximum(counts_here, 1.0)[:, None]
    regress = jnp.sum(row_weight * squared, axis=-1) / full_cols
    row_grad = (2.0 * loss_scale / full_cols * row_weight[..., None] * residue).astype(jnp.bfloat16)
    row_grad = row_grad.reshape(img_dev * patch_rows, local_cols)
    grad_rows = student_width // n_dp
    whole_term = lax.dot_general(
        tokens, row_grad, (((0,), (0,)), ((), ())), preferred_element_type=jnp.float32
    )
    summed = lax.psum(whole_term, "dp")
    head_grad = lax.dynamic_slice_in_dim(summed, own_index * grad_rows, grad_rows, 0)
    shard_rows = image_embed.shape[0]
    score_scale = image_embed.shape[1] ** (-0.5)
    text_piece = lax.all_gather(text_embed, ("dp", "cache"), axis=0, tiled=True)
    best_score = jnp.full((shard_rows,), -jnp.inf, jnp.float32)
    denom_sum = jnp.zeros((shard_rows,), jnp.float32)
    logits = jnp.dot(image_embed, text_piece.T, preferred_element_type=jnp.float32) * score_scale
    new_best = jnp.max(logits, axis=1)
    denom_sum = denom_sum * jnp.exp(best_score - new_best) + jnp.sum(
        jnp.exp(logits - new_best[:, None]), axis=1
    )
    column = jnp.arange(text_piece.shape[0], dtype=jnp.int32)
    target = jnp.sum(jnp.where(pair_ids[:, None] == column[None, :], logits, 0.0), axis=1)
    best_score, denom_sum, target = (new_best, denom_sum, target)
    contrast = best_score + jnp.log(denom_sum) - target
    local_regress = lax.dynamic_slice_in_dim(regress, cache_pos * shard_rows, shard_rows, 0)
    return (head_grad, local_regress + contrast)


def solution(mesh):
    in_specs = (
        P("dp", None, None),
        P(None, "cache"),
        P("dp", None, "cache"),
        P(),
        P("dp"),
        P(("dp", "cache"), None),
        P(("dp", "cache"), None),
        P(("dp", "cache")),
    )
    out_specs = (P("dp", "cache"), P(("dp", "cache")))
    return jax.shard_map(local, mesh=mesh, in_specs=in_specs, out_specs=out_specs, check_vma=False)
```

profile of v0, /device:TPU:2, one launch (start us, length us, event | category | flops | bytes accessed | tf_op | source)
XLA Modules:
  0.0 421.0 jit_solution(10415780288378715552)
XLA Ops:
  8.0 0.9 fusion.15
  8.9 0.7 compare_convert_fusion
  10.1 0.8 bitcast_subtract_fusion
  11.0 1.9 copy.21
  12.9 1.8 copy.24
  14.7 1.3 fusion.9
  16.0 1.9 multiply_reduce_fusion.1
  17.9 5.7 %gather_fusion = bf16[64,32,1280]{2,1,0:T(8,128)(2,1)} fusion(bf16[64,32,1280]{2,1,0:T(8,128)(2,1)} %param.10, s32[1024]{0:T(1024)S(1)} %pad_clamp_fusion.1), kind=kCustom, calls=%fused_computation | custom fusion | bytes 10486016 | tf_op jit(solution)/shard_map/jit(_take)/gather | solution.py:48
  23.6 5.3 %bitcast_select_fusion = bf16[64,1,32,1280]{3,2,1,0:T(8,128)(2,1)} fusion(bf16[64,32,1280]{2,1,0:T(8,128)(2,1)} %gather_fusion, pred[64]{0:T(512)(128)(4,1)S(1)} %compare_and_fusion), kind=kLoop, calls=%fused_computation.8 | loop fusion | flops 2621440 | bytes 10485824 | tf_op jit(solution)/shard_map/jit(_take)/select_n | solution.py:48
  28.9 12.3 %all-to-all-start = ((bf16[64,1,32,1280]{3,2,1,0:T(8,128)(2,1)}), bf16[64,1,32,1280]{3,2,1,0:T(8,128)(2,1)}, u32[]{:S(2)}, u32[]{:S(2)}) async-start(bf16[64,1,32,1280]{3,2,1,0:T(8,128)(2,1)} %bitcast_select_fusion), calls=%async_computation | async-start | bytes 10485760 | tf_op jit(solution)/shard_map/all_to_all | solution.py:61
  41.3 0.7 all-gather.2.cloned.1.call-update
  42.0 0.8 dynamic_slice.9
  43.0 0.8 compare_and_fusion.1
  43.8 117.7 %all-to-all-done = bf16[64,1,32,1280]{3,2,1,0:T(8,128)(2,1)} async-done(((bf16[64,1,32,1280]{3,2,1,0:T(8,128)(2,1)}), bf16[64,1,32,1280]{3,2,1,0:T(8,128)(2,1)}, u32[]{:S(2)}, u32[]{:S(2)}) %all-to-all-start) | async-done | bytes 5242912 | tf_op jit(solution)/shard_map/all_to_all | solution.py:61
  161.5 4.7 %gather_fusion.1 = bf16[32,32,1280]{2,1,0:T(8,128)(2,1)} fusion(bf16[64,32,1280]{2,1,0:T(8,128)(2,1)} %bitcast.6, s32[1024]{0:T(1024)S(1)} %pad_clamp_fusion), kind=kCustom, calls=%fused_computation.1 | custom fusion | bytes 5243008 | tf_op jit(solution)/shard_map/jit(_take)/gather | solution.py:62
  166.2 2.8 convert_reduce_fusion
  169.0 17.6 %all-reduce = (f32[32,32]{1,0:T(8,128)S(1)}, f32[32,32]{1,0:T(8,128)S(1)}) all-reduce(f32[32,32]{1,0:T(8,128)S(1)} %get-tuple-element.11, f32[32,32]{1,0:T(8,128)S(1)} %get-tuple-element.10), channel_id=1, replica_groups=mesh['dp'=64,'cache'=4] {'cache'}, use_global_device_ids=true, to_apply=%region_8.9 | all-reduce | flops 2048 | bytes 16384 | tf_op jit(solution)/shard_map/psum | solution.py:13
  186.6 7.9 %multiply_reduce_fusion = (f32[32,32]{1,0:T(8,128)S(1)}, f32[32,32,1280]{2,1,0:T(8,128)}) fusion(f32[32,32]{1,0:T(8,128)S(1)} %get-tuple-element.19, f32[32,32]{1,0:T(8,128)S(1)} %get-tuple-element.18, bf16[32,32,1280]{2,1,0:T(8,128)(2,1)} %gather_fusion.1, pred[32]{0:T(512)(128)(4,1)S(1)} %get-tuple-element.16, bf16[32,32,1024]{2,1,0:T(8,128)(2,1)} %param.8, ...), kind=kOutput, calls=%fused_computation.9 | convolution fusion | flops 2693528576 | bytes 12595232 | tf_op jit(solution)/shard_map/dot_general | solution.py:69
  194.5 14.4 %psum.31 = f32[32,32]{1,0:T(8,128)S(1)} all-reduce(f32[32,32]{1,0:T(8,128)S(1)} %get-tuple-element.22), channel_id=1, replica_groups=mesh['dp'=64,'cache'=4] {'cache'}, use_global_device_ids=true, to_apply=%region_11.12 | all-reduce | flops 1024 | bytes 8192 | tf_op jit(solution)/shard_map/psum | solution.py:17
  209.1 8.5 %convolution_bitcast_fusion = f32[1024,1280]{0,1:T(8,128)} fusion(bf16[32,32,1024]{2,1,0:T(8,128)(2,1)} %param.8, f32[32,32,1280]{2,1,0:T(8,128)} %get-tuple-element.23, f32[32,32]{1,0:T(8,128)S(1)} %get-tuple-element.21), kind=kOutput, calls=%fused_computation.11 | convolution fusion | flops 2686976000 | bytes 12587008 | tf_op jit(solution)/shard_map/dot_general | solution.py:80
  218.3 2.9 fusion.8
  222.0 189.3 %all-reduce.3.cloned.1.call-done = f32[1024,1280]{0,1:T(8,128)} async-done(((f32[1024,1280]{0,1:T(8,128)}), f32[1024,1280]{0,1:T(8,128)}) %all-reduce.3.cloned.1.call-update) | async-done | bytes 5242896 | tf_op jit(solution)/shard_map/psum | solution.py:83
  411.4 1.3 constant_dynamic-slice_fusion
  412.7 0.8 copy.25
  (31 shorter events, 2.7 us)
Async XLA Ops:
  8.0 178.6 %copy-start = (bf16[1024,1280]{1,0:T(8,128)(2,1)S(1)}, bf16[1024,1280]{1,0:T(8,128)(2,1)}, u32[]{:S(2)}) copy-start(bf16[1024,1280]{1,0:T(8,128)(2,1)} %param.9) | copy-start | bytes 7864324
  28.9 13.1 %copy-start.3 = (s32[32]{0:T(128)S(1)}, s32[32]{0:T(128)}, u32[]{:S(2)}) copy-start(s32[32]{0:T(128)} %param.12) | copy-start | bytes 388
  28.9 132.6 %all-to-all-start = ((bf16[64,1,32,1280]{3,2,1,0:T(8,128)(2,1)}), bf16[64,1,32,1280]{3,2,1,0:T(8,128)(2,1)}, u32[]{:S(2)}, u32[]{:S(2)}) async-start(bf16[64,1,32,1280]{3,2,1,0:T(8,128)(2,1)} %bitcast_select_fusion), calls=%async_computation | async-start | bytes 10485760 | tf_op jit(solution)/shard_map/all_to_all | solution.py:61
  41.2 176.4 %all-gather.2.cloned.1.call-start = ((), (), s32[]{:S(2)}) async-start(), calls=%async_computation.2 | async-start | bytes 3158016 | tf_op jit(solution)/shard_map/all_gather | solution.py:87
  41.9 369.4 %all-reduce.3.cloned.1.call-start = ((), (), s32[]{:S(2)}) async-start(), calls=%async_computation.1 | async-start | bytes 10485760 | tf_op jit(solution)/shard_map/psum | solution.py:83
  217.6 0.7 copy-start.1
  217.6 3.6 copy-start.2
Sparse Core Ops, SparseCore 0:
  45.8 132.1 all-gather.1
Sparse Core Ops, SparseCore 1:
  217.7 193.6 all-reduce.2
where the time goes:
time: 422 us; the launch traced here: 421 us
  waiting for transfers between devices  308 us (73%)
  blocking collectives  32 us (8%)
  matrix products  19.2 us (5%)
  local copies, waits for them, and re-layouts  18 us (4%)
  other arithmetic  15.9 us (4%)
  between operations  15.6 us (4%)
  starting transfers between devices  12.4 us (3%)
    psum x1, waiting for transfers between devices, local(): summed = lax.psum(whole_term, 'dp')  189 us
    all_to_all x1, waiting for transfers between devices, local(): lax.all_to_all(outgoing, 'dp', split_axis=0, concat_axis=0, tiled=True)  118 us
    psum x1, blocking collectives, row_errors(): first_sum, square_sum = lax.psum((first_sum, square_sum), 'cache')  17.6 us
    psum x1, blocking collectives, row_errors(): squared = lax.psum(jnp.sum(residue * residue, axis=-1), 'cache')  14.4 us
    all_to_all x1, starting transfers between devices, local(): lax.all_to_all(outgoing, 'dp', split_axis=0, concat_axis=0, tiled=True)  12.3 us
    dot_general x1, matrix products, local(): lax.dot_general(tokens, row_grad, (((0,), (0,)), ((), ())), preferred_ele...  8.47 us
  transfers between devices with their start and end apart: 3, of which 2 were waited for; matrix products, arithmetic and copies ran while one was open for 7% of the time, Pallas kernels for 0%

commit v1 on v0

v1 whole, which is shorter than its diff:
```python
import jax
import jax.numpy as jnp
from jax import lax
from jax.experimental import pallas as pl
from jax.experimental.pallas import tpu as pltpu
from jax.sharding import PartitionSpec as P

eps = 1e-06
loss_scale = 128.0

N_X, N_Z, N_CORE = 4, 8, 2
EXT = 128
VMEM_BYTES = 60 * 1024 * 1024

X_GROUPS = [[x * N_Z * N_CORE + r for x in range(N_X)] for r in range(N_Z * N_CORE)]
Z_GROUPS = [
    [(x * N_Z + z) * N_CORE + c for z in range(N_Z)] for x in range(N_X) for c in range(N_CORE)
]


def params():
    return pltpu.CompilerParams(vmem_limit_bytes=VMEM_BYTES)


def dispatch_rows(student_feats, image_of, cache_pos, cols):
    n_dp = image_of.shape[0]
    rows = student_feats.shape[1]

    def kernel(scalars, feats, out, sems):
        first = pl.multiple_of(scalars[n_dp] * cols, cols)

        def copy(h):
            return pltpu.make_async_copy(
                feats.at[scalars[h], :, pl.ds(first, cols)], out.at[h], sems.at[h]
            )

        for h in range(n_dp):
            copy(h).start()
        for h in range(n_dp):
            copy(h).wait()

    scalars = jnp.concatenate([image_of, cache_pos[None]]).astype(jnp.int32)
    return pl.pallas_call(
        kernel,
        grid_spec=pltpu.PrefetchScalarGridSpec(
            num_scalar_prefetch=1,
            grid=(1,),
            in_specs=[pl.BlockSpec(memory_space=pl.ANY)],
            out_specs=pl.BlockSpec(memory_space=pl.ANY),
            scratch_shapes=[pltpu.SemaphoreType.DMA((n_dp,))],
        ),
        out_shape=jax.ShapeDtypeStruct((n_dp, rows, cols), student_feats.dtype),
        compiler_params=params(),
        name="dispatch_rows",
    )(scalars, student_feats)


def head_terms(scalars, x_own, x_prev, x_next, x_far_a, x_far_b, head_weight, teacher, row_info, full_cols):
    rows, part = x_own.shape
    width, cols = head_weight.shape
    n_part = width // part
    block = 256
    steps = rows // block
    half = steps // 2
    patch = 32
    img_block = block // patch
    n_img = rows // patch
    owner_rows = width // n_img
    out_rows = width // N_CORE

    def kernel(sc, x0, x1, x2, x3a, x3b, w_ref, t_ref, info_ref, keep, send, acc, r_scr):
        step = pl.program_id(0)
        here, core = sc[0], sc[1]
        far = jnp.where(step < half, x3a[...], x3b[...])
        xs = [x0[...], x1[...], x2[...], far]
        places = [lax.rem(here + off, n_part) for off in (0, n_part - 1, 1, 2)]
        pred = jnp.zeros((block, cols), jnp.float32)
        for x, place in zip(xs, places):
            first = pl.multiple_of(place * part, part)
            pred = pred + jnp.dot(
                x, w_ref[pl.ds(first, part), :], preferred_element_type=jnp.float32
            )
        info = info_ref[...]
        mean, inv, coef, weight = (info[:, k : k + 1] for k in range(4))
        residue = pred - (t_ref[...].astype(jnp.float32) - mean) * inv
        row_grad = (coef * residue).astype(jnp.bfloat16)
        row_loss = weight * jnp.sum(residue * residue, axis=-1, keepdims=True)
        row_loss = jnp.broadcast_to(row_loss, (block, EXT)).reshape(img_block, patch, EXT)
        r_scr[pl.ds(pl.multiple_of(step * img_block, img_block), img_block), :] = (
            jnp.sum(row_loss, axis=1) / full_cols
        )
        for x, place in zip(xs, places):
            term = lax.dot_general(
                x, row_grad, (((0,), (0,)), ((), ())), preferred_element_type=jnp.float32
            )

            @pl.when(step == 0)
            def _():
                acc[place] = term

            @pl.when(step > 0)
            def _():
                acc[place] += term

        @pl.when(step == steps - 1)
        def _():
            lane = lax.broadcasted_iota(jnp.int32, (1, EXT), 1)
            top = lax.broadcasted_iota(jnp.int32, (owner_rows, EXT), 0) == 0
            for pair in range(n_img // N_CORE):
                place, z = divmod(pair, N_Z)
                for ref, own in ((keep, core), (send, 1 - core)):
                    src = pl.multiple_of(z * N_CORE * owner_rows + own * owner_rows, owner_rows)
                    dst = slice(pair * owner_rows, (pair + 1) * owner_rows)
                    ref[dst, :cols] = acc[place, pl.ds(src, owner_rows), :]
                    image = pair * N_CORE + own
                    line = jnp.where(lane == sc[2 + image], r_scr[pl.ds(image, 1), :], 0.0)
                    ref[dst, cols:] = jnp.where(top, line, 0.0)

    row_spec = lambda c: pl.BlockSpec((block, c), lambda i, s: (i, 0))
    out_spec = pl.BlockSpec((out_rows, cols + EXT), lambda i, s: (0, 0))
    out = jax.ShapeDtypeStruct((out_rows, cols + EXT), jnp.float32)
    return pl.pallas_call(
        kernel,
        grid_spec=pltpu.PrefetchScalarGridSpec(
            num_scalar_prefetch=1,
            grid=(steps,),
            in_specs=[
                row_spec(part),
                row_spec(part),
                row_spec(part),
                pl.BlockSpec((block, part), lambda i, s: (jnp.minimum(i, half - 1), 0)),
                pl.BlockSpec((block, part), lambda i, s: (jnp.maximum(i - half, 0), 0)),
                pl.BlockSpec((width, cols), lambda i, s: (0, 0)),
                row_spec(cols),
                row_spec(row_info.shape[1]),
            ],
            out_specs=[out_spec, out_spec],
            scratch_shapes=[
                pltpu.VMEM((n_part, part, cols), jnp.float32),
                pltpu.VMEM((n_img, EXT), jnp.float32),
            ],
        ),
        out_shape=[out, out],
        compiler_params=params(),
        cost_estimate=pl.CostEstimate(
            flops=4 * rows * width * cols, bytes_accessed=20 * 2**20, transcendentals=0
        ),
        name="head_terms",
    )(scalars, x_own, x_prev, x_next, x_far_a, x_far_b, head_weight, teacher, row_info)


def exponent(part):
    top = jnp.max(jnp.abs(part), axis=-1, keepdims=True)
    return jnp.ceil(jnp.log(jnp.maximum(top, 2.0**-100)) * 1.4426950408889634)


def code(values):
    cols = values.shape[-1] - EXT
    main, extra = values[:, :cols], values[:, cols:]
    main_exp, extra_exp = exponent(main), exponent(extra)
    main_code = jnp.floor(main * jnp.exp2(14.0 - main_exp) + 0.5).astype(jnp.int32)
    extra_code = jnp.floor(extra * jnp.exp2(14.0 - extra_exp) + 0.5)
    lane = lax.broadcasted_iota(jnp.int32, extra.shape, 1)
    extra_code = jnp.where(
        lane == EXT - 2, main_exp, jnp.where(lane == EXT - 1, extra_exp, extra_code)
    ).astype(jnp.int32)
    return main_code.astype(jnp.int16), extra_code.astype(jnp.int16)


def decode(codes):
    cols = codes.shape[-1] - EXT
    wide = codes.astype(jnp.int32).astype(jnp.float32)
    main, extra = wide[:, :cols], wide[:, cols:]
    main_exp = extra[:, EXT - 2 : EXT - 1]
    extra_exp = extra[:, EXT - 1 :]
    lane = lax.broadcasted_iota(jnp.int32, extra.shape, 1)
    extra = jnp.where(lane < EXT - 2, extra, 0.0)
    return main * jnp.exp2(main_exp - 14.0), extra * jnp.exp2(extra_exp - 14.0)


def add_and_code(keep, received):
    rows, cols = keep.shape
    block = rows // N_X

    def kernel(a, b, out):
        main, extra = code(a[...] + b[...])
        out[:, : cols - EXT] = main
        out[:, cols - EXT :] = extra

    spec = pl.BlockSpec((block, cols), lambda i: (i, 0))
    return pl.pallas_call(
        kernel,
        grid=(N_X,),
        in_specs=[spec, spec],
        out_specs=spec,
        out_shape=jax.ShapeDtypeStruct((rows, cols), jnp.int16),
        compiler_params=params(),
        name="add_and_code",
    )(keep, received)


def sum_and_code(received):
    n, rows, cols = received.shape
    block = 32

    def kernel(src, out):
        main, extra = decode(src[0])
        for k in range(1, n):
            m, e = decode(src[k])
            main, extra = main + m, extra + e
        main, extra = code(jnp.concatenate([main, extra], axis=1))
        out[:, : cols - EXT] = main
        out[:, cols - EXT :] = extra

    return pl.pallas_call(
        kernel,
        grid=(rows // block,),
        in_specs=[pl.BlockSpec((n, block, cols), lambda i: (0, i, 0))],
        out_specs=pl.BlockSpec((block, cols), lambda i: (i, 0)),
        out_shape=jax.ShapeDtypeStruct((rows, cols), jnp.int16),
        compiler_params=params(),
        name="sum_and_code",
    )(received)


def sum_blocks(received):
    n, rows, cols = received.shape

    def kernel(src, out, ext):
        main, extra = decode(src[0])
        for k in range(1, n):
            m, e = decode(src[k])
            main, extra = main + m, extra + e
        out[...] = main
        ext[...] = extra

    return pl.pallas_call(
        kernel,
        out_shape=[
            jax.ShapeDtypeStruct((rows, cols - EXT), jnp.float32),
            jax.ShapeDtypeStruct((rows, EXT), jnp.float32),
        ],
        compiler_params=params(),
        name="sum_blocks",
    )(received)


def local(
    student_feats,
    head_weight,
    teacher_cache,
    holder_index,
    valid_count,
    image_embed,
    text_embed,
    pair_ids,
):
    n_dp = lax.axis_size("dp")
    n_cache = lax.axis_size("cache")
    own_index = lax.axis_index("dp")
    cache_pos = lax.axis_index("cache")
    core = own_index % N_CORE
    img_dev, patch_rows, student_width = student_feats.shape
    slots, _, local_cols = teacher_cache.shape
    full_cols = local_cols * n_cache
    part = student_width // n_cache
    shard_rows, embed = image_embed.shape
    assert slots == n_dp and n_dp == N_X * N_Z * N_CORE

    def ring(x, step):
        return lax.ppermute(x, "cache", [(i, (i + step) % n_cache) for i in range(n_cache)])

    img_order = jnp.arange(img_dev, dtype=jnp.int32)
    own_holders = lax.dynamic_slice_in_dim(holder_index, own_index * img_dev, img_dev, 0)
    dp_order = jnp.arange(n_dp, dtype=jnp.int32)
    image_of = jnp.sum(
        jnp.where(own_holders[None, :] == dp_order[:, None], img_order[None, :], 0), axis=1
    )
    outgoing = dispatch_rows(student_feats, image_of, cache_pos, part)

    counts_line = jnp.zeros((shard_rows, EXT), jnp.bfloat16).at[0, :img_dev].set(
        valid_count.astype(jnp.bfloat16)
    )
    text_all = lax.all_gather(
        jnp.concatenate([text_embed, counts_line], axis=1), "dp", axis=0, tiled=True
    )
    pair_cols = jnp.concatenate(
        [
            (pair_ids // 64)[:, None],
            (pair_ids % 64)[:, None],
            jnp.zeros((shard_rows, EXT - 2), jnp.int32),
        ],
        axis=1,
    ).astype(jnp.bfloat16)
    image_all = lax.all_gather(
        jnp.concatenate([image_embed, pair_cols], axis=1), "cache", axis=0, tiled=True
    )

    with jax.named_scope("student_exchange"):
        mine = lax.all_to_all(outgoing, "dp", split_axis=0, concat_axis=0, tiled=True)
    with jax.named_scope("student_ring"):
        from_prev = ring(mine, 1)
        from_next = ring(mine, -1)
        far_a = ring(from_prev[: n_dp // 2], 1)
        far_b = ring(from_next[n_dp // 2 :], -1)

    with jax.named_scope("teacher_sums"):
        wide = teacher_cache.astype(jnp.float32)
        sums = jnp.stack([jnp.sum(wide, axis=-1), jnp.sum(wide * wide, axis=-1)])
        sums = sums + ring(sums, 1) + ring(sums, 2) + ring(sums, 3)
        row_mean = sums[0] / full_cols
        inv_scale = lax.rsqrt(sums[1] / full_cols - row_mean * row_mean + eps)

    is_held = holder_index.reshape(n_dp, img_dev) == own_index
    counts_all = text_all.reshape(n_dp, shard_rows, embed + EXT)[:, 0, embed : embed + img_dev]
    place_of = jnp.sum(jnp.where(is_held, img_order[None, :], 0), axis=1)
    held_count = jnp.sum(jnp.where(is_held, counts_all.astype(jnp.float32), 0.0), axis=1)
    row_index = jnp.arange(patch_rows, dtype=jnp.int32).astype(jnp.float32)
    valid_mask = (row_index[None, :] < held_count[:, None]).astype(jnp.float32)
    row_weight = valid_mask / jnp.maximum(held_count, 1.0)[:, None]
    coef = 2.0 * loss_scale / full_cols * row_weight
    inv_scale = jnp.where(held_count[:, None] > 0, inv_scale, 0.0)
    row_info = jnp.stack([row_mean, inv_scale, coef, row_weight], axis=-1).reshape(
        n_dp * patch_rows, 4
    )

    with jax.named_scope("contrast"):
        images, pair_code = image_all[:, :embed], image_all[:, embed:].astype(jnp.int32)
        pairs = pair_code[:, 0] * 64 + pair_code[:, 1]
        logits = jnp.dot(
            images, text_all[:, :embed].T, preferred_element_type=jnp.float32
        ) * (embed ** (-0.5))
        column = jnp.arange(n_dp * shard_rows, dtype=jnp.int32)
        text_id = (column // shard_rows) * img_dev + cache_pos * shard_rows + column % shard_rows
        best = jnp.max(logits, axis=1)
        denom = jnp.sum(jnp.exp(logits - best[:, None]), axis=1)
        target = jnp.sum(jnp.where(pairs[:, None] == text_id[None, :], logits, 0.0), axis=1)

    scalars = jnp.concatenate([jnp.stack([cache_pos, core]).astype(jnp.int32), place_of])
    flat = lambda x: x.reshape(-1, x.shape[-1])
    keep, send = head_terms(
        scalars,
        flat(mine),
        flat(from_prev),
        flat(from_next),
        flat(far_a),
        flat(far_b),
        head_weight,
        flat(teacher_cache),
        row_info,
        full_cols,
    )
    with jax.named_scope("grad_core"):
        received = lax.ppermute(send, "dp", [(i, i ^ 1) for i in range(n_dp)])
    codes = add_and_code(keep, received)
    with jax.named_scope("grad_x"):
        codes = lax.all_to_all(
            codes.reshape(N_X, -1, local_cols + EXT), "dp", 0, 0, axis_index_groups=X_GROUPS, tiled=True
        )
    codes = sum_and_code(codes)
    with jax.named_scope("grad_z"):
        codes = lax.all_to_all(
            codes.reshape(N_Z, -1, local_cols + EXT), "dp", 0, 0, axis_index_groups=Z_GROUPS, tiled=True
        )
    head_grad, extra = sum_blocks(codes)

    with jax.named_scope("loss_parts"):
        parts = jnp.stack([extra[0, :img_dev], best, denom, target])
        parts = parts.reshape(4, n_cache, shard_rows).transpose(1, 0, 2)
        parts = lax.all_to_all(parts, "cache", split_axis=0, concat_axis=0, tiled=True)
        top = jnp.max(parts[:, 1], axis=0)
        total = jnp.sum(parts[:, 2] * jnp.exp(parts[:, 1] - top[None, :]), axis=0)
        contrast = top + jnp.log(total) - jnp.sum(parts[:, 3], axis=0)
        image_loss = jnp.sum(parts[:, 0], axis=0) + contrast
    return (head_grad, image_loss)


def solution(mesh):
    in_specs = (
        P("dp", None, None),
        P(None, "cache"),
        P("dp", None, "cache"),
        P(),
        P("dp"),
        P(("dp", "cache"), None),
        P(("dp", "cache"), None),
        P(("dp", "cache")),
    )
    out_specs = (P("dp", "cache"), P(("dp", "cache")))
    return jax.shard_map(local, mesh=mesh, in_specs=in_specs, out_specs=out_specs, check_vma=False)
```

time: 422 us -> 265 us (0.63)
  waiting for transfers between devices: 308 us -> 57.9 us
  Pallas kernels: 0 us -> 74.1 us
  blocking collectives: 32 us -> 78.3 us
  starting transfers between devices: 12.4 us -> 35.2 us
  matrix products: 19.2 us -> 0.44 us
  between operations: 15.6 us -> 0.88 us
  other arithmetic: 15.9 us -> 7 us
  local copies, waits for them, and re-layouts: 18 us -> 9.96 us
    psum x1 -> x0, waiting for transfers between devices: 189 us -> none  [local(): summed = lax.psum(whole_term, 'dp')]
    all_to_all x1, waiting for transfers between devices: 118 us -> 0.01 us  [local(): lax.all_to_all(outgoing, 'dp', split_axis=0, concat_axis=0, tiled=True)]
    pallas_call x0 -> x5, Pallas kernels: none -> 74.1 us  [the longest x1 34.1 us: dispatch_rows(): pl.pallas_call(kernel, grid_spec=pltpu.PrefetchScalarGridSpec(num_scalar_...]
    all_gather x0 -> x2, blocking collectives: none -> 70.6 us  [the longest x1 58.7 us: local(): lax.all_gather(jnp.concatenate([text_embed, counts_line], axis=1), 'dp',...]
    ppermute x0 -> x8, waiting for transfers between devices: none -> 39.9 us  [the longest x7 34.4 us: ring(): lax.ppermute(x, 'cache', [(i, (i + step) % n_cache) for i in range(n_cach...]
    psum x2 -> x0, blocking collectives: 32 us -> none  [the longest x1 17.6 us: row_errors(): first_sum, square_sum = lax.psum((first_sum, square_sum), 'cache')]
    dot_general x3 -> x1, matrix products: 19.2 us -> 0.44 us  [local(): jnp.dot(images, text_all[:, :embed].T, preferred_element_type=jnp.float32)]
    all_to_all x0 -> x2, waiting for transfers between devices: none -> 18 us  [the longest x1 12.1 us: local(): lax.all_to_all(codes.reshape(N_Z, -1, local_cols + EXT), 'dp', 0, 0, axis...]
  transfers between devices with their start and end apart: 3 -> 11, of which waited for: 2 -> 6; matrix products, arithmetic and copies ran while one was open for 7% -> 4% of each run, Pallas kernels for 0% -> 0%
where the time goes in v1:
time: 265 us; the launch traced here: 264 us
  blocking collectives  78.3 us (30%)
  Pallas kernels  74.1 us (28%)
  waiting for transfers between devices  57.9 us (22%)
  starting transfers between devices  35.2 us (13%)
  local copies, waits for them, and re-layouts  9.96 us (4%)
  other arithmetic  7 us (3%)
    all_gather x1, blocking collectives, local(): lax.all_gather(jnp.concatenate([text_embed, counts_line], axis=1), 'dp',...  58.7 us
    ppermute x7, waiting for transfers between devices, ring(): lax.ppermute(x, 'cache', [(i, (i + step) % n_cache) for i in range(n_cach...  34.4 us
    pallas_call x1, Pallas kernels, dispatch_rows(): pl.pallas_call(kernel, grid_spec=pltpu.PrefetchScalarGridSpec(num_scalar_...  34.1 us
    pallas_call x1, Pallas kernels, head_terms(): pl.pallas_call(kernel, grid_spec=pltpu.PrefetchScalarGridSpec(num_scalar_...  29.7 us
    ppermute x7, starting transfers between devices, ring(): lax.ppermute(x, 'cache', [(i, (i + step) % n_cache) for i in range(n_cach...  12.5 us
    all_to_all x1, waiting for transfers between devices, local(): lax.all_to_all(codes.reshape(N_Z, -1, local_cols + EXT), 'dp', 0, 0, axis...  12.1 us
    all_to_all x1, starting transfers between devices, local(): lax.all_to_all(outgoing, 'dp', split_axis=0, concat_axis=0, tiled=True)  12 us
    all_gather x1, blocking collectives, local(): lax.all_gather(jnp.concatenate([image_embed, pair_cols], axis=1), 'cache'...  11.9 us
  transfers between devices with their start and end apart: 11, of which 6 were waited for; matrix products, arithmetic and copies ran while one was open for 4% of the time, Pallas kernels for 0%

profile of v1, /device:TPU:2, one launch (start us, length us, event | category | flops | bytes accessed | tf_op | source)
XLA Modules:
  0.0 263.7 jit_solution(11227520100011510517)
XLA Ops:
  2.1 34.1 %dispatch_rows.1 = bf16[64,32,256]{2,1,0:T(8,128)(2,1)} custom-call(s32[65]{0:T(128)} %pad_add_fusion.1.scalars, bf16[32,32,1024]{2,1,0:T(8,128)(2,1)} %feats.1), custom_call_target="tpu_custom_call" | custom-call | tf_op jit(solution)/shard_map/dispatch_rows/pallas_call | solution.py:43
  36.2 12.0 %all-to-all-start = ((bf16[64,32,256]{2,1,0:T(8,128)(2,1)}), bf16[64,32,256]{2,1,0:T(8,128)(2,1)S(1)}, u32[]{:S(2)}, u32[]{:S(2)}) async-start(bf16[64,32,256]{2,1,0:T(8,128)(2,1)} %dispatch_rows.1), calls=%async_computation | async-start | bytes 2097152 | tf_op jit(solution)/shard_map/student_exchange/all_to_all | solution.py:300
  48.3 4.3 %convert_reduce_fusion = (f32[64,32]{1,0:T(8,128)S(1)}, f32[64,32]{1,0:T(8,128)S(1)}) fusion(bf16[64,32,1280]{2,1,0:T(8,128)(2,1)} %param.12), kind=kLoop, calls=%fused_computation.1 | loop fusion | flops 10481664 | bytes 5259264 | tf_op jit(solution)/shard_map/teacher_sums/reduce_sum | solution.py:309
  52.6 3.3 %collective-permute-start.5 = (f32[2,64,32]{2,1,0:T(8,128)S(1)}, f32[2,64,32]{2,1,0:T(8,128)S(1)}, u32[]{:S(2)}, u32[]{:S(2)}) collective-permute-start(f32[2,64,32]{2,1,0:T(8,128)S(1)} %pad_maximum_fusion), channel_id=1, source_target_pairs={{0,2},{1,3},{2,0},{3,1},{4,6},{5,7},{6,4},{7,5},{8,10},{9,11},{10,... | collective-permute-start | bytes 49160 | tf_op jit(solution)/shard_map/teacher_sums/ppermute | solution.py:271
  58.1 58.7 %all_gather.6 = bf16[512,896]{1,0:T(8,128)(2,1)S(1)} all-gather(bf16[8,896]{1,0:T(8,128)(2,1)S(1)} %fusion.6), channel_id=1, replica_groups=mesh['dp'=64,'cache'=4] {'dp'}, dimensions={0}, use_global_device_ids=true | all-gather | bytes 931840 | tf_op jit(solution)/shard_map/all_gather | solution.py:284
  117.1 3.1 %collective-permute-start.1 = (bf16[64,32,256]{2,1,0:T(8,128)(2,1)S(1)}, bf16[64,32,256]{2,1,0:T(8,128)(2,1)}, u32[]{:S(2)}, u32[]{:S(2)}) collective-permute-start(bf16[64,32,256]{2,1,0:T(8,128)(2,1)S(1)} %all-to-all-done), channel_id=1, source_target_pairs={{0,3},{1,0},{2,1},{3,2},{4,7},{5,4},{6,5},{7,6},{8,11},{9,8},{10,9... | collective-permute-start | bytes 3145736 | tf_op jit(solution)/shard_map/student_ring/ppermute | solution.py:271
  121.6 21.5 %collective-permute-done.1 = bf16[64,32,256]{2,1,0:T(8,128)(2,1)} collective-permute-done((bf16[64,32,256]{2,1,0:T(8,128)(2,1)S(1)}, bf16[64,32,256]{2,1,0:T(8,128)(2,1)}, u32[]{:S(2)}, u32[]{:S(2)}) %collective-permute-start.1) | collective-permute-done | bytes 1048608 | tf_op jit(solution)/shard_map/student_ring/ppermute | solution.py:271
  144.2 3.9 %collective-permute-start.3 = (bf16[32,32,256]{2,1,0:T(8,128)(2,1)S(1)}, bf16[32,32,256]{2,1,0:T(8,128)(2,1)}, u32[]{:S(2)}, u32[]{:S(2)}) collective-permute-start(bf16[32,32,256]{2,1,0:T(8,128)(2,1)S(1)} %slice.78), channel_id=1, source_target_pairs={{0,3},{1,0},{2,1},{3,2},{4,7},{5,4},{6,5},{7,6},{8,11},{9,8},{10,9... | collective-permute-start | bytes 1572872 | tf_op jit(solution)/shard_map/student_ring/ppermute | solution.py:271
  149.5 1.4 copy.34.info_ref
  150.9 8.0 %collective-permute-done.3 = bf16[32,32,256]{2,1,0:T(8,128)(2,1)} collective-permute-done((bf16[32,32,256]{2,1,0:T(8,128)(2,1)S(1)}, bf16[32,32,256]{2,1,0:T(8,128)(2,1)}, u32[]{:S(2)}, u32[]{:S(2)}) %collective-permute-start.3) | collective-permute-done | bytes 524320 | tf_op jit(solution)/shard_map/student_ring/ppermute | solution.py:271
  158.9 4.9 %collective-permute-done.2 = bf16[32,32,256]{2,1,0:T(8,128)(2,1)} collective-permute-done((bf16[32,32,256]{2,1,0:T(8,128)(2,1)S(1)}, bf16[32,32,256]{2,1,0:T(8,128)(2,1)}, u32[]{:S(2)}, u32[]{:S(2)}) %collective-permute-start.2) | collective-permute-done | bytes 524320 | tf_op jit(solution)/shard_map/student_ring/ppermute | solution.py:271
  163.8 29.7 %head_terms.1 = (f32[512,1408]{1,0:T(8,128)}, f32[512,1408]{1,0:T(8,128)}) custom-call(s32[66]{0:T(128)} %pad_add_fusion.sc, bf16[2048,256]{1,0:T(8,128)(2,1)} %bitcast.33, bf16[2048,256]{1,0:T(8,128)(2,1)} %bitcast.3.x1, bf16[2048,256]{1,0:T(8,128)(2,1)} %bitcast.4.x2, bf16[1024,256]{1,0:T(8,128)(2,1)} %bitcast.5.x3a, bf16[1024,256]{1,0:T(8,128)(2,1)} %bitcast.6.x3b, ...), custom_call_target="tpu_custom_call" | custom-call | flops 10737418240 | bytes 20971520 | tf_op jit(solution)/shard_map/head_terms/pallas_call | solution.py:122
  193.5 5.5 %collective-permute-done.7.b = f32[512,1408]{1,0:T(8,128)S(1)} collective-permute-done((f32[512,1408]{1,0:T(8,128)}, f32[512,1408]{1,0:T(8,128)S(1)}, u32[]{:S(2)}, u32[]{:S(2)}) %collective-permute-start.7) | collective-permute-done | bytes 2883616 | tf_op jit(solution)/shard_map/grad_core/ppermute | solution.py:354
  199.0 1.6 copy-done.1
  200.6 4.7 %add_and_code.1 = s16[512,1408]{1,0:T(8,128)(2,1)} custom-call(f32[512,1408]{1,0:T(8,128)} %get-tuple-element.18.a, f32[512,1408]{1,0:T(8,128)} %copy-done.1), custom_call_target="tpu_custom_call" | custom-call | tf_op jit(solution)/shard_map/add_and_code/pallas_call | solution.py:191
  205.4 4.9 %all-to-all-start.1 = ((s16[4,128,1408]{2,1,0:T(8,128)(2,1)}), s16[4,128,1408]{2,1,0:T(8,128)(2,1)S(1)}, u32[]{:S(2)}, u32[]{:S(2)}) async-start(s16[4,128,1408]{2,1,0:T(8,128)(2,1)} %bitcast.30), calls=%async_computation.1 | async-start | bytes 2883584 | tf_op jit(solution)/shard_map/grad_x/all_to_all | solution.py:357
  210.6 11.9 %all_gather.7 = bf16[32,896]{1,0:T(8,128)(2,1)S(1)} all-gather(bf16[8,896]{1,0:T(8,128)(2,1)S(1)} %maximum_maximum_fusion), channel_id=1, replica_groups=mesh['dp'=64,'cache'=4] {'cache'}, dimensions={0}, use_global_device_ids=true | all-gather | bytes 71680 | tf_op jit(solution)/shard_map/all_gather | solution.py:295
  222.5 5.9 %all-to-all-done.1.src = s16[4,128,1408]{2,1,0:T(8,128)(2,1)S(1)} async-done(((s16[4,128,1408]{2,1,0:T(8,128)(2,1)}), s16[4,128,1408]{2,1,0:T(8,128)(2,1)S(1)}, u32[]{:S(2)}, u32[]{:S(2)}) %all-to-all-start.1) | async-done | bytes 1441824 | tf_op jit(solution)/shard_map/grad_x/all_to_all | solution.py:357
  228.4 1.1 copy-done
  229.5 3.8 %sum_and_code.1 = s16[128,1408]{1,0:T(8,128)(2,1)} custom-call(s16[4,128,1408]{2,1,0:T(8,128)(2,1)} %copy-done), custom_call_target="tpu_custom_call" | custom-call | tf_op jit(solution)/shard_map/sum_and_code/pallas_call | solution.py:215
  233.3 5.8 %all-to-all-start.2 = ((s16[8,16,1408]{2,1,0:T(8,128)(2,1)}), s16[8,16,1408]{2,1,0:T(8,128)(2,1)S(1)}, u32[]{:S(2)}, u32[]{:S(2)}) async-start(s16[8,16,1408]{2,1,0:T(8,128)(2,1)} %bitcast.32), calls=%async_computation.2 | async-start | bytes 720896 | tf_op jit(solution)/shard_map/grad_z/all_to_all | solution.py:362
  240.2 12.1 %all-to-all-done.2.src = s16[8,16,1408]{2,1,0:T(8,128)(2,1)S(1)} async-done(((s16[8,16,1408]{2,1,0:T(8,128)(2,1)}), s16[8,16,1408]{2,1,0:T(8,128)(2,1)S(1)}, u32[]{:S(2)}, u32[]{:S(2)}) %all-to-all-start.2) | async-done | bytes 360480 | tf_op jit(solution)/shard_map/grad_z/all_to_all | solution.py:362
  253.0 1.7 sum_blocks.1
  255.5 7.7 %all_to_all.20 = f32[4,4,8]{2,1,0:T(4,128)S(1)} all-to-all(f32[4,4,8]{2,1,0:T(4,128)S(1)} %copy.37), channel_id=1, replica_groups=mesh['dp'=64,'cache'=4] {'cache'}, dimensions={0} | all-to-all | bytes 1024 | tf_op jit(solution)/shard_map/loss_parts/all_to_all | solution.py:370
  (78 shorter events, 11.3 us)
Async XLA Ops:
  36.2 80.8 %all-to-all-start = ((bf16[64,32,256]{2,1,0:T(8,128)(2,1)}), bf16[64,32,256]{2,1,0:T(8,128)(2,1)S(1)}, u32[]{:S(2)}, u32[]{:S(2)}) async-start(bf16[64,32,256]{2,1,0:T(8,128)(2,1)} %dispatch_rows.1), calls=%async_computation | async-start | bytes 2097152 | tf_op jit(solution)/shard_map/student_exchange/all_to_all | solution.py:300
  48.3 9.7 %copy-start.6 = (s32[2048]{0:T(1024)S(1)}, s32[2048]{0:T(1024)}, u32[]{:S(2)}) copy-start(s32[2048]{0:T(1024)} %param.13) | copy-start | bytes 24580
  48.3 9.7 %copy-start.7 = (s32[32]{0:T(128)S(1)}, s32[32]{0:T(128)}, u32[]{:S(2)}) copy-start(s32[32]{0:T(128)} %param.14) | copy-start | bytes 388
  48.3 9.7 %copy-start.4 = (bf16[8,768]{1,0:T(8,128)(2,1)S(1)}, bf16[8,768]{1,0:T(8,128)(2,1)}, u32[]{:S(2)}) copy-start(bf16[8,768]{1,0:T(8,128)(2,1)} %param.16) | copy-start | bytes 36868
  52.6 68.7 %collective-permute-start.5 = (f32[2,64,32]{2,1,0:T(8,128)S(1)}, f32[2,64,32]{2,1,0:T(8,128)S(1)}, u32[]{:S(2)}, u32[]{:S(2)}) collective-permute-start(f32[2,64,32]{2,1,0:T(8,128)S(1)} %pad_maximum_fusion), channel_id=1, source_target_pairs={{0,2},{1,3},{2,0},{3,1},{4,6},{5,7},{6,4},{7,5},{8,10},{9,11},{10,... | collective-permute-start | bytes 49160 | tf_op jit(solution)/shard_map/teacher_sums/ppermute | solution.py:271
  55.9 65.4 %collective-permute-start.6 = (f32[2,64,32]{2,1,0:T(8,128)S(1)}, f32[2,64,32]{2,1,0:T(8,128)S(1)}, u32[]{:S(2)}, u32[]{:S(2)}) collective-permute-start(f32[2,64,32]{2,1,0:T(8,128)S(1)} %pad_maximum_fusion), channel_id=1, source_target_pairs={{0,3},{1,0},{2,1},{3,2},{4,7},{5,4},{6,5},{7,6},{8,11},{9,8},{10,9... | collective-permute-start | bytes 49160 | tf_op jit(solution)/shard_map/teacher_sums/ppermute | solution.py:271
  57.0 64.4 %collective-permute-start.4 = (f32[2,64,32]{2,1,0:T(8,128)S(1)}, f32[2,64,32]{2,1,0:T(8,128)S(1)}, u32[]{:S(2)}, u32[]{:S(2)}) collective-permute-start(f32[2,64,32]{2,1,0:T(8,128)S(1)} %pad_maximum_fusion), channel_id=1, source_target_pairs={{0,1},{1,2},{2,3},{3,0},{4,5},{5,6},{6,7},{7,4},{8,9},{9,10},{10,1... | collective-permute-start | bytes 49160 | tf_op jit(solution)/shard_map/teacher_sums/ppermute | solution.py:271
  117.1 46.7 %copy-start.3 = (bf16[64,32,256]{2,1,0:T(8,128)(2,1)}, bf16[64,32,256]{2,1,0:T(8,128)(2,1)S(1)}, u32[]{:S(2)}) copy-start(bf16[64,32,256]{2,1,0:T(8,128)(2,1)S(1)} %all-to-all-done) | copy-start | bytes 3145732
  117.1 26.0 %collective-permute-start.1 = (bf16[64,32,256]{2,1,0:T(8,128)(2,1)S(1)}, bf16[64,32,256]{2,1,0:T(8,128)(2,1)}, u32[]{:S(2)}, u32[]{:S(2)}) collective-permute-start(bf16[64,32,256]{2,1,0:T(8,128)(2,1)S(1)} %all-to-all-done), channel_id=1, source_target_pairs={{0,3},{1,0},{2,1},{3,2},{4,7},{5,4},{6,5},{7,6},{8,11},{9,8},{10,9... | collective-permute-start | bytes 3145736 | tf_op jit(solution)/shard_map/student_ring/ppermute | solution.py:271
  120.2 27.9 %collective-permute-start = (bf16[64,32,256]{2,1,0:T(8,128)(2,1)S(1)}, bf16[64,32,256]{2,1,0:T(8,128)(2,1)}, u32[]{:S(2)}, u32[]{:S(2)}) collective-permute-start(bf16[64,32,256]{2,1,0:T(8,128)(2,1)S(1)} %all-to-all-done), channel_id=1, source_target_pairs={{0,1},{1,2},{2,3},{3,0},{4,5},{5,6},{6,7},{7,4},{8,9},{9,10},{10,1... | collective-permute-start | bytes 3145736 | tf_op jit(solution)/shard_map/student_ring/ppermute | solution.py:271
  144.2 14.8 %collective-permute-start.3 = (bf16[32,32,256]{2,1,0:T(8,128)(2,1)S(1)}, bf16[32,32,256]{2,1,0:T(8,128)(2,1)}, u32[]{:S(2)}, u32[]{:S(2)}) collective-permute-start(bf16[32,32,256]{2,1,0:T(8,128)(2,1)S(1)} %slice.78), channel_id=1, source_target_pairs={{0,3},{1,0},{2,1},{3,2},{4,7},{5,4},{6,5},{7,6},{8,11},{9,8},{10,9... | collective-permute-start | bytes 1572872 | tf_op jit(solution)/shard_map/student_ring/ppermute | solution.py:271
  149.1 14.7 %collective-permute-start.2 = (bf16[32,32,256]{2,1,0:T(8,128)(2,1)S(1)}, bf16[32,32,256]{2,1,0:T(8,128)(2,1)}, u32[]{:S(2)}, u32[]{:S(2)}) collective-permute-start(bf16[32,32,256]{2,1,0:T(8,128)(2,1)S(1)} %slice.77), channel_id=1, source_target_pairs={{0,1},{1,2},{2,3},{3,0},{4,5},{5,6},{6,7},{7,4},{8,9},{9,10},{10,1... | collective-permute-start | bytes 1572872 | tf_op jit(solution)/shard_map/student_ring/ppermute | solution.py:271
  193.5 5.5 %collective-permute-start.7 = (f32[512,1408]{1,0:T(8,128)}, f32[512,1408]{1,0:T(8,128)S(1)}, u32[]{:S(2)}, u32[]{:S(2)}) collective-permute-start(f32[512,1408]{1,0:T(8,128)} %get-tuple-element.19), channel_id=1, source_target_pairs={{0,4},{4,0},{8,12},{12,8},{16,20},{20,16},{24,28},{28,24},{32,36},... | collective-permute-start | bytes 8650760 | tf_op jit(solution)/shard_map/grad_core/ppermute | solution.py:354
  199.0 1.6 copy-start.1
  205.4 4.9 %copy-start.8 = (s32[8]{0:T(128)S(1)}, s32[8]{0:T(128)}, u32[]{:S(2)}) copy-start(s32[8]{0:T(128)} %param.17) | copy-start | bytes 100
  205.4 5.2 %copy-start.5 = (bf16[8,768]{1,0:T(8,128)(2,1)S(1)}, bf16[8,768]{1,0:T(8,128)(2,1)}, u32[]{:S(2)}) copy-start(bf16[8,768]{1,0:T(8,128)(2,1)} %param.15) | copy-start | bytes 36868
  205.4 23.0 %all-to-all-start.1 = ((s16[4,128,1408]{2,1,0:T(8,128)(2,1)}), s16[4,128,1408]{2,1,0:T(8,128)(2,1)S(1)}, u32[]{:S(2)}, u32[]{:S(2)}) async-start(s16[4,128,1408]{2,1,0:T(8,128)(2,1)} %bitcast.30), calls=%async_computation.1 | async-start | bytes 2883584 | tf_op jit(solution)/shard_map/grad_x/all_to_all | solution.py:357
  228.4 1.1 copy-start
  233.3 18.9 %all-to-all-start.2 = ((s16[8,16,1408]{2,1,0:T(8,128)(2,1)}), s16[8,16,1408]{2,1,0:T(8,128)(2,1)S(1)}, u32[]{:S(2)}, u32[]{:S(2)}) async-start(s16[8,16,1408]{2,1,0:T(8,128)(2,1)} %bitcast.32), calls=%async_computation.2 | async-start | bytes 720896 | tf_op jit(solution)/shard_map/grad_z/all_to_all | solution.py:362
  252.2 0.7 copy-start.2

commit v2 on v1

v2 whole, which is shorter than its diff:
```python
import jax
import jax.numpy as jnp
from jax import lax
from jax.experimental import pallas as pl
from jax.experimental.pallas import tpu as pltpu
from jax.sharding import PartitionSpec as P

eps = 1e-06
loss_scale = 128.0

N_X, N_Z, N_CORE = 4, 8, 2
EXT = 128
VMEM_BYTES = 60 * 1024 * 1024

X_GROUPS = [[x * N_Z * N_CORE + r for x in range(N_X)] for r in range(N_Z * N_CORE)]
Z_GROUPS = [
    [(x * N_Z + z) * N_CORE + c for z in range(N_Z)] for x in range(N_X) for c in range(N_CORE)
]


def params():
    return pltpu.CompilerParams(vmem_limit_bytes=VMEM_BYTES)


def dispatch_rows(student_feats, image_of, cache_pos, cols):
    n_dp = image_of.shape[0]
    images, rows, _ = student_feats.shape

    def kernel(scalars, feats, out):
        for h in range(n_dp):
            out[h] = feats[scalars[h]]

    scalars = jnp.concatenate([image_of, cache_pos[None]]).astype(jnp.int32)
    return pl.pallas_call(
        kernel,
        grid_spec=pltpu.PrefetchScalarGridSpec(
            num_scalar_prefetch=1,
            grid=(1,),
            in_specs=[pl.BlockSpec((images, rows, cols), lambda i, s: (0, 0, s[n_dp]))],
            out_specs=pl.BlockSpec((n_dp, rows, cols), lambda i, s: (0, 0, 0)),
        ),
        out_shape=jax.ShapeDtypeStruct((n_dp, rows, cols), student_feats.dtype),
        compiler_params=params(),
        name="dispatch_rows",
    )(scalars, student_feats)


def predict_rows(cache_pos, x_own, x_prev, x_next, x_far_a, x_far_b, head_weight, teacher, row_info, first_row, full_cols):
    rows, part = x_own.shape
    width, cols = head_weight.shape
    n_part = width // part
    block = 256
    steps = rows // block
    half = steps // 2
    first_step = first_row // block
    patch = 32
    img_block = block // patch

    def kernel(sc, x0, x1, x2, x3a, x3b, w_ref, t_ref, info_ref, x_out, grad_out, r_out):
        step = pl.program_id(0)
        far = jnp.where(step < half, x3a[...], x3b[...])
        xs = [x0[...], x1[...], x2[...], far]
        for x, off in zip(xs, (0, n_part - 1, 1, 2)):
            place = lax.rem(sc[0] + off, n_part)
            x_out[:, pl.ds(pl.multiple_of(place * part, part), part)] = x
        pred = jnp.dot(x_out[...], w_ref[...], preferred_element_type=jnp.float32)
        info = info_ref[...]
        mean, inv, coef, weight = (info[:, k : k + 1] for k in range(4))
        residue = pred - (t_ref[...].astype(jnp.float32) - mean) * inv
        grad_out[...] = (coef * residue).astype(jnp.bfloat16)
        row_loss = weight * jnp.sum(residue * residue, axis=-1, keepdims=True)
        row_loss = jnp.broadcast_to(row_loss, (block, EXT)).reshape(img_block, patch, EXT)
        r_out[...] = jnp.sum(row_loss, axis=1) / full_cols

    row_spec = lambda c: pl.BlockSpec((block, c), lambda i, s: (i, 0))
    at_spec = lambda c: pl.BlockSpec((block, c), lambda i, s: (i + first_step, 0))
    return pl.pallas_call(
        kernel,
        grid_spec=pltpu.PrefetchScalarGridSpec(
            num_scalar_prefetch=1,
            grid=(steps,),
            in_specs=[
                row_spec(part),
                row_spec(part),
                row_spec(part),
                pl.BlockSpec((block, part), lambda i, s: (jnp.minimum(i, half - 1), 0)),
                pl.BlockSpec((block, part), lambda i, s: (jnp.maximum(i - half, 0), 0)),
                pl.BlockSpec((width, cols), lambda i, s: (0, 0)),
                at_spec(cols),
                at_spec(row_info.shape[1]),
            ],
            out_specs=[
                row_spec(width),
                row_spec(cols),
                pl.BlockSpec((img_block, EXT), lambda i, s: (i, 0)),
            ],
        ),
        out_shape=[
            jax.ShapeDtypeStruct((rows, width), jnp.bfloat16),
            jax.ShapeDtypeStruct((rows, cols), jnp.bfloat16),
            jax.ShapeDtypeStruct((rows // patch, EXT), jnp.float32),
        ],
        compiler_params=params(),
        cost_estimate=pl.CostEstimate(
            flops=2 * rows * width * cols, bytes_accessed=12 * 2**20, transcendentals=0
        ),
        name="predict_rows",
    )(cache_pos[None].astype(jnp.int32), x_own, x_prev, x_next, x_far_a, x_far_b, head_weight, teacher, row_info)


OUTER = (((0,), (0,)), ((), ()))


def grad_part(student, row_grad):
    rows, width = student.shape
    cols = row_grad.shape[1]
    tile = 256

    def kernel(x_ref, g_ref, out):
        out[...] = lax.dot_general(x_ref[...], g_ref[...], OUTER, preferred_element_type=jnp.float32)

    return pl.pallas_call(
        kernel,
        grid=(cols // tile,),
        in_specs=[
            pl.BlockSpec((rows, width), lambda i: (0, 0)),
            pl.BlockSpec((rows, tile), lambda i: (0, i)),
        ],
        out_specs=pl.BlockSpec((width, tile), lambda i: (0, i)),
        out_shape=jax.ShapeDtypeStruct((width, cols), jnp.float32),
        compiler_params=params(),
        cost_estimate=pl.CostEstimate(
            flops=2 * rows * width * cols, bytes_accessed=10 * 2**20, transcendentals=0
        ),
        name="grad_part",
    )(student, row_grad)


def grad_split(core, student, row_grad, before):
    rows, width = student.shape
    cols = row_grad.shape[1]
    tile = 256
    pairs = N_X * N_Z
    owner_rows = width // (pairs * N_CORE)
    out_rows = width // N_CORE

    def kernel(sc, x_ref, g_ref, before_ref, keep, send):
        term = before_ref[...] + lax.dot_general(
            x_ref[...], g_ref[...], OUTER, preferred_element_type=jnp.float32
        )
        term = term.reshape(pairs, N_CORE, owner_rows, tile)
        for mine, (first, second) in enumerate(((keep, send), (send, keep))):

            @pl.when(sc[0] == mine)
            def _():
                first[...] = term[:, 0].reshape(out_rows, tile)
                second[...] = term[:, 1].reshape(out_rows, tile)

    out_spec = pl.BlockSpec((out_rows, tile), lambda i, s: (0, i))
    out = jax.ShapeDtypeStruct((out_rows, cols), jnp.float32)
    return pl.pallas_call(
        kernel,
        grid_spec=pltpu.PrefetchScalarGridSpec(
            num_scalar_prefetch=1,
            grid=(cols // tile,),
            in_specs=[
                pl.BlockSpec((rows, width), lambda i, s: (0, 0)),
                pl.BlockSpec((rows, tile), lambda i, s: (0, i)),
                pl.BlockSpec((width, tile), lambda i, s: (0, i)),
            ],
            out_specs=[out_spec, out_spec],
        ),
        out_shape=[out, out],
        compiler_params=params(),
        cost_estimate=pl.CostEstimate(
            flops=2 * rows * width * cols, bytes_accessed=15 * 2**20, transcendentals=0
        ),
        name="grad_split",
    )(core[None].astype(jnp.int32), student, row_grad, before)


def exponent(part):
    top = jnp.max(jnp.abs(part), axis=-1, keepdims=True)
    return jnp.ceil(jnp.log(jnp.maximum(top, 2.0**-100)) * 1.4426950408889634)


def code(main, extra):
    main_exp, extra_exp = exponent(main), exponent(extra)
    main_code = jnp.floor(main * jnp.exp2(14.0 - main_exp) + 0.5).astype(jnp.int32)
    extra_code = jnp.floor(extra * jnp.exp2(14.0 - extra_exp) + 0.5)
    lane = lax.broadcasted_iota(jnp.int32, extra.shape, 1)
    extra_code = jnp.where(
        lane == EXT - 2, main_exp, jnp.where(lane == EXT - 1, extra_exp, extra_code)
    ).astype(jnp.int32)
    return main_code.astype(jnp.int16), extra_code.astype(jnp.int16)


def decode(codes):
    cols = codes.shape[-1] - EXT
    wide = codes.astype(jnp.int32).astype(jnp.float32)
    main, extra = wide[:, :cols], wide[:, cols:]
    main_exp = extra[:, EXT - 2 : EXT - 1]
    extra_exp = extra[:, EXT - 1 :]
    lane = lax.broadcasted_iota(jnp.int32, extra.shape, 1)
    extra = jnp.where(lane < EXT - 2, extra, 0.0)
    return main * jnp.exp2(main_exp - 14.0), extra * jnp.exp2(extra_exp - 14.0)


def add_and_code(keep, received, losses):
    rows, cols = keep.shape
    pairs = losses.shape[0]
    owner_rows = rows // pairs
    block = rows // N_X

    def kernel(a, b, line_ref, out):
        n = block // owner_rows
        lines = jnp.broadcast_to(line_ref[...][:, None, :], (n, owner_rows, EXT))
        top = lax.broadcasted_iota(jnp.int32, lines.shape, 1) == 0
        lines = jnp.where(top, lines, 0.0).reshape(block, EXT)
        main, extra = code(a[...] + b[...], lines)
        out[:, :cols] = main
        out[:, cols:] = extra

    spec = lambda r, c: pl.BlockSpec((r, c), lambda i: (i, 0))
    return pl.pallas_call(
        kernel,
        grid=(N_X,),
        in_specs=[spec(block, cols), spec(block, cols), spec(pairs // N_X, EXT)],
        out_specs=spec(block, cols + EXT),
        out_shape=jax.ShapeDtypeStruct((rows, cols + EXT), jnp.int16),
        compiler_params=params(),
        name="add_and_code",
    )(keep, received, losses)


def sum_and_code(received):
    n, rows, cols = received.shape
    block = 32

    def kernel(src, out):
        main, extra = decode(src[0])
        for k in range(1, n):
            m, e = decode(src[k])
            main, extra = main + m, extra + e
        main, extra = code(main, extra)
        out[:, : cols - EXT] = main
        out[:, cols - EXT :] = extra

    return pl.pallas_call(
        kernel,
        grid=(rows // block,),
        in_specs=[pl.BlockSpec((n, block, cols), lambda i: (0, i, 0))],
        out_specs=pl.BlockSpec((block, cols), lambda i: (i, 0)),
        out_shape=jax.ShapeDtypeStruct((rows, cols), jnp.int16),
        compiler_params=params(),
        name="sum_and_code",
    )(received)


def sum_blocks(received):
    n, rows, cols = received.shape

    def kernel(src, out, ext):
        main, extra = decode(src[0])
        for k in range(1, n):
            m, e = decode(src[k])
            main, extra = main + m, extra + e
        out[...] = main
        ext[...] = extra

    return pl.pallas_call(
        kernel,
        out_shape=[
            jax.ShapeDtypeStruct((rows, cols - EXT), jnp.float32),
            jax.ShapeDtypeStruct((rows, EXT), jnp.float32),
        ],
        compiler_params=params(),
        name="sum_blocks",
    )(received)


def local(
    student_feats,
    head_weight,
    teacher_cache,
    holder_index,
    valid_count,
    image_embed,
    text_embed,
    pair_ids,
):
    n_dp = lax.axis_size("dp")
    n_cache = lax.axis_size("cache")
    own_index = lax.axis_index("dp")
    cache_pos = lax.axis_index("cache")
    core = own_index % N_CORE
    img_dev, patch_rows, student_width = student_feats.shape
    slots, _, local_cols = teacher_cache.shape
    full_cols = local_cols * n_cache
    part = student_width // n_cache
    shard_rows, embed = image_embed.shape
    assert slots == n_dp and n_dp == N_X * N_Z * N_CORE

    def ring(x, step):
        return lax.ppermute(x, "cache", [(i, (i + step) % n_cache) for i in range(n_cache)])

    def flat(x):
        return x.reshape(-1, x.shape[-1])

    img_order = jnp.arange(img_dev, dtype=jnp.int32)
    own_holders = lax.dynamic_slice_in_dim(holder_index, own_index * img_dev, img_dev, 0)
    dp_order = jnp.arange(n_dp, dtype=jnp.int32)
    image_of = jnp.sum(
        jnp.where(own_holders[None, :] == dp_order[:, None], img_order[None, :], 0), axis=1
    )
    outgoing = dispatch_rows(student_feats, image_of, cache_pos, part)

    text_all = lax.all_gather(text_embed, ("dp", "cache"), axis=0, tiled=True)

    with jax.named_scope("student_exchange"):
        mine = lax.all_to_all(outgoing, "dp", split_axis=0, concat_axis=0, tiled=True)
    chunk = n_dp // 2
    chunks = []
    with jax.named_scope("student_ring"):
        for first in range(0, n_dp, chunk):
            own = mine[first : first + chunk]
            from_prev = ring(own, 1)
            from_next = ring(own, -1)
            far_a = ring(from_prev[: chunk // 2], 1)
            far_b = ring(from_next[chunk // 2 :], -1)
            chunks.append([flat(x) for x in (own, from_prev, from_next, far_a, far_b)])

    with jax.named_scope("teacher_sums"):
        wide = teacher_cache.astype(jnp.float32)
        sums = jnp.stack([jnp.sum(wide, axis=-1), jnp.sum(wide * wide, axis=-1)])
        sums = sums + ring(sums, 1) + ring(sums, 2) + ring(sums, 3)
        row_mean = sums[0] / full_cols
        inv_scale = lax.rsqrt(sums[1] / full_cols - row_mean * row_mean + eps)

    is_held = holder_index.reshape(n_dp, img_dev) == own_index
    counts_all = lax.all_gather(valid_count, "dp").reshape(n_dp, img_dev)
    place_of = jnp.sum(jnp.where(is_held, img_order[None, :], 0), axis=1)
    held_count = jnp.sum(jnp.where(is_held, counts_all.astype(jnp.float32), 0.0), axis=1)
    row_index = jnp.arange(patch_rows, dtype=jnp.int32).astype(jnp.float32)
    valid_mask = (row_index[None, :] < held_count[:, None]).astype(jnp.float32)
    row_weight = valid_mask / jnp.maximum(held_count, 1.0)[:, None]
    coef = 2.0 * loss_scale / full_cols * row_weight
    inv_scale = jnp.where(held_count[:, None] > 0, inv_scale, 0.0)
    row_info = jnp.stack([row_mean, inv_scale, coef, row_weight], axis=-1).reshape(
        n_dp * patch_rows, 4
    )

    with jax.named_scope("contrast"):
        logits = jnp.dot(
            image_embed, text_all.T, preferred_element_type=jnp.float32
        ) * (embed ** (-0.5))
        column = jnp.arange(text_all.shape[0], dtype=jnp.int32)
        best = jnp.max(logits, axis=1)
        denom = jnp.sum(jnp.exp(logits - best[:, None]), axis=1)
        target = jnp.sum(jnp.where(pair_ids[:, None] == column[None, :], logits, 0.0), axis=1)
        contrast = best + jnp.log(denom) - target

    outs = [
        predict_rows(cache_pos, *rows, head_weight, flat(teacher_cache), row_info, k * chunk * patch_rows, full_cols)
        for k, rows in enumerate(chunks)
    ]
    with jax.named_scope("image_sums"):
        r = jnp.concatenate([o[2] for o in outs])
        r = r + ring(r, 1) + ring(r, 2) + ring(r, 3)
        other_r = lax.ppermute(r, "dp", [(i, i ^ 1) for i in range(n_dp)])
        other_held = holder_index.reshape(n_dp, img_dev) == (own_index ^ 1)
        other_place = jnp.sum(jnp.where(other_held, img_order[None, :], 0), axis=1)
        lane = jnp.arange(EXT, dtype=jnp.int32)[None, :]
        losses = jnp.where(lane == place_of[:, None], r, 0.0) + jnp.where(
            lane == other_place[:, None], other_r, 0.0
        )
        losses = losses.reshape(n_dp // N_CORE, N_CORE, EXT)
        losses = jnp.where(core == 0, losses[:, 0], losses[:, 1])
    before = grad_part(outs[0][0], outs[0][1])
    keep, send = grad_split(core, outs[1][0], outs[1][1], before)
    with jax.named_scope("grad_core"):
        received = lax.ppermute(send, "dp", [(i, i ^ 1) for i in range(n_dp)])
    codes = add_and_code(keep, received, losses)
    with jax.named_scope("grad_x"):
        codes = lax.all_to_all(
            codes.reshape(N_X, -1, local_cols + EXT), "dp", 0, 0, axis_index_groups=X_GROUPS, tiled=True
        )
    codes = sum_and_code(codes)
    with jax.named_scope("grad_z"):
        codes = lax.all_to_all(
            codes.reshape(N_Z, -1, local_cols + EXT), "dp", 0, 0, axis_index_groups=Z_GROUPS, tiled=True
        )
    head_grad, extra = sum_blocks(codes)

    regress = lax.dynamic_slice_in_dim(extra[0], cache_pos * shard_rows, shard_rows, 0)
    image_loss = regress + contrast
    return (head_grad, image_loss)


def solution(mesh):
    in_specs = (
        P("dp", None, None),
        P(None, "cache"),
        P("dp", None, "cache"),
        P(),
        P("dp"),
        P(("dp", "cache"), None),
        P(("dp", "cache"), None),
        P(("dp", "cache")),
    )
    out_specs = (P("dp", "cache"), P(("dp", "cache")))
    return jax.shard_map(local, mesh=mesh, in_specs=in_specs, out_specs=out_specs, check_vma=False)
```

time: 265 us -> 206 us (0.78)
  waiting for transfers between devices: 57.9 us -> 28.4 us
  Pallas kernels: 74.1 us -> 47.3 us
  blocking collectives: 78.3 us -> 52.5 us
  between operations: 0.88 us -> 15.1 us
  starting transfers between devices: 35.2 us -> 40.3 us
    all_gather x2 -> x0, blocking collectives: 70.6 us -> none  [the longest x1 58.7 us: local(): lax.all_gather(jnp.concatenate([text_embed, counts_line], axis=1), 'dp',...]
    pallas_call x1, Pallas kernels: 34.1 us -> 2.76 us  [dispatch_rows(): pl.pallas_call(kernel, grid_spec=pltpu.PrefetchScalarGridSpec(num_scalar_...]
    unnamed x0 -> x1, blocking collectives: none -> 27.5 us
    ppermute x7 -> x14, waiting for transfers between devices: 34.4 us -> 17 us  [ring(): lax.ppermute(x, 'cache', [(i, (i + step) % n_cache) for i in range(n_cach...]
    all_to_all x1, blocking collectives: 7.65 us -> 25 us  [local(): lax.all_to_all(codes.reshape(N_X, -1, local_cols + EXT), 'dp', 0, 0, axis...]
    ppermute x7 -> x14, starting transfers between devices: 12.5 us -> 23.2 us  [ring(): lax.ppermute(x, 'cache', [(i, (i + step) % n_cache) for i in range(n_cach...]
    all_to_all x1 -> x0, waiting for transfers between devices: 5.9 us -> none  [local(): lax.all_to_all(codes.reshape(N_X, -1, local_cols + EXT), 'dp', 0, 0, axis...]
    ppermute x1, waiting for transfers between devices: 5.49 us -> 0.01 us  [local(): received = lax.ppermute(send, 'dp', [(i, i ^ 1) for i in range(n_dp)])]
  transfers between devices with their start and end apart: 11 -> 19, of which waited for: 6 -> 6; matrix products, arithmetic and copies ran while one was open for 4% -> 7% of each run, Pallas kernels for 0% -> 21%
where the time goes in v2:
time: 206 us; the launch traced here: 205 us
  blocking collectives  52.5 us (25%)
  Pallas kernels  47.3 us (23%)
  starting transfers between devices  40.3 us (20%)
  waiting for transfers between devices  28.4 us (14%)
  between operations  15.1 us (7%)
  local copies, waits for them, and re-layouts  11.6 us (6%)
  other arithmetic  6.88 us (3%)
  matrix products  2.92 us (1%)
    unnamed x1, blocking collectives  27.5 us
    all_to_all x1, blocking collectives, local(): lax.all_to_all(codes.reshape(N_X, -1, local_cols + EXT), 'dp', 0, 0, axis...  25 us
    ppermute x14, starting transfers between devices, ring(): lax.ppermute(x, 'cache', [(i, (i + step) % n_cache) for i in range(n_cach...  23.2 us
    ppermute x14, waiting for transfers between devices, ring(): lax.ppermute(x, 'cache', [(i, (i + step) % n_cache) for i in range(n_cach...  17 us
    pallas_call x2, Pallas kernels, predict_rows(): pl.pallas_call(kernel, grid_spec=pltpu.PrefetchScalarGridSpec(num_scalar_...  16.8 us
    all_to_all x1, starting transfers between devices, local(): lax.all_to_all(outgoing, 'dp', split_axis=0, concat_axis=0, tiled=True)  12 us
    all_to_all x1, waiting for transfers between devices, local(): lax.all_to_all(codes.reshape(N_Z, -1, local_cols + EXT), 'dp', 0, 0, axis...  10.3 us
    pallas_call x1, Pallas kernels, grad_split(): pl.pallas_call(kernel, grid_spec=pltpu.PrefetchScalarGridSpec(num_scalar_...  9.46 us
  transfers between devices with their start and end apart: 19, of which 6 were waited for; matrix products, arithmetic and copies ran while one was open for 7% of the time, Pallas kernels for 21%

profile of v2, /device:TPU:2, one launch (start us, length us, event | category | flops | bytes accessed | tf_op | source)
XLA Modules:
  0.0 205.0 jit_solution(9745019388124341063)
XLA Ops:
  8.7 2.8 %dispatch_rows.1 = bf16[64,32,256]{2,1,0:T(8,128)(2,1)} custom-call(s32[65]{0:T(128)} %pad_add_fusion.scalars, bf16[32,32,1024]{2,1,0:T(8,128)(2,1)} %feats.1), custom_call_target="tpu_custom_call" | custom-call | tf_op jit(solution)/shard_map/dispatch_rows/pallas_call | solution.py:34
  11.4 12.0 %all-to-all-start = ((bf16[64,32,256]{2,1,0:T(8,128)(2,1)}), bf16[64,32,256]{2,1,0:T(8,128)(2,1)S(1)}, u32[]{:S(2)}, u32[]{:S(2)}) async-start(bf16[64,32,256]{2,1,0:T(8,128)(2,1)} %dispatch_rows.1), calls=%async_computation | async-start | bytes 2097152 | tf_op jit(solution)/shard_map/student_exchange/all_to_all | solution.py:321
  23.5 4.3 %convert_reduce_fusion = (f32[64,32]{1,0:T(8,128)S(1)}, f32[64,32]{1,0:T(8,128)S(1)}) fusion(bf16[64,32,1280]{2,1,0:T(8,128)(2,1)} %param.10), kind=kLoop, calls=%fused_computation.1 | loop fusion | flops 10481664 | bytes 5259264 | tf_op jit(solution)/shard_map/teacher_sums/reduce_sum | solution.py:335
  27.8 1.7 collective-permute-start.4
  29.5 2.9 %collective-permute-start.5 = (f32[2,64,32]{2,1,0:T(8,128)S(1)}, f32[2,64,32]{2,1,0:T(8,128)S(1)}, u32[]{:S(2)}, u32[]{:S(2)}) collective-permute-start(f32[2,64,32]{2,1,0:T(8,128)S(1)} %pad_maximum_fusion), channel_id=1, source_target_pairs={{0,2},{1,3},{2,0},{3,1},{4,6},{5,7},{6,4},{7,5},{8,10},{9,11},{10,... | collective-permute-start | bytes 49160 | tf_op jit(solution)/shard_map/teacher_sums/ppermute | solution.py:305
  35.4 27.5 %all-reduce = s32[2048]{0:T(1024)S(1)} all-reduce(s32[2048]{0:T(1024)S(1)} %dynamic-update-slice), channel_id=2, replica_groups=mesh['dp'=64,'cache'=4] {'dp'}, use_global_device_ids=true, to_apply=%add | all-reduce | flops 2048 | bytes 16384
  64.9 1.7 collective-permute-start.8
  67.8 2.9 %collective-permute-start.1 = (bf16[32,32,256]{2,1,0:T(8,128)(2,1)S(1)}, bf16[32,32,256]{2,1,0:T(8,128)(2,1)S(1)}, u32[]{:S(2)}, u32[]{:S(2)}) collective-permute-start(bf16[32,32,256]{2,1,0:T(8,128)(2,1)S(1)} %get-tuple-element.29), channel_id=1, source_target_pairs={{0,3},{1,0},{2,1},{3,2},{4,7},{5,4},{6,5},{7,6},{8,11},{9,8},{10,9... | collective-permute-start | bytes 1572872 | tf_op jit(solution)/shard_map/student_ring/ppermute | solution.py:305
  70.7 8.7 %collective-permute-done.7 = bf16[32,32,256]{2,1,0:T(8,128)(2,1)S(1)} collective-permute-done((bf16[32,32,256]{2,1,0:T(8,128)(2,1)S(1)}, bf16[32,32,256]{2,1,0:T(8,128)(2,1)S(1)}, u32[]{:S(2)}, u32[]{:S(2)}) %collective-permute-start.7) | collective-permute-done | bytes 524320 | tf_op jit(solution)/shard_map/student_ring/ppermute | solution.py:305
  81.3 2.9 %collective-permute-start.10 = (bf16[16,32,256]{2,1,0:T(8,128)(2,1)}, bf16[16,32,256]{2,1,0:T(8,128)(2,1)}, u32[]{:S(2)}, u32[]{:S(2)}) collective-permute-start(bf16[16,32,256]{2,1,0:T(8,128)(2,1)} %slice.51), channel_id=1, source_target_pairs={{0,3},{1,0},{2,1},{3,2},{4,7},{5,4},{6,5},{7,6},{8,11},{9,8},{10,9... | collective-permute-start | bytes 786440 | tf_op jit(solution)/shard_map/student_ring/ppermute | solution.py:305
  85.6 5.5 %collective-permute-done = bf16[32,32,256]{2,1,0:T(8,128)(2,1)S(1)} collective-permute-done((bf16[32,32,256]{2,1,0:T(8,128)(2,1)S(1)}, bf16[32,32,256]{2,1,0:T(8,128)(2,1)S(1)}, u32[]{:S(2)}, u32[]{:S(2)}) %collective-permute-start) | collective-permute-done | bytes 524320 | tf_op jit(solution)/shard_map/student_ring/ppermute | solution.py:305
  93.0 3.0 %collective-permute-start.3 = (bf16[16,32,256]{2,1,0:T(8,128)(2,1)}, bf16[16,32,256]{2,1,0:T(8,128)(2,1)S(1)}, u32[]{:S(2)}, u32[]{:S(2)}) collective-permute-start(bf16[16,32,256]{2,1,0:T(8,128)(2,1)} %slice.46), channel_id=1, source_target_pairs={{0,3},{1,0},{2,1},{3,2},{4,7},{5,4},{6,5},{7,6},{8,11},{9,8},{10,9... | collective-permute-start | bytes 786440 | tf_op jit(solution)/shard_map/student_ring/ppermute | solution.py:305
  96.7 8.3 %predict_rows.3 = (bf16[1024,1024]{1,0:T(8,128)(2,1)}, bf16[1024,1280]{1,0:T(8,128)(2,1)}, f32[32,128]{1,0:T(8,128)}) custom-call(s32[1]{0:T(128)} %bitcast.1.sc, bf16[1024,256]{1,0:T(8,128)(2,1)} %bitcast.33, bf16[1024,256]{1,0:T(8,128)(2,1)} %bitcast.35, bf16[1024,256]{1,0:T(8,128)(2,1)} %bitcast.36, bf16[512,256]{1,0:T(8,128)(2,1)} %bitcast.43, ...), custom_call_target="tpu_custom_call" | custom-call | flops 2684354560 | bytes 12582912 | tf_op jit(solution)/shard_map/predict_rows/pallas_call | solution.py:77
  104.9 8.1 %grad_part.1.before_ref = f32[1024,1280]{1,0:T(8,128)} custom-call(bf16[1024,1024]{1,0:T(8,128)(2,1)} %get-tuple-element.14.x_ref, bf16[1024,1280]{1,0:T(8,128)(2,1)} %get-tuple-element.15.g_ref), custom_call_target="tpu_custom_call" | custom-call | flops 2684354560 | bytes 10485760 | tf_op jit(solution)/shard_map/grad_part/pallas_call | solution.py:122
  113.8 8.5 %predict_rows.2 = (bf16[1024,1024]{1,0:T(8,128)(2,1)}, bf16[1024,1280]{1,0:T(8,128)(2,1)}, f32[32,128]{1,0:T(8,128)}) custom-call(s32[1]{0:T(128)} %bitcast.1.sc, bf16[1024,256]{1,0:T(8,128)(2,1)} %bitcast.32, bf16[1024,256]{1,0:T(8,128)(2,1)} %bitcast.37, bf16[1024,256]{1,0:T(8,128)(2,1)} %bitcast.38, bf16[512,256]{1,0:T(8,128)(2,1)} %bitcast.44, ...), custom_call_target="tpu_custom_call" | custom-call | flops 2684354560 | bytes 12582912 | tf_op jit(solution)/shard_map/predict_rows/pallas_call | solution.py:77
  122.3 9.5 %grad_split.1 = (f32[512,1280]{1,0:T(8,128)}, f32[512,1280]{1,0:T(8,128)}) custom-call(s32[1]{0:T(128)} %bitcast.sc, bf16[1024,1024]{1,0:T(8,128)(2,1)} %get-tuple-element.12.x_ref, bf16[1024,1280]{1,0:T(8,128)(2,1)} %get-tuple-element.13.g_ref, f32[1024,1280]{1,0:T(8,128)} %grad_part.1.before_ref), custom_call_target="tpu_custom_call" | custom-call | flops 2684354560 | bytes 15728640 | tf_op jit(solution)/shard_map/grad_split/pallas_call | solution.py:161
  132.1 2.9 %collective-permute-start.13 = (f32[64,128]{1,0:T(8,128)S(1)}, f32[64,128]{1,0:T(8,128)S(1)}, u32[]{:S(2)}, u32[]{:S(2)}) collective-permute-start(f32[64,128]{1,0:T(8,128)S(1)} %constant_dynamic-update-slice_fusion), channel_id=1, source_target_pairs={{0,2},{1,3},{2,0},{3,1},{4,6},{5,7},{6,4},{7,5},{8,10},{9,11},{10,... | collective-permute-start | bytes 98312 | tf_op jit(solution)/shard_map/image_sums/ppermute | solution.py:305
  142.5 4.7 %add_and_code.1 = s16[512,1408]{1,0:T(8,128)(2,1)} custom-call(f32[512,1280]{1,0:T(8,128)} %get-tuple-element.16.a, f32[512,1280]{1,0:T(8,128)} %copy-done.1, f32[32,128]{1,0:T(8,128)} %select_bitcast_fusion.line_ref), custom_call_target="tpu_custom_call" | custom-call | tf_op jit(solution)/shard_map/add_and_code/pallas_call | solution.py:225
  147.2 25.0 %all_to_all.15.src = s16[4,128,1408]{2,1,0:T(8,128)(2,1)} all-to-all(s16[4,128,1408]{2,1,0:T(8,128)(2,1)} %bitcast.31), channel_id=1, replica_groups={{0,64,128,192},{4,68,132,196},{8,72,136,200},{12,76,140,204},{16,80,144..., dimensions={0} | all-to-all | bytes 2883584 | tf_op jit(solution)/shard_map/grad_x/all_to_all | solution.py:385
  172.2 3.8 %sum_and_code.1 = s16[128,1408]{1,0:T(8,128)(2,1)} custom-call(s16[4,128,1408]{2,1,0:T(8,128)(2,1)} %all_to_all.15.src), custom_call_target="tpu_custom_call" | custom-call | tf_op jit(solution)/shard_map/sum_and_code/pallas_call | solution.py:249
  176.0 4.9 %all-to-all-start.2 = ((s16[8,16,1408]{2,1,0:T(8,128)(2,1)}), s16[8,16,1408]{2,1,0:T(8,128)(2,1)S(1)}, u32[]{:S(2)}, u32[]{:S(2)}) async-start(s16[8,16,1408]{2,1,0:T(8,128)(2,1)} %bitcast.34), calls=%async_computation.2 | async-start | bytes 720896 | tf_op jit(solution)/shard_map/grad_z/all_to_all | solution.py:390
  180.9 2.9 %fusion.5 = (f32[8]{0:T(128)S(1)}, f32[8,2048]{1,0:T(8,128)S(1)}) fusion(bf16[8,768]{1,0:T(8,128)(2,1)S(1)} %copy-done, bf16[2048,768]{1,0:T(8,128)(2,1)} %all-gather.3.cloned.1.call-done), kind=kOutput, calls=%fused_computation.37 | convolution fusion | flops 25198584 | bytes 3223584 | tf_op jit(solution)/shard_map/contrast/dot_general | solution.py:354
  184.1 10.3 %all-to-all-done.2.src = s16[8,16,1408]{2,1,0:T(8,128)(2,1)S(1)} async-done(((s16[8,16,1408]{2,1,0:T(8,128)(2,1)}), s16[8,16,1408]{2,1,0:T(8,128)(2,1)S(1)}, u32[]{:S(2)}, u32[]{:S(2)}) %all-to-all-start.2) | async-done | bytes 360480 | tf_op jit(solution)/shard_map/grad_z/all_to_all | solution.py:390
  195.1 1.7 sum_blocks.1
  (109 shorter events, 23.6 us)
Async XLA Ops:
  7.2 173.8 %copy-start = (bf16[8,768]{1,0:T(8,128)(2,1)S(1)}, bf16[8,768]{1,0:T(8,128)(2,1)}, u32[]{:S(2)}) copy-start(bf16[8,768]{1,0:T(8,128)(2,1)} %param.13) | copy-start | bytes 36868
  11.4 51.7 %all-to-all-start = ((bf16[64,32,256]{2,1,0:T(8,128)(2,1)}), bf16[64,32,256]{2,1,0:T(8,128)(2,1)S(1)}, u32[]{:S(2)}, u32[]{:S(2)}) async-start(bf16[64,32,256]{2,1,0:T(8,128)(2,1)} %dispatch_rows.1), calls=%async_computation | async-start | bytes 2097152 | tf_op jit(solution)/shard_map/student_exchange/all_to_all | solution.py:321
  23.5 157.4 %all-gather.3.cloned.1.call-start = ((), (), s32[]{:S(2)}) async-start(), calls=%async_computation.3 | async-start | bytes 3158016 | tf_op jit(solution)/shard_map/all_gather | solution.py:318
  27.8 39.3 %collective-permute-start.4 = (f32[2,64,32]{2,1,0:T(8,128)S(1)}, f32[2,64,32]{2,1,0:T(8,128)S(1)}, u32[]{:S(2)}, u32[]{:S(2)}) collective-permute-start(f32[2,64,32]{2,1,0:T(8,128)S(1)} %pad_maximum_fusion), channel_id=1, source_target_pairs={{0,1},{1,2},{2,3},{3,0},{4,5},{5,6},{6,7},{7,4},{8,9},{9,10},{10,1... | collective-permute-start | bytes 49160 | tf_op jit(solution)/shard_map/teacher_sums/ppermute | solution.py:305
  29.5 37.7 %collective-permute-start.5 = (f32[2,64,32]{2,1,0:T(8,128)S(1)}, f32[2,64,32]{2,1,0:T(8,128)S(1)}, u32[]{:S(2)}, u32[]{:S(2)}) collective-permute-start(f32[2,64,32]{2,1,0:T(8,128)S(1)} %pad_maximum_fusion), channel_id=1, source_target_pairs={{0,2},{1,3},{2,0},{3,1},{4,6},{5,7},{6,4},{7,5},{8,10},{9,11},{10,... | collective-permute-start | bytes 49160 | tf_op jit(solution)/shard_map/teacher_sums/ppermute | solution.py:305
  32.4 34.8 %collective-permute-start.6 = (f32[2,64,32]{2,1,0:T(8,128)S(1)}, f32[2,64,32]{2,1,0:T(8,128)S(1)}, u32[]{:S(2)}, u32[]{:S(2)}) collective-permute-start(f32[2,64,32]{2,1,0:T(8,128)S(1)} %pad_maximum_fusion), channel_id=1, source_target_pairs={{0,3},{1,0},{2,1},{3,2},{4,7},{5,4},{6,5},{7,6},{8,11},{9,8},{10,9... | collective-permute-start | bytes 49160 | tf_op jit(solution)/shard_map/teacher_sums/ppermute | solution.py:305
  63.2 32.7 %copy-start.3 = (bf16[32,32,256]{2,1,0:T(8,128)(2,1)}, bf16[32,32,256]{2,1,0:T(8,128)(2,1)S(1)}, u32[]{:S(2)}) copy-start(bf16[32,32,256]{2,1,0:T(8,128)(2,1)S(1)} %get-tuple-element.28) | copy-start | bytes 1572868
  63.2 41.7 %copy-start.2 = (bf16[32,32,256]{2,1,0:T(8,128)(2,1)}, bf16[32,32,256]{2,1,0:T(8,128)(2,1)S(1)}, u32[]{:S(2)}) copy-start(bf16[32,32,256]{2,1,0:T(8,128)(2,1)S(1)} %get-tuple-element.29) | copy-start | bytes 1572868
  63.2 16.2 %collective-permute-start.7 = (bf16[32,32,256]{2,1,0:T(8,128)(2,1)S(1)}, bf16[32,32,256]{2,1,0:T(8,128)(2,1)S(1)}, u32[]{:S(2)}, u32[]{:S(2)}) collective-permute-start(bf16[32,32,256]{2,1,0:T(8,128)(2,1)S(1)} %get-tuple-element.28), channel_id=1, source_target_pairs={{0,1},{1,2},{2,3},{3,0},{4,5},{5,6},{6,7},{7,4},{8,9},{9,10},{10,1... | collective-permute-start | bytes 1572872 | tf_op jit(solution)/shard_map/student_ring/ppermute | solution.py:305
  64.9 15.7 %collective-permute-start.8 = (bf16[32,32,256]{2,1,0:T(8,128)(2,1)S(1)}, bf16[32,32,256]{2,1,0:T(8,128)(2,1)S(1)}, u32[]{:S(2)}, u32[]{:S(2)}) collective-permute-start(bf16[32,32,256]{2,1,0:T(8,128)(2,1)S(1)} %get-tuple-element.28), channel_id=1, source_target_pairs={{0,3},{1,0},{2,1},{3,2},{4,7},{5,4},{6,5},{7,6},{8,11},{9,8},{10,9... | collective-permute-start | bytes 1572872 | tf_op jit(solution)/shard_map/student_ring/ppermute | solution.py:305
  67.4 23.8 %collective-permute-start = (bf16[32,32,256]{2,1,0:T(8,128)(2,1)S(1)}, bf16[32,32,256]{2,1,0:T(8,128)(2,1)S(1)}, u32[]{:S(2)}, u32[]{:S(2)}) collective-permute-start(bf16[32,32,256]{2,1,0:T(8,128)(2,1)S(1)} %get-tuple-element.29), channel_id=1, source_target_pairs={{0,1},{1,2},{2,3},{3,0},{4,5},{5,6},{6,7},{7,4},{8,9},{9,10},{10,1... | collective-permute-start | bytes 1572872 | tf_op jit(solution)/shard_map/student_ring/ppermute | solution.py:305
  67.8 24.4 %collective-permute-start.1 = (bf16[32,32,256]{2,1,0:T(8,128)(2,1)S(1)}, bf16[32,32,256]{2,1,0:T(8,128)(2,1)S(1)}, u32[]{:S(2)}, u32[]{:S(2)}) collective-permute-start(bf16[32,32,256]{2,1,0:T(8,128)(2,1)S(1)} %get-tuple-element.29), channel_id=1, source_target_pairs={{0,3},{1,0},{2,1},{3,2},{4,7},{5,4},{6,5},{7,6},{8,11},{9,8},{10,9... | collective-permute-start | bytes 1572872 | tf_op jit(solution)/shard_map/student_ring/ppermute | solution.py:305
  79.4 16.6 %copy-start.5 = (bf16[32,32,256]{2,1,0:T(8,128)(2,1)}, bf16[32,32,256]{2,1,0:T(8,128)(2,1)S(1)}, u32[]{:S(2)}) copy-start(bf16[32,32,256]{2,1,0:T(8,128)(2,1)S(1)} %collective-permute-done.7) | copy-start | bytes 1572868
  80.2 15.8 %collective-permute-start.9 = (bf16[16,32,256]{2,1,0:T(8,128)(2,1)}, bf16[16,32,256]{2,1,0:T(8,128)(2,1)S(1)}, u32[]{:S(2)}, u32[]{:S(2)}) collective-permute-start(bf16[16,32,256]{2,1,0:T(8,128)(2,1)} %slice.50), channel_id=1, source_target_pairs={{0,1},{1,2},{2,3},{3,0},{4,5},{5,6},{6,7},{7,4},{8,9},{9,10},{10,1... | collective-permute-start | bytes 786440 | tf_op jit(solution)/shard_map/student_ring/ppermute | solution.py:305
  80.5 15.4 %copy-start.6 = (bf16[32,32,256]{2,1,0:T(8,128)(2,1)}, bf16[32,32,256]{2,1,0:T(8,128)(2,1)S(1)}, u32[]{:S(2)}) copy-start(bf16[32,32,256]{2,1,0:T(8,128)(2,1)S(1)} %collective-permute-done.8) | copy-start | bytes 1572868
  81.3 14.7 %collective-permute-start.10 = (bf16[16,32,256]{2,1,0:T(8,128)(2,1)}, bf16[16,32,256]{2,1,0:T(8,128)(2,1)}, u32[]{:S(2)}, u32[]{:S(2)}) collective-permute-start(bf16[16,32,256]{2,1,0:T(8,128)(2,1)} %slice.51), channel_id=1, source_target_pairs={{0,3},{1,0},{2,1},{3,2},{4,7},{5,4},{6,5},{7,6},{8,11},{9,8},{10,9... | collective-permute-start | bytes 786440 | tf_op jit(solution)/shard_map/student_ring/ppermute | solution.py:305
  91.9 21.1 %collective-permute-start.2 = (bf16[16,32,256]{2,1,0:T(8,128)(2,1)}, bf16[16,32,256]{2,1,0:T(8,128)(2,1)S(1)}, u32[]{:S(2)}, u32[]{:S(2)}) collective-permute-start(bf16[16,32,256]{2,1,0:T(8,128)(2,1)} %slice.45), channel_id=1, source_target_pairs={{0,1},{1,2},{2,3},{3,0},{4,5},{5,6},{6,7},{7,4},{8,9},{9,10},{10,1... | collective-permute-start | bytes 786440 | tf_op jit(solution)/shard_map/student_ring/ppermute | solution.py:305
  93.0 20.0 %collective-permute-start.3 = (bf16[16,32,256]{2,1,0:T(8,128)(2,1)}, bf16[16,32,256]{2,1,0:T(8,128)(2,1)S(1)}, u32[]{:S(2)}, u32[]{:S(2)}) collective-permute-start(bf16[16,32,256]{2,1,0:T(8,128)(2,1)} %slice.46), channel_id=1, source_target_pairs={{0,3},{1,0},{2,1},{3,2},{4,7},{5,4},{6,5},{7,6},{8,11},{9,8},{10,9... | collective-permute-start | bytes 786440 | tf_op jit(solution)/shard_map/student_ring/ppermute | solution.py:305
  131.8 9.1 %collective-permute-start.11 = (f32[512,1280]{1,0:T(8,128)}, f32[512,1280]{1,0:T(8,128)S(1)}, u32[]{:S(2)}, u32[]{:S(2)}) collective-permute-start(f32[512,1280]{1,0:T(8,128)} %get-tuple-element.17), channel_id=1, source_target_pairs={{0,4},{4,0},{8,12},{12,8},{16,20},{20,16},{24,28},{28,24},{32,36},... | collective-permute-start | bytes 7864328 | tf_op jit(solution)/shard_map/grad_core/ppermute | solution.py:382
  131.8 5.9 %collective-permute-start.12 = (f32[64,128]{1,0:T(8,128)S(1)}, f32[64,128]{1,0:T(8,128)S(1)}, u32[]{:S(2)}, u32[]{:S(2)}) collective-permute-start(f32[64,128]{1,0:T(8,128)S(1)} %constant_dynamic-update-slice_fusion), channel_id=1, source_target_pairs={{0,1},{1,2},{2,3},{3,0},{4,5},{5,6},{6,7},{7,4},{8,9},{9,10},{10,1... | collective-permute-start | bytes 98312 | tf_op jit(solution)/shard_map/image_sums/ppermute | solution.py:305
  132.1 5.6 %collective-permute-start.13 = (f32[64,128]{1,0:T(8,128)S(1)}, f32[64,128]{1,0:T(8,128)S(1)}, u32[]{:S(2)}, u32[]{:S(2)}) collective-permute-start(f32[64,128]{1,0:T(8,128)S(1)} %constant_dynamic-update-slice_fusion), channel_id=1, source_target_pairs={{0,2},{1,3},{2,0},{3,1},{4,6},{5,7},{6,4},{7,5},{8,10},{9,11},{10,... | collective-permute-start | bytes 98312 | tf_op jit(solution)/shard_map/image_sums/ppermute | solution.py:305
  135.0 3.9 %collective-permute-start.14 = (f32[64,128]{1,0:T(8,128)S(1)}, f32[64,128]{1,0:T(8,128)S(1)}, u32[]{:S(2)}, u32[]{:S(2)}) collective-permute-start(f32[64,128]{1,0:T(8,128)S(1)} %constant_dynamic-update-slice_fusion), channel_id=1, source_target_pairs={{0,3},{1,0},{2,1},{3,2},{4,7},{5,4},{6,5},{7,6},{8,11},{9,8},{10,9... | collective-permute-start | bytes 98312 | tf_op jit(solution)/shard_map/image_sums/ppermute | solution.py:305
  138.9 1.3 collective-permute-start.15
  176.0 18.4 %all-to-all-start.2 = ((s16[8,16,1408]{2,1,0:T(8,128)(2,1)}), s16[8,16,1408]{2,1,0:T(8,128)(2,1)S(1)}, u32[]{:S(2)}, u32[]{:S(2)}) async-start(s16[8,16,1408]{2,1,0:T(8,128)(2,1)} %bitcast.34), calls=%async_computation.2 | async-start | bytes 720896 | tf_op jit(solution)/shard_map/grad_z/all_to_all | solution.py:390
  (13 other events, 94.1 us)
Sparse Core Ops, SparseCore 0:
  33.9 104.2 all-gather.2

commit v3 on v1

v3 whole, which is shorter than its diff:
```python
import jax
import jax.numpy as jnp
from jax import lax
from jax.experimental import pallas as pl
from jax.experimental.pallas import tpu as pltpu
from jax.sharding import PartitionSpec as P

eps = 1e-06
loss_scale = 128.0

N_X, N_Z, N_CORE = 4, 8, 2
EXT = 128
VMEM_BYTES = 60 * 1024 * 1024

X_GROUPS = [[x * N_Z * N_CORE + r for x in range(N_X)] for r in range(N_Z * N_CORE)]
Z_GROUPS = [
    [(x * N_Z + z) * N_CORE + c for z in range(N_Z)] for x in range(N_X) for c in range(N_CORE)
]


def params():
    return pltpu.CompilerParams(vmem_limit_bytes=VMEM_BYTES)


def dispatch_rows(student_feats, image_of, cache_pos, cols):
    n_dp = image_of.shape[0]
    images, rows, _ = student_feats.shape

    def kernel(scalars, feats, out):
        for h in range(n_dp):
            out[h] = feats[scalars[h]]

    scalars = jnp.concatenate([image_of, cache_pos[None]]).astype(jnp.int32)
    return pl.pallas_call(
        kernel,
        grid_spec=pltpu.PrefetchScalarGridSpec(
            num_scalar_prefetch=1,
            grid=(1,),
            in_specs=[pl.BlockSpec((images, rows, cols), lambda i, s: (0, 0, s[n_dp]))],
            out_specs=pl.BlockSpec((n_dp, rows, cols), lambda i, s: (0, 0, 0)),
        ),
        out_shape=jax.ShapeDtypeStruct((n_dp, rows, cols), student_feats.dtype),
        compiler_params=params(),
        name="dispatch_rows",
    )(scalars, student_feats)


OUTER = (((0,), (0,)), ((), ()))


def head_terms(scalars, rows_by_place, head_weight, teacher, row_info, first_row, full_cols, before=None):
    rows, part = rows_by_place[0].shape
    width, cols = head_weight.shape
    n_part = width // part
    block, tile, patch = 256, 256, 32
    steps = rows // block
    half = steps // 2
    first_step = first_row // block
    img_block = block // patch
    pairs = N_X * N_Z
    owner_rows = width // (pairs * N_CORE)
    out_rows = width // N_CORE
    last = before is not None

    def kernel(sc, x0, x1, x2, x3a, x3b, w_ref, t_ref, info_ref, *rest):
        before_ref = rest[0] if last else None
        grads, (r_out, x_scr, g_scr) = (rest[1:3], rest[3:]) if last else (rest[:1], rest[1:])
        step = pl.program_id(0)

        @pl.when(step < steps)
        def _():
            here = pl.ds(pl.multiple_of(step * block, block), block)
            far = jnp.where(step < half, x3a[...], x3b[...])
            xs = [x0[...], x1[...], x2[...], far]
            for x, off in zip(xs, (0, n_part - 1, 1, 2)):
                place = lax.rem(sc[0] + off, n_part)
                x_scr[here, pl.ds(pl.multiple_of(place * part, part), part)] = x
            pred = jnp.dot(x_scr[here, :], w_ref[...], preferred_element_type=jnp.float32)
            info = info_ref[...]
            mean, inv, coef, weight = (info[:, k : k + 1] for k in range(4))
            residue = pred - (t_ref[...].astype(jnp.float32) - mean) * inv
            g_scr[here, :] = (coef * residue).astype(jnp.bfloat16)
            row_loss = weight * jnp.sum(residue * residue, axis=-1, keepdims=True)
            row_loss = jnp.broadcast_to(row_loss, (block, EXT)).reshape(img_block, patch, EXT)
            r_out[pl.ds(pl.multiple_of(step * img_block, img_block), img_block), :] = (
                jnp.sum(row_loss, axis=1) / full_cols
            )

        @pl.when(step >= steps)
        def _():
            first = pl.multiple_of((step - steps) * tile, tile)
            term = lax.dot_general(
                x_scr[...], g_scr[:, pl.ds(first, tile)], OUTER, preferred_element_type=jnp.float32
            )
            if not last:
                grads[0][...] = term
                return
            term = (before_ref[...] + term).reshape(pairs, N_CORE, owner_rows, tile)
            keep, send = grads
            for mine, (one, two) in enumerate(((keep, send), (send, keep))):

                @pl.when(sc[1] == mine)
                def _():
                    one[...] = term[:, 0].reshape(out_rows, tile)
                    two[...] = term[:, 1].reshape(out_rows, tile)

    row_at = lambda i: jnp.minimum(i, steps - 1)
    col_at = lambda i: jnp.maximum(i - steps, 0)
    row_spec = lambda c: pl.BlockSpec((block, c), lambda i, s: (row_at(i), 0))
    at_spec = lambda c: pl.BlockSpec((block, c), lambda i, s: (row_at(i) + first_step, 0))
    far_spec = lambda f: pl.BlockSpec((block, part), lambda i, s: (jnp.clip(f(i), 0, half - 1), 0))
    col_spec = lambda r: pl.BlockSpec((r, tile), lambda i, s: (0, col_at(i)))
    grad_shapes = [(out_rows, cols)] * 2 if last else [(width, cols)]
    return pl.pallas_call(
        kernel,
        grid_spec=pltpu.PrefetchScalarGridSpec(
            num_scalar_prefetch=1,
            grid=(steps + cols // tile,),
            in_specs=[
                row_spec(part),
                row_spec(part),
                row_spec(part),
                far_spec(lambda i: i),
                far_spec(lambda i: i - half),
                pl.BlockSpec((width, cols), lambda i, s: (0, 0)),
                at_spec(cols),
                at_spec(row_info.shape[1]),
            ]
            + ([col_spec(width)] if last else []),
            out_specs=[col_spec(g[0]) for g in grad_shapes]
            + [pl.BlockSpec((rows // patch, EXT), lambda i, s: (0, 0))],
            scratch_shapes=[
                pltpu.VMEM((rows, width), jnp.bfloat16),
                pltpu.VMEM((rows, cols), jnp.bfloat16),
            ],
        ),
        out_shape=[jax.ShapeDtypeStruct(g, jnp.float32) for g in grad_shapes]
        + [jax.ShapeDtypeStruct((rows // patch, EXT), jnp.float32)],
        compiler_params=params(),
        cost_estimate=pl.CostEstimate(
            flops=4 * rows * width * cols, bytes_accessed=20 * 2**20, transcendentals=0
        ),
        name="head_terms",
    )(scalars, *rows_by_place, head_weight, teacher, row_info, *([before] if last else []))


def quantize(part):
    top = jnp.max(jnp.abs(part), axis=-1, keepdims=True)
    exp = jnp.ceil(jnp.log(jnp.maximum(top, 2.0**-100)) * 1.4426950408889634)
    codes = jnp.floor(part * jnp.exp2(14.0 - exp) + 0.5).astype(jnp.int32)
    return codes.astype(jnp.int16), exp


def widen(codes):
    return codes.astype(jnp.int32).astype(jnp.float32)


def add_and_code(keep, received):
    rows, cols = keep.shape
    block = rows // N_X

    def kernel(a, b, out):
        out[:, :cols], exp = quantize(a[...] + b[...])
        out[:, cols:] = jnp.broadcast_to(exp, (block, EXT)).astype(jnp.int32).astype(jnp.int16)

    spec = lambda c: pl.BlockSpec((block, c), lambda i: (i, 0))
    return pl.pallas_call(
        kernel,
        grid=(N_X,),
        in_specs=[spec(cols), spec(cols)],
        out_specs=spec(cols + EXT),
        out_shape=jax.ShapeDtypeStruct((rows, cols + EXT), jnp.int16),
        compiler_params=params(),
        name="add_and_code",
    )(keep, received)


def sum_codes(src, n, cols):
    total = 0.0
    for k in range(n):
        total = total + widen(src[k, :, :cols]) * jnp.exp2(widen(src[k, :, cols:])[:, EXT - 1 :] - 14.0)
    return total


def sum_and_code(received, losses):
    n, rows, wide = received.shape
    cols = wide - EXT
    block = 32

    def kernel(src, loss_ref, out):
        out[:, :cols], exp = quantize(sum_codes(src, n, cols))
        loss = loss_ref[...]
        loss_code, loss_exp = quantize(loss)
        lane = lax.broadcasted_iota(jnp.int32, loss.shape, 1)
        extra = jnp.where(lane == EXT - 2, loss_exp, widen(loss_code))
        extra = jnp.where(lane == EXT - 1, exp, extra)
        out[:, cols:] = extra.astype(jnp.int32).astype(jnp.int16)

    return pl.pallas_call(
        kernel,
        grid=(rows // block,),
        in_specs=[
            pl.BlockSpec((n, block, wide), lambda i: (0, i, 0)),
            pl.BlockSpec((block, EXT), lambda i: (i, 0)),
        ],
        out_specs=pl.BlockSpec((block, wide), lambda i: (i, 0)),
        out_shape=jax.ShapeDtypeStruct((rows, wide), jnp.int16),
        compiler_params=params(),
        name="sum_and_code",
    )(received, losses)


def sum_blocks(received):
    n, rows, wide = received.shape
    cols = wide - EXT

    def kernel(src, out, ext):
        out[...] = sum_codes(src, n, cols)
        total = 0.0
        for k in range(n):
            extra = widen(src[k, :, cols:])
            total = total + extra * jnp.exp2(extra[:, EXT - 2 : EXT - 1] - 14.0)
        ext[...] = total

    return pl.pallas_call(
        kernel,
        out_shape=[
            jax.ShapeDtypeStruct((rows, cols), jnp.float32),
            jax.ShapeDtypeStruct((rows, EXT), jnp.float32),
        ],
        compiler_params=params(),
        name="sum_blocks",
    )(received)


def local(
    student_feats,
    head_weight,
    teacher_cache,
    holder_index,
    valid_count,
    image_embed,
    text_embed,
    pair_ids,
):
    n_dp = lax.axis_size("dp")
    n_cache = lax.axis_size("cache")
    own_index = lax.axis_index("dp")
    cache_pos = lax.axis_index("cache")
    core = own_index % N_CORE
    img_dev, patch_rows, student_width = student_feats.shape
    slots, _, local_cols = teacher_cache.shape
    full_cols = local_cols * n_cache
    part = student_width // n_cache
    shard_rows, embed = image_embed.shape
    assert slots == n_dp and n_dp == N_X * N_Z * N_CORE

    def ring(x, step):
        return lax.ppermute(x, "cache", [(i, (i + step) % n_cache) for i in range(n_cache)])

    def flat(x):
        return x.reshape(-1, x.shape[-1])

    img_order = jnp.arange(img_dev, dtype=jnp.int32)
    own_holders = lax.dynamic_slice_in_dim(holder_index, own_index * img_dev, img_dev, 0)
    dp_order = jnp.arange(n_dp, dtype=jnp.int32)
    image_of = jnp.sum(
        jnp.where(own_holders[None, :] == dp_order[:, None], img_order[None, :], 0), axis=1
    )
    outgoing = dispatch_rows(student_feats, image_of, cache_pos, part)

    def swap(x, bit):
        return lax.ppermute(x, "dp", [(i, i ^ bit) for i in range(n_dp)])

    def both(x, other, bit, index):
        upper = (index // bit) % 2 == 1
        return jnp.concatenate([jnp.where(upper, other, x), jnp.where(upper, x, other)])

    with jax.named_scope("texts"):
        counts_line = jnp.zeros((shard_rows, EXT), jnp.bfloat16).at[0, :img_dev].set(
            valid_count.astype(jnp.bfloat16)
        )
        texts = jnp.concatenate([text_embed, counts_line], axis=1)
        for bit in (1, 2 * N_Z, 4 * N_Z):
            texts = both(texts, swap(texts, bit), bit, own_index)
        counts_line = texts.reshape(N_X * N_CORE, shard_rows, embed + EXT)[:, 0, embed:]
        texts = texts[:, :embed]
        for bit in (1, 2):
            other = lax.ppermute(texts, "cache", [(i, i ^ bit) for i in range(n_cache)])
            texts = both(texts, other, bit, cache_pos)
    with jax.named_scope("images"):
        pair_cols = jnp.concatenate(
            [
                (pair_ids // 64)[:, None],
                (pair_ids % 64)[:, None],
                jnp.zeros((shard_rows, EXT - 2), jnp.int32),
            ],
            axis=1,
        ).astype(jnp.bfloat16)
        images = jnp.concatenate([image_embed, pair_cols, counts_line], axis=1)
        for bit in (2, 4, 8):
            images = both(images, swap(images, bit), bit, own_index)

    with jax.named_scope("student_exchange"):
        mine = lax.all_to_all(outgoing, "dp", split_axis=0, concat_axis=0, tiled=True)
    chunk = n_dp // 2
    chunks = []
    with jax.named_scope("student_ring"):
        for first in range(0, n_dp, chunk):
            own = mine[first : first + chunk]
            if chunks:
                own = lax.optimization_barrier((own, from_prev, from_next))[0]
            from_prev = ring(own, 1)
            from_next = ring(own, -1)
            far_a = ring(from_prev[: chunk // 2], 1)
            far_b = ring(from_next[chunk // 2 :], -1)
            chunks.append([flat(x) for x in (own, from_prev, from_next, far_a, far_b)])

    with jax.named_scope("teacher_sums"):
        wide = teacher_cache.astype(jnp.float32)
        sums = jnp.stack([jnp.sum(wide, axis=-1), jnp.sum(wide * wide, axis=-1)])
        sums = sums + ring(sums, 1) + ring(sums, 2) + ring(sums, 3)
        row_mean = sums[0] / full_cols
        inv_scale = lax.rsqrt(sums[1] / full_cols - row_mean * row_mean + eps)

    is_held = holder_index.reshape(n_dp, img_dev) == own_index
    counts_all = (
        images[:, embed + EXT : embed + EXT + img_dev]
        .reshape(N_Z, N_X, N_CORE, img_dev)
        .transpose(1, 0, 2, 3)
        .reshape(n_dp, img_dev)
    )
    place_of = jnp.sum(jnp.where(is_held, img_order[None, :], 0), axis=1)
    held_count = jnp.sum(jnp.where(is_held, counts_all.astype(jnp.float32), 0.0), axis=1)
    row_index = jnp.arange(patch_rows, dtype=jnp.int32).astype(jnp.float32)
    valid_mask = (row_index[None, :] < held_count[:, None]).astype(jnp.float32)
    row_weight = valid_mask / jnp.maximum(held_count, 1.0)[:, None]
    coef = 2.0 * loss_scale / full_cols * row_weight
    inv_scale = jnp.where(held_count[:, None] > 0, inv_scale, 0.0)
    row_info = jnp.stack([row_mean, inv_scale, coef, row_weight], axis=-1).reshape(
        n_dp * patch_rows, 4
    )

    with jax.named_scope("contrast"):
        pair_code = images[:, embed : embed + 2].astype(jnp.int32)
        pairs = pair_code[:, 0] * 64 + pair_code[:, 1]
        logits = jnp.dot(
            images[:, :embed], texts.T, preferred_element_type=jnp.float32
        ) * (embed ** (-0.5))
        column = jnp.arange(texts.shape[0], dtype=jnp.int32)
        text_row, text_core = column % shard_rows, column // shard_rows % N_CORE
        text_x = column // (shard_rows * N_CORE) % N_X
        text_y = column // (shard_rows * N_CORE * N_X)
        text_dp = (text_x * N_Z + own_index // N_CORE % N_Z) * N_CORE + text_core
        text_id = text_dp * img_dev + text_y * shard_rows + text_row
        best = jnp.max(logits, axis=1)
        denom = jnp.sum(jnp.exp(logits - best[:, None]), axis=1)
        target = jnp.sum(jnp.where(pairs[:, None] == text_id[None, :], logits, 0.0), axis=1)
    row_info, best, denom, target = lax.optimization_barrier((row_info, best, denom, target))

    scalars = jnp.stack([cache_pos, core]).astype(jnp.int32)
    before, r_first = head_terms(
        scalars, chunks[0], head_weight, flat(teacher_cache), row_info, 0, full_cols
    )
    keep, send, r_second = head_terms(
        scalars,
        chunks[1],
        head_weight,
        flat(teacher_cache),
        row_info,
        chunk * patch_rows,
        full_cols,
        before,
    )
    with jax.named_scope("grad_core"):
        received = swap(send, 1)
    codes = add_and_code(keep, received)
    codes, r_first, r_second, best, denom, target = lax.optimization_barrier(
        (codes, r_first, r_second, best, denom, target)
    )
    with jax.named_scope("grad_x"):
        codes = lax.all_to_all(
            codes.reshape(N_X, -1, local_cols + EXT), "dp", 0, 0, axis_index_groups=X_GROUPS, tiled=True
        )
    with jax.named_scope("image_sums"):
        r = jnp.concatenate([r_first, r_second])
        r = r + ring(r, 1) + ring(r, 2) + ring(r, 3)
        other_r = swap(r, 1)
        other_held = holder_index.reshape(n_dp, img_dev) == (own_index ^ 1)
        other_place = jnp.sum(jnp.where(other_held, img_order[None, :], 0), axis=1)
        lane = jnp.arange(EXT, dtype=jnp.int32)[None, :]
        losses = jnp.where(lane == place_of[:, None], r, 0.0) + jnp.where(
            lane == other_place[:, None], other_r, 0.0
        )
        losses = losses.reshape(N_X, N_Z, N_CORE, EXT)
        losses = jnp.where(core == 0, losses[:, :, 0], losses[:, :, 1])
        own_x = own_index // (N_Z * N_CORE)

        def for_x(step):
            return lax.dynamic_index_in_dim(losses, (own_x + step) % N_X, 0, keepdims=False)

        x_stride = N_Z * N_CORE
        total = for_x(0)
        for step in range(1, N_X):
            total = total + lax.ppermute(
                for_x(step), "dp", [(i, (i + step * x_stride) % n_dp) for i in range(n_dp)]
            )
        owner_rows = student_width // n_dp
        losses = jnp.zeros((N_Z, owner_rows, EXT), jnp.float32).at[:, 0].set(total)
        losses = losses.reshape(N_Z * owner_rows, EXT)
    with jax.named_scope("contrast_merge"):
        for bit in (2, 4, 8):
            other = swap(jnp.stack([best, denom, target]), bit)
            top = jnp.maximum(best, other[0])
            denom = denom * jnp.exp(best - top) + other[1] * jnp.exp(other[0] - top)
            best, target = top, target + other[2]
        contrast = best + jnp.log(denom) - target
        own_z = own_index // N_CORE % N_Z
        contrast = lax.dynamic_slice_in_dim(contrast, own_z * shard_rows, shard_rows, 0)
    codes = sum_and_code(codes, losses)
    with jax.named_scope("grad_z"):
        codes = lax.all_to_all(
            codes.reshape(N_Z, -1, local_cols + EXT), "dp", 0, 0, axis_index_groups=Z_GROUPS, tiled=True
        )
    head_grad, extra = sum_blocks(codes)

    regress = lax.dynamic_slice_in_dim(extra[0], cache_pos * shard_rows, shard_rows, 0)
    image_loss = regress + contrast
    return (head_grad, image_loss)


def solution(mesh):
    in_specs = (
        P("dp", None, None),
        P(None, "cache"),
        P("dp", None, "cache"),
        P(),
        P("dp"),
        P(("dp", "cache"), None),
        P(("dp", "cache"), None),
        P(("dp", "cache")),
    )
    out_specs = (P("dp", "cache"), P(("dp", "cache")))
    return jax.shard_map(local, mesh=mesh, in_specs=in_specs, out_specs=out_specs, check_vma=False)
```

time: 265 us -> 202 us (0.76)
  blocking collectives: 78.3 us -> 0 us
  starting transfers between devices: 35.2 us -> 68.3 us
  Pallas kernels: 74.1 us -> 42.1 us
  waiting for transfers between devices: 57.9 us -> 68.5 us
    all_gather x2 -> x0, blocking collectives: 70.6 us -> none  [the longest x1 58.7 us: local(): lax.all_gather(jnp.concatenate([text_embed, counts_line], axis=1), 'dp',...]
    ppermute x1 -> x16, waiting for transfers between devices: 5.49 us -> 46.5 us  [the longest x11 35.6 us: swap(): return lax.ppermute(x, 'dp', [(i, i ^ bit) for i in range(n_dp)])]
    pallas_call x1, Pallas kernels: 34.1 us -> 2.92 us  [dispatch_rows(): pl.pallas_call(kernel, grid_spec=pltpu.PrefetchScalarGridSpec(num_scalar_...]
    ppermute x1 -> x16, starting transfers between devices: 0.01 us -> 28.2 us  [the longest x11 21.3 us: swap(): return lax.ppermute(x, 'dp', [(i, i ^ bit) for i in range(n_dp)])]
    ppermute x7 -> x14, waiting for transfers between devices: 34.4 us -> 22 us  [ring(): lax.ppermute(x, 'cache', [(i, (i + step) % n_cache) for i in range(n_cach...]
    all_to_all x1, waiting for transfers between devices: 12.1 us -> 0.01 us  [local(): lax.all_to_all(codes.reshape(N_Z, -1, local_cols + EXT), 'dp', 0, 0, axis...]
    all_to_all x1 -> x0, blocking collectives: 7.65 us -> none  [local(): lax.all_to_all(parts, 'cache', split_axis=0, concat_axis=0, tiled=True)]
    ppermute x7 -> x14, starting transfers between devices: 12.5 us -> 18.9 us  [ring(): lax.ppermute(x, 'cache', [(i, (i + step) % n_cache) for i in range(n_cach...]
  transfers between devices with their start and end apart: 11 -> 33, of which waited for: 6 -> 16; matrix products, arithmetic and copies ran while one was open for 4% -> 4% of each run, Pallas kernels for 0% -> 8%
where the time goes in v3:
time: 202 us; the launch traced here: 198 us
  waiting for transfers between devices  68.5 us (34%)
  starting transfers between devices  68.3 us (34%)
  Pallas kernels  42.1 us (21%)
  local copies, waits for them, and re-layouts  10.2 us (5%)
  other arithmetic  7.47 us (4%)
    ppermute x11, waiting for transfers between devices, swap(): return lax.ppermute(x, 'dp', [(i, i ^ bit) for i in range(n_dp)])  35.6 us
    pallas_call x2, Pallas kernels, head_terms(): pl.pallas_call(kernel, grid_spec=pltpu.PrefetchScalarGridSpec(num_scalar_...  29 us
    ppermute x14, waiting for transfers between devices, ring(): lax.ppermute(x, 'cache', [(i, (i + step) % n_cache) for i in range(n_cach...  22 us
    ppermute x11, starting transfers between devices, swap(): return lax.ppermute(x, 'dp', [(i, i ^ bit) for i in range(n_dp)])  21.3 us
    ppermute x14, starting transfers between devices, ring(): lax.ppermute(x, 'cache', [(i, (i + step) % n_cache) for i in range(n_cach...  18.9 us
    all_to_all x1, starting transfers between devices, local(): lax.all_to_all(outgoing, 'dp', split_axis=0, concat_axis=0, tiled=True)  12.2 us
    ppermute x3, waiting for transfers between devices, local(): lax.ppermute(for_x(step), 'dp', [(i, (i + step * x_stride) % n_dp) for i...  10.9 us
    ppermute x3, starting transfers between devices, local(): lax.ppermute(for_x(step), 'dp', [(i, (i + step * x_stride) % n_dp) for i...  5.38 us
  transfers between devices with their start and end apart: 33, of which 16 were waited for; matrix products, arithmetic and copies ran while one was open for 4% of the time, Pallas kernels for 8%

profile of v3, /device:TPU:2, one launch (start us, length us, event | category | flops | bytes accessed | tf_op | source)
XLA Modules:
  0.0 198.3 jit_solution(8033679274953039996)
XLA Ops:
  0.7 4.3 %convert_reduce_fusion = (f32[64,32]{1,0:T(8,128)S(1)}, f32[64,32]{1,0:T(8,128)S(1)}) fusion(bf16[64,32,1280]{2,1,0:T(8,128)(2,1)} %param.14), kind=kLoop, calls=%fused_computation.1 | loop fusion | flops 10481664 | bytes 5259264 | tf_op jit(solution)/shard_map/teacher_sums/reduce_sum | solution.py:321
  5.0 3.3 %collective-permute-start.7 = (f32[2,64,32]{2,1,0:T(8,128)S(1)}, f32[2,64,32]{2,1,0:T(8,128)S(1)}, u32[]{:S(2)}, u32[]{:S(2)}) collective-permute-start(f32[2,64,32]{2,1,0:T(8,128)S(1)} %pad_maximum_fusion.2), channel_id=1, source_target_pairs={{0,2},{1,3},{2,0},{3,1},{4,6},{5,7},{6,4},{7,5},{8,10},{9,11},{10,... | collective-permute-start | bytes 49160 | tf_op jit(solution)/shard_map/teacher_sums/ppermute | solution.py:259
  14.1 12.2 %all-to-all-start = ((bf16[64,32,256]{2,1,0:T(8,128)(2,1)}), bf16[64,32,256]{2,1,0:T(8,128)(2,1)S(1)}, u32[]{:S(2)}, u32[]{:S(2)}) async-start(bf16[64,32,256]{2,1,0:T(8,128)(2,1)} %dispatch_rows.1), calls=%async_computation | async-start | bytes 2097152 | tf_op jit(solution)/shard_map/student_exchange/all_to_all | solution.py:305
  32.9 3.7 %collective-permute-done.11 = bf16[32,896]{1,0:T(8,128)(2,1)S(1)} collective-permute-done((bf16[32,896]{1,0:T(8,128)(2,1)S(1)}, bf16[32,896]{1,0:T(8,128)(2,1)S(1)}, u32[]{:S(2)}, u32[]{:S(2)}) %collective-permute-start.11) | collective-permute-done | bytes 57376 | tf_op jit(solution)/shard_map/texts/ppermute | solution.py:273
  38.8 12.7 %collective-permute-done.12 = bf16[8,1024]{1,0:T(8,128)(2,1)S(1)} collective-permute-done((bf16[8,1024]{1,0:T(8,128)(2,1)S(1)}, bf16[8,1024]{1,0:T(8,128)(2,1)S(1)}, u32[]{:S(2)}, u32[]{:S(2)}) %collective-permute-start.12) | collective-permute-done | bytes 16416 | tf_op jit(solution)/shard_map/images/ppermute | solution.py:273
  53.0 3.4 %collective-permute-done.13 = bf16[16,1024]{1,0:T(8,128)(2,1)S(1)} collective-permute-done((bf16[16,1024]{1,0:T(8,128)(2,1)S(1)}, bf16[16,1024]{1,0:T(8,128)(2,1)S(1)}, u32[]{:S(2)}, u32[]{:S(2)}) %collective-permute-start.13) | collective-permute-done | bytes 32800 | tf_op jit(solution)/shard_map/images/ppermute | solution.py:273
  56.5 4.7 %collective-permute-start.14 = (bf16[32,1024]{1,0:T(8,128)(2,1)S(1)}, bf16[32,1024]{1,0:T(8,128)(2,1)S(1)}, u32[]{:S(2)}, u32[]{:S(2)}) collective-permute-start(bf16[32,1024]{1,0:T(8,128)(2,1)S(1)} %pad_maximum_fusion.3), channel_id=1, source_target_pairs={{0,32},{4,36},{8,40},{12,44},{16,48},{20,52},{24,56},{28,60},{32,0... | collective-permute-start | bytes 196616 | tf_op jit(solution)/shard_map/images/ppermute | solution.py:273
  62.0 3.1 %collective-permute-done.14 = bf16[32,1024]{1,0:T(8,128)(2,1)S(1)} collective-permute-done((bf16[32,1024]{1,0:T(8,128)(2,1)S(1)}, bf16[32,1024]{1,0:T(8,128)(2,1)S(1)}, u32[]{:S(2)}, u32[]{:S(2)}) %collective-permute-start.14) | collective-permute-done | bytes 65568 | tf_op jit(solution)/shard_map/images/ppermute | solution.py:273
  68.4 10.9 %collective-permute-done.1 = bf16[32,32,256]{2,1,0:T(8,128)(2,1)S(1)} collective-permute-done((bf16[32,32,256]{2,1,0:T(8,128)(2,1)S(1)}, bf16[32,32,256]{2,1,0:T(8,128)(2,1)S(1)}, u32[]{:S(2)}, u32[]{:S(2)}) %collective-permute-start.1) | collective-permute-done | bytes 524320 | tf_op jit(solution)/shard_map/student_ring/ppermute | solution.py:259
  82.6 3.3 %collective-permute-start.18 = (bf16[16,32,256]{2,1,0:T(8,128)(2,1)S(1)}, bf16[16,32,256]{2,1,0:T(8,128)(2,1)S(1)}, u32[]{:S(2)}, u32[]{:S(2)}) collective-permute-start(bf16[16,32,256]{2,1,0:T(8,128)(2,1)S(1)} %slice.160), channel_id=1, source_target_pairs={{0,3},{1,0},{2,1},{3,2},{4,7},{5,4},{6,5},{7,6},{8,11},{9,8},{10,9... | collective-permute-start | bytes 786440 | tf_op jit(solution)/shard_map/student_ring/ppermute | solution.py:259
  88.1 7.3 %collective-permute-done.3 = bf16[32,32,256]{2,1,0:T(8,128)(2,1)} collective-permute-done((bf16[32,32,256]{2,1,0:T(8,128)(2,1)S(1)}, bf16[32,32,256]{2,1,0:T(8,128)(2,1)}, u32[]{:S(2)}, u32[]{:S(2)}) %collective-permute-start.3) | collective-permute-done | bytes 524320 | tf_op jit(solution)/shard_map/student_ring/ppermute | solution.py:259
  96.4 3.3 %collective-permute-start.5 = (bf16[16,32,256]{2,1,0:T(8,128)(2,1)S(1)}, bf16[16,32,256]{2,1,0:T(8,128)(2,1)S(1)}, u32[]{:S(2)}, u32[]{:S(2)}) collective-permute-start(bf16[16,32,256]{2,1,0:T(8,128)(2,1)S(1)} %slice.149), channel_id=1, source_target_pairs={{0,3},{1,0},{2,1},{3,2},{4,7},{5,4},{6,5},{7,6},{8,11},{9,8},{10,9... | collective-permute-start | bytes 786440 | tf_op jit(solution)/shard_map/student_ring/ppermute | solution.py:259
  103.4 13.6 %head_terms.2 = (f32[1024,1280]{1,0:T(8,128)}, f32[32,128]{1,0:T(8,128)}) custom-call(s32[2]{0:T(128)} %pad_add_fusion.sc, bf16[1024,256]{1,0:T(8,128)(2,1)} %bitcast.131, bf16[1024,256]{1,0:T(8,128)(2,1)} %bitcast.140, bf16[1024,256]{1,0:T(8,128)(2,1)} %bitcast.139, bf16[512,256]{1,0:T(8,128)(2,1)} %bitcast.21.x3a, bf16[512,256]{1,0:T(8,128)(2,1)} %bitcast.155, ...), custom_call_target="tpu_custom_call" | custom-call | flops 5368709120 | bytes 20971520 | tf_op jit(solution)/shard_map/head_terms/pallas_call | solution.py:114
  117.7 15.5 %head_terms.3 = (f32[512,1280]{1,0:T(8,128)}, f32[512,1280]{1,0:T(8,128)}, f32[32,128]{1,0:T(8,128)}) custom-call(s32[2]{0:T(128)} %pad_add_fusion.sc, bf16[1024,256]{1,0:T(8,128)(2,1)} %bitcast.130, bf16[1024,256]{1,0:T(8,128)(2,1)} %bitcast.3.x1, bf16[1024,256]{1,0:T(8,128)(2,1)} %bitcast.4.x2, bf16[512,256]{1,0:T(8,128)(2,1)} %bitcast.157, ...), custom_call_target="tpu_custom_call" | custom-call | flops 5368709120 | bytes 20971520 | tf_op jit(solution)/shard_map/head_terms/pallas_call | solution.py:114
  133.4 5.0 %collective-permute-done.19.b = f32[512,1280]{1,0:T(8,128)S(1)} collective-permute-done((f32[512,1280]{1,0:T(8,128)}, f32[512,1280]{1,0:T(8,128)S(1)}, u32[]{:S(2)}, u32[]{:S(2)}) %collective-permute-start.19) | collective-permute-done | bytes 2621472 | tf_op jit(solution)/shard_map/grad_core/ppermute | solution.py:273
  139.9 4.7 %add_and_code.1 = s16[512,1408]{1,0:T(8,128)(2,1)} custom-call(f32[512,1280]{1,0:T(8,128)} %get-tuple-element.47.a, f32[512,1280]{1,0:T(8,128)} %copy-done.1), custom_call_target="tpu_custom_call" | custom-call | tf_op jit(solution)/shard_map/add_and_code/pallas_call | solution.py:167
  147.2 4.8 %all-to-all-start.1 = ((s16[4,128,1408]{2,1,0:T(8,128)(2,1)}), s16[4,128,1408]{2,1,0:T(8,128)(2,1)S(1)}, u32[]{:S(2)}, u32[]{:S(2)}) async-start(s16[4,128,1408]{2,1,0:T(8,128)(2,1)} %bitcast.126), calls=%async_computation.1 | async-start | bytes 2883584 | tf_op jit(solution)/shard_map/grad_x/all_to_all | solution.py:382
  155.6 3.3 %collective-permute-start.25 = (f32[8,128]{1,0:T(8,128)S(1)}, f32[8,128]{1,0:T(8,128)S(1)}, u32[]{:S(2)}, u32[]{:S(2)}) collective-permute-start(f32[8,128]{1,0:T(8,128)S(1)} %bitcast.152), channel_id=1, source_target_pairs={{0,128},{4,132},{8,136},{12,140},{16,144},{20,148},{24,152},{28,15... | collective-permute-start | bytes 12296 | tf_op jit(solution)/shard_map/image_sums/ppermute | solution.py:405
  158.9 8.4 %collective-permute-done.26 = f32[8,128]{1,0:T(8,128)S(1)} collective-permute-done((f32[8,128]{1,0:T(8,128)S(1)}, f32[8,128]{1,0:T(8,128)S(1)}, u32[]{:S(2)}, u32[]{:S(2)}) %collective-permute-start.26) | collective-permute-done | bytes 4128 | tf_op jit(solution)/shard_map/image_sums/ppermute | solution.py:405
  171.6 3.7 %sum_and_code.1 = s16[128,1408]{1,0:T(8,128)(2,1)} custom-call(s16[4,128,1408]{2,1,0:T(8,128)(2,1)} %copy-done, f32[128,128]{1,0:T(8,128)} %bitcast.136), custom_call_target="tpu_custom_call" | custom-call | tf_op jit(solution)/shard_map/sum_and_code/pallas_call | solution.py:199
  175.3 4.2 %all-to-all-start.2 = ((s16[8,16,1408]{2,1,0:T(8,128)(2,1)}), s16[8,16,1408]{2,1,0:T(8,128)(2,1)S(1)}, u32[]{:S(2)}, u32[]{:S(2)}) async-start(s16[8,16,1408]{2,1,0:T(8,128)(2,1)} %bitcast.129), calls=%async_computation.2 | async-start | bytes 720896 | tf_op jit(solution)/shard_map/grad_z/all_to_all | solution.py:422
  179.5 3.0 %collective-permute-start.28 = (f32[3,64]{1,0:T(4,128)S(1)}, f32[3,64]{1,0:T(4,128)S(1)}, u32[]{:S(2)}, u32[]{:S(2)}) collective-permute-start(f32[3,64]{1,0:T(4,128)S(1)} %pad_maximum_fusion.10), channel_id=1, source_target_pairs={{0,16},{4,20},{8,24},{12,28},{16,0},{20,4},{24,8},{28,12},{32,48},... | collective-permute-start | bytes 2312 | tf_op jit(solution)/shard_map/contrast_merge/ppermute | solution.py:273
  182.5 3.5 %collective-permute-done.28 = f32[3,64]{1,0:T(4,128)S(1)} collective-permute-done((f32[3,64]{1,0:T(4,128)S(1)}, f32[3,64]{1,0:T(4,128)S(1)}, u32[]{:S(2)}, u32[]{:S(2)}) %collective-permute-start.28) | collective-permute-done | bytes 800 | tf_op jit(solution)/shard_map/contrast_merge/ppermute | solution.py:273
  186.1 6.9 %collective-permute-start.29 = (f32[3,64]{1,0:T(4,128)S(1)}, f32[3,64]{1,0:T(4,128)S(1)}, u32[]{:S(2)}, u32[]{:S(2)}) collective-permute-start(f32[3,64]{1,0:T(4,128)S(1)} %pad_maximum_fusion.11), channel_id=1, source_target_pairs={{0,32},{4,36},{8,40},{12,44},{16,48},{20,52},{24,56},{28,60},{32,0... | collective-permute-start | bytes 2312 | tf_op jit(solution)/shard_map/contrast_merge/ppermute | solution.py:273
  (163 shorter events, 48.2 us)
Async XLA Ops:
  5.0 27.9 %collective-permute-start.7 = (f32[2,64,32]{2,1,0:T(8,128)S(1)}, f32[2,64,32]{2,1,0:T(8,128)S(1)}, u32[]{:S(2)}, u32[]{:S(2)}) collective-permute-start(f32[2,64,32]{2,1,0:T(8,128)S(1)} %pad_maximum_fusion.2), channel_id=1, source_target_pairs={{0,2},{1,3},{2,0},{3,1},{4,6},{5,7},{6,4},{7,5},{8,10},{9,11},{10,... | collective-permute-start | bytes 49160 | tf_op jit(solution)/shard_map/teacher_sums/ppermute | solution.py:259
  8.3 24.6 %collective-permute-start.8 = (f32[2,64,32]{2,1,0:T(8,128)S(1)}, f32[2,64,32]{2,1,0:T(8,128)S(1)}, u32[]{:S(2)}, u32[]{:S(2)}) collective-permute-start(f32[2,64,32]{2,1,0:T(8,128)S(1)} %pad_maximum_fusion.2), channel_id=1, source_target_pairs={{0,3},{1,0},{2,1},{3,2},{4,7},{5,4},{6,5},{7,6},{8,11},{9,8},{10,9... | collective-permute-start | bytes 49160 | tf_op jit(solution)/shard_map/teacher_sums/ppermute | solution.py:259
  9.3 23.6 %collective-permute-start.6 = (f32[2,64,32]{2,1,0:T(8,128)S(1)}, f32[2,64,32]{2,1,0:T(8,128)S(1)}, u32[]{:S(2)}, u32[]{:S(2)}) collective-permute-start(f32[2,64,32]{2,1,0:T(8,128)S(1)} %pad_maximum_fusion.2), channel_id=1, source_target_pairs={{0,1},{1,2},{2,3},{3,0},{4,5},{5,6},{6,7},{7,4},{8,9},{9,10},{10,1... | collective-permute-start | bytes 49160 | tf_op jit(solution)/shard_map/teacher_sums/ppermute | solution.py:259
  10.3 16.2 %collective-permute-start.9 = (bf16[8,896]{1,0:T(8,128)(2,1)S(1)}, bf16[8,896]{1,0:T(8,128)(2,1)S(1)}, u32[]{:S(2)}, u32[]{:S(2)}) collective-permute-start(bf16[8,896]{1,0:T(8,128)(2,1)S(1)} %fusion.11), channel_id=1, source_target_pairs={{0,4},{4,0},{8,12},{12,8},{16,20},{20,16},{24,28},{28,24},{32,36},... | collective-permute-start | bytes 43016 | tf_op jit(solution)/shard_map/texts/ppermute | solution.py:273
  14.1 51.7 %all-to-all-start = ((bf16[64,32,256]{2,1,0:T(8,128)(2,1)}), bf16[64,32,256]{2,1,0:T(8,128)(2,1)S(1)}, u32[]{:S(2)}, u32[]{:S(2)}) async-start(bf16[64,32,256]{2,1,0:T(8,128)(2,1)} %dispatch_rows.1), calls=%async_computation | async-start | bytes 2097152 | tf_op jit(solution)/shard_map/student_exchange/all_to_all | solution.py:305
  36.8 14.7 %collective-permute-start.12 = (bf16[8,1024]{1,0:T(8,128)(2,1)S(1)}, bf16[8,1024]{1,0:T(8,128)(2,1)S(1)}, u32[]{:S(2)}, u32[]{:S(2)}) collective-permute-start(bf16[8,1024]{1,0:T(8,128)(2,1)S(1)} %concatenate.49), channel_id=1, source_target_pairs={{0,8},{4,12},{8,0},{12,4},{16,24},{20,28},{24,16},{28,20},{32,40},... | collective-permute-start | bytes 49160 | tf_op jit(solution)/shard_map/images/ppermute | solution.py:273
  52.2 8.9 %collective-permute-start.15 = (bf16[64,768]{1,0:T(8,128)(2,1)S(1)}, bf16[64,768]{1,0:T(8,128)(2,1)S(1)}, u32[]{:S(2)}, u32[]{:S(2)}) collective-permute-start(bf16[64,768]{1,0:T(8,128)(2,1)S(1)} %fusion.5), channel_id=1, source_target_pairs={{0,1},{1,0},{2,3},{3,2},{4,5},{5,4},{6,7},{7,6},{8,9},{9,8},{10,11... | collective-permute-start | bytes 294920 | tf_op jit(solution)/shard_map/texts/ppermute | solution.py:289
  56.5 8.6 %collective-permute-start.14 = (bf16[32,1024]{1,0:T(8,128)(2,1)S(1)}, bf16[32,1024]{1,0:T(8,128)(2,1)S(1)}, u32[]{:S(2)}, u32[]{:S(2)}) collective-permute-start(bf16[32,1024]{1,0:T(8,128)(2,1)S(1)} %pad_maximum_fusion.3), channel_id=1, source_target_pairs={{0,32},{4,36},{8,40},{12,44},{16,48},{20,52},{24,56},{28,60},{32,0... | collective-permute-start | bytes 196616 | tf_op jit(solution)/shard_map/images/ppermute | solution.py:273
  61.2 24.9 %collective-permute-start.16 = (bf16[128,768]{1,0:T(8,128)(2,1)S(1)}, bf16[128,768]{1,0:T(8,128)(2,1)S(1)}, u32[]{:S(2)}, u32[]{:S(2)}) collective-permute-start(bf16[128,768]{1,0:T(8,128)(2,1)S(1)} %pad_maximum_fusion), channel_id=1, source_target_pairs={{0,2},{1,3},{2,0},{3,1},{4,6},{5,7},{6,4},{7,5},{8,10},{9,11},{10,... | collective-permute-start | bytes 589832 | tf_op jit(solution)/shard_map/texts/ppermute | solution.py:289
  65.9 13.4 %collective-permute-start.1 = (bf16[32,32,256]{2,1,0:T(8,128)(2,1)S(1)}, bf16[32,32,256]{2,1,0:T(8,128)(2,1)S(1)}, u32[]{:S(2)}, u32[]{:S(2)}) collective-permute-start(bf16[32,32,256]{2,1,0:T(8,128)(2,1)S(1)} %get-tuple-element.70), channel_id=1, source_target_pairs={{0,3},{1,0},{2,1},{3,2},{4,7},{5,4},{6,5},{7,6},{8,11},{9,8},{10,9... | collective-permute-start | bytes 1572872 | tf_op jit(solution)/shard_map/student_ring/ppermute | solution.py:259
  68.3 12.2 %collective-permute-start = (bf16[32,32,256]{2,1,0:T(8,128)(2,1)S(1)}, bf16[32,32,256]{2,1,0:T(8,128)(2,1)S(1)}, u32[]{:S(2)}, u32[]{:S(2)}) collective-permute-start(bf16[32,32,256]{2,1,0:T(8,128)(2,1)S(1)} %get-tuple-element.70), channel_id=1, source_target_pairs={{0,1},{1,2},{2,3},{3,0},{4,5},{5,6},{6,7},{7,4},{8,9},{9,10},{10,1... | collective-permute-start | bytes 1572872 | tf_op jit(solution)/shard_map/student_ring/ppermute | solution.py:259
  80.4 15.0 %collective-permute-start.3 = (bf16[32,32,256]{2,1,0:T(8,128)(2,1)S(1)}, bf16[32,32,256]{2,1,0:T(8,128)(2,1)}, u32[]{:S(2)}, u32[]{:S(2)}) collective-permute-start(bf16[32,32,256]{2,1,0:T(8,128)(2,1)S(1)} %get-tuple-element.44), channel_id=1, source_target_pairs={{0,3},{1,0},{2,1},{3,2},{4,7},{5,4},{6,5},{7,6},{8,11},{9,8},{10,9... | collective-permute-start | bytes 1572872 | tf_op jit(solution)/shard_map/student_ring/ppermute | solution.py:259
  82.4 17.2 %collective-permute-start.2 = (bf16[32,32,256]{2,1,0:T(8,128)(2,1)S(1)}, bf16[32,32,256]{2,1,0:T(8,128)(2,1)}, u32[]{:S(2)}, u32[]{:S(2)}) collective-permute-start(bf16[32,32,256]{2,1,0:T(8,128)(2,1)S(1)} %get-tuple-element.44), channel_id=1, source_target_pairs={{0,1},{1,2},{2,3},{3,0},{4,5},{5,6},{6,7},{7,4},{8,9},{9,10},{10,1... | collective-permute-start | bytes 1572872 | tf_op jit(solution)/shard_map/student_ring/ppermute | solution.py:259
  82.6 18.1 %collective-permute-start.18 = (bf16[16,32,256]{2,1,0:T(8,128)(2,1)S(1)}, bf16[16,32,256]{2,1,0:T(8,128)(2,1)S(1)}, u32[]{:S(2)}, u32[]{:S(2)}) collective-permute-start(bf16[16,32,256]{2,1,0:T(8,128)(2,1)S(1)} %slice.160), channel_id=1, source_target_pairs={{0,3},{1,0},{2,1},{3,2},{4,7},{5,4},{6,5},{7,6},{8,11},{9,8},{10,9... | collective-permute-start | bytes 786440 | tf_op jit(solution)/shard_map/student_ring/ppermute | solution.py:259
  86.0 17.4 %collective-permute-start.17 = (bf16[16,32,256]{2,1,0:T(8,128)(2,1)S(1)}, bf16[16,32,256]{2,1,0:T(8,128)(2,1)}, u32[]{:S(2)}, u32[]{:S(2)}) collective-permute-start(bf16[16,32,256]{2,1,0:T(8,128)(2,1)S(1)} %slice.159), channel_id=1, source_target_pairs={{0,1},{1,2},{2,3},{3,0},{4,5},{5,6},{6,7},{7,4},{8,9},{9,10},{10,1... | collective-permute-start | bytes 786440 | tf_op jit(solution)/shard_map/student_ring/ppermute | solution.py:259
  96.4 20.6 %collective-permute-start.5 = (bf16[16,32,256]{2,1,0:T(8,128)(2,1)S(1)}, bf16[16,32,256]{2,1,0:T(8,128)(2,1)S(1)}, u32[]{:S(2)}, u32[]{:S(2)}) collective-permute-start(bf16[16,32,256]{2,1,0:T(8,128)(2,1)S(1)} %slice.149), channel_id=1, source_target_pairs={{0,3},{1,0},{2,1},{3,2},{4,7},{5,4},{6,5},{7,6},{8,11},{9,8},{10,9... | collective-permute-start | bytes 786440 | tf_op jit(solution)/shard_map/student_ring/ppermute | solution.py:259
  100.6 16.3 %collective-permute-start.4 = (bf16[16,32,256]{2,1,0:T(8,128)(2,1)S(1)}, bf16[16,32,256]{2,1,0:T(8,128)(2,1)S(1)}, u32[]{:S(2)}, u32[]{:S(2)}) collective-permute-start(bf16[16,32,256]{2,1,0:T(8,128)(2,1)S(1)} %slice.148), channel_id=1, source_target_pairs={{0,1},{1,2},{2,3},{3,0},{4,5},{5,6},{6,7},{7,4},{8,9},{9,10},{10,1... | collective-permute-start | bytes 786440 | tf_op jit(solution)/shard_map/student_ring/ppermute | solution.py:259
  144.6 7.4 %collective-permute-start.22 = (f32[64,128]{1,0:T(8,128)S(1)}, f32[64,128]{1,0:T(8,128)S(1)}, u32[]{:S(2)}, u32[]{:S(2)}) collective-permute-start(f32[64,128]{1,0:T(8,128)S(1)} %constant_dynamic-update-slice_fusion), channel_id=1, source_target_pairs={{0,3},{1,0},{2,1},{3,2},{4,7},{5,4},{6,5},{7,6},{8,11},{9,8},{10,9... | collective-permute-start | bytes 98312 | tf_op jit(solution)/shard_map/image_sums/ppermute | solution.py:259
  147.2 23.2 %all-to-all-start.1 = ((s16[4,128,1408]{2,1,0:T(8,128)(2,1)}), s16[4,128,1408]{2,1,0:T(8,128)(2,1)S(1)}, u32[]{:S(2)}, u32[]{:S(2)}) async-start(s16[4,128,1408]{2,1,0:T(8,128)(2,1)} %bitcast.126), calls=%async_computation.1 | async-start | bytes 2883584 | tf_op jit(solution)/shard_map/grad_x/all_to_all | solution.py:382
  153.5 13.8 %collective-permute-start.26 = (f32[8,128]{1,0:T(8,128)S(1)}, f32[8,128]{1,0:T(8,128)S(1)}, u32[]{:S(2)}, u32[]{:S(2)}) collective-permute-start(f32[8,128]{1,0:T(8,128)S(1)} %bitcast.154), channel_id=1, source_target_pairs={{0,192},{4,196},{8,200},{12,204},{16,208},{20,212},{24,216},{28,22... | collective-permute-start | bytes 12296 | tf_op jit(solution)/shard_map/image_sums/ppermute | solution.py:405
  153.9 14.1 %collective-permute-start.24 = (f32[8,128]{1,0:T(8,128)S(1)}, f32[8,128]{1,0:T(8,128)S(1)}, u32[]{:S(2)}, u32[]{:S(2)}) collective-permute-start(f32[8,128]{1,0:T(8,128)S(1)} %bitcast.153), channel_id=1, source_target_pairs={{0,64},{4,68},{8,72},{12,76},{16,80},{20,84},{24,88},{28,92},{32,9... | collective-permute-start | bytes 12296 | tf_op jit(solution)/shard_map/image_sums/ppermute | solution.py:405
  155.6 14.2 %collective-permute-start.25 = (f32[8,128]{1,0:T(8,128)S(1)}, f32[8,128]{1,0:T(8,128)S(1)}, u32[]{:S(2)}, u32[]{:S(2)}) collective-permute-start(f32[8,128]{1,0:T(8,128)S(1)} %bitcast.152), channel_id=1, source_target_pairs={{0,128},{4,132},{8,136},{12,140},{16,144},{20,148},{24,152},{28,15... | collective-permute-start | bytes 12296 | tf_op jit(solution)/shard_map/image_sums/ppermute | solution.py:405
  175.3 19.2 %all-to-all-start.2 = ((s16[8,16,1408]{2,1,0:T(8,128)(2,1)}), s16[8,16,1408]{2,1,0:T(8,128)(2,1)S(1)}, u32[]{:S(2)}, u32[]{:S(2)}) async-start(s16[8,16,1408]{2,1,0:T(8,128)(2,1)} %bitcast.129), calls=%async_computation.2 | async-start | bytes 720896 | tf_op jit(solution)/shard_map/grad_z/all_to_all | solution.py:422
  186.1 8.4 %collective-permute-start.29 = (f32[3,64]{1,0:T(4,128)S(1)}, f32[3,64]{1,0:T(4,128)S(1)}, u32[]{:S(2)}, u32[]{:S(2)}) collective-permute-start(f32[3,64]{1,0:T(4,128)S(1)} %pad_maximum_fusion.11), channel_id=1, source_target_pairs={{0,32},{4,36},{8,40},{12,44},{16,48},{20,52},{24,56},{28,60},{32,0... | collective-permute-start | bytes 2312 | tf_op jit(solution)/shard_map/contrast_merge/ppermute | solution.py:273
  (26 other events, 229.6 us)

commit v4 on v3

--- a/solution.py
+++ b/solution.py
@@ -12,7 +12,6 @@
 EXT = 128
 VMEM_BYTES = 60 * 1024 * 1024
 
-X_GROUPS = [[x * N_Z * N_CORE + r for x in range(N_X)] for r in range(N_Z * N_CORE)]
 Z_GROUPS = [
     [(x * N_Z + z) * N_CORE + c for z in range(N_Z)] for x in range(N_X) for c in range(N_CORE)
 ]
@@ -155,39 +154,55 @@
     return codes.astype(jnp.int32).astype(jnp.float32)
 
 
-def add_and_code(keep, received):
+def add_and_code(own_x, keep, received):
     rows, cols = keep.shape
     block = rows // N_X
-
-    def kernel(a, b, out):
-        out[:, :cols], exp = quantize(a[...] + b[...])
-        out[:, cols:] = jnp.broadcast_to(exp, (block, EXT)).astype(jnp.int32).astype(jnp.int16)
-
-    spec = lambda c: pl.BlockSpec((block, c), lambda i: (i, 0))
+    order = (2, 1, 3, 0)
+
+    def kernel(sc, a, b, *outs):
+        codes, exp = quantize(a[...] + b[...])
+        exp = jnp.broadcast_to(exp, (block, EXT)).astype(jnp.int32).astype(jnp.int16)
+        for k, ahead in enumerate(order):
+
+            @pl.when(pl.program_id(0) == k)
+            def _():
+                outs[ahead][:, :cols] = codes
+                outs[ahead][:, cols:] = exp
+
+    def block_of(i, s):
+        ahead = jnp.where(i == 0, order[0], jnp.where(i == 1, order[1], jnp.where(i == 2, order[2], order[3])))
+        return (lax.rem(s[0] + ahead, N_X), 0)
+
+    spec = pl.BlockSpec((block, cols), block_of)
     return pl.pallas_call(
         kernel,
-        grid=(N_X,),
-        in_specs=[spec(cols), spec(cols)],
-        out_specs=spec(cols + EXT),
-        out_shape=jax.ShapeDtypeStruct((rows, cols + EXT), jnp.int16),
+        grid_spec=pltpu.PrefetchScalarGridSpec(
+            num_scalar_prefetch=1,
+            grid=(N_X,),
+            in_specs=[spec, spec],
+            out_specs=[pl.BlockSpec((block, cols + EXT), lambda i, s: (0, 0))] * N_X,
+        ),
+        out_shape=[jax.ShapeDtypeStruct((block, cols + EXT), jnp.int16)] * N_X,
         compiler_params=params(),
         name="add_and_code",
-    )(keep, received)
+    )(own_x[None].astype(jnp.int32), keep, received)
 
 
 def sum_codes(src, n, cols):
     total = 0.0
     for k in range(n):
-        total = total + widen(src[k, :, :cols]) * jnp.exp2(widen(src[k, :, cols:])[:, EXT - 1 :] - 14.0)
+        total = total + widen(src[k][:, :cols]) * jnp.exp2(widen(src[k][:, cols:])[:, EXT - 1 :] - 14.0)
     return total
 
 
-def sum_and_code(received, losses):
-    n, rows, wide = received.shape
+def sum_and_code(blocks, losses):
+    n = len(blocks)
+    rows, wide = blocks[0].shape
     cols = wide - EXT
     block = 32
 
-    def kernel(src, loss_ref, out):
+    def kernel(*refs):
+        src, loss_ref, out = refs[:n], refs[n], refs[n + 1]
         out[:, :cols], exp = quantize(sum_codes(src, n, cols))
         loss = loss_ref[...]
         loss_code, loss_exp = quantize(loss)
@@ -196,18 +211,16 @@
         extra = jnp.where(lane == EXT - 1, exp, extra)
         out[:, cols:] = extra.astype(jnp.int32).astype(jnp.int16)
 
+    spec = lambda c: pl.BlockSpec((block, c), lambda i: (i, 0))
     return pl.pallas_call(
         kernel,
         grid=(rows // block,),
-        in_specs=[
-            pl.BlockSpec((n, block, wide), lambda i: (0, i, 0)),
-            pl.BlockSpec((block, EXT), lambda i: (i, 0)),
-        ],
-        out_specs=pl.BlockSpec((block, wide), lambda i: (i, 0)),
+        in_specs=[spec(wide)] * n + [spec(EXT)],
+        out_specs=spec(wide),
         out_shape=jax.ShapeDtypeStruct((rows, wide), jnp.int16),
         compiler_params=params(),
         name="sum_and_code",
-    )(received, losses)
+    )(*blocks, losses)
 
 
 def sum_blocks(received):
@@ -215,7 +228,7 @@
     cols = wide - EXT
 
     def kernel(src, out, ext):
-        out[...] = sum_codes(src, n, cols)
+        out[...] = sum_codes([src[k] for k in range(n)], n, cols)
         total = 0.0
         for k in range(n):
             extra = widen(src[k, :, cols:])
@@ -272,23 +285,41 @@
     def swap(x, bit):
         return lax.ppermute(x, "dp", [(i, i ^ bit) for i in range(n_dp)])
 
-    def both(x, other, bit, index):
-        upper = (index // bit) % 2 == 1
+    def both(x, bit):
+        other = swap(x, bit)
+        upper = (own_index // bit) % 2 == 1
         return jnp.concatenate([jnp.where(upper, other, x), jnp.where(upper, x, other)])
 
     with jax.named_scope("texts"):
         counts_line = jnp.zeros((shard_rows, EXT), jnp.bfloat16).at[0, :img_dev].set(
             valid_count.astype(jnp.bfloat16)
         )
-        texts = jnp.concatenate([text_embed, counts_line], axis=1)
-        for bit in (1, 2 * N_Z, 4 * N_Z):
-            texts = both(texts, swap(texts, bit), bit, own_index)
-        counts_line = texts.reshape(N_X * N_CORE, shard_rows, embed + EXT)[:, 0, embed:]
-        texts = texts[:, :embed]
-        for bit in (1, 2):
-            other = lax.ppermute(texts, "cache", [(i, i ^ bit) for i in range(n_cache)])
-            texts = both(texts, other, bit, cache_pos)
-    with jax.named_scope("images"):
+        texts = both(jnp.concatenate([text_embed, counts_line], axis=1), 2)
+        outgoing, texts, teacher_in = lax.optimization_barrier((outgoing, texts, teacher_cache))
+        for bit in (4, 8):
+            texts = both(texts, bit)
+
+    with jax.named_scope("student_exchange"):
+        mine = lax.all_to_all(outgoing, "dp", split_axis=0, concat_axis=0, tiled=True)
+    mine, texts = lax.optimization_barrier((mine, texts))
+    chunk = n_dp // 2
+    chunks = []
+    with jax.named_scope("student_ring"):
+        for first in range(0, n_dp, chunk):
+            own = mine[first : first + chunk]
+            if chunks:
+                own = lax.optimization_barrier((own, far_a, far_b))[0]
+            from_prev = ring(own, 1)
+            from_next = ring(own, -1)
+            if chunks:
+                break
+            far_a = ring(from_prev[: chunk // 2], 1)
+            far_b = ring(from_next[chunk // 2 :], -1)
+            chunks.append([flat(x) for x in (own, from_prev, from_next, far_a, far_b)])
+
+    with jax.named_scope("teacher_sums"):
+        wide = teacher_in.astype(jnp.float32)
+        sums = jnp.stack([jnp.sum(wide, axis=-1), jnp.sum(wide * wide, axis=-1)])
         pair_cols = jnp.concatenate(
             [
                 (pair_ids // 64)[:, None],
@@ -296,40 +327,26 @@
                 jnp.zeros((shard_rows, EXT - 2), jnp.int32),
             ],
             axis=1,
-        ).astype(jnp.bfloat16)
-        images = jnp.concatenate([image_embed, pair_cols, counts_line], axis=1)
-        for bit in (2, 4, 8):
-            images = both(images, swap(images, bit), bit, own_index)
-
-    with jax.named_scope("student_exchange"):
-        mine = lax.all_to_all(outgoing, "dp", split_axis=0, concat_axis=0, tiled=True)
-    chunk = n_dp // 2
-    chunks = []
-    with jax.named_scope("student_ring"):
-        for first in range(0, n_dp, chunk):
-            own = mine[first : first + chunk]
-            if chunks:
-                own = lax.optimization_barrier((own, from_prev, from_next))[0]
-            from_prev = ring(own, 1)
-            from_next = ring(own, -1)
-            far_a = ring(from_prev[: chunk // 2], 1)
-            far_b = ring(from_next[chunk // 2 :], -1)
-            chunks.append([flat(x) for x in (own, from_prev, from_next, far_a, far_b)])
-
+        ).astype(jnp.float32)
+        images = jnp.concatenate([image_embed.astype(jnp.float32), pair_cols], axis=1)
+        packed = jnp.concatenate([sums.reshape(-1, EXT), images.reshape(-1, EXT)])
+        packed = [packed] + [ring(packed, step) for step in range(1, n_cache)]
+        n_sum = sums.size // EXT
+        sums = sum(p[:n_sum] for p in packed).reshape(sums.shape)
+        images = jnp.concatenate([p[n_sum:] for p in packed]).reshape(img_dev, embed + EXT)
+    with jax.named_scope("texts"):
+        for bit in (2 * N_Z, 4 * N_Z, 1):
+            texts = both(texts, bit)
+        counts_all = (
+            texts.reshape(N_CORE, N_X, N_Z, shard_rows, embed + EXT)[:, :, :, 0, embed : embed + img_dev]
+            .transpose(1, 2, 0, 3)
+            .reshape(n_dp, img_dev)
+        )
     with jax.named_scope("teacher_sums"):
-        wide = teacher_cache.astype(jnp.float32)
-        sums = jnp.stack([jnp.sum(wide, axis=-1), jnp.sum(wide * wide, axis=-1)])
-        sums = sums + ring(sums, 1) + ring(sums, 2) + ring(sums, 3)
         row_mean = sums[0] / full_cols
         inv_scale = lax.rsqrt(sums[1] / full_cols - row_mean * row_mean + eps)
 
     is_held = holder_index.reshape(n_dp, img_dev) == own_index
-    counts_all = (
-        images[:, embed + EXT : embed + EXT + img_dev]
-        .reshape(N_Z, N_X, N_CORE, img_dev)
-        .transpose(1, 0, 2, 3)
-        .reshape(n_dp, img_dev)
-    )
     place_of = jnp.sum(jnp.where(is_held, img_order[None, :], 0), axis=1)
     held_count = jnp.sum(jnp.where(is_held, counts_all.astype(jnp.float32), 0.0), axis=1)
     row_index = jnp.arange(patch_rows, dtype=jnp.int32).astype(jnp.float32)
@@ -341,30 +358,38 @@
         n_dp * patch_rows, 4
     )
 
-    with jax.named_scope("contrast"):
-        pair_code = images[:, embed : embed + 2].astype(jnp.int32)
-        pairs = pair_code[:, 0] * 64 + pair_code[:, 1]
-        logits = jnp.dot(
-            images[:, :embed], texts.T, preferred_element_type=jnp.float32
-        ) * (embed ** (-0.5))
-        column = jnp.arange(texts.shape[0], dtype=jnp.int32)
-        text_row, text_core = column % shard_rows, column // shard_rows % N_CORE
-        text_x = column // (shard_rows * N_CORE) % N_X
-        text_y = column // (shard_rows * N_CORE * N_X)
-        text_dp = (text_x * N_Z + own_index // N_CORE % N_Z) * N_CORE + text_core
-        text_id = text_dp * img_dev + text_y * shard_rows + text_row
-        best = jnp.max(logits, axis=1)
-        denom = jnp.sum(jnp.exp(logits - best[:, None]), axis=1)
-        target = jnp.sum(jnp.where(pairs[:, None] == text_id[None, :], logits, 0.0), axis=1)
-    row_info, best, denom, target = lax.optimization_barrier((row_info, best, denom, target))
-
     scalars = jnp.stack([cache_pos, core]).astype(jnp.int32)
     before, r_first = head_terms(
         scalars, chunks[0], head_weight, flat(teacher_cache), row_info, 0, full_cols
     )
+    with jax.named_scope("student_ring"):
+        from_prev, from_next, before, images, texts = lax.optimization_barrier(
+            (from_prev, from_next, before, images, texts)
+        )
+        far_a = ring(from_prev[: chunk // 2], 1)
+        far_b = ring(from_next[chunk // 2 :], -1)
+        second = [flat(x) for x in (own, from_prev, from_next, far_a, far_b)]
+    with jax.named_scope("contrast"):
+        pairs = images[:, embed].astype(jnp.int32) * 64 + images[:, embed + 1].astype(jnp.int32)
+        logits = jnp.dot(
+            images[:, :embed].astype(jnp.bfloat16),
+            texts[:, :embed].T,
+            preferred_element_type=jnp.float32,
+        ) * (embed ** (-0.5))
+        column = jnp.arange(texts.shape[0], dtype=jnp.int32)
+        text_row, text_z = column % shard_rows, column // shard_rows % N_Z
+        text_x = column // (shard_rows * N_Z) % N_X
+        text_core = column // (shard_rows * N_Z * N_X)
+        text_dp = (text_x * N_Z + text_z) * N_CORE + text_core
+        text_id = text_dp * img_dev + cache_pos * shard_rows + text_row
+        best = jnp.max(logits, axis=1)
+        denom = jnp.sum(jnp.exp(logits - best[:, None]), axis=1)
+        target = jnp.sum(jnp.where(pairs[:, None] == text_id[None, :], logits, 0.0), axis=1)
+        partial = jnp.pad(jnp.stack([best, denom, target]), ((0, 5), (0, EXT - img_dev)))
+        second[0], partial = lax.optimization_barrier((second[0], partial))
     keep, send, r_second = head_terms(
         scalars,
-        chunks[1],
+        second,
         head_weight,
         flat(teacher_cache),
         row_info,
@@ -374,17 +399,26 @@
     )
     with jax.named_scope("grad_core"):
         received = swap(send, 1)
-    codes = add_and_code(keep, received)
-    codes, r_first, r_second, best, denom, target = lax.optimization_barrier(
-        (codes, r_first, r_second, best, denom, target)
-    )
+    with jax.named_scope("image_sums"):
+        r = jnp.concatenate([r_first, r_second, partial])
+        r = [r] + [ring(r, step) for step in range(1, n_cache)]
+        partials = []
+        for k, got in enumerate(r):
+            first = (n_cache - k) % n_cache * shard_rows
+            partials.append(got[n_dp : n_dp + 3, first : first + shard_rows])
+        r = sum(got[:n_dp] for got in r)
+    own_x = own_index // (N_Z * N_CORE)
+
+    def to_x(x, step):
+        stride = N_Z * N_CORE
+        return lax.ppermute(x, "dp", [(i, (i + step * stride) % n_dp) for i in range(n_dp)])
+
+    own_codes, *codes = add_and_code(own_x, keep, received)
     with jax.named_scope("grad_x"):
-        codes = lax.all_to_all(
-            codes.reshape(N_X, -1, local_cols + EXT), "dp", 0, 0, axis_index_groups=X_GROUPS, tiled=True
-        )
+        far_codes = to_x(codes[1], 2)
+        blocks = [own_codes, to_x(codes[0], 1), far_codes, to_x(codes[2], 3)]
+    r = lax.optimization_barrier((r, *codes))[0]
     with jax.named_scope("image_sums"):
-        r = jnp.concatenate([r_first, r_second])
-        r = r + ring(r, 1) + ring(r, 2) + ring(r, 3)
         other_r = swap(r, 1)
         other_held = holder_index.reshape(n_dp, img_dev) == (own_index ^ 1)
         other_place = jnp.sum(jnp.where(other_held, img_order[None, :], 0), axis=1)
@@ -394,30 +428,22 @@
         )
         losses = losses.reshape(N_X, N_Z, N_CORE, EXT)
         losses = jnp.where(core == 0, losses[:, :, 0], losses[:, :, 1])
-        own_x = own_index // (N_Z * N_CORE)
 
         def for_x(step):
             return lax.dynamic_index_in_dim(losses, (own_x + step) % N_X, 0, keepdims=False)
 
-        x_stride = N_Z * N_CORE
         total = for_x(0)
         for step in range(1, N_X):
-            total = total + lax.ppermute(
-                for_x(step), "dp", [(i, (i + step * x_stride) % n_dp) for i in range(n_dp)]
-            )
+            total = total + to_x(for_x(step), step)
         owner_rows = student_width // n_dp
         losses = jnp.zeros((N_Z, owner_rows, EXT), jnp.float32).at[:, 0].set(total)
         losses = losses.reshape(N_Z * owner_rows, EXT)
-    with jax.named_scope("contrast_merge"):
-        for bit in (2, 4, 8):
-            other = swap(jnp.stack([best, denom, target]), bit)
-            top = jnp.maximum(best, other[0])
-            denom = denom * jnp.exp(best - top) + other[1] * jnp.exp(other[0] - top)
-            best, target = top, target + other[2]
-        contrast = best + jnp.log(denom) - target
-        own_z = own_index // N_CORE % N_Z
-        contrast = lax.dynamic_slice_in_dim(contrast, own_z * shard_rows, shard_rows, 0)
-    codes = sum_and_code(codes, losses)
+    codes = sum_and_code(blocks, losses)
+    with jax.named_scope("contrast"):
+        partials = jnp.stack(partials)
+        best = jnp.max(partials[:, 0], axis=0)
+        denom = jnp.sum(partials[:, 1] * jnp.exp(partials[:, 0] - best[None, :]), axis=0)
+        contrast = best + jnp.log(denom) - jnp.sum(partials[:, 2], axis=0)
     with jax.named_scope("grad_z"):
         codes = lax.all_to_all(
             codes.reshape(N_Z, -1, local_cols + EXT), "dp", 0, 0, axis_index_groups=Z_GROUPS, tiled=True

time: 202 us -> 201 us (level); the launches traced: 198 us -> 200 us
  starting transfers between devices: 68.3 us -> 62.1 us
  other arithmetic: 7.47 us -> 11.2 us
  waiting for transfers between devices: 68.5 us -> 71.7 us
    all_to_all x1, waiting for transfers between devices: 0.01 us -> 13.9 us  [local(): lax.all_to_all(codes.reshape(N_Z, -1, local_cols + EXT), 'dp', 0, 0, axis...]
    ppermute x11 -> x8, waiting for transfers between devices: 35.6 us -> 22.1 us  [swap(): return lax.ppermute(x, 'dp', [(i, i ^ bit) for i in range(n_dp)])]
    ppermute x11 -> x8, starting transfers between devices: 21.3 us -> 12.5 us  [swap(): return lax.ppermute(x, 'dp', [(i, i ^ bit) for i in range(n_dp)])]
    ppermute x14, starting transfers between devices: 18.9 us -> 23.8 us  [ring(): lax.ppermute(x, 'cache', [(i, (i + step) % n_cache) for i in range(n_cach...]
    all_to_all x1 -> x0, starting transfers between devices: 4.79 us -> none  [local(): lax.all_to_all(codes.reshape(N_X, -1, local_cols + EXT), 'dp', 0, 0, axis...]
    all_to_all x1, starting transfers between devices: 4.17 us -> 6.23 us  [local(): lax.all_to_all(codes.reshape(N_Z, -1, local_cols + EXT), 'dp', 0, 0, axis...]
    ppermute x5 -> x6, starting transfers between devices: 6.96 us -> 8.47 us  [to_x(): lax.ppermute(x, 'dp', [(i, (i + step * stride) % n_dp) for i in range(n_d...]
    ppermute x5 -> x6, waiting for transfers between devices: 10.9 us -> 12.1 us  [to_x(): lax.ppermute(x, 'dp', [(i, (i + step * stride) % n_dp) for i in range(n_d...]
  transfers between devices with their start and end apart: 33 -> 30, of which waited for: 16 -> 15; matrix products, arithmetic and copies ran while one was open for 4% -> 8% of each run, Pallas kernels for 8% -> 8%
where the time goes in v4:
time: 201 us; the launch traced here: 200 us
  waiting for transfers between devices  71.7 us (36%)
  starting transfers between devices  62.1 us (31%)
  Pallas kernels  42.3 us (21%)
  other arithmetic  11.2 us (6%)
  local copies, waits for them, and re-layouts  10.6 us (5%)
    pallas_call x2, Pallas kernels, head_terms(): pl.pallas_call(kernel, grid_spec=pltpu.PrefetchScalarGridSpec(num_scalar_...  29.1 us
    ppermute x14, starting transfers between devices, ring(): lax.ppermute(x, 'cache', [(i, (i + step) % n_cache) for i in range(n_cach...  23.8 us
    ppermute x14, waiting for transfers between devices, ring(): lax.ppermute(x, 'cache', [(i, (i + step) % n_cache) for i in range(n_cach...  23.5 us
    ppermute x8, waiting for transfers between devices, swap(): return lax.ppermute(x, 'dp', [(i, i ^ bit) for i in range(n_dp)])  22.1 us
    all_to_all x1, waiting for transfers between devices, local(): lax.all_to_all(codes.reshape(N_Z, -1, local_cols + EXT), 'dp', 0, 0, axis...  13.9 us
    ppermute x8, starting transfers between devices, swap(): return lax.ppermute(x, 'dp', [(i, i ^ bit) for i in range(n_dp)])  12.5 us
    ppermute x6, waiting for transfers between devices, to_x(): lax.ppermute(x, 'dp', [(i, (i + step * stride) % n_dp) for i in range(n_d...  12.1 us
    all_to_all x1, starting transfers between devices, local(): lax.all_to_all(outgoing, 'dp', split_axis=0, concat_axis=0, tiled=True)  11.1 us
  transfers between devices with their start and end apart: 30, of which 15 were waited for; matrix products, arithmetic and copies ran while one was open for 8% of the time, Pallas kernels for 8%

profile of v4, /device:TPU:2, one launch (start us, length us, event | category | flops | bytes accessed | tf_op | source)
XLA Modules:
  0.0 199.6 jit_solution(15896260741993776423)
XLA Ops:
  7.1 2.9 %dispatch_rows.1 = bf16[64,32,256]{2,1,0:T(8,128)(2,1)} custom-call(s32[65]{0:T(128)} %pad_add_fusion.1.scalars, bf16[32,32,1024]{2,1,0:T(8,128)(2,1)} %feats.1), custom_call_target="tpu_custom_call" | custom-call | tf_op jit(solution)/shard_map/dispatch_rows/pallas_call | solution.py:33
  10.0 11.1 %all-to-all-start = ((bf16[64,32,256]{2,1,0:T(8,128)(2,1)}), bf16[64,32,256]{2,1,0:T(8,128)(2,1)S(1)}, u32[]{:S(2)}, u32[]{:S(2)}) async-start(bf16[64,32,256]{2,1,0:T(8,128)(2,1)} %dispatch_rows.1), calls=%async_computation | async-start | bytes 2097152 | tf_op jit(solution)/shard_map/student_exchange/all_to_all | solution.py:303
  21.3 4.3 %convert_reduce_fusion = (f32[64,32]{1,0:T(8,128)S(1)}, f32[64,32]{1,0:T(8,128)S(1)}) fusion(bf16[64,32,1280]{2,1,0:T(8,128)(2,1)} %param.14), kind=kLoop, calls=%fused_computation.1 | loop fusion | flops 10481664 | bytes 5259264 | tf_op jit(solution)/shard_map/teacher_sums/reduce_sum | solution.py:322
  28.1 19.2 %collective-permute-done.1 = bf16[16,896]{1,0:T(8,128)(2,1)S(1)} collective-permute-done((bf16[16,896]{1,0:T(8,128)(2,1)S(1)}, bf16[16,896]{1,0:T(8,128)(2,1)S(1)}, u32[]{:S(2)}, u32[]{:S(2)}) %collective-permute-start.1) | collective-permute-done | bytes 28704 | tf_op jit(solution)/shard_map/texts/ppermute | solution.py:286
  47.4 4.4 %collective-permute-start.2 = (bf16[32,896]{1,0:T(8,128)(2,1)S(1)}, bf16[32,896]{1,0:T(8,128)(2,1)S(1)}, u32[]{:S(2)}, u32[]{:S(2)}) collective-permute-start(bf16[32,896]{1,0:T(8,128)(2,1)S(1)} %pad_maximum_fusion.6), channel_id=1, source_target_pairs={{0,32},{4,36},{8,40},{12,44},{16,48},{20,52},{24,56},{28,60},{32,0... | collective-permute-start | bytes 172040 | tf_op jit(solution)/shard_map/texts/ppermute | solution.py:286
  51.8 3.2 %collective-permute-start.10 = (f32[88,128]{1,0:T(8,128)S(1)}, f32[88,128]{1,0:T(8,128)S(1)}, u32[]{:S(2)}, u32[]{:S(2)}) collective-permute-start(f32[88,128]{1,0:T(8,128)S(1)} %constant_dynamic-update-slice_fusion), channel_id=1, source_target_pairs={{0,2},{1,3},{2,0},{3,1},{4,6},{5,7},{6,4},{7,5},{8,10},{9,11},{10,... | collective-permute-start | bytes 135176 | tf_op jit(solution)/shard_map/teacher_sums/ppermute | solution.py:272
  58.5 2.9 %collective-permute-done.9 = f32[88,128]{1,0:T(8,128)S(1)} collective-permute-done((f32[88,128]{1,0:T(8,128)S(1)}, f32[88,128]{1,0:T(8,128)S(1)}, u32[]{:S(2)}, u32[]{:S(2)}) %collective-permute-start.9) | collective-permute-done | bytes 45088 | tf_op jit(solution)/shard_map/teacher_sums/ppermute | solution.py:272
  62.1 3.0 %collective-permute-start.13 = (bf16[128,896]{1,0:T(8,128)(2,1)S(1)}, bf16[128,896]{1,0:T(8,128)(2,1)S(1)}, u32[]{:S(2)}, u32[]{:S(2)}) collective-permute-start(bf16[128,896]{1,0:T(8,128)(2,1)S(1)} %pad_maximum_fusion.2), channel_id=1, source_target_pairs={{0,128},{4,132},{8,136},{12,140},{16,144},{20,148},{24,152},{28,15... | collective-permute-start | bytes 688136 | tf_op jit(solution)/shard_map/texts/ppermute | solution.py:286
  69.9 7.3 %collective-permute-done.3 = bf16[32,32,256]{2,1,0:T(8,128)(2,1)S(1)} collective-permute-done((bf16[32,32,256]{2,1,0:T(8,128)(2,1)S(1)}, bf16[32,32,256]{2,1,0:T(8,128)(2,1)S(1)}, u32[]{:S(2)}, u32[]{:S(2)}) %collective-permute-start.3) | collective-permute-done | bytes 524320 | tf_op jit(solution)/shard_map/student_ring/ppermute | solution.py:272
  77.4 3.5 %collective-permute-start.6 = (bf16[16,32,256]{2,1,0:T(8,128)(2,1)S(1)}, bf16[16,32,256]{2,1,0:T(8,128)(2,1)}, u32[]{:S(2)}, u32[]{:S(2)}) collective-permute-start(bf16[16,32,256]{2,1,0:T(8,128)(2,1)S(1)} %slice.170), channel_id=1, source_target_pairs={{0,3},{1,0},{2,1},{3,2},{4,7},{5,4},{6,5},{7,6},{8,11},{9,8},{10,9... | collective-permute-start | bytes 786440 | tf_op jit(solution)/shard_map/student_ring/ppermute | solution.py:272
  80.9 5.2 %collective-permute-done.4 = bf16[16,32,256]{2,1,0:T(8,128)(2,1)S(1)} collective-permute-done((bf16[16,32,256]{2,1,0:T(8,128)(2,1)S(1)}, bf16[16,32,256]{2,1,0:T(8,128)(2,1)S(1)}, u32[]{:S(2)}, u32[]{:S(2)}) %collective-permute-start.4) | collective-permute-done | bytes 262176 | tf_op jit(solution)/shard_map/student_ring/ppermute | solution.py:272
  86.6 3.8 %collective-permute-start.8 = (bf16[32,32,256]{2,1,0:T(8,128)(2,1)S(1)}, bf16[32,32,256]{2,1,0:T(8,128)(2,1)}, u32[]{:S(2)}, u32[]{:S(2)}) collective-permute-start(bf16[32,32,256]{2,1,0:T(8,128)(2,1)S(1)} %get-tuple-element.54), channel_id=1, source_target_pairs={{0,3},{1,0},{2,1},{3,2},{4,7},{5,4},{6,5},{7,6},{8,11},{9,8},{10,9... | collective-permute-start | bytes 1572872 | tf_op jit(solution)/shard_map/student_ring/ppermute | solution.py:272
  92.8 13.6 %head_terms.2 = (f32[1024,1280]{1,0:T(8,128)}, f32[32,128]{1,0:T(8,128)}) custom-call(s32[2]{0:T(128)} %pad_add_fusion.sc, bf16[1024,256]{1,0:T(8,128)(2,1)} %bitcast.65, bf16[1024,256]{1,0:T(8,128)(2,1)} %bitcast.68, bf16[1024,256]{1,0:T(8,128)(2,1)} %bitcast.69, bf16[512,256]{1,0:T(8,128)(2,1)} %bitcast.87, bf16[512,256]{1,0:T(8,128)(2,1)} %bitcast.9.x3b, ...), custom_call_target="tpu_custom_call" | custom-call | flops 5368709120 | bytes 20971520 | tf_op jit(solution)/shard_map/head_terms/pallas_call | solution.py:113
  107.5 3.2 %collective-permute-start.16 = (bf16[16,32,256]{2,1,0:T(8,128)(2,1)S(1)}, bf16[16,32,256]{2,1,0:T(8,128)(2,1)S(1)}, u32[]{:S(2)}, u32[]{:S(2)}) collective-permute-start(bf16[16,32,256]{2,1,0:T(8,128)(2,1)S(1)} %slice.155), channel_id=1, source_target_pairs={{0,3},{1,0},{2,1},{3,2},{4,7},{5,4},{6,5},{7,6},{8,11},{9,8},{10,9... | collective-permute-start | bytes 786440 | tf_op jit(solution)/shard_map/student_ring/ppermute | solution.py:272
  115.4 15.6 %head_terms.3 = (f32[512,1280]{1,0:T(8,128)}, f32[512,1280]{1,0:T(8,128)}, f32[32,128]{1,0:T(8,128)}) custom-call(s32[2]{0:T(128)} %pad_add_fusion.sc, bf16[1024,256]{1,0:T(8,128)(2,1)} %bitcast.64, bf16[1024,256]{1,0:T(8,128)(2,1)} %bitcast.70, bf16[1024,256]{1,0:T(8,128)(2,1)} %bitcast.25.x2, bf16[512,256]{1,0:T(8,128)(2,1)} %bitcast.88, ...), custom_call_target="tpu_custom_call" | custom-call | flops 5368709120 | bytes 20971520 | tf_op jit(solution)/shard_map/head_terms/pallas_call | solution.py:113
  131.8 3.7 %collective-permute-start.23 = (f32[72,128]{1,0:T(8,128)S(1)}, f32[72,128]{1,0:T(8,128)S(1)}, u32[]{:S(2)}, u32[]{:S(2)}) collective-permute-start(f32[72,128]{1,0:T(8,128)S(1)} %constant_dynamic-update-slice_fusion.2), channel_id=1, source_target_pairs={{0,3},{1,0},{2,1},{3,2},{4,7},{5,4},{6,5},{7,6},{8,11},{9,8},{10,9... | collective-permute-start | bytes 110600 | tf_op jit(solution)/shard_map/image_sums/ppermute | solution.py:272
  137.7 3.3 %collective-permute-done.22 = f32[72,128]{1,0:T(8,128)S(1)} collective-permute-done((f32[72,128]{1,0:T(8,128)S(1)}, f32[72,128]{1,0:T(8,128)S(1)}, u32[]{:S(2)}, u32[]{:S(2)}) %collective-permute-start.22) | collective-permute-done | bytes 36896 | tf_op jit(solution)/shard_map/image_sums/ppermute | solution.py:272
  143.3 4.8 %add_and_code.1 = (s16[128,1408]{1,0:T(8,128)(2,1)}, s16[128,1408]{1,0:T(8,128)(2,1)}, s16[128,1408]{1,0:T(8,128)(2,1)}, s16[128,1408]{1,0:T(8,128)(2,1)}) custom-call(s32[1]{0:T(128)} %bitcast.sc, f32[512,1280]{1,0:T(8,128)} %get-tuple-element.64.a, f32[512,1280]{1,0:T(8,128)} %copy-done), custom_call_target="tpu_custom_call" | custom-call | tf_op jit(solution)/shard_map/add_and_code/pallas_call | solution.py:177
  150.5 3.3 %collective-permute-start.19 = (s16[128,1408]{1,0:T(8,128)(2,1)}, s16[128,1408]{1,0:T(8,128)(2,1)S(1)}, u32[]{:S(2)}, u32[]{:S(2)}) collective-permute-start(s16[128,1408]{1,0:T(8,128)(2,1)} %get-tuple-element.68), channel_id=1, source_target_pairs={{0,128},{4,132},{8,136},{12,140},{16,144},{20,148},{24,152},{28,15... | collective-permute-start | bytes 1081352 | tf_op jit(solution)/shard_map/grad_x/ppermute | solution.py:414
  154.8 3.1 %collective-permute-start.27 = (f32[8,128]{1,0:T(8,128)S(1)}, f32[8,128]{1,0:T(8,128)S(1)}, u32[]{:S(2)}, u32[]{:S(2)}) collective-permute-start(f32[8,128]{1,0:T(8,128)S(1)} %bitcast.82), channel_id=1, source_target_pairs={{0,192},{4,196},{8,200},{12,204},{16,208},{20,212},{24,216},{28,22... | collective-permute-start | bytes 12296 | tf_op jit(solution)/shard_map/image_sums/ppermute | solution.py:414
  158.0 12.1 %collective-permute-done.26 = f32[8,128]{1,0:T(8,128)S(1)} collective-permute-done((f32[8,128]{1,0:T(8,128)S(1)}, f32[8,128]{1,0:T(8,128)S(1)}, u32[]{:S(2)}, u32[]{:S(2)}) %collective-permute-start.26) | collective-permute-done | bytes 4128 | tf_op jit(solution)/shard_map/image_sums/ppermute | solution.py:414
  171.8 3.8 %sum_and_code.1 = s16[128,1408]{1,0:T(8,128)(2,1)} custom-call(s16[128,1408]{1,0:T(8,128)(2,1)} %get-tuple-element.66.refs_0_, s16[128,1408]{1,0:T(8,128)(2,1)} %copy-done.4, s16[128,1408]{1,0:T(8,128)(2,1)} %copy-done.5, s16[128,1408]{1,0:T(8,128)(2,1)} %copy-done.6, f32[128,128]{1,0:T(8,128)} %bitcast.66), custom_call_target="tpu_custom_call" | custom-call | tf_op jit(solution)/shard_map/sum_and_code/pallas_call | solution.py:215
  175.5 6.2 %all-to-all-start.1 = ((s16[8,16,1408]{2,1,0:T(8,128)(2,1)}), s16[8,16,1408]{2,1,0:T(8,128)(2,1)S(1)}, u32[]{:S(2)}, u32[]{:S(2)}) async-start(s16[8,16,1408]{2,1,0:T(8,128)(2,1)} %bitcast.63), calls=%async_computation.1 | async-start | bytes 720896 | tf_op jit(solution)/shard_map/grad_z/all_to_all | solution.py:448
  182.0 13.9 %all-to-all-done.1.src = s16[8,16,1408]{2,1,0:T(8,128)(2,1)S(1)} async-done(((s16[8,16,1408]{2,1,0:T(8,128)(2,1)}), s16[8,16,1408]{2,1,0:T(8,128)(2,1)S(1)}, u32[]{:S(2)}, u32[]{:S(2)}) %all-to-all-start.1) | async-done | bytes 360480 | tf_op jit(solution)/shard_map/grad_z/all_to_all | solution.py:448
  (161 shorter events, 40.9 us)
Async XLA Ops:
  2.0 8.0 %collective-permute-start = (bf16[8,896]{1,0:T(8,128)(2,1)S(1)}, bf16[8,896]{1,0:T(8,128)(2,1)S(1)}, u32[]{:S(2)}, u32[]{:S(2)}) collective-permute-start(bf16[8,896]{1,0:T(8,128)(2,1)S(1)} %fusion.4), channel_id=1, source_target_pairs={{0,8},{4,12},{8,0},{12,4},{16,24},{20,28},{24,16},{28,20},{32,40},... | collective-permute-start | bytes 43016 | tf_op jit(solution)/shard_map/texts/ppermute | solution.py:286
  10.0 47.1 %all-to-all-start = ((bf16[64,32,256]{2,1,0:T(8,128)(2,1)}), bf16[64,32,256]{2,1,0:T(8,128)(2,1)S(1)}, u32[]{:S(2)}, u32[]{:S(2)}) async-start(bf16[64,32,256]{2,1,0:T(8,128)(2,1)} %dispatch_rows.1), calls=%async_computation | async-start | bytes 2097152 | tf_op jit(solution)/shard_map/student_exchange/all_to_all | solution.py:303
  25.7 21.7 %collective-permute-start.1 = (bf16[16,896]{1,0:T(8,128)(2,1)S(1)}, bf16[16,896]{1,0:T(8,128)(2,1)S(1)}, u32[]{:S(2)}, u32[]{:S(2)}) collective-permute-start(bf16[16,896]{1,0:T(8,128)(2,1)S(1)} %pad_maximum_fusion.8), channel_id=1, source_target_pairs={{0,16},{4,20},{8,24},{12,28},{16,0},{20,4},{24,8},{28,12},{32,48},... | collective-permute-start | bytes 86024 | tf_op jit(solution)/shard_map/texts/ppermute | solution.py:286
  47.4 9.7 %collective-permute-start.2 = (bf16[32,896]{1,0:T(8,128)(2,1)S(1)}, bf16[32,896]{1,0:T(8,128)(2,1)S(1)}, u32[]{:S(2)}, u32[]{:S(2)}) collective-permute-start(bf16[32,896]{1,0:T(8,128)(2,1)S(1)} %pad_maximum_fusion.6), channel_id=1, source_target_pairs={{0,32},{4,36},{8,40},{12,44},{16,48},{20,52},{24,56},{28,60},{32,0... | collective-permute-start | bytes 172040 | tf_op jit(solution)/shard_map/texts/ppermute | solution.py:286
  51.8 9.5 %collective-permute-start.10 = (f32[88,128]{1,0:T(8,128)S(1)}, f32[88,128]{1,0:T(8,128)S(1)}, u32[]{:S(2)}, u32[]{:S(2)}) collective-permute-start(f32[88,128]{1,0:T(8,128)S(1)} %constant_dynamic-update-slice_fusion), channel_id=1, source_target_pairs={{0,2},{1,3},{2,0},{3,1},{4,6},{5,7},{6,4},{7,5},{8,10},{9,11},{10,... | collective-permute-start | bytes 135176 | tf_op jit(solution)/shard_map/teacher_sums/ppermute | solution.py:272
  55.0 6.3 %collective-permute-start.11 = (f32[88,128]{1,0:T(8,128)S(1)}, f32[88,128]{1,0:T(8,128)S(1)}, u32[]{:S(2)}, u32[]{:S(2)}) collective-permute-start(f32[88,128]{1,0:T(8,128)S(1)} %constant_dynamic-update-slice_fusion), channel_id=1, source_target_pairs={{0,3},{1,0},{2,1},{3,2},{4,7},{5,4},{6,5},{7,6},{8,11},{9,8},{10,9... | collective-permute-start | bytes 135176 | tf_op jit(solution)/shard_map/teacher_sums/ppermute | solution.py:272
  62.1 7.6 %collective-permute-start.13 = (bf16[128,896]{1,0:T(8,128)(2,1)S(1)}, bf16[128,896]{1,0:T(8,128)(2,1)S(1)}, u32[]{:S(2)}, u32[]{:S(2)}) collective-permute-start(bf16[128,896]{1,0:T(8,128)(2,1)S(1)} %pad_maximum_fusion.2), channel_id=1, source_target_pairs={{0,128},{4,132},{8,136},{12,140},{16,144},{20,148},{24,152},{28,15... | collective-permute-start | bytes 688136 | tf_op jit(solution)/shard_map/texts/ppermute | solution.py:286
  65.1 12.1 %collective-permute-start.3 = (bf16[32,32,256]{2,1,0:T(8,128)(2,1)S(1)}, bf16[32,32,256]{2,1,0:T(8,128)(2,1)S(1)}, u32[]{:S(2)}, u32[]{:S(2)}) collective-permute-start(bf16[32,32,256]{2,1,0:T(8,128)(2,1)S(1)} %get-tuple-element.84), channel_id=1, source_target_pairs={{0,1},{1,2},{2,3},{3,0},{4,5},{5,6},{6,7},{7,4},{8,9},{9,10},{10,1... | collective-permute-start | bytes 1572872 | tf_op jit(solution)/shard_map/student_ring/ppermute | solution.py:272
  65.9 11.4 %collective-permute-start.5 = (bf16[32,32,256]{2,1,0:T(8,128)(2,1)S(1)}, bf16[32,32,256]{2,1,0:T(8,128)(2,1)S(1)}, u32[]{:S(2)}, u32[]{:S(2)}) collective-permute-start(bf16[32,32,256]{2,1,0:T(8,128)(2,1)S(1)} %get-tuple-element.84), channel_id=1, source_target_pairs={{0,3},{1,0},{2,1},{3,2},{4,7},{5,4},{6,5},{7,6},{8,11},{9,8},{10,9... | collective-permute-start | bytes 1572872 | tf_op jit(solution)/shard_map/student_ring/ppermute | solution.py:272
  69.8 20.6 %collective-permute-start.14 = (bf16[256,896]{1,0:T(8,128)(2,1)S(1)}, bf16[256,896]{1,0:T(8,128)(2,1)S(1)}, u32[]{:S(2)}, u32[]{:S(2)}) collective-permute-start(bf16[256,896]{1,0:T(8,128)(2,1)S(1)} %pad_maximum_fusion.1), channel_id=1, source_target_pairs={{0,4},{4,0},{8,12},{12,8},{16,20},{20,16},{24,28},{28,24},{32,36},... | collective-permute-start | bytes 1376264 | tf_op jit(solution)/shard_map/texts/ppermute | solution.py:286
  77.2 8.9 %collective-permute-start.4 = (bf16[16,32,256]{2,1,0:T(8,128)(2,1)S(1)}, bf16[16,32,256]{2,1,0:T(8,128)(2,1)S(1)}, u32[]{:S(2)}, u32[]{:S(2)}) collective-permute-start(bf16[16,32,256]{2,1,0:T(8,128)(2,1)S(1)} %slice.169), channel_id=1, source_target_pairs={{0,1},{1,2},{2,3},{3,0},{4,5},{5,6},{6,7},{7,4},{8,9},{9,10},{10,1... | collective-permute-start | bytes 786440 | tf_op jit(solution)/shard_map/student_ring/ppermute | solution.py:272
  77.4 9.2 %collective-permute-start.6 = (bf16[16,32,256]{2,1,0:T(8,128)(2,1)S(1)}, bf16[16,32,256]{2,1,0:T(8,128)(2,1)}, u32[]{:S(2)}, u32[]{:S(2)}) collective-permute-start(bf16[16,32,256]{2,1,0:T(8,128)(2,1)S(1)} %slice.170), channel_id=1, source_target_pairs={{0,3},{1,0},{2,1},{3,2},{4,7},{5,4},{6,5},{7,6},{8,11},{9,8},{10,9... | collective-permute-start | bytes 786440 | tf_op jit(solution)/shard_map/student_ring/ppermute | solution.py:272
  86.6 19.8 %collective-permute-start.7 = (bf16[32,32,256]{2,1,0:T(8,128)(2,1)S(1)}, bf16[32,32,256]{2,1,0:T(8,128)(2,1)S(1)}, u32[]{:S(2)}, u32[]{:S(2)}) collective-permute-start(bf16[32,32,256]{2,1,0:T(8,128)(2,1)S(1)} %get-tuple-element.54), channel_id=1, source_target_pairs={{0,1},{1,2},{2,3},{3,0},{4,5},{5,6},{6,7},{7,4},{8,9},{9,10},{10,1... | collective-permute-start | bytes 1572872 | tf_op jit(solution)/shard_map/student_ring/ppermute | solution.py:272
  86.6 19.8 %collective-permute-start.8 = (bf16[32,32,256]{2,1,0:T(8,128)(2,1)S(1)}, bf16[32,32,256]{2,1,0:T(8,128)(2,1)}, u32[]{:S(2)}, u32[]{:S(2)}) collective-permute-start(bf16[32,32,256]{2,1,0:T(8,128)(2,1)S(1)} %get-tuple-element.54), channel_id=1, source_target_pairs={{0,3},{1,0},{2,1},{3,2},{4,7},{5,4},{6,5},{7,6},{8,11},{9,8},{10,9... | collective-permute-start | bytes 1572872 | tf_op jit(solution)/shard_map/student_ring/ppermute | solution.py:272
  106.4 7.7 %collective-permute-start.15 = (bf16[16,32,256]{2,1,0:T(8,128)(2,1)S(1)}, bf16[16,32,256]{2,1,0:T(8,128)(2,1)S(1)}, u32[]{:S(2)}, u32[]{:S(2)}) collective-permute-start(bf16[16,32,256]{2,1,0:T(8,128)(2,1)S(1)} %slice.154), channel_id=1, source_target_pairs={{0,1},{1,2},{2,3},{3,0},{4,5},{5,6},{6,7},{7,4},{8,9},{9,10},{10,1... | collective-permute-start | bytes 786440 | tf_op jit(solution)/shard_map/student_ring/ppermute | solution.py:272
  107.5 7.1 %collective-permute-start.16 = (bf16[16,32,256]{2,1,0:T(8,128)(2,1)S(1)}, bf16[16,32,256]{2,1,0:T(8,128)(2,1)S(1)}, u32[]{:S(2)}, u32[]{:S(2)}) collective-permute-start(bf16[16,32,256]{2,1,0:T(8,128)(2,1)S(1)} %slice.155), channel_id=1, source_target_pairs={{0,3},{1,0},{2,1},{3,2},{4,7},{5,4},{6,5},{7,6},{8,11},{9,8},{10,9... | collective-permute-start | bytes 786440 | tf_op jit(solution)/shard_map/student_ring/ppermute | solution.py:272
  130.9 10.9 %collective-permute-start.17 = (f32[512,1280]{1,0:T(8,128)}, f32[512,1280]{1,0:T(8,128)S(1)}, u32[]{:S(2)}, u32[]{:S(2)}) collective-permute-start(f32[512,1280]{1,0:T(8,128)} %get-tuple-element.65), channel_id=1, source_target_pairs={{0,4},{4,0},{8,12},{12,8},{16,20},{20,16},{24,28},{28,24},{32,36},... | collective-permute-start | bytes 7864328 | tf_op jit(solution)/shard_map/grad_core/ppermute | solution.py:286
  131.8 5.9 %collective-permute-start.23 = (f32[72,128]{1,0:T(8,128)S(1)}, f32[72,128]{1,0:T(8,128)S(1)}, u32[]{:S(2)}, u32[]{:S(2)}) collective-permute-start(f32[72,128]{1,0:T(8,128)S(1)} %constant_dynamic-update-slice_fusion.2), channel_id=1, source_target_pairs={{0,3},{1,0},{2,1},{3,2},{4,7},{5,4},{6,5},{7,6},{8,11},{9,8},{10,9... | collective-permute-start | bytes 110600 | tf_op jit(solution)/shard_map/image_sums/ppermute | solution.py:272
  149.8 21.0 %collective-permute-start.18 = (s16[128,1408]{1,0:T(8,128)(2,1)}, s16[128,1408]{1,0:T(8,128)(2,1)S(1)}, u32[]{:S(2)}, u32[]{:S(2)}) collective-permute-start(s16[128,1408]{1,0:T(8,128)(2,1)} %get-tuple-element.67), channel_id=1, source_target_pairs={{0,64},{4,68},{8,72},{12,76},{16,80},{20,84},{24,88},{28,92},{32,9... | collective-permute-start | bytes 1081352 | tf_op jit(solution)/shard_map/grad_x/ppermute | solution.py:414
  150.5 20.3 %collective-permute-start.19 = (s16[128,1408]{1,0:T(8,128)(2,1)}, s16[128,1408]{1,0:T(8,128)(2,1)S(1)}, u32[]{:S(2)}, u32[]{:S(2)}) collective-permute-start(s16[128,1408]{1,0:T(8,128)(2,1)} %get-tuple-element.68), channel_id=1, source_target_pairs={{0,128},{4,132},{8,136},{12,140},{16,144},{20,148},{24,152},{28,15... | collective-permute-start | bytes 1081352 | tf_op jit(solution)/shard_map/grad_x/ppermute | solution.py:414
  153.8 17.0 %collective-permute-start.20 = (s16[128,1408]{1,0:T(8,128)(2,1)}, s16[128,1408]{1,0:T(8,128)(2,1)S(1)}, u32[]{:S(2)}, u32[]{:S(2)}) collective-permute-start(s16[128,1408]{1,0:T(8,128)(2,1)} %get-tuple-element.69), channel_id=1, source_target_pairs={{0,192},{4,196},{8,200},{12,204},{16,208},{20,212},{24,216},{28,22... | collective-permute-start | bytes 1081352 | tf_op jit(solution)/shard_map/grad_x/ppermute | solution.py:414
  154.7 15.4 %collective-permute-start.26 = (f32[8,128]{1,0:T(8,128)S(1)}, f32[8,128]{1,0:T(8,128)S(1)}, u32[]{:S(2)}, u32[]{:S(2)}) collective-permute-start(f32[8,128]{1,0:T(8,128)S(1)} %bitcast.83), channel_id=1, source_target_pairs={{0,128},{4,132},{8,136},{12,140},{16,144},{20,148},{24,152},{28,15... | collective-permute-start | bytes 12296 | tf_op jit(solution)/shard_map/image_sums/ppermute | solution.py:414
  154.8 15.3 %collective-permute-start.27 = (f32[8,128]{1,0:T(8,128)S(1)}, f32[8,128]{1,0:T(8,128)S(1)}, u32[]{:S(2)}, u32[]{:S(2)}) collective-permute-start(f32[8,128]{1,0:T(8,128)S(1)} %bitcast.82), channel_id=1, source_target_pairs={{0,192},{4,196},{8,200},{12,204},{16,208},{20,212},{24,216},{28,22... | collective-permute-start | bytes 12296 | tf_op jit(solution)/shard_map/image_sums/ppermute | solution.py:414
  175.5 20.4 %all-to-all-start.1 = ((s16[8,16,1408]{2,1,0:T(8,128)(2,1)}), s16[8,16,1408]{2,1,0:T(8,128)(2,1)S(1)}, u32[]{:S(2)}, u32[]{:S(2)}) async-start(s16[8,16,1408]{2,1,0:T(8,128)(2,1)} %bitcast.63), calls=%async_computation.1 | async-start | bytes 720896 | tf_op jit(solution)/shard_map/grad_z/all_to_all | solution.py:448
  (22 other events, 146.2 us)

commit v5 on v4

v5 whole, which is shorter than its diff:
```python
import jax
import jax.numpy as jnp
from jax import lax
from jax.experimental import pallas as pl
from jax.experimental.pallas import tpu as pltpu
from jax.sharding import PartitionSpec as P

eps = 1e-06
loss_scale = 128.0

N_X, N_Z, N_CORE = 4, 8, 2
EXT = 128
VMEM_BYTES = 60 * 1024 * 1024

Z_GROUPS = [
    [(x * N_Z + z) * N_CORE + c for z in range(N_Z)] for x in range(N_X) for c in range(N_CORE)
]


def params():
    return pltpu.CompilerParams(vmem_limit_bytes=VMEM_BYTES)


LANES = 128
COUNT_ROWS = 8


def dispatch_rows(student_feats, image_of, count_of, cache_pos, cols):
    n_dp = image_of.shape[0]
    images, rows, _ = student_feats.shape
    parts = cols // LANES

    def kernel(scalars, feats, out):
        for h in range(n_dp):
            block = feats[scalars[h]]
            for k in range(parts):
                out[h, k * rows : (k + 1) * rows, :] = block[:, k * LANES : (k + 1) * LANES]
            count = jnp.full((COUNT_ROWS, LANES), scalars[n_dp + h].astype(jnp.float32))
            out[h, parts * rows :, :] = count.astype(out.dtype)

    scalars = jnp.concatenate([image_of, count_of, cache_pos[None]]).astype(jnp.int32)
    out_rows = parts * rows + COUNT_ROWS
    return pl.pallas_call(
        kernel,
        grid_spec=pltpu.PrefetchScalarGridSpec(
            num_scalar_prefetch=1,
            grid=(1,),
            in_specs=[pl.BlockSpec((images, rows, cols), lambda i, s: (0, 0, s[2 * n_dp]))],
            out_specs=pl.BlockSpec((n_dp, out_rows, LANES), lambda i, s: (0, 0, 0)),
        ),
        out_shape=jax.ShapeDtypeStruct((n_dp, out_rows, LANES), student_feats.dtype),
        compiler_params=params(),
        name="dispatch_rows",
    )(scalars, student_feats)


OUTER = (((0,), (0,)), ((), ()))


def head_terms(scalars, rows_by_place, head_weight, teacher, row_info, full_cols):
    n_img, split_rows, lanes = rows_by_place[0].shape
    width, cols = head_weight.shape
    block, tile, patch = 512, 256, 32
    splits = split_rows // patch
    part = splits * lanes
    rows = n_img * patch
    n_part = width // part
    steps, tiles = rows // block, cols // tile
    half = steps // 2
    img_block = block // patch
    pairs = N_X * N_Z
    owner_rows = width // (pairs * N_CORE)
    out_rows = width // N_CORE

    def kernel(sc, x0, x1, x2, x3a, x3b, w_ref, t_ref, info_ref, keep, send, x_scr, g_scr, r_scr):
        step = pl.program_id(0)

        @pl.when(step < steps)
        def _():
            here = pl.ds(pl.multiple_of(step * block, block), block)
            far = jnp.where(step < half, x3a[...], x3b[...])
            xs = [x0[...], x1[...], x2[...], far]
            for x, off in zip(xs, (0, n_part - 1, 1, 2)):
                first = lax.rem(sc[0] + off, n_part) * part
                for k in range(splits):
                    x_scr[here, pl.ds(pl.multiple_of(first + k * lanes, lanes), lanes)] = x[
                        :, k * patch : (k + 1) * patch, :
                    ].reshape(block, lanes)
            pred = jnp.dot(x_scr[here, :], w_ref[...], preferred_element_type=jnp.float32)
            info = info_ref[...]
            mean, inv, coef, weight = (info[:, k : k + 1] for k in range(4))
            residue = pred - (t_ref[...].astype(jnp.float32) - mean) * inv
            g_scr[here, :] = (coef * residue).astype(jnp.bfloat16)
            row_loss = weight * jnp.sum(residue * residue, axis=-1, keepdims=True)
            row_loss = jnp.broadcast_to(row_loss, (block, EXT)).reshape(img_block, patch, EXT)
            r_scr[pl.ds(pl.multiple_of(step * img_block, img_block), img_block), :] = (
                jnp.sum(row_loss, axis=1) / full_cols
            )

        @pl.when((step >= steps) & (step < steps + tiles))
        def _():
            first = pl.multiple_of((step - steps) * tile, tile)
            term = lax.dot_general(
                x_scr[...], g_scr[:, pl.ds(first, tile)], OUTER, preferred_element_type=jnp.float32
            )
            term = term.reshape(pairs, N_CORE, owner_rows, tile)
            for mine, (one, two) in enumerate(((keep, send), (send, keep))):

                @pl.when(sc[1] == mine)
                def _():
                    one[...] = term[:, 0].reshape(out_rows, tile)
                    two[...] = term[:, 1].reshape(out_rows, tile)

        @pl.when(step == steps + tiles)
        def _():
            lane = lax.broadcasted_iota(jnp.int32, (1, EXT), 1)
            top = lax.broadcasted_iota(jnp.int32, (owner_rows, EXT), 0) == 0
            for ref, own in ((keep, sc[1]), (send, 1 - sc[1])):
                ref[...] = jnp.zeros_like(ref)
                for pair in range(pairs):
                    image = pair * N_CORE + own
                    line = jnp.where(lane == sc[2 + image], r_scr[pl.ds(image, 1), :], 0.0)
                    ref[pair * owner_rows : (pair + 1) * owner_rows, :EXT] = jnp.where(top, line, 0.0)

    row_at = lambda i: jnp.minimum(i, steps - 1)
    row_spec = lambda c: pl.BlockSpec((block, c), lambda i, s: (row_at(i), 0))
    img_spec = lambda f: pl.BlockSpec((img_block, split_rows, lanes), lambda i, s: (f(i), 0, 0))
    far_spec = lambda f: img_spec(lambda i: jnp.clip(f(i), 0, half - 1))
    out_spec = pl.BlockSpec((out_rows, tile), lambda i, s: (0, jnp.maximum(i - steps, 0)))
    out = jax.ShapeDtypeStruct((out_rows, cols + tile), jnp.float32)
    return pl.pallas_call(
        kernel,
        grid_spec=pltpu.PrefetchScalarGridSpec(
            num_scalar_prefetch=1,
            grid=(steps + tiles + 1,),
            in_specs=[
                img_spec(row_at),
                img_spec(row_at),
                img_spec(row_at),
                far_spec(lambda i: i),
                far_spec(lambda i: i - half),
                pl.BlockSpec((width, cols), lambda i, s: (0, 0)),
                row_spec(cols),
                row_spec(row_info.shape[1]),
            ],
            out_specs=[out_spec, out_spec],
            scratch_shapes=[
                pltpu.VMEM((rows, width), jnp.bfloat16),
                pltpu.VMEM((rows, cols), jnp.bfloat16),
                pltpu.VMEM((n_img, EXT), jnp.float32),
            ],
        ),
        out_shape=[out, out],
        compiler_params=params(),
        cost_estimate=pl.CostEstimate(
            flops=4 * rows * width * cols, bytes_accessed=25 * 2**20, transcendentals=0
        ),
        name="head_terms",
    )(scalars, *rows_by_place, head_weight, teacher, row_info)


def exponent(part):
    top = jnp.max(jnp.abs(part), axis=-1, keepdims=True)
    return jnp.ceil(jnp.log(jnp.maximum(top, 2.0**-100)) * 1.4426950408889634)


def code(main, extra):
    main_exp, extra_exp = exponent(main), exponent(extra)
    main_code = jnp.floor(main * jnp.exp2(14.0 - main_exp) + 0.5).astype(jnp.int32)
    extra_code = jnp.floor(extra * jnp.exp2(14.0 - extra_exp) + 0.5)
    lane = lax.broadcasted_iota(jnp.int32, extra.shape, 1)
    extra_code = jnp.where(
        lane == EXT - 2, main_exp, jnp.where(lane == EXT - 1, extra_exp, extra_code)
    ).astype(jnp.int32)
    return main_code.astype(jnp.int16), extra_code.astype(jnp.int16)


def decode(codes):
    cols = codes.shape[-1] - EXT
    wide = codes.astype(jnp.int32).astype(jnp.float32)
    main, extra = wide[:, :cols], wide[:, cols:]
    main_exp = extra[:, EXT - 2 : EXT - 1]
    extra_exp = extra[:, EXT - 1 :]
    lane = lax.broadcasted_iota(jnp.int32, extra.shape, 1)
    extra = jnp.where(lane < EXT - 2, extra, 0.0)
    return main * jnp.exp2(main_exp - 14.0), extra * jnp.exp2(extra_exp - 14.0)


def add_and_code(own_x, keep, received):
    rows, wide = keep.shape
    cols = wide - 2 * EXT
    block = rows // N_X
    order = (2, 1, 3, 0)

    def kernel(sc, a, b, *outs):
        main, extra = code(a[:, :cols] + b[:, :cols], a[:, cols : cols + EXT] + b[:, cols : cols + EXT])
        for k, ahead in enumerate(order):

            @pl.when(pl.program_id(0) == k)
            def _():
                outs[ahead][:, :cols] = main
                outs[ahead][:, cols:] = extra

    def block_of(i, s):
        ahead = jnp.where(i == 0, order[0], jnp.where(i == 1, order[1], jnp.where(i == 2, order[2], order[3])))
        return (lax.rem(s[0] + ahead, N_X), 0)

    spec = pl.BlockSpec((block, wide), block_of)
    return pl.pallas_call(
        kernel,
        grid_spec=pltpu.PrefetchScalarGridSpec(
            num_scalar_prefetch=1,
            grid=(N_X,),
            in_specs=[spec, spec],
            out_specs=[pl.BlockSpec((block, cols + EXT), lambda i, s: (0, 0))] * N_X,
        ),
        out_shape=[jax.ShapeDtypeStruct((block, cols + EXT), jnp.int16)] * N_X,
        compiler_params=params(),
        name="add_and_code",
    )(own_x[None].astype(jnp.int32), keep, received)


def sum_blocks(blocks):
    main, extra = decode(blocks[0])
    for block in blocks[1:]:
        m, e = decode(block)
        main, extra = main + m, extra + e
    return main, extra


def sum_and_code(blocks):
    rows, wide = blocks[0].shape
    cols = wide - EXT
    block = 32

    def kernel(*refs):
        *src, out = refs
        main, extra = code(*sum_blocks([ref[...] for ref in src]))
        out[:, :cols] = main
        out[:, cols:] = extra

    spec = pl.BlockSpec((block, wide), lambda i: (i, 0))
    return pl.pallas_call(
        kernel,
        grid=(rows // block,),
        in_specs=[spec] * len(blocks),
        out_specs=spec,
        out_shape=jax.ShapeDtypeStruct((rows, wide), jnp.int16),
        compiler_params=params(),
        name="sum_and_code",
    )(*blocks)


def sum_last(received):
    n, rows, wide = received.shape

    def kernel(src, out, ext):
        main, extra = sum_blocks([src[k] for k in range(n)])
        out[...] = main
        ext[...] = extra

    return pl.pallas_call(
        kernel,
        out_shape=[
            jax.ShapeDtypeStruct((rows, wide - EXT), jnp.float32),
            jax.ShapeDtypeStruct((rows, EXT), jnp.float32),
        ],
        compiler_params=params(),
        name="sum_last",
    )(received)


def local(
    student_feats,
    head_weight,
    teacher_cache,
    holder_index,
    valid_count,
    image_embed,
    text_embed,
    pair_ids,
):
    n_dp = lax.axis_size("dp")
    n_cache = lax.axis_size("cache")
    own_index = lax.axis_index("dp")
    cache_pos = lax.axis_index("cache")
    core = own_index % N_CORE
    img_dev, patch_rows, student_width = student_feats.shape
    slots, _, local_cols = teacher_cache.shape
    full_cols = local_cols * n_cache
    part = student_width // n_cache
    shard_rows, embed = image_embed.shape
    assert slots == n_dp and n_dp == N_X * N_Z * N_CORE

    def ring(x, step):
        return lax.ppermute(x, "cache", [(i, (i + step) % n_cache) for i in range(n_cache)])

    def flat(x):
        return x.reshape(-1, x.shape[-1])

    img_order = jnp.arange(img_dev, dtype=jnp.int32)
    own_holders = lax.dynamic_slice_in_dim(holder_index, own_index * img_dev, img_dev, 0)
    dp_order = jnp.arange(n_dp, dtype=jnp.int32)
    image_of = jnp.sum(
        jnp.where(own_holders[None, :] == dp_order[:, None], img_order[None, :], 0), axis=1
    )
    count_of = jnp.sum(
        jnp.where(own_holders[None, :] == dp_order[:, None], valid_count[None, :], 0), axis=1
    )
    outgoing = dispatch_rows(student_feats, image_of, count_of, cache_pos, part)

    def swap(x, bit):
        return lax.ppermute(x, "dp", [(i, i ^ bit) for i in range(n_dp)])

    def both(x, bit):
        other = swap(x, bit)
        upper = (own_index // bit) % 2 == 1
        return jnp.concatenate([jnp.where(upper, other, x), jnp.where(upper, x, other)])

    texts = both(text_embed, 2)
    outgoing, texts, teacher_in = lax.optimization_barrier((outgoing, texts, teacher_cache))

    with jax.named_scope("student_exchange"):
        mine = lax.all_to_all(outgoing, "dp", split_axis=0, concat_axis=0, tiled=True)
    with jax.named_scope("teacher_sums"):
        wide = teacher_in.astype(jnp.float32)
        sums = jnp.stack([jnp.sum(wide, axis=-1), jnp.sum(wide * wide, axis=-1)])
        pair_cols = jnp.concatenate(
            [
                (pair_ids // 64)[:, None],
                (pair_ids % 64)[:, None],
                jnp.zeros((shard_rows, EXT - 2), jnp.int32),
            ],
            axis=1,
        ).astype(jnp.float32)
        images = jnp.concatenate([image_embed.astype(jnp.float32), pair_cols], axis=1)
        packed = jnp.concatenate([sums.reshape(-1, EXT), images.reshape(-1, EXT)])
        packed = [packed] + [ring(packed, step) for step in range(1, n_cache)]
        n_sum = sums.size // EXT
        sums = sum(p[:n_sum] for p in packed).reshape(sums.shape)
        images = jnp.concatenate([p[n_sum:] for p in packed]).reshape(img_dev, embed + EXT)
    texts = both(texts, 4)
    mine, sums, images, texts = lax.optimization_barrier((mine, sums, images, texts))
    with jax.named_scope("student_ring"):
        counts_sent, mine = mine[:, -COUNT_ROWS:], mine[:, :-COUNT_ROWS]
        from_prev = ring(mine, 1)
        from_next = ring(mine, -1)
        from_prev, from_next, sums, counts_sent = lax.optimization_barrier(
            (from_prev, from_next, sums, counts_sent)
        )
        far_a = ring(from_prev[: n_dp // 2], 1)
        far_b = ring(from_next[n_dp // 2 :], -1)
    with jax.named_scope("teacher_sums"):
        row_mean = sums[0] / full_cols
        inv_scale = lax.rsqrt(sums[1] / full_cols - row_mean * row_mean + eps)

    is_held = holder_index.reshape(n_dp, img_dev) == own_index
    place_of = jnp.sum(jnp.where(is_held, img_order[None, :], 0), axis=1)
    held_any = jnp.sum(is_held.astype(jnp.int32), axis=1) > 0
    held_count = jnp.where(held_any, counts_sent[:, 0, 0].astype(jnp.float32), 0.0)
    row_index = jnp.arange(patch_rows, dtype=jnp.int32).astype(jnp.float32)
    valid_mask = (row_index[None, :] < held_count[:, None]).astype(jnp.float32)
    row_weight = valid_mask / jnp.maximum(held_count, 1.0)[:, None]
    coef = 2.0 * loss_scale / full_cols * row_weight
    inv_scale = jnp.where(held_count[:, None] > 0, inv_scale, 0.0)
    row_info = jnp.stack([row_mean, inv_scale, coef, row_weight], axis=-1).reshape(
        n_dp * patch_rows, 4
    )

    scalars = jnp.concatenate([jnp.stack([cache_pos, core]).astype(jnp.int32), place_of])
    far_a, far_b, texts = lax.optimization_barrier((far_a, far_b, texts))
    texts = both(texts, 8)
    keep, send = head_terms(
        scalars,
        [mine, from_prev, from_next, far_a, far_b],
        head_weight,
        flat(teacher_cache),
        row_info,
        full_cols,
    )
    keep, send, texts = lax.optimization_barrier((keep, send, texts))
    with jax.named_scope("grad_core"):
        received = swap(send, 1)
    texts = both(texts, 2 * N_Z)
    own_x = own_index // (N_Z * N_CORE)
    codes = add_and_code(own_x, keep, received)
    with jax.named_scope("grad_x"):
        blocks = [codes[0]] + [
            lax.ppermute(
                codes[step], "dp", [(i, (i + step * N_Z * N_CORE) % n_dp) for i in range(n_dp)]
            )
            for step in (2, 1, 3)
        ]
    texts = lax.optimization_barrier((texts, *codes))[0]
    texts = both(texts, 4 * N_Z)
    codes = sum_and_code(blocks)
    codes, images, texts = lax.optimization_barrier((codes, images, texts))
    texts = both(texts, 1)
    with jax.named_scope("contrast"):
        pairs = images[:, embed].astype(jnp.int32) * 64 + images[:, embed + 1].astype(jnp.int32)
        logits = jnp.dot(
            images[:, :embed].astype(jnp.bfloat16),
            texts.T,
            preferred_element_type=jnp.float32,
        ) * (embed ** (-0.5))
        column = jnp.arange(texts.shape[0], dtype=jnp.int32)
        text_row, text_z = column % shard_rows, column // shard_rows % N_Z
        text_x = column // (shard_rows * N_Z) % N_X
        text_core = column // (shard_rows * N_Z * N_X)
        text_dp = (text_x * N_Z + text_z) * N_CORE + text_core
        text_id = text_dp * img_dev + cache_pos * shard_rows + text_row
        best = jnp.max(logits, axis=1)
        denom = jnp.sum(jnp.exp(logits - best[:, None]), axis=1)
        target = jnp.sum(jnp.where(pairs[:, None] == text_id[None, :], logits, 0.0), axis=1)
        partial = jnp.pad(jnp.stack([best, denom, target]), ((0, 5), (0, EXT - img_dev)))
    with jax.named_scope("grad_z"):
        codes = lax.all_to_all(
            codes.reshape(N_Z, -1, local_cols + EXT), "dp", 0, 0, axis_index_groups=Z_GROUPS, tiled=True
        )
    head_grad, extra = sum_last(codes)

    with jax.named_scope("loss_parts"):
        parts = jnp.concatenate([partial[:3], extra[:1], partial[4:]])
        parts = [parts] + [ring(parts, step) for step in range(1, n_cache)]
        partials = []
        for k, got in enumerate(parts):
            first = (n_cache - k) % n_cache * shard_rows
            partials.append(got[:3, first : first + shard_rows])
        partials = jnp.stack(partials)
        best = jnp.max(partials[:, 0], axis=0)
        denom = jnp.sum(partials[:, 1] * jnp.exp(partials[:, 0] - best[None, :]), axis=0)
        contrast = best + jnp.log(denom) - jnp.sum(partials[:, 2], axis=0)
        regress = sum(got[3] for got in parts)
        regress = lax.dynamic_slice_in_dim(regress, cache_pos * shard_rows, shard_rows, 0)
    return (head_grad, regress + contrast)


def solution(mesh):
    in_specs = (
        P("dp", None, None),
        P(None, "cache"),
        P("dp", None, "cache"),
        P(),
        P("dp"),
        P(("dp", "cache"), None),
        P(("dp", "cache"), None),
        P(("dp", "cache")),
    )
    out_specs = (P("dp", "cache"), P(("dp", "cache")))
    return jax.shard_map(local, mesh=mesh, in_specs=in_specs, out_specs=out_specs, check_vma=False)
```

time: 201 us -> 194 us (0.965)
  waiting for transfers between devices: 71.7 us -> 91.1 us
  starting transfers between devices: 62.1 us -> 45.2 us
  Pallas kernels: 42.3 us -> 36.5 us
    ppermute x14 -> x10, waiting for transfers between devices: 23.5 us -> 36.6 us  [ring(): lax.ppermute(x, 'cache', [(i, (i + step) % n_cache) for i in range(n_cach...]
    ppermute x14 -> x10, starting transfers between devices: 23.8 us -> 15.5 us  [ring(): lax.ppermute(x, 'cache', [(i, (i + step) % n_cache) for i in range(n_cach...]
    pallas_call x2 -> x1, Pallas kernels: 29.1 us -> 22.9 us  [head_terms(): pl.pallas_call(kernel, grid_spec=pltpu.PrefetchScalarGridSpec(num_scalar_...]
    ppermute x6 -> x3, starting transfers between devices: 8.47 us -> 2.85 us  [local(): lax.ppermute(codes[step], 'dp', [(i, (i + step * N_Z * N_CORE) % n_dp) fo...]
    ppermute x8 -> x7, starting transfers between devices: 12.5 us -> 9.53 us  [swap(): return lax.ppermute(x, 'dp', [(i, i ^ bit) for i in range(n_dp)])]
    ppermute x6 -> x3, waiting for transfers between devices: 12.1 us -> 14.9 us  [local(): lax.ppermute(codes[step], 'dp', [(i, (i + step * N_Z * N_CORE) % n_dp) fo...]
    ppermute x8 -> x7, waiting for transfers between devices: 22.1 us -> 24.5 us  [swap(): return lax.ppermute(x, 'dp', [(i, i ^ bit) for i in range(n_dp)])]
    unnamed x35 -> x23, local copies, waits for them, and re-layouts: 4.66 us -> 3.93 us
  transfers between devices with their start and end apart: 30 -> 22, of which waited for: 15 -> 14; matrix products, arithmetic and copies ran while one was open for 8% -> 7% of each run, Pallas kernels for 8% -> 13%
where the time goes in v5:
time: 194 us; the launch traced here: 193 us
  waiting for transfers between devices  91.1 us (47%)
  starting transfers between devices  45.2 us (23%)
  Pallas kernels  36.5 us (19%)
  local copies, waits for them, and re-layouts  9.51 us (5%)
  other arithmetic  9.21 us (5%)
    ppermute x10, waiting for transfers between devices, ring(): lax.ppermute(x, 'cache', [(i, (i + step) % n_cache) for i in range(n_cach...  36.6 us
    ppermute x7, waiting for transfers between devices, swap(): return lax.ppermute(x, 'dp', [(i, i ^ bit) for i in range(n_dp)])  24.5 us
    pallas_call x1, Pallas kernels, head_terms(): pl.pallas_call(kernel, grid_spec=pltpu.PrefetchScalarGridSpec(num_scalar_...  22.9 us
    ppermute x10, starting transfers between devices, ring(): lax.ppermute(x, 'cache', [(i, (i + step) % n_cache) for i in range(n_cach...  15.5 us
    ppermute x3, waiting for transfers between devices, local(): lax.ppermute(codes[step], 'dp', [(i, (i + step * N_Z * N_CORE) % n_dp) fo...  14.9 us
    all_to_all x1, waiting for transfers between devices, local(): lax.all_to_all(codes.reshape(N_Z, -1, local_cols + EXT), 'dp', 0, 0, axis...  13.7 us
    all_to_all x1, starting transfers between devices, local(): lax.all_to_all(outgoing, 'dp', split_axis=0, concat_axis=0, tiled=True)  11.1 us
    ppermute x7, starting transfers between devices, swap(): return lax.ppermute(x, 'dp', [(i, i ^ bit) for i in range(n_dp)])  9.53 us
  transfers between devices with their start and end apart: 22, of which 14 were waited for; matrix products, arithmetic and copies ran while one was open for 7% of the time, Pallas kernels for 13%

profile of v5, /device:TPU:2, one launch (start us, length us, event | category | flops | bytes accessed | tf_op | source)
XLA Modules:
  0.0 193.0 jit_solution(17318066022641066313)
XLA Ops:
  0.7 2.0 %collective-permute-start = (bf16[8,768]{1,0:T(8,128)(2,1)}, bf16[8,768]{1,0:T(8,128)(2,1)S(1)}, u32[]{:S(2)}, u32[]{:S(2)}) collective-permute-start(bf16[8,768]{1,0:T(8,128)(2,1)} %param.14), channel_id=1, source_target_pairs={{0,8},{4,12},{8,0},{12,4},{16,24},{20,28},{24,16},{28,20},{32,40},... | collective-permute-start | bytes 36872 | tf_op jit(solution)/shard_map/ppermute | solution.py:313
  4.8 2.9 %dispatch_rows.1 = bf16[64,72,128]{2,1,0:T(8,128)(2,1)} custom-call(s32[129]{0:T(256)} %pad_add_fusion.scalars, bf16[32,32,1024]{2,1,0:T(8,128)(2,1)} %feats.1), custom_call_target="tpu_custom_call" | custom-call | tf_op jit(solution)/shard_map/dispatch_rows/pallas_call | solution.py:43
  7.8 11.1 %all-to-all-start = ((bf16[64,72,128]{2,1,0:T(8,128)(2,1)}), bf16[64,72,128]{2,1,0:T(8,128)(2,1)S(1)}, u32[]{:S(2)}, u32[]{:S(2)}) async-start(bf16[64,72,128]{2,1,0:T(8,128)(2,1)} %dispatch_rows.1), calls=%async_computation | async-start | bytes 2359296 | tf_op jit(solution)/shard_map/student_exchange/all_to_all | solution.py:324
  19.4 4.3 %convert_reduce_fusion = (f32[64,32]{1,0:T(8,128)S(1)}, f32[64,32]{1,0:T(8,128)S(1)}) fusion(bf16[64,32,1280]{2,1,0:T(8,128)(2,1)} %param.10), kind=kLoop, calls=%fused_computation.1 | loop fusion | flops 10481664 | bytes 5259264 | tf_op jit(solution)/shard_map/teacher_sums/reduce_sum | solution.py:327
  23.8 2.5 %collective-permute-start.4 = (bf16[16,768]{1,0:T(8,128)(2,1)S(1)}, bf16[16,768]{1,0:T(8,128)(2,1)S(1)}, u32[]{:S(2)}, u32[]{:S(2)}) collective-permute-start(bf16[16,768]{1,0:T(8,128)(2,1)S(1)} %pad_maximum_fusion.8), channel_id=1, source_target_pairs={{0,16},{4,20},{8,24},{12,28},{16,0},{20,4},{24,8},{28,12},{32,48},... | collective-permute-start | bytes 73736 | tf_op jit(solution)/shard_map/ppermute | solution.py:313
  26.2 3.0 %collective-permute-start.3 = (f32[88,128]{1,0:T(8,128)S(1)}, f32[88,128]{1,0:T(8,128)S(1)}, u32[]{:S(2)}, u32[]{:S(2)}) collective-permute-start(f32[88,128]{1,0:T(8,128)S(1)} %constant_dynamic-update-slice_fusion), channel_id=1, source_target_pairs={{0,3},{1,0},{2,1},{3,2},{4,7},{5,4},{6,5},{7,6},{8,11},{9,8},{10,9... | collective-permute-start | bytes 135176 | tf_op jit(solution)/shard_map/teacher_sums/ppermute | solution.py:296
  30.8 16.9 %collective-permute-done.4 = bf16[16,768]{1,0:T(8,128)(2,1)S(1)} collective-permute-done((bf16[16,768]{1,0:T(8,128)(2,1)S(1)}, bf16[16,768]{1,0:T(8,128)(2,1)S(1)}, u32[]{:S(2)}, u32[]{:S(2)}) %collective-permute-start.4) | collective-permute-done | bytes 24608 | tf_op jit(solution)/shard_map/ppermute | solution.py:313
  53.7 22.8 %collective-permute-done.5.x1 = bf16[64,64,128]{2,1,0:T(8,128)(2,1)S(1)} collective-permute-done((bf16[64,64,128]{2,1,0:T(8,128)(2,1)S(1)}, bf16[64,64,128]{2,1,0:T(8,128)(2,1)S(1)}, u32[]{:S(2)}, u32[]{:S(2)}) %collective-permute-start.5) | collective-permute-done | bytes 1048608 | tf_op jit(solution)/shard_map/student_ring/ppermute | solution.py:296
  84.3 8.2 %collective-permute-done.7.x3a = bf16[32,64,128]{2,1,0:T(8,128)(2,1)} collective-permute-done((bf16[32,64,128]{2,1,0:T(8,128)(2,1)S(1)}, bf16[32,64,128]{2,1,0:T(8,128)(2,1)}, u32[]{:S(2)}, u32[]{:S(2)}) %collective-permute-start.7) | collective-permute-done | bytes 524320 | tf_op jit(solution)/shard_map/student_ring/ppermute | solution.py:296
  93.9 22.9 %head_terms.1 = (f32[512,1536]{1,0:T(8,128)}, f32[512,1536]{1,0:T(8,128)}) custom-call(s32[66]{0:T(128)} %pad_add_fusion.1.sc, bf16[64,64,128]{2,1,0:T(8,128)(2,1)} %copy-done.2, bf16[64,64,128]{2,1,0:T(8,128)(2,1)} %copy-done.6, bf16[64,64,128]{2,1,0:T(8,128)(2,1)} %collective-permute-done.6.x2, bf16[32,64,128]{2,1,0:T(8,128)(2,1)} %collective-permute-done.7.x3a, ...), custom_call_target="tpu_custom_call" | custom-call | flops 10737418240 | bytes 26214400 | tf_op jit(solution)/shard_map/head_terms/pallas_call | solution.py:131
  117.0 2.0 %collective-permute-start.14 = (bf16[64,768]{1,0:T(8,128)(2,1)S(1)}, bf16[64,768]{1,0:T(8,128)(2,1)S(1)}, u32[]{:S(2)}, u32[]{:S(2)}) collective-permute-start(bf16[64,768]{1,0:T(8,128)(2,1)S(1)} %pad_maximum_fusion.3), channel_id=1, source_target_pairs={{0,64},{4,68},{8,72},{12,76},{16,80},{20,84},{24,88},{28,92},{32,9... | collective-permute-start | bytes 294920 | tf_op jit(solution)/shard_map/ppermute | solution.py:313
  119.0 3.4 %collective-permute-done.14 = bf16[64,768]{1,0:T(8,128)(2,1)S(1)} collective-permute-done((bf16[64,768]{1,0:T(8,128)(2,1)S(1)}, bf16[64,768]{1,0:T(8,128)(2,1)S(1)}, u32[]{:S(2)}, u32[]{:S(2)}) %collective-permute-start.14) | collective-permute-done | bytes 98336 | tf_op jit(solution)/shard_map/ppermute | solution.py:313
  124.5 5.0 %add_and_code.1 = (s16[128,1408]{1,0:T(8,128)(2,1)}, s16[128,1408]{1,0:T(8,128)(2,1)}, s16[128,1408]{1,0:T(8,128)(2,1)}, s16[128,1408]{1,0:T(8,128)(2,1)}) custom-call(s32[1]{0:T(128)} %bitcast.sc, f32[512,1536]{1,0:T(8,128)} %get-tuple-element.46.a, f32[512,1536]{1,0:T(8,128)} %copy-done), custom_call_target="tpu_custom_call" | custom-call | tf_op jit(solution)/shard_map/add_and_code/pallas_call | solution.py:209
  129.6 2.7 %collective-permute-start.15 = (bf16[128,768]{1,0:T(8,128)(2,1)S(1)}, bf16[128,768]{1,0:T(8,128)(2,1)S(1)}, u32[]{:S(2)}, u32[]{:S(2)}) collective-permute-start(bf16[128,768]{1,0:T(8,128)(2,1)S(1)} %pad_maximum_fusion.1), channel_id=1, source_target_pairs={{0,128},{4,132},{8,136},{12,140},{16,144},{20,148},{24,152},{28,15... | collective-permute-start | bytes 589832 | tf_op jit(solution)/shard_map/ppermute | solution.py:313
  133.1 1.9 collective-permute-start.12
  135.1 3.8 %collective-permute-done.15 = bf16[128,768]{1,0:T(8,128)(2,1)S(1)} collective-permute-done((bf16[128,768]{1,0:T(8,128)(2,1)S(1)}, bf16[128,768]{1,0:T(8,128)(2,1)S(1)}, u32[]{:S(2)}, u32[]{:S(2)}) %collective-permute-start.15) | collective-permute-done | bytes 196640 | tf_op jit(solution)/shard_map/ppermute | solution.py:313
  139.0 7.6 %collective-permute-done.11.refs_1_ = s16[128,1408]{1,0:T(8,128)(2,1)S(1)} collective-permute-done((s16[128,1408]{1,0:T(8,128)(2,1)}, s16[128,1408]{1,0:T(8,128)(2,1)S(1)}, u32[]{:S(2)}, u32[]{:S(2)}) %collective-permute-start.11) | collective-permute-done | bytes 360480 | tf_op jit(solution)/shard_map/grad_x/ppermute | solution.py:389
  146.6 7.3 %collective-permute-done.12.refs_2_ = s16[128,1408]{1,0:T(8,128)(2,1)S(1)} collective-permute-done((s16[128,1408]{1,0:T(8,128)(2,1)}, s16[128,1408]{1,0:T(8,128)(2,1)S(1)}, u32[]{:S(2)}, u32[]{:S(2)}) %collective-permute-start.12) | collective-permute-done | bytes 360480 | tf_op jit(solution)/shard_map/grad_x/ppermute | solution.py:389
  155.4 3.8 %sum_and_code.1 = s16[128,1408]{1,0:T(8,128)(2,1)} custom-call(s16[128,1408]{1,0:T(8,128)(2,1)} %get-tuple-element.48.refs_0_, s16[128,1408]{1,0:T(8,128)(2,1)} %copy-done.3, s16[128,1408]{1,0:T(8,128)(2,1)} %copy-done.4, s16[128,1408]{1,0:T(8,128)(2,1)} %copy-done.5), custom_call_target="tpu_custom_call" | custom-call | tf_op jit(solution)/shard_map/sum_and_code/pallas_call | solution.py:243
  159.4 6.2 %all-to-all-start.1 = ((s16[8,16,1408]{2,1,0:T(8,128)(2,1)}), s16[8,16,1408]{2,1,0:T(8,128)(2,1)S(1)}, u32[]{:S(2)}, u32[]{:S(2)}) async-start(s16[8,16,1408]{2,1,0:T(8,128)(2,1)} %bitcast.29), calls=%async_computation.1 | async-start | bytes 720896 | tf_op jit(solution)/shard_map/grad_z/all_to_all | solution.py:417
  166.5 13.7 %all-to-all-done.1.src = s16[8,16,1408]{2,1,0:T(8,128)(2,1)S(1)} async-done(((s16[8,16,1408]{2,1,0:T(8,128)(2,1)}), s16[8,16,1408]{2,1,0:T(8,128)(2,1)S(1)}, u32[]{:S(2)}, u32[]{:S(2)}) %all-to-all-start.1) | async-done | bytes 360480 | tf_op jit(solution)/shard_map/grad_z/all_to_all | solution.py:417
  180.9 1.7 sum_last.1
  183.4 2.9 %collective-permute-start.19 = (f32[8,128]{1,0:T(8,128)S(1)}, f32[8,128]{1,0:T(8,128)S(1)}, u32[]{:S(2)}, u32[]{:S(2)}) collective-permute-start(f32[8,128]{1,0:T(8,128)S(1)} %maximum_maximum_fusion), channel_id=1, source_target_pairs={{0,3},{1,0},{2,1},{3,2},{4,7},{5,4},{6,5},{7,6},{8,11},{9,8},{10,9... | collective-permute-start | bytes 12296 | tf_op jit(solution)/shard_map/loss_parts/ppermute | solution.py:296
  187.7 3.7 %collective-permute-done.18 = f32[8,128]{1,0:T(8,128)S(1)} collective-permute-done((f32[8,128]{1,0:T(8,128)S(1)}, f32[8,128]{1,0:T(8,128)S(1)}, u32[]{:S(2)}, u32[]{:S(2)}) %collective-permute-start.18) | collective-permute-done | bytes 4128 | tf_op jit(solution)/shard_map/loss_parts/ppermute | solution.py:296
  (126 shorter events, 29.4 us)
Async XLA Ops:
  0.7 7.1 %collective-permute-start = (bf16[8,768]{1,0:T(8,128)(2,1)}, bf16[8,768]{1,0:T(8,128)(2,1)S(1)}, u32[]{:S(2)}, u32[]{:S(2)}) collective-permute-start(bf16[8,768]{1,0:T(8,128)(2,1)} %param.14), channel_id=1, source_target_pairs={{0,8},{4,12},{8,0},{12,4},{16,24},{20,28},{24,16},{28,20},{32,40},... | collective-permute-start | bytes 36872 | tf_op jit(solution)/shard_map/ppermute | solution.py:313
  7.8 41.5 %all-to-all-start = ((bf16[64,72,128]{2,1,0:T(8,128)(2,1)}), bf16[64,72,128]{2,1,0:T(8,128)(2,1)S(1)}, u32[]{:S(2)}, u32[]{:S(2)}) async-start(bf16[64,72,128]{2,1,0:T(8,128)(2,1)} %dispatch_rows.1), calls=%async_computation | async-start | bytes 2359296 | tf_op jit(solution)/shard_map/student_exchange/all_to_all | solution.py:324
  19.4 33.4 %copy-start.9 = (s32[2048]{0:T(1024)S(1)}, s32[2048]{0:T(1024)}, u32[]{:S(2)}) copy-start(s32[2048]{0:T(1024)} %param.11) | copy-start | bytes 24580
  23.8 24.0 %collective-permute-start.4 = (bf16[16,768]{1,0:T(8,128)(2,1)S(1)}, bf16[16,768]{1,0:T(8,128)(2,1)S(1)}, u32[]{:S(2)}, u32[]{:S(2)}) collective-permute-start(bf16[16,768]{1,0:T(8,128)(2,1)S(1)} %pad_maximum_fusion.8), channel_id=1, source_target_pairs={{0,16},{4,20},{8,24},{12,28},{16,0},{20,4},{24,8},{28,12},{32,48},... | collective-permute-start | bytes 73736 | tf_op jit(solution)/shard_map/ppermute | solution.py:313
  26.2 21.6 %collective-permute-start.3 = (f32[88,128]{1,0:T(8,128)S(1)}, f32[88,128]{1,0:T(8,128)S(1)}, u32[]{:S(2)}, u32[]{:S(2)}) collective-permute-start(f32[88,128]{1,0:T(8,128)S(1)} %constant_dynamic-update-slice_fusion), channel_id=1, source_target_pairs={{0,3},{1,0},{2,1},{3,2},{4,7},{5,4},{6,5},{7,6},{8,11},{9,8},{10,9... | collective-permute-start | bytes 135176 | tf_op jit(solution)/shard_map/teacher_sums/ppermute | solution.py:296
  29.2 18.6 %collective-permute-start.2 = (f32[88,128]{1,0:T(8,128)S(1)}, f32[88,128]{1,0:T(8,128)S(1)}, u32[]{:S(2)}, u32[]{:S(2)}) collective-permute-start(f32[88,128]{1,0:T(8,128)S(1)} %constant_dynamic-update-slice_fusion), channel_id=1, source_target_pairs={{0,2},{1,3},{2,0},{3,1},{4,6},{5,7},{6,4},{7,5},{8,10},{9,11},{10,... | collective-permute-start | bytes 135176 | tf_op jit(solution)/shard_map/teacher_sums/ppermute | solution.py:296
  29.9 17.9 %collective-permute-start.1 = (f32[88,128]{1,0:T(8,128)S(1)}, f32[88,128]{1,0:T(8,128)S(1)}, u32[]{:S(2)}, u32[]{:S(2)}) collective-permute-start(f32[88,128]{1,0:T(8,128)S(1)} %constant_dynamic-update-slice_fusion), channel_id=1, source_target_pairs={{0,1},{1,2},{2,3},{3,0},{4,5},{5,6},{6,7},{7,4},{8,9},{9,10},{10,1... | collective-permute-start | bytes 135176 | tf_op jit(solution)/shard_map/teacher_sums/ppermute | solution.py:296
  49.5 44.5 %copy-start.2 = (bf16[64,64,128]{2,1,0:T(8,128)(2,1)}, bf16[64,64,128]{2,1,0:T(8,128)(2,1)S(1)}, u32[]{:S(2)}) copy-start(bf16[64,64,128]{2,1,0:T(8,128)(2,1)S(1)} %slice.97.x0) | copy-start | bytes 3145732
  49.5 27.1 %collective-permute-start.5 = (bf16[64,64,128]{2,1,0:T(8,128)(2,1)S(1)}, bf16[64,64,128]{2,1,0:T(8,128)(2,1)S(1)}, u32[]{:S(2)}, u32[]{:S(2)}) collective-permute-start(bf16[64,64,128]{2,1,0:T(8,128)(2,1)S(1)} %slice.97.x0), channel_id=1, source_target_pairs={{0,1},{1,2},{2,3},{3,0},{4,5},{5,6},{6,7},{7,4},{8,9},{9,10},{10,1... | collective-permute-start | bytes 3145736 | tf_op jit(solution)/shard_map/student_ring/ppermute | solution.py:296
  51.1 26.0 %collective-permute-start.6 = (bf16[64,64,128]{2,1,0:T(8,128)(2,1)S(1)}, bf16[64,64,128]{2,1,0:T(8,128)(2,1)}, u32[]{:S(2)}, u32[]{:S(2)}) collective-permute-start(bf16[64,64,128]{2,1,0:T(8,128)(2,1)S(1)} %slice.97.x0), channel_id=1, source_target_pairs={{0,3},{1,0},{2,1},{3,2},{4,7},{5,4},{6,5},{7,6},{8,11},{9,8},{10,9... | collective-permute-start | bytes 3145736 | tf_op jit(solution)/shard_map/student_ring/ppermute | solution.py:296
  77.2 15.3 %collective-permute-start.7 = (bf16[32,64,128]{2,1,0:T(8,128)(2,1)S(1)}, bf16[32,64,128]{2,1,0:T(8,128)(2,1)}, u32[]{:S(2)}, u32[]{:S(2)}) collective-permute-start(bf16[32,64,128]{2,1,0:T(8,128)(2,1)S(1)} %slice.99), channel_id=1, source_target_pairs={{0,1},{1,2},{2,3},{3,0},{4,5},{5,6},{6,7},{7,4},{8,9},{9,10},{10,1... | collective-permute-start | bytes 1572872 | tf_op jit(solution)/shard_map/student_ring/ppermute | solution.py:296
  79.9 13.7 %collective-permute-start.8 = (bf16[32,64,128]{2,1,0:T(8,128)(2,1)S(1)}, bf16[32,64,128]{2,1,0:T(8,128)(2,1)}, u32[]{:S(2)}, u32[]{:S(2)}) collective-permute-start(bf16[32,64,128]{2,1,0:T(8,128)(2,1)S(1)} %slice.100), channel_id=1, source_target_pairs={{0,3},{1,0},{2,1},{3,2},{4,7},{5,4},{6,5},{7,6},{8,11},{9,8},{10,9... | collective-permute-start | bytes 1572872 | tf_op jit(solution)/shard_map/student_ring/ppermute | solution.py:296
  93.7 23.2 %collective-permute-start.9 = (bf16[32,768]{1,0:T(8,128)(2,1)S(1)}, bf16[32,768]{1,0:T(8,128)(2,1)S(1)}, u32[]{:S(2)}, u32[]{:S(2)}) collective-permute-start(bf16[32,768]{1,0:T(8,128)(2,1)S(1)} %pad_maximum_fusion.5), channel_id=1, source_target_pairs={{0,32},{4,36},{8,40},{12,44},{16,48},{20,52},{24,56},{28,60},{32,0... | collective-permute-start | bytes 147464 | tf_op jit(solution)/shard_map/ppermute | solution.py:313
  116.9 6.0 %collective-permute-start.10 = (f32[512,1536]{1,0:T(8,128)}, f32[512,1536]{1,0:T(8,128)S(1)}, u32[]{:S(2)}, u32[]{:S(2)}) collective-permute-start(f32[512,1536]{1,0:T(8,128)} %get-tuple-element.47), channel_id=1, source_target_pairs={{0,4},{4,0},{8,12},{12,8},{16,20},{20,16},{24,28},{28,24},{32,36},... | collective-permute-start | bytes 9437192 | tf_op jit(solution)/shard_map/grad_core/ppermute | solution.py:313
  117.0 5.4 %collective-permute-start.14 = (bf16[64,768]{1,0:T(8,128)(2,1)S(1)}, bf16[64,768]{1,0:T(8,128)(2,1)S(1)}, u32[]{:S(2)}, u32[]{:S(2)}) collective-permute-start(bf16[64,768]{1,0:T(8,128)(2,1)S(1)} %pad_maximum_fusion.3), channel_id=1, source_target_pairs={{0,64},{4,68},{8,72},{12,76},{16,80},{20,84},{24,88},{28,92},{32,9... | collective-permute-start | bytes 294920 | tf_op jit(solution)/shard_map/ppermute | solution.py:313
  129.6 9.3 %collective-permute-start.15 = (bf16[128,768]{1,0:T(8,128)(2,1)S(1)}, bf16[128,768]{1,0:T(8,128)(2,1)S(1)}, u32[]{:S(2)}, u32[]{:S(2)}) collective-permute-start(bf16[128,768]{1,0:T(8,128)(2,1)S(1)} %pad_maximum_fusion.1), channel_id=1, source_target_pairs={{0,128},{4,132},{8,136},{12,140},{16,144},{20,148},{24,152},{28,15... | collective-permute-start | bytes 589832 | tf_op jit(solution)/shard_map/ppermute | solution.py:313
  132.3 14.3 %collective-permute-start.11 = (s16[128,1408]{1,0:T(8,128)(2,1)}, s16[128,1408]{1,0:T(8,128)(2,1)S(1)}, u32[]{:S(2)}, u32[]{:S(2)}) collective-permute-start(s16[128,1408]{1,0:T(8,128)(2,1)} %get-tuple-element.49), channel_id=1, source_target_pairs={{0,128},{4,132},{8,136},{12,140},{16,144},{20,148},{24,152},{28,15... | collective-permute-start | bytes 1081352 | tf_op jit(solution)/shard_map/grad_x/ppermute | solution.py:389
  133.1 20.8 %collective-permute-start.12 = (s16[128,1408]{1,0:T(8,128)(2,1)}, s16[128,1408]{1,0:T(8,128)(2,1)S(1)}, u32[]{:S(2)}, u32[]{:S(2)}) collective-permute-start(s16[128,1408]{1,0:T(8,128)(2,1)} %get-tuple-element.50), channel_id=1, source_target_pairs={{0,64},{4,68},{8,72},{12,76},{16,80},{20,84},{24,88},{28,92},{32,9... | collective-permute-start | bytes 1081352 | tf_op jit(solution)/shard_map/grad_x/ppermute | solution.py:389
  135.0 18.9 %collective-permute-start.13 = (s16[128,1408]{1,0:T(8,128)(2,1)}, s16[128,1408]{1,0:T(8,128)(2,1)S(1)}, u32[]{:S(2)}, u32[]{:S(2)}) collective-permute-start(s16[128,1408]{1,0:T(8,128)(2,1)} %get-tuple-element.51), channel_id=1, source_target_pairs={{0,192},{4,196},{8,200},{12,204},{16,208},{20,212},{24,216},{28,22... | collective-permute-start | bytes 1081352 | tf_op jit(solution)/shard_map/grad_x/ppermute | solution.py:389
  159.3 6.5 %collective-permute-start.16 = (bf16[256,768]{1,0:T(8,128)(2,1)S(1)}, bf16[256,768]{1,0:T(8,128)(2,1)S(1)}, u32[]{:S(2)}, u32[]{:S(2)}) collective-permute-start(bf16[256,768]{1,0:T(8,128)(2,1)S(1)} %pad_maximum_fusion), channel_id=1, source_target_pairs={{0,4},{4,0},{8,12},{12,8},{16,20},{20,16},{24,28},{28,24},{32,36},... | collective-permute-start | bytes 1179656 | tf_op jit(solution)/shard_map/ppermute | solution.py:313
  159.4 20.8 %all-to-all-start.1 = ((s16[8,16,1408]{2,1,0:T(8,128)(2,1)}), s16[8,16,1408]{2,1,0:T(8,128)(2,1)S(1)}, u32[]{:S(2)}, u32[]{:S(2)}) async-start(s16[8,16,1408]{2,1,0:T(8,128)(2,1)} %bitcast.29), calls=%async_computation.1 | async-start | bytes 720896 | tf_op jit(solution)/shard_map/grad_z/all_to_all | solution.py:417
  183.4 4.2 %collective-permute-start.19 = (f32[8,128]{1,0:T(8,128)S(1)}, f32[8,128]{1,0:T(8,128)S(1)}, u32[]{:S(2)}, u32[]{:S(2)}) collective-permute-start(f32[8,128]{1,0:T(8,128)S(1)} %maximum_maximum_fusion), channel_id=1, source_target_pairs={{0,3},{1,0},{2,1},{3,2},{4,7},{5,4},{6,5},{7,6},{8,11},{9,8},{10,9... | collective-permute-start | bytes 12296 | tf_op jit(solution)/shard_map/loss_parts/ppermute | solution.py:296
  186.3 5.1 %collective-permute-start.18 = (f32[8,128]{1,0:T(8,128)S(1)}, f32[8,128]{1,0:T(8,128)S(1)}, u32[]{:S(2)}, u32[]{:S(2)}) collective-permute-start(f32[8,128]{1,0:T(8,128)S(1)} %maximum_maximum_fusion), channel_id=1, source_target_pairs={{0,2},{1,3},{2,0},{3,1},{4,6},{5,7},{6,4},{7,5},{8,10},{9,11},{10,... | collective-permute-start | bytes 12296 | tf_op jit(solution)/shard_map/loss_parts/ppermute | solution.py:296
  186.8 4.8 %collective-permute-start.17 = (f32[8,128]{1,0:T(8,128)S(1)}, f32[8,128]{1,0:T(8,128)S(1)}, u32[]{:S(2)}, u32[]{:S(2)}) collective-permute-start(f32[8,128]{1,0:T(8,128)S(1)} %maximum_maximum_fusion), channel_id=1, source_target_pairs={{0,1},{1,2},{2,3},{3,0},{4,5},{5,6},{6,7},{7,4},{8,9},{9,10},{10,1... | collective-permute-start | bytes 12296 | tf_op jit(solution)/shard_map/loss_parts/ppermute | solution.py:296
  (9 other events, 72.7 us)

commit v6 on v5

--- a/solution.py
+++ b/solution.py
@@ -12,9 +12,7 @@
 EXT = 128
 VMEM_BYTES = 60 * 1024 * 1024
 
-Z_GROUPS = [
-    [(x * N_Z + z) * N_CORE + c for z in range(N_Z)] for x in range(N_X) for c in range(N_CORE)
-]
+XZ_GROUPS = [[k * N_CORE + c for k in range(N_X * N_Z)] for c in range(N_CORE)]
 
 
 def params():
@@ -25,40 +23,89 @@
 COUNT_ROWS = 8
 
 
-def dispatch_rows(student_feats, image_of, count_of, cache_pos, cols):
-    n_dp = image_of.shape[0]
-    images, rows, _ = student_feats.shape
+def dispatch_rows(student_feats, holder_index, valid_count, own_index, cache_pos, cols):
+    images, rows, width = student_feats.shape
+    n_dp = holder_index.shape[0] // images
     parts = cols // LANES
 
-    def kernel(scalars, feats, out):
-        for h in range(n_dp):
-            block = feats[scalars[h]]
+    def kernel(place, holders, counts, feats, out):
+        out[...] = jnp.zeros_like(out)
+        for i in range(images):
+            h = holders[place[0] * images + i]
             for k in range(parts):
-                out[h, k * rows : (k + 1) * rows, :] = block[:, k * LANES : (k + 1) * LANES]
-            count = jnp.full((COUNT_ROWS, LANES), scalars[n_dp + h].astype(jnp.float32))
+                out[h, k * rows : (k + 1) * rows, :] = feats[i, :, k * LANES : (k + 1) * LANES]
+            count = jnp.full((COUNT_ROWS, LANES), counts[i].astype(jnp.float32))
             out[h, parts * rows :, :] = count.astype(out.dtype)
 
-    scalars = jnp.concatenate([image_of, count_of, cache_pos[None]]).astype(jnp.int32)
     out_rows = parts * rows + COUNT_ROWS
     return pl.pallas_call(
         kernel,
         grid_spec=pltpu.PrefetchScalarGridSpec(
-            num_scalar_prefetch=1,
+            num_scalar_prefetch=3,
             grid=(1,),
-            in_specs=[pl.BlockSpec((images, rows, cols), lambda i, s: (0, 0, s[2 * n_dp]))],
-            out_specs=pl.BlockSpec((n_dp, out_rows, LANES), lambda i, s: (0, 0, 0)),
+            in_specs=[pl.BlockSpec((images, rows, cols), lambda i, p, h, c: (0, 0, p[1]))],
+            out_specs=pl.BlockSpec((n_dp, out_rows, LANES), lambda i, p, h, c: (0, 0, 0)),
         ),
         out_shape=jax.ShapeDtypeStruct((n_dp, out_rows, LANES), student_feats.dtype),
         compiler_params=params(),
         name="dispatch_rows",
-    )(scalars, student_feats)
-
-
-OUTER = (((0,), (0,)), ((), ()))
-
-
-def head_terms(scalars, rows_by_place, head_weight, teacher, row_info, full_cols):
-    n_img, split_rows, lanes = rows_by_place[0].shape
+    )(jnp.stack([own_index, cache_pos]).astype(jnp.int32), holder_index, valid_count, student_feats)
+
+
+def near_terms(cache_pos, near, head_weight):
+    n_img, split_rows, lanes = near[0].shape
+    width, cols = head_weight.shape
+    block, patch = 512, 32
+    splits = split_rows // patch
+    part = splits * lanes
+    n_part = width // part
+    rows = n_img * patch
+    img_block = block // patch
+
+    def kernel(sc, x0, x1, x2, w_ref, pred_out, xt_out):
+        xt_out[...] = jnp.zeros_like(xt_out)
+        pred = jnp.zeros((block, cols), jnp.float32)
+        for ref, off in ((x0, 0), (x1, n_part - 1), (x2, 1)):
+            first = lax.rem(sc[0] + off, n_part) * part
+            pieces = [
+                ref[:, k * patch : (k + 1) * patch, :].reshape(block, lanes) for k in range(splits)
+            ]
+            for k, piece in enumerate(pieces):
+                xt_out[pl.ds(pl.multiple_of(first + k * lanes, lanes), lanes), :] = piece.T
+            pred = pred + jnp.dot(
+                jnp.concatenate(pieces, axis=1),
+                w_ref[pl.ds(pl.multiple_of(first, part), part), :],
+                preferred_element_type=jnp.float32,
+            )
+        pred_out[...] = pred
+
+    img_spec = pl.BlockSpec((img_block, split_rows, lanes), lambda i, s: (i, 0, 0))
+    return pl.pallas_call(
+        kernel,
+        grid_spec=pltpu.PrefetchScalarGridSpec(
+            num_scalar_prefetch=1,
+            grid=(rows // block,),
+            in_specs=[img_spec] * 3 + [pl.BlockSpec((width, cols), lambda i, s: (0, 0))],
+            out_specs=[
+                pl.BlockSpec((block, cols), lambda i, s: (i, 0)),
+                pl.BlockSpec((width, block), lambda i, s: (0, i)),
+            ],
+        ),
+        out_shape=[
+            jax.ShapeDtypeStruct((rows, cols), jnp.float32),
+            jax.ShapeDtypeStruct((width, rows), near[0].dtype),
+        ],
+        compiler_params=params(),
+        cost_estimate=pl.CostEstimate(
+            flops=2 * rows * 3 * part * cols, bytes_accessed=20 * 2**20, transcendentals=0
+        ),
+        name="near_terms",
+    )(cache_pos[None].astype(jnp.int32), *near, head_weight)
+
+
+def head_terms(scalars, near_pred, near_cols, far_a, far_b, head_weight, teacher, row_info, full_cols):
+    half_img, split_rows, lanes = far_a.shape
+    n_img = 2 * half_img
     width, cols = head_weight.shape
     block, tile, patch = 512, 256, 32
     splits = split_rows // patch
@@ -72,21 +119,21 @@
     owner_rows = width // (pairs * N_CORE)
     out_rows = width // N_CORE
 
-    def kernel(sc, x0, x1, x2, x3a, x3b, w_ref, t_ref, info_ref, keep, send, x_scr, g_scr, r_scr):
+    def kernel(sc, pred_ref, xt_ref, fa, fb, w_ref, t_ref, info_ref, keep, send, x_scr, g_scr, r_scr):
         step = pl.program_id(0)
 
         @pl.when(step < steps)
         def _():
             here = pl.ds(pl.multiple_of(step * block, block), block)
-            far = jnp.where(step < half, x3a[...], x3b[...])
-            xs = [x0[...], x1[...], x2[...], far]
-            for x, off in zip(xs, (0, n_part - 1, 1, 2)):
-                first = lax.rem(sc[0] + off, n_part) * part
-                for k in range(splits):
-                    x_scr[here, pl.ds(pl.multiple_of(first + k * lanes, lanes), lanes)] = x[
-                        :, k * patch : (k + 1) * patch, :
-                    ].reshape(block, lanes)
-            pred = jnp.dot(x_scr[here, :], w_ref[...], preferred_element_type=jnp.float32)
+            far = jnp.where(step < half, fa[...], fb[...])
+            pieces = [far[:, k * patch : (k + 1) * patch, :].reshape(block, lanes) for k in range(splits)]
+            x_scr[:, here] = xt_ref[...]
+            first = lax.rem(sc[0] + 2, n_part) * part
+            for k, piece in enumerate(pieces):
+                x_scr[pl.ds(pl.multiple_of(first + k * lanes, lanes), lanes), here] = piece.T
+            pred = pred_ref[...] + jnp.dot(
+                jnp.concatenate(pieces, axis=1), w_ref[...], preferred_element_type=jnp.float32
+            )
             info = info_ref[...]
             mean, inv, coef, weight = (info[:, k : k + 1] for k in range(4))
             residue = pred - (t_ref[...].astype(jnp.float32) - mean) * inv
@@ -100,9 +147,7 @@
         @pl.when((step >= steps) & (step < steps + tiles))
         def _():
             first = pl.multiple_of((step - steps) * tile, tile)
-            term = lax.dot_general(
-                x_scr[...], g_scr[:, pl.ds(first, tile)], OUTER, preferred_element_type=jnp.float32
-            )
+            term = jnp.dot(x_scr[...], g_scr[:, pl.ds(first, tile)], preferred_element_type=jnp.float32)
             term = term.reshape(pairs, N_CORE, owner_rows, tile)
             for mine, (one, two) in enumerate(((keep, send), (send, keep))):
 
@@ -124,8 +169,9 @@
 
     row_at = lambda i: jnp.minimum(i, steps - 1)
     row_spec = lambda c: pl.BlockSpec((block, c), lambda i, s: (row_at(i), 0))
-    img_spec = lambda f: pl.BlockSpec((img_block, split_rows, lanes), lambda i, s: (f(i), 0, 0))
-    far_spec = lambda f: img_spec(lambda i: jnp.clip(f(i), 0, half - 1))
+    far_spec = lambda f: pl.BlockSpec(
+        (img_block, split_rows, lanes), lambda i, s: (jnp.clip(f(i), 0, half - 1), 0, 0)
+    )
     out_spec = pl.BlockSpec((out_rows, tile), lambda i, s: (0, jnp.maximum(i - steps, 0)))
     out = jax.ShapeDtypeStruct((out_rows, cols + tile), jnp.float32)
     return pl.pallas_call(
@@ -134,18 +180,17 @@
             num_scalar_prefetch=1,
             grid=(steps + tiles + 1,),
             in_specs=[
-                img_spec(row_at),
-                img_spec(row_at),
-                img_spec(row_at),
+                row_spec(cols),
+                pl.BlockSpec((width, block), lambda i, s: (0, row_at(i))),
                 far_spec(lambda i: i),
                 far_spec(lambda i: i - half),
-                pl.BlockSpec((width, cols), lambda i, s: (0, 0)),
+                pl.BlockSpec((part, cols), lambda i, s: (lax.rem(s[0] + 2, n_part), 0)),
                 row_spec(cols),
                 row_spec(row_info.shape[1]),
             ],
             out_specs=[out_spec, out_spec],
             scratch_shapes=[
-                pltpu.VMEM((rows, width), jnp.bfloat16),
+                pltpu.VMEM((width, rows), jnp.bfloat16),
                 pltpu.VMEM((rows, cols), jnp.bfloat16),
                 pltpu.VMEM((n_img, EXT), jnp.float32),
             ],
@@ -153,10 +198,10 @@
         out_shape=[out, out],
         compiler_params=params(),
         cost_estimate=pl.CostEstimate(
-            flops=4 * rows * width * cols, bytes_accessed=25 * 2**20, transcendentals=0
+            flops=3 * rows * width * cols, bytes_accessed=30 * 2**20, transcendentals=0
         ),
         name="head_terms",
-    )(scalars, *rows_by_place, head_weight, teacher, row_info)
+    )(scalars, near_pred, near_cols, far_a, far_b, head_weight, teacher, row_info)
 
 
 def exponent(part):
@@ -186,38 +231,26 @@
     return main * jnp.exp2(main_exp - 14.0), extra * jnp.exp2(extra_exp - 14.0)
 
 
-def add_and_code(own_x, keep, received):
+def add_and_code(keep, received):
     rows, wide = keep.shape
     cols = wide - 2 * EXT
-    block = rows // N_X
-    order = (2, 1, 3, 0)
-
-    def kernel(sc, a, b, *outs):
+    block = rows // 4
+
+    def kernel(a, b, out):
         main, extra = code(a[:, :cols] + b[:, :cols], a[:, cols : cols + EXT] + b[:, cols : cols + EXT])
-        for k, ahead in enumerate(order):
-
-            @pl.when(pl.program_id(0) == k)
-            def _():
-                outs[ahead][:, :cols] = main
-                outs[ahead][:, cols:] = extra
-
-    def block_of(i, s):
-        ahead = jnp.where(i == 0, order[0], jnp.where(i == 1, order[1], jnp.where(i == 2, order[2], order[3])))
-        return (lax.rem(s[0] + ahead, N_X), 0)
-
-    spec = pl.BlockSpec((block, wide), block_of)
+        out[:, :cols] = main
+        out[:, cols:] = extra
+
+    spec = pl.BlockSpec((block, wide), lambda i: (i, 0))
     return pl.pallas_call(
         kernel,
-        grid_spec=pltpu.PrefetchScalarGridSpec(
-            num_scalar_prefetch=1,
-            grid=(N_X,),
-            in_specs=[spec, spec],
-            out_specs=[pl.BlockSpec((block, cols + EXT), lambda i, s: (0, 0))] * N_X,
-        ),
-        out_shape=[jax.ShapeDtypeStruct((block, cols + EXT), jnp.int16)] * N_X,
+        grid=(rows // block,),
+        in_specs=[spec, spec],
+        out_specs=pl.BlockSpec((block, cols + EXT), lambda i: (i, 0)),
+        out_shape=jax.ShapeDtypeStruct((rows, cols + EXT), jnp.int16),
         compiler_params=params(),
         name="add_and_code",
-    )(own_x[None].astype(jnp.int32), keep, received)
+    )(keep, received)
 
 
 def sum_blocks(blocks):
@@ -226,29 +259,6 @@
         m, e = decode(block)
         main, extra = main + m, extra + e
     return main, extra
-
-
-def sum_and_code(blocks):
-    rows, wide = blocks[0].shape
-    cols = wide - EXT
-    block = 32
-
-    def kernel(*refs):
-        *src, out = refs
-        main, extra = code(*sum_blocks([ref[...] for ref in src]))
-        out[:, :cols] = main
-        out[:, cols:] = extra
-
-    spec = pl.BlockSpec((block, wide), lambda i: (i, 0))
-    return pl.pallas_call(
-        kernel,
-        grid=(rows // block,),
-        in_specs=[spec] * len(blocks),
-        out_specs=spec,
-        out_shape=jax.ShapeDtypeStruct((rows, wide), jnp.int16),
-        compiler_params=params(),
-        name="sum_and_code",
-    )(*blocks)
 
 
 def sum_last(received):
@@ -299,15 +309,7 @@
         return x.reshape(-1, x.shape[-1])
 
     img_order = jnp.arange(img_dev, dtype=jnp.int32)
-    own_holders = lax.dynamic_slice_in_dim(holder_index, own_index * img_dev, img_dev, 0)
-    dp_order = jnp.arange(n_dp, dtype=jnp.int32)
-    image_of = jnp.sum(
-        jnp.where(own_holders[None, :] == dp_order[:, None], img_order[None, :], 0), axis=1
-    )
-    count_of = jnp.sum(
-        jnp.where(own_holders[None, :] == dp_order[:, None], valid_count[None, :], 0), axis=1
-    )
-    outgoing = dispatch_rows(student_feats, image_of, count_of, cache_pos, part)
+    outgoing = dispatch_rows(student_feats, holder_index, valid_count, own_index, cache_pos, part)
 
     def swap(x, bit):
         return lax.ppermute(x, "dp", [(i, i ^ bit) for i in range(n_dp)])
@@ -317,8 +319,16 @@
         upper = (own_index // bit) % 2 == 1
         return jnp.concatenate([jnp.where(upper, other, x), jnp.where(upper, x, other)])
 
-    texts = both(text_embed, 2)
-    outgoing, texts, teacher_in = lax.optimization_barrier((outgoing, texts, teacher_cache))
+    def four(x, bit):
+        low, high = (own_index // bit) % 2 == 1, (own_index // (2 * bit)) % 2 == 1
+        a, b, c, d = x, swap(x, bit), swap(x, 2 * bit), swap(x, 3 * bit)
+        a, b = jnp.where(low, b, a), jnp.where(low, a, b)
+        c, d = jnp.where(low, d, c), jnp.where(low, c, d)
+        a, c = jnp.where(high, c, a), jnp.where(high, a, c)
+        b, d = jnp.where(high, d, b), jnp.where(high, b, d)
+        return jnp.concatenate([a, b, c, d])
+
+    outgoing, texts, teacher_in = lax.optimization_barrier((outgoing, text_embed, teacher_cache))
 
     with jax.named_scope("student_exchange"):
         mine = lax.all_to_all(outgoing, "dp", split_axis=0, concat_axis=0, tiled=True)
@@ -339,7 +349,7 @@
         n_sum = sums.size // EXT
         sums = sum(p[:n_sum] for p in packed).reshape(sums.shape)
         images = jnp.concatenate([p[n_sum:] for p in packed]).reshape(img_dev, embed + EXT)
-    texts = both(texts, 4)
+    texts = four(both(texts, 1), 2)
     mine, sums, images, texts = lax.optimization_barrier((mine, sums, images, texts))
     with jax.named_scope("student_ring"):
         counts_sent, mine = mine[:, -COUNT_ROWS:], mine[:, :-COUNT_ROWS]
@@ -350,6 +360,7 @@
         )
         far_a = ring(from_prev[: n_dp // 2], 1)
         far_b = ring(from_next[n_dp // 2 :], -1)
+    near_pred, near_cols = near_terms(cache_pos, [mine, from_prev, from_next], head_weight)
     with jax.named_scope("teacher_sums"):
         row_mean = sums[0] / full_cols
         inv_scale = lax.rsqrt(sums[1] / full_cols - row_mean * row_mean + eps)
@@ -369,10 +380,13 @@
 
     scalars = jnp.concatenate([jnp.stack([cache_pos, core]).astype(jnp.int32), place_of])
     far_a, far_b, texts = lax.optimization_barrier((far_a, far_b, texts))
-    texts = both(texts, 8)
+    texts = both(texts, N_Z)
     keep, send = head_terms(
         scalars,
-        [mine, from_prev, from_next, far_a, far_b],
+        near_pred,
+        near_cols,
+        far_a,
+        far_b,
         head_weight,
         flat(teacher_cache),
         row_info,
@@ -382,20 +396,9 @@
     with jax.named_scope("grad_core"):
         received = swap(send, 1)
     texts = both(texts, 2 * N_Z)
-    own_x = own_index // (N_Z * N_CORE)
-    codes = add_and_code(own_x, keep, received)
-    with jax.named_scope("grad_x"):
-        blocks = [codes[0]] + [
-            lax.ppermute(
-                codes[step], "dp", [(i, (i + step * N_Z * N_CORE) % n_dp) for i in range(n_dp)]
-            )
-            for step in (2, 1, 3)
-        ]
-    texts = lax.optimization_barrier((texts, *codes))[0]
+    codes = add_and_code(keep, received)
+    codes, images, texts = lax.optimization_barrier((codes, images, texts))
     texts = both(texts, 4 * N_Z)
-    codes = sum_and_code(blocks)
-    codes, images, texts = lax.optimization_barrier((codes, images, texts))
-    texts = both(texts, 1)
     with jax.named_scope("contrast"):
         pairs = images[:, embed].astype(jnp.int32) * 64 + images[:, embed + 1].astype(jnp.int32)
         logits = jnp.dot(
@@ -404,18 +407,14 @@
             preferred_element_type=jnp.float32,
         ) * (embed ** (-0.5))
         column = jnp.arange(texts.shape[0], dtype=jnp.int32)
-        text_row, text_z = column % shard_rows, column // shard_rows % N_Z
-        text_x = column // (shard_rows * N_Z) % N_X
-        text_core = column // (shard_rows * N_Z * N_X)
-        text_dp = (text_x * N_Z + text_z) * N_CORE + text_core
-        text_id = text_dp * img_dev + cache_pos * shard_rows + text_row
+        text_id = column // shard_rows * img_dev + cache_pos * shard_rows + column % shard_rows
         best = jnp.max(logits, axis=1)
         denom = jnp.sum(jnp.exp(logits - best[:, None]), axis=1)
         target = jnp.sum(jnp.where(pairs[:, None] == text_id[None, :], logits, 0.0), axis=1)
         partial = jnp.pad(jnp.stack([best, denom, target]), ((0, 5), (0, EXT - img_dev)))
-    with jax.named_scope("grad_z"):
+    with jax.named_scope("grad_xz"):
         codes = lax.all_to_all(
-            codes.reshape(N_Z, -1, local_cols + EXT), "dp", 0, 0, axis_index_groups=Z_GROUPS, tiled=True
+            codes.reshape(N_X * N_Z, -1, local_cols + EXT), "dp", 0, 0, axis_index_groups=XZ_GROUPS, tiled=True
         )
     head_grad, extra = sum_last(codes)
 

time: 194 us -> 189 us (0.974)
  waiting for transfers between devices: 91.1 us -> 79.8 us
  Pallas kernels: 36.5 us -> 40.2 us
  starting transfers between devices: 45.2 us -> 47.3 us
    ppermute x3 -> x0, waiting for transfers between devices: 14.9 us -> none  [local(): lax.ppermute(codes[step], 'dp', [(i, (i + step * N_Z * N_CORE) % n_dp) fo...]
    ppermute x7 -> x8, waiting for transfers between devices: 24.5 us -> 38 us  [swap(): return lax.ppermute(x, 'dp', [(i, i ^ bit) for i in range(n_dp)])]
    ppermute x10, waiting for transfers between devices: 36.6 us -> 26.8 us  [ring(): lax.ppermute(x, 'cache', [(i, (i + step) % n_cache) for i in range(n_cach...]
    pallas_call x2, Pallas kernels: 8.88 us -> 15.1 us  [the longest x1 10.2 us: near_terms(): pl.pallas_call(kernel, grid_spec=pltpu.PrefetchScalarGridSpec(num_scalar_...]
    pallas_call x1, Pallas kernels: 22.9 us -> 19.6 us  [head_terms(): pl.pallas_call(kernel, grid_spec=pltpu.PrefetchScalarGridSpec(num_scalar_...]
    ppermute x7 -> x8, starting transfers between devices: 9.53 us -> 12.5 us  [swap(): return lax.ppermute(x, 'dp', [(i, i ^ bit) for i in range(n_dp)])]
    ppermute x3 -> x0, starting transfers between devices: 2.85 us -> none  [local(): lax.ppermute(codes[step], 'dp', [(i, (i + step * N_Z * N_CORE) % n_dp) fo...]
    unnamed x23 -> x19, local copies, waits for them, and re-layouts: 3.93 us -> 2.78 us
  transfers between devices with their start and end apart: 22 -> 20, of which waited for: 14 -> 8; matrix products, arithmetic and copies ran while one was open for 7% -> 7% of each run, Pallas kernels for 13% -> 16%
where the time goes in v6:
time: 189 us; the launch traced here: 186 us
  waiting for transfers between devices  79.8 us (42%)
  starting transfers between devices  47.3 us (25%)
  Pallas kernels  40.2 us (21%)
  other arithmetic  9.17 us (5%)
  local copies, waits for them, and re-layouts  8.25 us (4%)
    ppermute x8, waiting for transfers between devices, swap(): return lax.ppermute(x, 'dp', [(i, i ^ bit) for i in range(n_dp)])  38 us
    ppermute x10, waiting for transfers between devices, ring(): lax.ppermute(x, 'cache', [(i, (i + step) % n_cache) for i in range(n_cach...  26.8 us
    pallas_call x1, Pallas kernels, head_terms(): pl.pallas_call(kernel, grid_spec=pltpu.PrefetchScalarGridSpec(num_scalar_...  19.6 us
    all_to_all x1, waiting for transfers between devices, local(): lax.all_to_all(codes.reshape(N_X * N_Z, -1, local_cols + EXT), 'dp', 0, 0...  15 us
    ppermute x10, starting transfers between devices, ring(): lax.ppermute(x, 'cache', [(i, (i + step) % n_cache) for i in range(n_cach...  14.9 us
    ppermute x8, starting transfers between devices, swap(): return lax.ppermute(x, 'dp', [(i, i ^ bit) for i in range(n_dp)])  12.5 us
    all_to_all x1, starting transfers between devices, local(): lax.all_to_all(outgoing, 'dp', split_axis=0, concat_axis=0, tiled=True)  12 us
    pallas_call x1, Pallas kernels, near_terms(): pl.pallas_call(kernel, grid_spec=pltpu.PrefetchScalarGridSpec(num_scalar_...  10.2 us
  transfers between devices with their start and end apart: 20, of which 8 were waited for; matrix products, arithmetic and copies ran while one was open for 7% of the time, Pallas kernels for 16%

profile of v6, /device:TPU:2, one launch (start us, length us, event | category | flops | bytes accessed | tf_op | source)
XLA Modules:
  0.0 186.2 jit_solution(12052611286274049190)
XLA Ops:
  1.2 3.1 %dispatch_rows.1 = bf16[64,72,128]{2,1,0:T(8,128)(2,1)} custom-call(s32[2]{0:T(128)} %pad_add_fusion.1.place, s32[2048]{0:T(1024)} %holders.1, s32[32]{0:T(128)} %counts.1, bf16[32,32,1024]{2,1,0:T(8,128)(2,1)} %feats.1), custom_call_target="tpu_custom_call" | custom-call | tf_op jit(solution)/shard_map/dispatch_rows/pallas_call | solution.py:41
  4.4 12.0 %all-to-all-start = ((bf16[64,72,128]{2,1,0:T(8,128)(2,1)}), bf16[64,72,128]{2,1,0:T(8,128)(2,1)S(1)}, u32[]{:S(2)}, u32[]{:S(2)}) async-start(bf16[64,72,128]{2,1,0:T(8,128)(2,1)} %dispatch_rows.1), calls=%async_computation | async-start | bytes 2359296 | tf_op jit(solution)/shard_map/student_exchange/all_to_all | solution.py:334
  16.7 4.3 %convert_reduce_fusion = (f32[64,32]{1,0:T(8,128)S(1)}, f32[64,32]{1,0:T(8,128)S(1)}) fusion(bf16[64,32,1280]{2,1,0:T(8,128)(2,1)} %param.10), kind=kLoop, calls=%fused_computation.1 | loop fusion | flops 10481664 | bytes 5259264 | tf_op jit(solution)/shard_map/teacher_sums/reduce_sum | solution.py:337
  21.5 3.4 %collective-permute-start.4 = (bf16[16,768]{1,0:T(8,128)(2,1)S(1)}, bf16[16,768]{1,0:T(8,128)(2,1)S(1)}, u32[]{:S(2)}, u32[]{:S(2)}) collective-permute-start(bf16[16,768]{1,0:T(8,128)(2,1)S(1)} %pad_maximum_fusion.7), channel_id=1, source_target_pairs={{0,24},{4,28},{8,16},{12,20},{16,8},{20,12},{24,0},{28,4},{32,56},... | collective-permute-start | bytes 73736 | tf_op jit(solution)/shard_map/ppermute | solution.py:315
  26.0 3.0 %collective-permute-start.2 = (f32[88,128]{1,0:T(8,128)S(1)}, f32[88,128]{1,0:T(8,128)S(1)}, u32[]{:S(2)}, u32[]{:S(2)}) collective-permute-start(f32[88,128]{1,0:T(8,128)S(1)} %constant_dynamic-update-slice_fusion), channel_id=1, source_target_pairs={{0,3},{1,0},{2,1},{3,2},{4,7},{5,4},{6,5},{7,6},{8,11},{9,8},{10,9... | collective-permute-start | bytes 135176 | tf_op jit(solution)/shard_map/teacher_sums/ppermute | solution.py:306
  29.6 16.2 %collective-permute-done.4 = bf16[16,768]{1,0:T(8,128)(2,1)S(1)} collective-permute-done((bf16[16,768]{1,0:T(8,128)(2,1)S(1)}, bf16[16,768]{1,0:T(8,128)(2,1)S(1)}, u32[]{:S(2)}, u32[]{:S(2)}) %collective-permute-start.4) | collective-permute-done | bytes 24608 | tf_op jit(solution)/shard_map/ppermute | solution.py:315
  45.8 1.6 collective-permute-start
  47.5 3.6 %collective-permute-done = f32[88,128]{1,0:T(8,128)S(1)} collective-permute-done((f32[88,128]{1,0:T(8,128)S(1)}, f32[88,128]{1,0:T(8,128)S(1)}, u32[]{:S(2)}, u32[]{:S(2)}) %collective-permute-start) | collective-permute-done | bytes 45088 | tf_op jit(solution)/shard_map/teacher_sums/ppermute | solution.py:306
  52.5 2.9 %collective-permute-start.8 = (bf16[64,64,128]{2,1,0:T(8,128)(2,1)S(1)}, bf16[64,64,128]{2,1,0:T(8,128)(2,1)}, u32[]{:S(2)}, u32[]{:S(2)}) collective-permute-start(bf16[64,64,128]{2,1,0:T(8,128)(2,1)S(1)} %slice.97.x0), channel_id=1, source_target_pairs={{0,3},{1,0},{2,1},{3,2},{4,7},{5,4},{6,5},{7,6},{8,11},{9,8},{10,9... | collective-permute-start | bytes 3145736 | tf_op jit(solution)/shard_map/student_ring/ppermute | solution.py:306
  56.3 19.1 %collective-permute-done.7.x1 = bf16[64,64,128]{2,1,0:T(8,128)(2,1)S(1)} collective-permute-done((bf16[64,64,128]{2,1,0:T(8,128)(2,1)S(1)}, bf16[64,64,128]{2,1,0:T(8,128)(2,1)S(1)}, u32[]{:S(2)}, u32[]{:S(2)}) %collective-permute-start.7) | collective-permute-done | bytes 1048608 | tf_op jit(solution)/shard_map/student_ring/ppermute | solution.py:306
  77.2 3.0 %collective-permute-start.10 = (bf16[32,64,128]{2,1,0:T(8,128)(2,1)S(1)}, bf16[32,64,128]{2,1,0:T(8,128)(2,1)}, u32[]{:S(2)}, u32[]{:S(2)}) collective-permute-start(bf16[32,64,128]{2,1,0:T(8,128)(2,1)S(1)} %slice.100), channel_id=1, source_target_pairs={{0,3},{1,0},{2,1},{3,2},{4,7},{5,4},{6,5},{7,6},{8,11},{9,8},{10,9... | collective-permute-start | bytes 1572872 | tf_op jit(solution)/shard_map/student_ring/ppermute | solution.py:306
  82.8 10.2 %near_terms.1 = (f32[2048,1280]{1,0:T(8,128)}, bf16[1024,2048]{1,0:T(8,128)(2,1)}) custom-call(s32[1]{0:T(128)} %bitcast.sc, bf16[64,64,128]{2,1,0:T(8,128)(2,1)} %copy-done.2, bf16[64,64,128]{2,1,0:T(8,128)(2,1)} %copy-done.3, bf16[64,64,128]{2,1,0:T(8,128)(2,1)} %collective-permute-done.8.x2, bf16[1024,1280]{1,0:T(8,128)(2,1)} %w_ref.3), custom_call_target="tpu_custom_call" | custom-call | flops 4026531840 | bytes 20971520 | tf_op jit(solution)/shard_map/near_terms/pallas_call | solution.py:83
  93.0 4.8 %collective-permute-start.11 = (bf16[64,768]{1,0:T(8,128)(2,1)S(1)}, bf16[64,768]{1,0:T(8,128)(2,1)S(1)}, u32[]{:S(2)}, u32[]{:S(2)}) collective-permute-start(bf16[64,768]{1,0:T(8,128)(2,1)S(1)} %pad_maximum_fusion.3), channel_id=1, source_target_pairs={{0,32},{4,36},{8,40},{12,44},{16,48},{20,52},{24,56},{28,60},{32,0... | collective-permute-start | bytes 294920 | tf_op jit(solution)/shard_map/ppermute | solution.py:315
  97.8 19.6 %head_terms.1 = (f32[512,1536]{1,0:T(8,128)}, f32[512,1536]{1,0:T(8,128)}) custom-call(s32[66]{0:T(128)} %pad_add_fusion.sc, f32[2048,1280]{1,0:T(8,128)} %get-tuple-element.35.pred_ref, bf16[1024,2048]{1,0:T(8,128)(2,1)} %get-tuple-element.36.xt_ref, bf16[32,64,128]{2,1,0:T(8,128)(2,1)} %collective-permute-done.9.fa, ...), custom_call_target="tpu_custom_call" | custom-call | flops 8053063680 | bytes 31457280 | tf_op jit(solution)/shard_map/head_terms/pallas_call | solution.py:177
  118.2 6.7 %collective-permute-done.13 = bf16[128,768]{1,0:T(8,128)(2,1)S(1)} collective-permute-done((bf16[128,768]{1,0:T(8,128)(2,1)S(1)}, bf16[128,768]{1,0:T(8,128)(2,1)S(1)}, u32[]{:S(2)}, u32[]{:S(2)}) %collective-permute-start.13) | collective-permute-done | bytes 196640 | tf_op jit(solution)/shard_map/ppermute | solution.py:315
  125.0 1.6 copy-done.1
  126.6 4.9 %add_and_code.1 = s16[512,1408]{1,0:T(8,128)(2,1)} custom-call(f32[512,1536]{1,0:T(8,128)} %get-tuple-element.45.a, f32[512,1536]{1,0:T(8,128)} %copy-done.1), custom_call_target="tpu_custom_call" | custom-call | tf_op jit(solution)/shard_map/add_and_code/pallas_call | solution.py:245
  131.5 7.9 %all-to-all-start.1 = ((s16[32,16,1408]{2,1,0:T(8,128)(2,1)}), s16[32,16,1408]{2,1,0:T(8,128)(2,1)S(1)}, u32[]{:S(2)}, u32[]{:S(2)}) async-start(s16[32,16,1408]{2,1,0:T(8,128)(2,1)} %bitcast.28), calls=%async_computation.1 | async-start | bytes 2883584 | tf_op jit(solution)/shard_map/grad_xz/all_to_all | solution.py:416
  139.4 2.2 %collective-permute-start.14 = (bf16[256,768]{1,0:T(8,128)(2,1)S(1)}, bf16[256,768]{1,0:T(8,128)(2,1)S(1)}, u32[]{:S(2)}, u32[]{:S(2)}) collective-permute-start(bf16[256,768]{1,0:T(8,128)(2,1)S(1)} %pad_maximum_fusion), channel_id=1, source_target_pairs={{0,128},{4,132},{8,136},{12,140},{16,144},{20,148},{24,152},{28,15... | collective-permute-start | bytes 1179656 | tf_op jit(solution)/shard_map/ppermute | solution.py:315
  142.7 15.1 %collective-permute-done.14 = bf16[256,768]{1,0:T(8,128)(2,1)S(1)} collective-permute-done((bf16[256,768]{1,0:T(8,128)(2,1)S(1)}, bf16[256,768]{1,0:T(8,128)(2,1)S(1)}, u32[]{:S(2)}, u32[]{:S(2)}) %collective-permute-start.14) | collective-permute-done | bytes 393248 | tf_op jit(solution)/shard_map/ppermute | solution.py:315
  158.5 15.0 %all-to-all-done.1.src = s16[32,16,1408]{2,1,0:T(8,128)(2,1)S(1)} async-done(((s16[32,16,1408]{2,1,0:T(8,128)(2,1)}), s16[32,16,1408]{2,1,0:T(8,128)(2,1)S(1)}, u32[]{:S(2)}, u32[]{:S(2)}) %all-to-all-start.1) | async-done | bytes 1441824 | tf_op jit(solution)/shard_map/grad_xz/all_to_all | solution.py:416
  174.6 2.4 %sum_last.1 = (f32[16,1280]{1,0:T(8,128)}, f32[16,128]{1,0:T(8,128)}) custom-call(s16[32,16,1408]{2,1,0:T(8,128)(2,1)} %copy-done), custom_call_target="tpu_custom_call" | custom-call | tf_op jit(solution)/shard_map/sum_last/pallas_call | solution.py:272
  177.8 1.9 collective-permute-start.17
  181.5 3.3 %collective-permute-done.16 = f32[8,128]{1,0:T(8,128)S(1)} collective-permute-done((f32[8,128]{1,0:T(8,128)S(1)}, f32[8,128]{1,0:T(8,128)S(1)}, u32[]{:S(2)}, u32[]{:S(2)}) %collective-permute-start.16) | collective-permute-done | bytes 4128 | tf_op jit(solution)/shard_map/loss_parts/ppermute | solution.py:306
  (114 shorter events, 17.5 us)
Async XLA Ops:
  0.6 15.8 %copy-start.7 = (bf16[8,768]{1,0:T(8,128)(2,1)S(1)}, bf16[8,768]{1,0:T(8,128)(2,1)}, u32[]{:S(2)}) copy-start(bf16[8,768]{1,0:T(8,128)(2,1)} %param.14) | copy-start | bytes 36868
  4.4 47.5 %all-to-all-start = ((bf16[64,72,128]{2,1,0:T(8,128)(2,1)}), bf16[64,72,128]{2,1,0:T(8,128)(2,1)S(1)}, u32[]{:S(2)}, u32[]{:S(2)}) async-start(bf16[64,72,128]{2,1,0:T(8,128)(2,1)} %dispatch_rows.1), calls=%async_computation | async-start | bytes 2359296 | tf_op jit(solution)/shard_map/student_exchange/all_to_all | solution.py:334
  16.4 5.0 %collective-permute-start.3 = (bf16[8,768]{1,0:T(8,128)(2,1)S(1)}, bf16[8,768]{1,0:T(8,128)(2,1)S(1)}, u32[]{:S(2)}, u32[]{:S(2)}) collective-permute-start(bf16[8,768]{1,0:T(8,128)(2,1)S(1)} %copy-done.7), channel_id=1, source_target_pairs={{0,4},{4,0},{8,12},{12,8},{16,20},{20,16},{24,28},{28,24},{32,36},... | collective-permute-start | bytes 36872 | tf_op jit(solution)/shard_map/ppermute | solution.py:315
  20.9 34.4 %copy-start.5 = (s32[2048]{0:T(1024)S(1)}, s32[2048]{0:T(1024)}, u32[]{:S(2)}) copy-start(s32[2048]{0:T(1024)} %holders.1) | copy-start | bytes 24580
  21.5 24.4 %collective-permute-start.4 = (bf16[16,768]{1,0:T(8,128)(2,1)S(1)}, bf16[16,768]{1,0:T(8,128)(2,1)S(1)}, u32[]{:S(2)}, u32[]{:S(2)}) collective-permute-start(bf16[16,768]{1,0:T(8,128)(2,1)S(1)} %pad_maximum_fusion.7), channel_id=1, source_target_pairs={{0,24},{4,28},{8,16},{12,20},{16,8},{20,12},{24,0},{28,4},{32,56},... | collective-permute-start | bytes 73736 | tf_op jit(solution)/shard_map/ppermute | solution.py:315
  24.9 22.6 %collective-permute-start.5 = (bf16[16,768]{1,0:T(8,128)(2,1)S(1)}, bf16[16,768]{1,0:T(8,128)(2,1)S(1)}, u32[]{:S(2)}, u32[]{:S(2)}) collective-permute-start(bf16[16,768]{1,0:T(8,128)(2,1)S(1)} %pad_maximum_fusion.7), channel_id=1, source_target_pairs={{0,16},{4,20},{8,24},{12,28},{16,0},{20,4},{24,8},{28,12},{32,48},... | collective-permute-start | bytes 73736 | tf_op jit(solution)/shard_map/ppermute | solution.py:315
  24.9 22.6 %collective-permute-start.6 = (bf16[16,768]{1,0:T(8,128)(2,1)S(1)}, bf16[16,768]{1,0:T(8,128)(2,1)S(1)}, u32[]{:S(2)}, u32[]{:S(2)}) collective-permute-start(bf16[16,768]{1,0:T(8,128)(2,1)S(1)} %pad_maximum_fusion.7), channel_id=1, source_target_pairs={{0,8},{4,12},{8,0},{12,4},{16,24},{20,28},{24,16},{28,20},{32,40},... | collective-permute-start | bytes 73736 | tf_op jit(solution)/shard_map/ppermute | solution.py:315
  26.0 21.5 %collective-permute-start.2 = (f32[88,128]{1,0:T(8,128)S(1)}, f32[88,128]{1,0:T(8,128)S(1)}, u32[]{:S(2)}, u32[]{:S(2)}) collective-permute-start(f32[88,128]{1,0:T(8,128)S(1)} %constant_dynamic-update-slice_fusion), channel_id=1, source_target_pairs={{0,3},{1,0},{2,1},{3,2},{4,7},{5,4},{6,5},{7,6},{8,11},{9,8},{10,9... | collective-permute-start | bytes 135176 | tf_op jit(solution)/shard_map/teacher_sums/ppermute | solution.py:306
  29.0 18.5 %collective-permute-start.1 = (f32[88,128]{1,0:T(8,128)S(1)}, f32[88,128]{1,0:T(8,128)S(1)}, u32[]{:S(2)}, u32[]{:S(2)}) collective-permute-start(f32[88,128]{1,0:T(8,128)S(1)} %constant_dynamic-update-slice_fusion), channel_id=1, source_target_pairs={{0,2},{1,3},{2,0},{3,1},{4,6},{5,7},{6,4},{7,5},{8,10},{9,11},{10,... | collective-permute-start | bytes 135176 | tf_op jit(solution)/shard_map/teacher_sums/ppermute | solution.py:306
  45.8 5.3 %collective-permute-start = (f32[88,128]{1,0:T(8,128)S(1)}, f32[88,128]{1,0:T(8,128)S(1)}, u32[]{:S(2)}, u32[]{:S(2)}) collective-permute-start(f32[88,128]{1,0:T(8,128)S(1)} %constant_dynamic-update-slice_fusion), channel_id=1, source_target_pairs={{0,1},{1,2},{2,3},{3,0},{4,5},{5,6},{6,7},{7,4},{8,9},{9,10},{10,1... | collective-permute-start | bytes 135176 | tf_op jit(solution)/shard_map/teacher_sums/ppermute | solution.py:306
  52.0 30.8 %copy-start.2 = (bf16[64,64,128]{2,1,0:T(8,128)(2,1)}, bf16[64,64,128]{2,1,0:T(8,128)(2,1)S(1)}, u32[]{:S(2)}) copy-start(bf16[64,64,128]{2,1,0:T(8,128)(2,1)S(1)} %slice.97.x0) | copy-start | bytes 3145732
  52.1 23.4 %collective-permute-start.7 = (bf16[64,64,128]{2,1,0:T(8,128)(2,1)S(1)}, bf16[64,64,128]{2,1,0:T(8,128)(2,1)S(1)}, u32[]{:S(2)}, u32[]{:S(2)}) collective-permute-start(bf16[64,64,128]{2,1,0:T(8,128)(2,1)S(1)} %slice.97.x0), channel_id=1, source_target_pairs={{0,1},{1,2},{2,3},{3,0},{4,5},{5,6},{6,7},{7,4},{8,9},{9,10},{10,1... | collective-permute-start | bytes 3145736 | tf_op jit(solution)/shard_map/student_ring/ppermute | solution.py:306
  52.5 22.9 %collective-permute-start.8 = (bf16[64,64,128]{2,1,0:T(8,128)(2,1)S(1)}, bf16[64,64,128]{2,1,0:T(8,128)(2,1)}, u32[]{:S(2)}, u32[]{:S(2)}) collective-permute-start(bf16[64,64,128]{2,1,0:T(8,128)(2,1)S(1)} %slice.97.x0), channel_id=1, source_target_pairs={{0,3},{1,0},{2,1},{3,2},{4,7},{5,4},{6,5},{7,6},{8,11},{9,8},{10,9... | collective-permute-start | bytes 3145736 | tf_op jit(solution)/shard_map/student_ring/ppermute | solution.py:306
  75.5 17.6 %collective-permute-start.9 = (bf16[32,64,128]{2,1,0:T(8,128)(2,1)S(1)}, bf16[32,64,128]{2,1,0:T(8,128)(2,1)}, u32[]{:S(2)}, u32[]{:S(2)}) collective-permute-start(bf16[32,64,128]{2,1,0:T(8,128)(2,1)S(1)} %slice.99), channel_id=1, source_target_pairs={{0,1},{1,2},{2,3},{3,0},{4,5},{5,6},{6,7},{7,4},{8,9},{9,10},{10,1... | collective-permute-start | bytes 1572872 | tf_op jit(solution)/shard_map/student_ring/ppermute | solution.py:306
  77.2 15.9 %collective-permute-start.10 = (bf16[32,64,128]{2,1,0:T(8,128)(2,1)S(1)}, bf16[32,64,128]{2,1,0:T(8,128)(2,1)}, u32[]{:S(2)}, u32[]{:S(2)}) collective-permute-start(bf16[32,64,128]{2,1,0:T(8,128)(2,1)S(1)} %slice.100), channel_id=1, source_target_pairs={{0,3},{1,0},{2,1},{3,2},{4,7},{5,4},{6,5},{7,6},{8,11},{9,8},{10,9... | collective-permute-start | bytes 1572872 | tf_op jit(solution)/shard_map/student_ring/ppermute | solution.py:306
  93.0 24.4 %collective-permute-start.11 = (bf16[64,768]{1,0:T(8,128)(2,1)S(1)}, bf16[64,768]{1,0:T(8,128)(2,1)S(1)}, u32[]{:S(2)}, u32[]{:S(2)}) collective-permute-start(bf16[64,768]{1,0:T(8,128)(2,1)S(1)} %pad_maximum_fusion.3), channel_id=1, source_target_pairs={{0,32},{4,36},{8,40},{12,44},{16,48},{20,52},{24,56},{28,60},{32,0... | collective-permute-start | bytes 294920 | tf_op jit(solution)/shard_map/ppermute | solution.py:315
  117.5 7.5 %collective-permute-start.12 = (f32[512,1536]{1,0:T(8,128)}, f32[512,1536]{1,0:T(8,128)S(1)}, u32[]{:S(2)}, u32[]{:S(2)}) collective-permute-start(f32[512,1536]{1,0:T(8,128)} %get-tuple-element.46), channel_id=1, source_target_pairs={{0,4},{4,0},{8,12},{12,8},{16,20},{20,16},{24,28},{28,24},{32,36},... | collective-permute-start | bytes 9437192 | tf_op jit(solution)/shard_map/grad_core/ppermute | solution.py:315
  117.6 7.3 %collective-permute-start.13 = (bf16[128,768]{1,0:T(8,128)(2,1)S(1)}, bf16[128,768]{1,0:T(8,128)(2,1)S(1)}, u32[]{:S(2)}, u32[]{:S(2)}) collective-permute-start(bf16[128,768]{1,0:T(8,128)(2,1)S(1)} %pad_maximum_fusion.1), channel_id=1, source_target_pairs={{0,64},{4,68},{8,72},{12,76},{16,80},{20,84},{24,88},{28,92},{32,9... | collective-permute-start | bytes 589832 | tf_op jit(solution)/shard_map/ppermute | solution.py:315
  131.5 26.3 %copy-start.4 = (f32[32,896]{1,0:T(8,128)S(1)}, f32[32,896]{1,0:T(8,128)}, u32[]{:S(2)}) copy-start(f32[32,896]{1,0:T(8,128)} %reshape.227) | copy-start | bytes 344068
  131.5 42.0 %all-to-all-start.1 = ((s16[32,16,1408]{2,1,0:T(8,128)(2,1)}), s16[32,16,1408]{2,1,0:T(8,128)(2,1)S(1)}, u32[]{:S(2)}, u32[]{:S(2)}) async-start(s16[32,16,1408]{2,1,0:T(8,128)(2,1)} %bitcast.28), calls=%async_computation.1 | async-start | bytes 2883584 | tf_op jit(solution)/shard_map/grad_xz/all_to_all | solution.py:416
  139.4 18.3 %collective-permute-start.14 = (bf16[256,768]{1,0:T(8,128)(2,1)S(1)}, bf16[256,768]{1,0:T(8,128)(2,1)S(1)}, u32[]{:S(2)}, u32[]{:S(2)}) collective-permute-start(bf16[256,768]{1,0:T(8,128)(2,1)S(1)} %pad_maximum_fusion), channel_id=1, source_target_pairs={{0,128},{4,132},{8,136},{12,140},{16,144},{20,148},{24,152},{28,15... | collective-permute-start | bytes 1179656 | tf_op jit(solution)/shard_map/ppermute | solution.py:315
  177.8 3.6 %collective-permute-start.17 = (f32[8,128]{1,0:T(8,128)S(1)}, f32[8,128]{1,0:T(8,128)S(1)}, u32[]{:S(2)}, u32[]{:S(2)}) collective-permute-start(f32[8,128]{1,0:T(8,128)S(1)} %maximum_maximum_fusion), channel_id=1, source_target_pairs={{0,3},{1,0},{2,1},{3,2},{4,7},{5,4},{6,5},{7,6},{8,11},{9,8},{10,9... | collective-permute-start | bytes 12296 | tf_op jit(solution)/shard_map/loss_parts/ppermute | solution.py:306
  179.6 5.1 %collective-permute-start.16 = (f32[8,128]{1,0:T(8,128)S(1)}, f32[8,128]{1,0:T(8,128)S(1)}, u32[]{:S(2)}, u32[]{:S(2)}) collective-permute-start(f32[8,128]{1,0:T(8,128)S(1)} %maximum_maximum_fusion), channel_id=1, source_target_pairs={{0,2},{1,3},{2,0},{3,1},{4,6},{5,7},{6,4},{7,5},{8,10},{9,11},{10,... | collective-permute-start | bytes 12296 | tf_op jit(solution)/shard_map/loss_parts/ppermute | solution.py:306
  179.6 5.2 %collective-permute-start.15 = (f32[8,128]{1,0:T(8,128)S(1)}, f32[8,128]{1,0:T(8,128)S(1)}, u32[]{:S(2)}, u32[]{:S(2)}) collective-permute-start(f32[8,128]{1,0:T(8,128)S(1)} %maximum_maximum_fusion), channel_id=1, source_target_pairs={{0,1},{1,2},{2,3},{3,0},{4,5},{5,6},{6,7},{7,4},{8,9},{9,10},{10,1... | collective-permute-start | bytes 12296 | tf_op jit(solution)/shard_map/loss_parts/ppermute | solution.py:306
  (5 other events, 19.7 us)

commit v7 on v6

--- a/solution.py
+++ b/solution.py
@@ -10,7 +10,7 @@
 
 N_X, N_Z, N_CORE = 4, 8, 2
 EXT = 128
-VMEM_BYTES = 60 * 1024 * 1024
+VMEM_BYTES = 62 * 1024 * 1024
 
 XZ_GROUPS = [[k * N_CORE + c for k in range(N_X * N_Z)] for c in range(N_CORE)]
 
@@ -319,14 +319,12 @@
         upper = (own_index // bit) % 2 == 1
         return jnp.concatenate([jnp.where(upper, other, x), jnp.where(upper, x, other)])
 
-    def four(x, bit):
-        low, high = (own_index // bit) % 2 == 1, (own_index // (2 * bit)) % 2 == 1
-        a, b, c, d = x, swap(x, bit), swap(x, 2 * bit), swap(x, 3 * bit)
-        a, b = jnp.where(low, b, a), jnp.where(low, a, b)
-        c, d = jnp.where(low, d, c), jnp.where(low, c, d)
-        a, c = jnp.where(high, c, a), jnp.where(high, a, c)
-        b, d = jnp.where(high, d, b), jnp.where(high, b, d)
-        return jnp.concatenate([a, b, c, d])
+    def spread(x, bit, count):
+        blocks = [x] + [swap(x, bit * k) for k in range(1, 2**count)]
+        for n in range(count):
+            upper = (own_index // (bit * 2**n)) % 2 == 1
+            blocks = [jnp.where(upper, blocks[k ^ 2**n], blocks[k]) for k in range(2**count)]
+        return jnp.concatenate(blocks)
 
     outgoing, texts, teacher_in = lax.optimization_barrier((outgoing, text_embed, teacher_cache))
 
@@ -349,7 +347,8 @@
         n_sum = sums.size // EXT
         sums = sum(p[:n_sum] for p in packed).reshape(sums.shape)
         images = jnp.concatenate([p[n_sum:] for p in packed]).reshape(img_dev, embed + EXT)
-    texts = four(both(texts, 1), 2)
+    texts, sums, images = lax.optimization_barrier((both(texts, 1), sums, images))
+    texts = spread(texts, 2, 3)
     mine, sums, images, texts = lax.optimization_barrier((mine, sums, images, texts))
     with jax.named_scope("student_ring"):
         counts_sent, mine = mine[:, -COUNT_ROWS:], mine[:, :-COUNT_ROWS]
@@ -379,8 +378,6 @@
     )
 
     scalars = jnp.concatenate([jnp.stack([cache_pos, core]).astype(jnp.int32), place_of])
-    far_a, far_b, texts = lax.optimization_barrier((far_a, far_b, texts))
-    texts = both(texts, N_Z)
     keep, send = head_terms(
         scalars,
         near_pred,
@@ -392,13 +389,11 @@
         row_info,
         full_cols,
     )
-    keep, send, texts = lax.optimization_barrier((keep, send, texts))
     with jax.named_scope("grad_core"):
         received = swap(send, 1)
-    texts = both(texts, 2 * N_Z)
     codes = add_and_code(keep, received)
     codes, images, texts = lax.optimization_barrier((codes, images, texts))
-    texts = both(texts, 4 * N_Z)
+    texts = spread(texts, 2 * N_Z, 2)
     with jax.named_scope("contrast"):
         pairs = images[:, embed].astype(jnp.int32) * 64 + images[:, embed + 1].astype(jnp.int32)
         logits = jnp.dot(

time: 189 us -> 196 us (1.037)
  starting transfers between devices: 47.3 us -> 55.2 us
    ppermute x8 -> x12, starting transfers between devices: 12.5 us -> 20.1 us  [swap(): return lax.ppermute(x, 'dp', [(i, i ^ bit) for i in range(n_dp)])]
    ppermute x8 -> x12, waiting for transfers between devices: 38 us -> 41 us  [swap(): return lax.ppermute(x, 'dp', [(i, i ^ bit) for i in range(n_dp)])]
    ppermute x10, waiting for transfers between devices: 26.8 us -> 24.5 us  [ring(): lax.ppermute(x, 'cache', [(i, (i + step) % n_cache) for i in range(n_cach...]
  transfers between devices with their start and end apart: 20 -> 24, of which waited for: 8 -> 10; matrix products, arithmetic and copies ran while one was open for 7% -> 5% of each run, Pallas kernels for 16% -> 5%
where the time goes in v7:
time: 196 us; the launch traced here: 193 us
  waiting for transfers between devices  79.9 us (41%)
  starting transfers between devices  55.2 us (28%)
  Pallas kernels  40.2 us (21%)
  other arithmetic  8.46 us (4%)
  local copies, waits for them, and re-layouts  7.85 us (4%)
    ppermute x12, waiting for transfers between devices, swap(): return lax.ppermute(x, 'dp', [(i, i ^ bit) for i in range(n_dp)])  41 us
    ppermute x10, waiting for transfers between devices, ring(): lax.ppermute(x, 'cache', [(i, (i + step) % n_cache) for i in range(n_cach...  24.5 us
    ppermute x12, starting transfers between devices, swap(): return lax.ppermute(x, 'dp', [(i, i ^ bit) for i in range(n_dp)])  20.1 us
    pallas_call x1, Pallas kernels, head_terms(): pl.pallas_call(kernel, grid_spec=pltpu.PrefetchScalarGridSpec(num_scalar_...  19.6 us
    ppermute x10, starting transfers between devices, ring(): lax.ppermute(x, 'cache', [(i, (i + step) % n_cache) for i in range(n_cach...  15.8 us
    all_to_all x1, waiting for transfers between devices, local(): lax.all_to_all(codes.reshape(N_X * N_Z, -1, local_cols + EXT), 'dp', 0, 0...  14.4 us
    all_to_all x1, starting transfers between devices, local(): lax.all_to_all(outgoing, 'dp', split_axis=0, concat_axis=0, tiled=True)  12 us
    pallas_call x1, Pallas kernels, near_terms(): pl.pallas_call(kernel, grid_spec=pltpu.PrefetchScalarGridSpec(num_scalar_...  10.2 us
  transfers between devices with their start and end apart: 24, of which 10 were waited for; matrix products, arithmetic and copies ran while one was open for 5% of the time, Pallas kernels for 5%

profile of v7, /device:TPU:2, one launch (start us, length us, event | category | flops | bytes accessed | tf_op | source)
XLA Modules:
  0.0 193.1 jit_solution(14627014243624112163)
XLA Ops:
  1.2 3.1 %dispatch_rows.1 = bf16[64,72,128]{2,1,0:T(8,128)(2,1)} custom-call(s32[2]{0:T(128)} %pad_add_fusion.1.place, s32[2048]{0:T(1024)} %holders.1, s32[32]{0:T(128)} %counts.1, bf16[32,32,1024]{2,1,0:T(8,128)(2,1)} %feats.1), custom_call_target="tpu_custom_call" | custom-call | tf_op jit(solution)/shard_map/dispatch_rows/pallas_call | solution.py:41
  4.4 4.3 %convert_reduce_fusion = (f32[64,32]{1,0:T(8,128)S(1)}, f32[64,32]{1,0:T(8,128)S(1)}) fusion(bf16[64,32,1280]{2,1,0:T(8,128)(2,1)} %param.10), kind=kLoop, calls=%fused_computation.1 | loop fusion | flops 10481664 | bytes 5259264 | tf_op jit(solution)/shard_map/teacher_sums/reduce_sum | solution.py:335
  10.8 2.9 %collective-permute-start.2 = (f32[88,128]{1,0:T(8,128)S(1)}, f32[88,128]{1,0:T(8,128)S(1)}, u32[]{:S(2)}, u32[]{:S(2)}) collective-permute-start(f32[88,128]{1,0:T(8,128)S(1)} %constant_dynamic-update-slice_fusion), channel_id=1, source_target_pairs={{0,2},{1,3},{2,0},{3,1},{4,6},{5,7},{6,4},{7,5},{8,10},{9,11},{10,... | collective-permute-start | bytes 135176 | tf_op jit(solution)/shard_map/teacher_sums/ppermute | solution.py:306
  15.1 12.0 %all-to-all-start = ((bf16[64,72,128]{2,1,0:T(8,128)(2,1)}), bf16[64,72,128]{2,1,0:T(8,128)(2,1)S(1)}, u32[]{:S(2)}, u32[]{:S(2)}) async-start(bf16[64,72,128]{2,1,0:T(8,128)(2,1)} %dispatch_rows.1), calls=%async_computation | async-start | bytes 2359296 | tf_op jit(solution)/shard_map/student_exchange/all_to_all | solution.py:332
  28.9 2.7 %collective-permute-start.4 = (bf16[16,768]{1,0:T(8,128)(2,1)S(1)}, bf16[16,768]{1,0:T(8,128)(2,1)S(1)}, u32[]{:S(2)}, u32[]{:S(2)}) collective-permute-start(bf16[16,768]{1,0:T(8,128)(2,1)S(1)} %pad_maximum_fusion.4), channel_id=1, source_target_pairs={{0,56},{4,60},{8,48},{12,52},{16,40},{20,44},{24,32},{28,36},{32,2... | collective-permute-start | bytes 73736 | tf_op jit(solution)/shard_map/ppermute | solution.py:315
  33.0 3.6 %collective-permute-start.6 = (bf16[16,768]{1,0:T(8,128)(2,1)S(1)}, bf16[16,768]{1,0:T(8,128)(2,1)S(1)}, u32[]{:S(2)}, u32[]{:S(2)}) collective-permute-start(bf16[16,768]{1,0:T(8,128)(2,1)S(1)} %pad_maximum_fusion.4), channel_id=1, source_target_pairs={{0,40},{4,44},{8,32},{12,36},{16,56},{20,60},{24,48},{28,52},{32,8... | collective-permute-start | bytes 73736 | tf_op jit(solution)/shard_map/ppermute | solution.py:315
  36.7 1.8 collective-permute-start.7
  38.5 18.3 %collective-permute-done.10 = bf16[16,768]{1,0:T(8,128)(2,1)S(1)} collective-permute-done((bf16[16,768]{1,0:T(8,128)(2,1)S(1)}, bf16[16,768]{1,0:T(8,128)(2,1)S(1)}, u32[]{:S(2)}, u32[]{:S(2)}) %collective-permute-start.10) | collective-permute-done | bytes 24608 | tf_op jit(solution)/shard_map/ppermute | solution.py:315
  56.7 2.1 %collective-permute-start.8 = (bf16[16,768]{1,0:T(8,128)(2,1)S(1)}, bf16[16,768]{1,0:T(8,128)(2,1)S(1)}, u32[]{:S(2)}, u32[]{:S(2)}) collective-permute-start(bf16[16,768]{1,0:T(8,128)(2,1)S(1)} %pad_maximum_fusion.4), channel_id=1, source_target_pairs={{0,24},{4,28},{8,16},{12,20},{16,8},{20,12},{24,0},{28,4},{32,56},... | collective-permute-start | bytes 73736 | tf_op jit(solution)/shard_map/ppermute | solution.py:315
  58.8 2.8 %collective-permute-start.9 = (bf16[16,768]{1,0:T(8,128)(2,1)S(1)}, bf16[16,768]{1,0:T(8,128)(2,1)S(1)}, u32[]{:S(2)}, u32[]{:S(2)}) collective-permute-start(bf16[16,768]{1,0:T(8,128)(2,1)S(1)} %pad_maximum_fusion.4), channel_id=1, source_target_pairs={{0,16},{4,20},{8,24},{12,28},{16,0},{20,4},{24,8},{28,12},{32,48},... | collective-permute-start | bytes 73736 | tf_op jit(solution)/shard_map/ppermute | solution.py:315
  64.7 2.6 %collective-permute-start.12 = (bf16[64,64,128]{2,1,0:T(8,128)(2,1)S(1)}, bf16[64,64,128]{2,1,0:T(8,128)(2,1)}, u32[]{:S(2)}, u32[]{:S(2)}) collective-permute-start(bf16[64,64,128]{2,1,0:T(8,128)(2,1)S(1)} %slice.97.x0), channel_id=1, source_target_pairs={{0,3},{1,0},{2,1},{3,2},{4,7},{5,4},{6,5},{7,6},{8,11},{9,8},{10,9... | collective-permute-start | bytes 3145736 | tf_op jit(solution)/shard_map/student_ring/ppermute | solution.py:306
  68.2 20.7 %collective-permute-done.11.x1 = bf16[64,64,128]{2,1,0:T(8,128)(2,1)} collective-permute-done((bf16[64,64,128]{2,1,0:T(8,128)(2,1)S(1)}, bf16[64,64,128]{2,1,0:T(8,128)(2,1)}, u32[]{:S(2)}, u32[]{:S(2)}) %collective-permute-start.11) | collective-permute-done | bytes 1048608 | tf_op jit(solution)/shard_map/student_ring/ppermute | solution.py:306
  91.3 1.9 slice.100
  93.2 3.2 %collective-permute-start.14 = (bf16[32,64,128]{2,1,0:T(8,128)(2,1)}, bf16[32,64,128]{2,1,0:T(8,128)(2,1)}, u32[]{:S(2)}, u32[]{:S(2)}) collective-permute-start(bf16[32,64,128]{2,1,0:T(8,128)(2,1)} %slice.100), channel_id=1, source_target_pairs={{0,3},{1,0},{2,1},{3,2},{4,7},{5,4},{6,5},{7,6},{8,11},{9,8},{10,9... | collective-permute-start | bytes 1572872 | tf_op jit(solution)/shard_map/student_ring/ppermute | solution.py:306
  97.9 10.2 %near_terms.1 = (f32[2048,1280]{1,0:T(8,128)}, bf16[1024,2048]{1,0:T(8,128)(2,1)}) custom-call(s32[1]{0:T(128)} %bitcast.sc, bf16[64,64,128]{2,1,0:T(8,128)(2,1)} %copy-done.1, bf16[64,64,128]{2,1,0:T(8,128)(2,1)} %collective-permute-done.11.x1, bf16[64,64,128]{2,1,0:T(8,128)(2,1)} %collective-permute-done.12.x2, bf16[1024,1280]{1,0:T(8,128)(2,1)} %w_ref.3), custom_call_target="tpu_custom_call" | custom-call | flops 4026531840 | bytes 20971520 | tf_op jit(solution)/shard_map/near_terms/pallas_call | solution.py:83
  108.1 19.6 %head_terms.1 = (f32[512,1536]{1,0:T(8,128)}, f32[512,1536]{1,0:T(8,128)}) custom-call(s32[66]{0:T(128)} %pad_add_fusion.sc, f32[2048,1280]{1,0:T(8,128)} %get-tuple-element.35.pred_ref, bf16[1024,2048]{1,0:T(8,128)(2,1)} %get-tuple-element.36.xt_ref, bf16[32,64,128]{2,1,0:T(8,128)(2,1)} %collective-permute-done.13.fa, ...), custom_call_target="tpu_custom_call" | custom-call | flops 8053063680 | bytes 31457280 | tf_op jit(solution)/shard_map/head_terms/pallas_call | solution.py:177
  127.7 6.0 %collective-permute-done.15.b = f32[512,1536]{1,0:T(8,128)} collective-permute-done((f32[512,1536]{1,0:T(8,128)}, f32[512,1536]{1,0:T(8,128)}, u32[]{:S(2)}, u32[]{:S(2)}) %collective-permute-start.15) | collective-permute-done | bytes 3145760 | tf_op jit(solution)/shard_map/grad_core/ppermute | solution.py:315
  133.7 4.9 %add_and_code.1 = s16[512,1408]{1,0:T(8,128)(2,1)} custom-call(f32[512,1536]{1,0:T(8,128)} %get-tuple-element.39.a, f32[512,1536]{1,0:T(8,128)} %collective-permute-done.15.b), custom_call_target="tpu_custom_call" | custom-call | tf_op jit(solution)/shard_map/add_and_code/pallas_call | solution.py:245
  138.6 7.2 %all-to-all-start.1 = ((s16[32,16,1408]{2,1,0:T(8,128)(2,1)}), s16[32,16,1408]{2,1,0:T(8,128)(2,1)S(1)}, u32[]{:S(2)}, u32[]{:S(2)}) async-start(s16[32,16,1408]{2,1,0:T(8,128)(2,1)} %bitcast.28), calls=%async_computation.1 | async-start | bytes 2883584 | tf_op jit(solution)/shard_map/grad_xz/all_to_all | solution.py:411
  148.2 1.8 collective-permute-start.18
  150.2 13.4 %collective-permute-done.16 = bf16[128,768]{1,0:T(8,128)(2,1)S(1)} collective-permute-done((bf16[128,768]{1,0:T(8,128)(2,1)S(1)}, bf16[128,768]{1,0:T(8,128)(2,1)S(1)}, u32[]{:S(2)}, u32[]{:S(2)}) %collective-permute-start.16) | collective-permute-done | bytes 196640 | tf_op jit(solution)/shard_map/ppermute | solution.py:315
  165.8 14.4 %all-to-all-done.1.src = s16[32,16,1408]{2,1,0:T(8,128)(2,1)S(1)} async-done(((s16[32,16,1408]{2,1,0:T(8,128)(2,1)}), s16[32,16,1408]{2,1,0:T(8,128)(2,1)S(1)}, u32[]{:S(2)}, u32[]{:S(2)}) %all-to-all-start.1) | async-done | bytes 1441824 | tf_op jit(solution)/shard_map/grad_xz/all_to_all | solution.py:411
  181.3 2.4 %sum_last.1 = (f32[16,1280]{1,0:T(8,128)}, f32[16,128]{1,0:T(8,128)}) custom-call(s16[32,16,1408]{2,1,0:T(8,128)(2,1)} %copy-done), custom_call_target="tpu_custom_call" | custom-call | tf_op jit(solution)/shard_map/sum_last/pallas_call | solution.py:272
  188.2 3.5 %collective-permute-done.20 = f32[8,128]{1,0:T(8,128)S(1)} collective-permute-done((f32[8,128]{1,0:T(8,128)S(1)}, f32[8,128]{1,0:T(8,128)S(1)}, u32[]{:S(2)}, u32[]{:S(2)}) %collective-permute-start.20) | collective-permute-done | bytes 4128 | tf_op jit(solution)/shard_map/loss_parts/ppermute | solution.py:306
  (118 shorter events, 26.7 us)
Async XLA Ops:
  4.4 22.7 %collective-permute-start = (bf16[8,768]{1,0:T(8,128)(2,1)S(1)}, bf16[8,768]{1,0:T(8,128)(2,1)S(1)}, u32[]{:S(2)}, u32[]{:S(2)}) collective-permute-start(bf16[8,768]{1,0:T(8,128)(2,1)S(1)} %copy-done.4), channel_id=1, source_target_pairs={{0,4},{4,0},{8,12},{12,8},{16,20},{20,16},{24,28},{28,24},{32,36},... | collective-permute-start | bytes 36872 | tf_op jit(solution)/shard_map/ppermute | solution.py:315
  9.2 18.0 %collective-permute-start.1 = (f32[88,128]{1,0:T(8,128)S(1)}, f32[88,128]{1,0:T(8,128)S(1)}, u32[]{:S(2)}, u32[]{:S(2)}) collective-permute-start(f32[88,128]{1,0:T(8,128)S(1)} %constant_dynamic-update-slice_fusion), channel_id=1, source_target_pairs={{0,1},{1,2},{2,3},{3,0},{4,5},{5,6},{6,7},{7,4},{8,9},{9,10},{10,1... | collective-permute-start | bytes 135176 | tf_op jit(solution)/shard_map/teacher_sums/ppermute | solution.py:306
  10.8 16.3 %collective-permute-start.2 = (f32[88,128]{1,0:T(8,128)S(1)}, f32[88,128]{1,0:T(8,128)S(1)}, u32[]{:S(2)}, u32[]{:S(2)}) collective-permute-start(f32[88,128]{1,0:T(8,128)S(1)} %constant_dynamic-update-slice_fusion), channel_id=1, source_target_pairs={{0,2},{1,3},{2,0},{3,1},{4,6},{5,7},{6,4},{7,5},{8,10},{9,11},{10,... | collective-permute-start | bytes 135176 | tf_op jit(solution)/shard_map/teacher_sums/ppermute | solution.py:306
  13.7 13.5 %collective-permute-start.3 = (f32[88,128]{1,0:T(8,128)S(1)}, f32[88,128]{1,0:T(8,128)S(1)}, u32[]{:S(2)}, u32[]{:S(2)}) collective-permute-start(f32[88,128]{1,0:T(8,128)S(1)} %constant_dynamic-update-slice_fusion), channel_id=1, source_target_pairs={{0,3},{1,0},{2,1},{3,2},{4,7},{5,4},{6,5},{7,6},{8,11},{9,8},{10,9... | collective-permute-start | bytes 135176 | tf_op jit(solution)/shard_map/teacher_sums/ppermute | solution.py:306
  15.1 48.8 %all-to-all-start = ((bf16[64,72,128]{2,1,0:T(8,128)(2,1)}), bf16[64,72,128]{2,1,0:T(8,128)(2,1)S(1)}, u32[]{:S(2)}, u32[]{:S(2)}) async-start(bf16[64,72,128]{2,1,0:T(8,128)(2,1)} %dispatch_rows.1), calls=%async_computation | async-start | bytes 2359296 | tf_op jit(solution)/shard_map/student_exchange/all_to_all | solution.py:332
  27.4 29.4 %collective-permute-start.10 = (bf16[16,768]{1,0:T(8,128)(2,1)S(1)}, bf16[16,768]{1,0:T(8,128)(2,1)S(1)}, u32[]{:S(2)}, u32[]{:S(2)}) collective-permute-start(bf16[16,768]{1,0:T(8,128)(2,1)S(1)} %pad_maximum_fusion.4), channel_id=1, source_target_pairs={{0,8},{4,12},{8,0},{12,4},{16,24},{20,28},{24,16},{28,20},{32,40},... | collective-permute-start | bytes 73736 | tf_op jit(solution)/shard_map/ppermute | solution.py:315
  28.9 29.9 %collective-permute-start.4 = (bf16[16,768]{1,0:T(8,128)(2,1)S(1)}, bf16[16,768]{1,0:T(8,128)(2,1)S(1)}, u32[]{:S(2)}, u32[]{:S(2)}) collective-permute-start(bf16[16,768]{1,0:T(8,128)(2,1)S(1)} %pad_maximum_fusion.4), channel_id=1, source_target_pairs={{0,56},{4,60},{8,48},{12,52},{16,40},{20,44},{24,32},{28,36},{32,2... | collective-permute-start | bytes 73736 | tf_op jit(solution)/shard_map/ppermute | solution.py:315
  31.6 30.0 %collective-permute-start.5 = (bf16[16,768]{1,0:T(8,128)(2,1)S(1)}, bf16[16,768]{1,0:T(8,128)(2,1)S(1)}, u32[]{:S(2)}, u32[]{:S(2)}) collective-permute-start(bf16[16,768]{1,0:T(8,128)(2,1)S(1)} %pad_maximum_fusion.4), channel_id=1, source_target_pairs={{0,48},{4,52},{8,56},{12,60},{16,32},{20,36},{24,40},{28,44},{32,1... | collective-permute-start | bytes 73736 | tf_op jit(solution)/shard_map/ppermute | solution.py:315
  33.0 28.6 %collective-permute-start.6 = (bf16[16,768]{1,0:T(8,128)(2,1)S(1)}, bf16[16,768]{1,0:T(8,128)(2,1)S(1)}, u32[]{:S(2)}, u32[]{:S(2)}) collective-permute-start(bf16[16,768]{1,0:T(8,128)(2,1)S(1)} %pad_maximum_fusion.4), channel_id=1, source_target_pairs={{0,40},{4,44},{8,32},{12,36},{16,56},{20,60},{24,48},{28,52},{32,8... | collective-permute-start | bytes 73736 | tf_op jit(solution)/shard_map/ppermute | solution.py:315
  36.7 25.0 %collective-permute-start.7 = (bf16[16,768]{1,0:T(8,128)(2,1)S(1)}, bf16[16,768]{1,0:T(8,128)(2,1)S(1)}, u32[]{:S(2)}, u32[]{:S(2)}) collective-permute-start(bf16[16,768]{1,0:T(8,128)(2,1)S(1)} %pad_maximum_fusion.4), channel_id=1, source_target_pairs={{0,32},{4,36},{8,40},{12,44},{16,48},{20,52},{24,56},{28,60},{32,0... | collective-permute-start | bytes 73736 | tf_op jit(solution)/shard_map/ppermute | solution.py:315
  56.7 6.6 %collective-permute-start.8 = (bf16[16,768]{1,0:T(8,128)(2,1)S(1)}, bf16[16,768]{1,0:T(8,128)(2,1)S(1)}, u32[]{:S(2)}, u32[]{:S(2)}) collective-permute-start(bf16[16,768]{1,0:T(8,128)(2,1)S(1)} %pad_maximum_fusion.4), channel_id=1, source_target_pairs={{0,24},{4,28},{8,16},{12,20},{16,8},{20,12},{24,0},{28,4},{32,56},... | collective-permute-start | bytes 73736 | tf_op jit(solution)/shard_map/ppermute | solution.py:315
  58.8 4.8 %collective-permute-start.9 = (bf16[16,768]{1,0:T(8,128)(2,1)S(1)}, bf16[16,768]{1,0:T(8,128)(2,1)S(1)}, u32[]{:S(2)}, u32[]{:S(2)}) collective-permute-start(bf16[16,768]{1,0:T(8,128)(2,1)S(1)} %pad_maximum_fusion.4), channel_id=1, source_target_pairs={{0,16},{4,20},{8,24},{12,28},{16,0},{20,4},{24,8},{28,12},{32,48},... | collective-permute-start | bytes 73736 | tf_op jit(solution)/shard_map/ppermute | solution.py:315
  64.0 24.9 %collective-permute-start.11 = (bf16[64,64,128]{2,1,0:T(8,128)(2,1)S(1)}, bf16[64,64,128]{2,1,0:T(8,128)(2,1)}, u32[]{:S(2)}, u32[]{:S(2)}) collective-permute-start(bf16[64,64,128]{2,1,0:T(8,128)(2,1)S(1)} %slice.97.x0), channel_id=1, source_target_pairs={{0,1},{1,2},{2,3},{3,0},{4,5},{5,6},{6,7},{7,4},{8,9},{9,10},{10,1... | collective-permute-start | bytes 3145736 | tf_op jit(solution)/shard_map/student_ring/ppermute | solution.py:306
  64.7 24.1 %collective-permute-start.12 = (bf16[64,64,128]{2,1,0:T(8,128)(2,1)S(1)}, bf16[64,64,128]{2,1,0:T(8,128)(2,1)}, u32[]{:S(2)}, u32[]{:S(2)}) collective-permute-start(bf16[64,64,128]{2,1,0:T(8,128)(2,1)S(1)} %slice.97.x0), channel_id=1, source_target_pairs={{0,3},{1,0},{2,1},{3,2},{4,7},{5,4},{6,5},{7,6},{8,11},{9,8},{10,9... | collective-permute-start | bytes 3145736 | tf_op jit(solution)/shard_map/student_ring/ppermute | solution.py:306
  91.2 16.8 %collective-permute-start.13 = (bf16[32,64,128]{2,1,0:T(8,128)(2,1)S(1)}, bf16[32,64,128]{2,1,0:T(8,128)(2,1)}, u32[]{:S(2)}, u32[]{:S(2)}) collective-permute-start(bf16[32,64,128]{2,1,0:T(8,128)(2,1)S(1)} %slice.99), channel_id=1, source_target_pairs={{0,1},{1,2},{2,3},{3,0},{4,5},{5,6},{6,7},{7,4},{8,9},{9,10},{10,1... | collective-permute-start | bytes 1572872 | tf_op jit(solution)/shard_map/student_ring/ppermute | solution.py:306
  93.2 14.9 %collective-permute-start.14 = (bf16[32,64,128]{2,1,0:T(8,128)(2,1)}, bf16[32,64,128]{2,1,0:T(8,128)(2,1)}, u32[]{:S(2)}, u32[]{:S(2)}) collective-permute-start(bf16[32,64,128]{2,1,0:T(8,128)(2,1)} %slice.100), channel_id=1, source_target_pairs={{0,3},{1,0},{2,1},{3,2},{4,7},{5,4},{6,5},{7,6},{8,11},{9,8},{10,9... | collective-permute-start | bytes 1572872 | tf_op jit(solution)/shard_map/student_ring/ppermute | solution.py:306
  127.7 6.0 %collective-permute-start.15 = (f32[512,1536]{1,0:T(8,128)}, f32[512,1536]{1,0:T(8,128)}, u32[]{:S(2)}, u32[]{:S(2)}) collective-permute-start(f32[512,1536]{1,0:T(8,128)} %get-tuple-element.40), channel_id=1, source_target_pairs={{0,4},{4,0},{8,12},{12,8},{16,20},{20,16},{24,28},{28,24},{32,36},... | collective-permute-start | bytes 9437192 | tf_op jit(solution)/shard_map/grad_core/ppermute | solution.py:315
  138.6 41.7 %all-to-all-start.1 = ((s16[32,16,1408]{2,1,0:T(8,128)(2,1)}), s16[32,16,1408]{2,1,0:T(8,128)(2,1)S(1)}, u32[]{:S(2)}, u32[]{:S(2)}) async-start(s16[32,16,1408]{2,1,0:T(8,128)(2,1)} %bitcast.28), calls=%async_computation.1 | async-start | bytes 2883584 | tf_op jit(solution)/shard_map/grad_xz/all_to_all | solution.py:411
  145.9 17.7 %collective-permute-start.16 = (bf16[128,768]{1,0:T(8,128)(2,1)S(1)}, bf16[128,768]{1,0:T(8,128)(2,1)S(1)}, u32[]{:S(2)}, u32[]{:S(2)}) collective-permute-start(bf16[128,768]{1,0:T(8,128)(2,1)S(1)} %select_dynamic-update-slice_fusion), channel_id=1, source_target_pairs={{0,192},{4,196},{8,200},{12,204},{16,208},{20,212},{24,216},{28,22... | collective-permute-start | bytes 589832 | tf_op jit(solution)/shard_map/ppermute | solution.py:315
  147.4 16.2 %collective-permute-start.17 = (bf16[128,768]{1,0:T(8,128)(2,1)S(1)}, bf16[128,768]{1,0:T(8,128)(2,1)S(1)}, u32[]{:S(2)}, u32[]{:S(2)}) collective-permute-start(bf16[128,768]{1,0:T(8,128)(2,1)S(1)} %select_dynamic-update-slice_fusion), channel_id=1, source_target_pairs={{0,128},{4,132},{8,136},{12,140},{16,144},{20,148},{24,152},{28,15... | collective-permute-start | bytes 589832 | tf_op jit(solution)/shard_map/ppermute | solution.py:315
  148.2 16.8 %collective-permute-start.18 = (bf16[128,768]{1,0:T(8,128)(2,1)S(1)}, bf16[128,768]{1,0:T(8,128)(2,1)S(1)}, u32[]{:S(2)}, u32[]{:S(2)}) collective-permute-start(bf16[128,768]{1,0:T(8,128)(2,1)S(1)} %select_dynamic-update-slice_fusion), channel_id=1, source_target_pairs={{0,64},{4,68},{8,72},{12,76},{16,80},{20,84},{24,88},{28,92},{32,9... | collective-permute-start | bytes 589832 | tf_op jit(solution)/shard_map/ppermute | solution.py:315
  184.5 3.6 %collective-permute-start.21 = (f32[8,128]{1,0:T(8,128)S(1)}, f32[8,128]{1,0:T(8,128)S(1)}, u32[]{:S(2)}, u32[]{:S(2)}) collective-permute-start(f32[8,128]{1,0:T(8,128)S(1)} %maximum_maximum_fusion), channel_id=1, source_target_pairs={{0,3},{1,0},{2,1},{3,2},{4,7},{5,4},{6,5},{7,6},{8,11},{9,8},{10,9... | collective-permute-start | bytes 12296 | tf_op jit(solution)/shard_map/loss_parts/ppermute | solution.py:306
  186.2 5.5 %collective-permute-start.19 = (f32[8,128]{1,0:T(8,128)S(1)}, f32[8,128]{1,0:T(8,128)S(1)}, u32[]{:S(2)}, u32[]{:S(2)}) collective-permute-start(f32[8,128]{1,0:T(8,128)S(1)} %maximum_maximum_fusion), channel_id=1, source_target_pairs={{0,1},{1,2},{2,3},{3,0},{4,5},{5,6},{6,7},{7,4},{8,9},{9,10},{10,1... | collective-permute-start | bytes 12296 | tf_op jit(solution)/shard_map/loss_parts/ppermute | solution.py:306
  186.5 5.1 %collective-permute-start.20 = (f32[8,128]{1,0:T(8,128)S(1)}, f32[8,128]{1,0:T(8,128)S(1)}, u32[]{:S(2)}, u32[]{:S(2)}) collective-permute-start(f32[8,128]{1,0:T(8,128)S(1)} %maximum_maximum_fusion), channel_id=1, source_target_pairs={{0,2},{1,3},{2,0},{3,1},{4,6},{5,7},{6,4},{7,5},{8,10},{9,11},{10,... | collective-permute-start | bytes 12296 | tf_op jit(solution)/shard_map/loss_parts/ppermute | solution.py:306
  (6 other events, 87.9 us)

commit v8 on v7

--- a/solution.py
+++ b/solution.py
@@ -261,23 +261,24 @@
     return main, extra
 
 
-def sum_last(received):
+def sum_last(received, partial):
     n, rows, wide = received.shape
 
-    def kernel(src, out, ext):
+    def kernel(src, partial_ref, out, parts):
         main, extra = sum_blocks([src[k] for k in range(n)])
         out[...] = main
-        ext[...] = extra
+        row = lax.broadcasted_iota(jnp.int32, partial.shape, 0)
+        parts[...] = jnp.where(row == 3, extra[:1], partial_ref[...])
 
     return pl.pallas_call(
         kernel,
         out_shape=[
             jax.ShapeDtypeStruct((rows, wide - EXT), jnp.float32),
-            jax.ShapeDtypeStruct((rows, EXT), jnp.float32),
+            jax.ShapeDtypeStruct(partial.shape, jnp.float32),
         ],
         compiler_params=params(),
         name="sum_last",
-    )(received)
+    )(received, partial)
 
 
 def local(
@@ -326,7 +327,8 @@
             blocks = [jnp.where(upper, blocks[k ^ 2**n], blocks[k]) for k in range(2**count)]
         return jnp.concatenate(blocks)
 
-    outgoing, texts, teacher_in = lax.optimization_barrier((outgoing, text_embed, teacher_cache))
+    outgoing, texts = lax.optimization_barrier((outgoing, both(text_embed, N_Z)))
+    texts, teacher_in = lax.optimization_barrier((both(texts, 1), teacher_cache))
 
     with jax.named_scope("student_exchange"):
         mine = lax.all_to_all(outgoing, "dp", split_axis=0, concat_axis=0, tiled=True)
@@ -347,8 +349,7 @@
         n_sum = sums.size // EXT
         sums = sum(p[:n_sum] for p in packed).reshape(sums.shape)
         images = jnp.concatenate([p[n_sum:] for p in packed]).reshape(img_dev, embed + EXT)
-    texts, sums, images = lax.optimization_barrier((both(texts, 1), sums, images))
-    texts = spread(texts, 2, 3)
+    texts = both(texts, 4)
     mine, sums, images, texts = lax.optimization_barrier((mine, sums, images, texts))
     with jax.named_scope("student_ring"):
         counts_sent, mine = mine[:, -COUNT_ROWS:], mine[:, :-COUNT_ROWS]
@@ -391,6 +392,7 @@
     )
     with jax.named_scope("grad_core"):
         received = swap(send, 1)
+    texts = both(lax.optimization_barrier((texts, send))[0], 2)
     codes = add_and_code(keep, received)
     codes, images, texts = lax.optimization_barrier((codes, images, texts))
     texts = spread(texts, 2 * N_Z, 2)
@@ -402,7 +404,10 @@
             preferred_element_type=jnp.float32,
         ) * (embed ** (-0.5))
         column = jnp.arange(texts.shape[0], dtype=jnp.int32)
-        text_id = column // shard_rows * img_dev + cache_pos * shard_rows + column % shard_rows
+        text_dp = column // (16 * shard_rows) * 16
+        for n, bit in enumerate((N_Z, 1, 4, 2)):
+            text_dp = text_dp + column // (shard_rows * 2**n) % 2 * bit
+        text_id = text_dp * img_dev + cache_pos * shard_rows + column % shard_rows
         best = jnp.max(logits, axis=1)
         denom = jnp.sum(jnp.exp(logits - best[:, None]), axis=1)
         target = jnp.sum(jnp.where(pairs[:, None] == text_id[None, :], logits, 0.0), axis=1)
@@ -411,10 +416,9 @@
         codes = lax.all_to_all(
             codes.reshape(N_X * N_Z, -1, local_cols + EXT), "dp", 0, 0, axis_index_groups=XZ_GROUPS, tiled=True
         )
-    head_grad, extra = sum_last(codes)
+    head_grad, parts = sum_last(codes, partial)
 
     with jax.named_scope("loss_parts"):
-        parts = jnp.concatenate([partial[:3], extra[:1], partial[4:]])
         parts = [parts] + [ring(parts, step) for step in range(1, n_cache)]
         partials = []
         for k, got in enumerate(parts):

time: 196 us -> 185 us (0.944)
  starting transfers between devices: 55.2 us -> 47.2 us
  waiting for transfers between devices: 79.9 us -> 77.6 us
    ppermute x12 -> x8, starting transfers between devices: 20.1 us -> 14.1 us  [swap(): return lax.ppermute(x, 'dp', [(i, i ^ bit) for i in range(n_dp)])]
    ppermute x12 -> x8, waiting for transfers between devices: 41 us -> 37.2 us  [swap(): return lax.ppermute(x, 'dp', [(i, i ^ bit) for i in range(n_dp)])]
    all_to_all x1, starting transfers between devices: 12 us -> 8.82 us  [local(): lax.all_to_all(outgoing, 'dp', split_axis=0, concat_axis=0, tiled=True)]
  transfers between devices with their start and end apart: 24 -> 20, of which waited for: 10 -> 13; matrix products, arithmetic and copies ran while one was open for 5% -> 7% of each run, Pallas kernels for 5% -> 7%
where the time goes in v8:
time: 185 us; the launch traced here: 183 us
  waiting for transfers between devices  77.6 us (42%)
  starting transfers between devices  47.2 us (26%)
  Pallas kernels  40.2 us (22%)
  other arithmetic  8.85 us (5%)
  local copies, waits for them, and re-layouts  7.79 us (4%)
    ppermute x8, waiting for transfers between devices, swap(): return lax.ppermute(x, 'dp', [(i, i ^ bit) for i in range(n_dp)])  37.2 us
    ppermute x10, waiting for transfers between devices, ring(): lax.ppermute(x, 'cache', [(i, (i + step) % n_cache) for i in range(n_cach...  26.4 us
    pallas_call x1, Pallas kernels, head_terms(): pl.pallas_call(kernel, grid_spec=pltpu.PrefetchScalarGridSpec(num_scalar_...  19.6 us
    ppermute x10, starting transfers between devices, ring(): lax.ppermute(x, 'cache', [(i, (i + step) % n_cache) for i in range(n_cach...  17.7 us
    ppermute x8, starting transfers between devices, swap(): return lax.ppermute(x, 'dp', [(i, i ^ bit) for i in range(n_dp)])  14.1 us
    all_to_all x1, waiting for transfers between devices, local(): lax.all_to_all(codes.reshape(N_X * N_Z, -1, local_cols + EXT), 'dp', 0, 0...  13.9 us
    pallas_call x1, Pallas kernels, near_terms(): pl.pallas_call(kernel, grid_spec=pltpu.PrefetchScalarGridSpec(num_scalar_...  10.1 us
    all_to_all x1, starting transfers between devices, local(): lax.all_to_all(outgoing, 'dp', split_axis=0, concat_axis=0, tiled=True)  8.82 us
  transfers between devices with their start and end apart: 20, of which 13 were waited for; matrix products, arithmetic and copies ran while one was open for 7% of the time, Pallas kernels for 7%

profile of v8, /device:TPU:2, one launch (start us, length us, event | category | flops | bytes accessed | tf_op | source)
XLA Modules:
  0.0 183.1 jit_solution(10029601226563310313)
XLA Ops:
  0.6 7.3 %collective-permute-start = (bf16[8,768]{1,0:T(8,128)(2,1)}, bf16[8,768]{1,0:T(8,128)(2,1)S(1)}, u32[]{:S(2)}, u32[]{:S(2)}) collective-permute-start(bf16[8,768]{1,0:T(8,128)(2,1)} %param.14), channel_id=1, source_target_pairs={{0,32},{4,36},{8,40},{12,44},{16,48},{20,52},{24,56},{28,60},{32,0... | collective-permute-start | bytes 36872 | tf_op jit(solution)/shard_map/ppermute | solution.py:316
  8.5 3.2 %dispatch_rows.1 = bf16[64,72,128]{2,1,0:T(8,128)(2,1)} custom-call(s32[2]{0:T(128)} %pad_add_fusion.1.place, s32[2048]{0:T(1024)} %holders.1, s32[32]{0:T(128)} %counts.1, bf16[32,32,1024]{2,1,0:T(8,128)(2,1)} %feats.1), custom_call_target="tpu_custom_call" | custom-call | tf_op jit(solution)/shard_map/dispatch_rows/pallas_call | solution.py:41
  11.8 8.8 %all-to-all-start = ((bf16[64,72,128]{2,1,0:T(8,128)(2,1)}), bf16[64,72,128]{2,1,0:T(8,128)(2,1)S(1)}, u32[]{:S(2)}, u32[]{:S(2)}) async-start(bf16[64,72,128]{2,1,0:T(8,128)(2,1)} %dispatch_rows.1), calls=%async_computation | async-start | bytes 2359296 | tf_op jit(solution)/shard_map/student_exchange/all_to_all | solution.py:334
  22.2 4.3 %convert_reduce_fusion = (f32[64,32]{1,0:T(8,128)S(1)}, f32[64,32]{1,0:T(8,128)S(1)}) fusion(bf16[64,32,1280]{2,1,0:T(8,128)(2,1)} %param.10), kind=kLoop, calls=%fused_computation.1 | loop fusion | flops 10481664 | bytes 5259264 | tf_op jit(solution)/shard_map/teacher_sums/reduce_sum | solution.py:337
  26.6 1.7 collective-permute-start.2
  28.3 2.9 %collective-permute-start.3 = (f32[88,128]{1,0:T(8,128)S(1)}, f32[88,128]{1,0:T(8,128)S(1)}, u32[]{:S(2)}, u32[]{:S(2)}) collective-permute-start(f32[88,128]{1,0:T(8,128)S(1)} %constant_dynamic-update-slice_fusion), channel_id=1, source_target_pairs={{0,2},{1,3},{2,0},{3,1},{4,6},{5,7},{6,4},{7,5},{8,10},{9,11},{10,... | collective-permute-start | bytes 135176 | tf_op jit(solution)/shard_map/teacher_sums/ppermute | solution.py:307
  32.5 2.4 %collective-permute-start.5 = (bf16[32,768]{1,0:T(8,128)(2,1)S(1)}, bf16[32,768]{1,0:T(8,128)(2,1)S(1)}, u32[]{:S(2)}, u32[]{:S(2)}) collective-permute-start(bf16[32,768]{1,0:T(8,128)(2,1)S(1)} %pad_maximum_fusion.4), channel_id=1, source_target_pairs={{0,16},{4,20},{8,24},{12,28},{16,0},{20,4},{24,8},{28,12},{32,48},... | collective-permute-start | bytes 147464 | tf_op jit(solution)/shard_map/ppermute | solution.py:316
  35.4 15.5 %collective-permute-done.5 = bf16[32,768]{1,0:T(8,128)(2,1)S(1)} collective-permute-done((bf16[32,768]{1,0:T(8,128)(2,1)S(1)}, bf16[32,768]{1,0:T(8,128)(2,1)S(1)}, u32[]{:S(2)}, u32[]{:S(2)}) %collective-permute-start.5) | collective-permute-done | bytes 49184 | tf_op jit(solution)/shard_map/ppermute | solution.py:316
  52.8 1.7 collective-permute-start.7
  55.4 23.0 %collective-permute-done.6.x1 = bf16[64,64,128]{2,1,0:T(8,128)(2,1)} collective-permute-done((bf16[64,64,128]{2,1,0:T(8,128)(2,1)S(1)}, bf16[64,64,128]{2,1,0:T(8,128)(2,1)}, u32[]{:S(2)}, u32[]{:S(2)}) %collective-permute-start.6) | collective-permute-done | bytes 1048608 | tf_op jit(solution)/shard_map/student_ring/ppermute | solution.py:307
  81.1 1.7 collective-permute-start.8
  82.8 1.9 %slice.92 = bf16[32,64,128]{2,1,0:T(8,128)(2,1)} slice(bf16[64,64,128]{2,1,0:T(8,128)(2,1)} %collective-permute-done.7.x2), slice={[32:64], [0:64], [0:128]} | slice | bytes 1048576 | tf_op jit(solution)/shard_map/student_ring/slice | solution.py:362
  84.7 1.7 collective-permute-start.9
  87.8 10.1 %near_terms.1 = (f32[2048,1280]{1,0:T(8,128)}, bf16[1024,2048]{1,0:T(8,128)(2,1)}) custom-call(s32[1]{0:T(128)} %bitcast.sc, bf16[64,64,128]{2,1,0:T(8,128)(2,1)} %copy-done.1, bf16[64,64,128]{2,1,0:T(8,128)(2,1)} %collective-permute-done.6.x1, bf16[64,64,128]{2,1,0:T(8,128)(2,1)} %collective-permute-done.7.x2, bf16[1024,1280]{1,0:T(8,128)(2,1)} %w_ref.3), custom_call_target="tpu_custom_call" | custom-call | flops 4026531840 | bytes 20971520 | tf_op jit(solution)/shard_map/near_terms/pallas_call | solution.py:83
  98.5 19.6 %head_terms.1 = (f32[512,1536]{1,0:T(8,128)}, f32[512,1536]{1,0:T(8,128)}) custom-call(s32[66]{0:T(128)} %pad_add_fusion.sc, f32[2048,1280]{1,0:T(8,128)} %get-tuple-element.32.pred_ref, bf16[1024,2048]{1,0:T(8,128)(2,1)} %get-tuple-element.33.xt_ref, bf16[32,64,128]{2,1,0:T(8,128)(2,1)} %collective-permute-done.8.fa, ...), custom_call_target="tpu_custom_call" | custom-call | flops 8053063680 | bytes 31457280 | tf_op jit(solution)/shard_map/head_terms/pallas_call | solution.py:177
  118.2 5.1 %collective-permute-done.11 = bf16[64,768]{1,0:T(8,128)(2,1)S(1)} collective-permute-done((bf16[64,768]{1,0:T(8,128)(2,1)S(1)}, bf16[64,768]{1,0:T(8,128)(2,1)S(1)}, u32[]{:S(2)}, u32[]{:S(2)}) %collective-permute-start.11) | collective-permute-done | bytes 98336 | tf_op jit(solution)/shard_map/ppermute | solution.py:316
  124.1 4.9 %add_and_code.1 = s16[512,1408]{1,0:T(8,128)(2,1)} custom-call(f32[512,1536]{1,0:T(8,128)} %get-tuple-element.36.a, f32[512,1536]{1,0:T(8,128)} %collective-permute-done.10.b), custom_call_target="tpu_custom_call" | custom-call | tf_op jit(solution)/shard_map/add_and_code/pallas_call | solution.py:245
  129.0 6.6 %all-to-all-start.1 = ((s16[32,16,1408]{2,1,0:T(8,128)(2,1)}), s16[32,16,1408]{2,1,0:T(8,128)(2,1)S(1)}, u32[]{:S(2)}, u32[]{:S(2)}) async-start(s16[32,16,1408]{2,1,0:T(8,128)(2,1)} %bitcast.28), calls=%async_computation.1 | async-start | bytes 2883584 | tf_op jit(solution)/shard_map/grad_xz/all_to_all | solution.py:416
  138.0 1.8 collective-permute-start.14
  140.0 13.4 %collective-permute-done.12 = bf16[128,768]{1,0:T(8,128)(2,1)S(1)} collective-permute-done((bf16[128,768]{1,0:T(8,128)(2,1)S(1)}, bf16[128,768]{1,0:T(8,128)(2,1)S(1)}, u32[]{:S(2)}, u32[]{:S(2)}) %collective-permute-start.12) | collective-permute-done | bytes 196640 | tf_op jit(solution)/shard_map/ppermute | solution.py:316
  156.2 13.9 %all-to-all-done.1.src = s16[32,16,1408]{2,1,0:T(8,128)(2,1)S(1)} async-done(((s16[32,16,1408]{2,1,0:T(8,128)(2,1)}), s16[32,16,1408]{2,1,0:T(8,128)(2,1)S(1)}, u32[]{:S(2)}, u32[]{:S(2)}) %all-to-all-start.1) | async-done | bytes 1441824 | tf_op jit(solution)/shard_map/grad_xz/all_to_all | solution.py:416
  171.2 2.4 %sum_last.1 = (f32[16,1280]{1,0:T(8,128)}, f32[8,128]{1,0:T(8,128)}) custom-call(s16[32,16,1408]{2,1,0:T(8,128)(2,1)} %copy-done, f32[8,128]{1,0:T(8,128)} %select_maximum_fusion.partial_ref), custom_call_target="tpu_custom_call" | custom-call | tf_op jit(solution)/shard_map/sum_last/pallas_call | solution.py:273
  174.3 3.4 %collective-permute-start.16 = (f32[8,128]{1,0:T(8,128)}, f32[8,128]{1,0:T(8,128)S(1)}, u32[]{:S(2)}, u32[]{:S(2)}) collective-permute-start(f32[8,128]{1,0:T(8,128)} %get-tuple-element.45), channel_id=1, source_target_pairs={{0,2},{1,3},{2,0},{3,1},{4,6},{5,7},{6,4},{7,5},{8,10},{9,11},{10,... | collective-permute-start | bytes 12296 | tf_op jit(solution)/shard_map/loss_parts/ppermute | solution.py:307
  179.4 2.1 %collective-permute-done.17 = f32[8,128]{1,0:T(8,128)S(1)} collective-permute-done((f32[8,128]{1,0:T(8,128)}, f32[8,128]{1,0:T(8,128)S(1)}, u32[]{:S(2)}, u32[]{:S(2)}) %collective-permute-start.17) | collective-permute-done | bytes 4128 | tf_op jit(solution)/shard_map/loss_parts/ppermute | solution.py:307
  (103 shorter events, 22.9 us)
Async XLA Ops:
  0.6 11.1 %collective-permute-start = (bf16[8,768]{1,0:T(8,128)(2,1)}, bf16[8,768]{1,0:T(8,128)(2,1)S(1)}, u32[]{:S(2)}, u32[]{:S(2)}) collective-permute-start(bf16[8,768]{1,0:T(8,128)(2,1)} %param.14), channel_id=1, source_target_pairs={{0,32},{4,36},{8,40},{12,44},{16,48},{20,52},{24,56},{28,60},{32,0... | collective-permute-start | bytes 36872 | tf_op jit(solution)/shard_map/ppermute | solution.py:316
  8.5 12.1 %copy-start.5 = (s32[8]{0:T(128)S(1)}, s32[8]{0:T(128)}, u32[]{:S(2)}) copy-start(s32[8]{0:T(128)} %param.15) | copy-start | bytes 100
  8.5 12.4 %copy-start.4 = (bf16[8,768]{1,0:T(8,128)(2,1)S(1)}, bf16[8,768]{1,0:T(8,128)(2,1)}, u32[]{:S(2)}) copy-start(bf16[8,768]{1,0:T(8,128)(2,1)} %param.13) | copy-start | bytes 36868
  11.8 39.3 %all-to-all-start = ((bf16[64,72,128]{2,1,0:T(8,128)(2,1)}), bf16[64,72,128]{2,1,0:T(8,128)(2,1)S(1)}, u32[]{:S(2)}, u32[]{:S(2)}) async-start(bf16[64,72,128]{2,1,0:T(8,128)(2,1)} %dispatch_rows.1), calls=%async_computation | async-start | bytes 2359296 | tf_op jit(solution)/shard_map/student_exchange/all_to_all | solution.py:334
  21.0 1.2 collective-permute-start.1
  26.5 28.0 %copy-start.2 = (s32[2048]{0:T(1024)S(1)}, s32[2048]{0:T(1024)}, u32[]{:S(2)}) copy-start(s32[2048]{0:T(1024)} %holders.1) | copy-start | bytes 24580
  26.6 8.3 %collective-permute-start.2 = (f32[88,128]{1,0:T(8,128)S(1)}, f32[88,128]{1,0:T(8,128)S(1)}, u32[]{:S(2)}, u32[]{:S(2)}) collective-permute-start(f32[88,128]{1,0:T(8,128)S(1)} %constant_dynamic-update-slice_fusion), channel_id=1, source_target_pairs={{0,1},{1,2},{2,3},{3,0},{4,5},{5,6},{6,7},{7,4},{8,9},{9,10},{10,1... | collective-permute-start | bytes 135176 | tf_op jit(solution)/shard_map/teacher_sums/ppermute | solution.py:307
  28.3 6.6 %collective-permute-start.3 = (f32[88,128]{1,0:T(8,128)S(1)}, f32[88,128]{1,0:T(8,128)S(1)}, u32[]{:S(2)}, u32[]{:S(2)}) collective-permute-start(f32[88,128]{1,0:T(8,128)S(1)} %constant_dynamic-update-slice_fusion), channel_id=1, source_target_pairs={{0,2},{1,3},{2,0},{3,1},{4,6},{5,7},{6,4},{7,5},{8,10},{9,11},{10,... | collective-permute-start | bytes 135176 | tf_op jit(solution)/shard_map/teacher_sums/ppermute | solution.py:307
  31.2 4.0 %collective-permute-start.4 = (f32[88,128]{1,0:T(8,128)S(1)}, f32[88,128]{1,0:T(8,128)S(1)}, u32[]{:S(2)}, u32[]{:S(2)}) collective-permute-start(f32[88,128]{1,0:T(8,128)S(1)} %constant_dynamic-update-slice_fusion), channel_id=1, source_target_pairs={{0,3},{1,0},{2,1},{3,2},{4,7},{5,4},{6,5},{7,6},{8,11},{9,8},{10,9... | collective-permute-start | bytes 135176 | tf_op jit(solution)/shard_map/teacher_sums/ppermute | solution.py:307
  32.5 18.3 %collective-permute-start.5 = (bf16[32,768]{1,0:T(8,128)(2,1)S(1)}, bf16[32,768]{1,0:T(8,128)(2,1)S(1)}, u32[]{:S(2)}, u32[]{:S(2)}) collective-permute-start(bf16[32,768]{1,0:T(8,128)(2,1)S(1)} %pad_maximum_fusion.4), channel_id=1, source_target_pairs={{0,16},{4,20},{8,24},{12,28},{16,0},{20,4},{24,8},{28,12},{32,48},... | collective-permute-start | bytes 147464 | tf_op jit(solution)/shard_map/ppermute | solution.py:316
  51.2 36.6 %copy-start.1 = (bf16[64,64,128]{2,1,0:T(8,128)(2,1)}, bf16[64,64,128]{2,1,0:T(8,128)(2,1)S(1)}, u32[]{:S(2)}) copy-start(bf16[64,64,128]{2,1,0:T(8,128)(2,1)S(1)} %slice.89.x0) | copy-start | bytes 3145732
  51.2 27.3 %collective-permute-start.6 = (bf16[64,64,128]{2,1,0:T(8,128)(2,1)S(1)}, bf16[64,64,128]{2,1,0:T(8,128)(2,1)}, u32[]{:S(2)}, u32[]{:S(2)}) collective-permute-start(bf16[64,64,128]{2,1,0:T(8,128)(2,1)S(1)} %slice.89.x0), channel_id=1, source_target_pairs={{0,1},{1,2},{2,3},{3,0},{4,5},{5,6},{6,7},{7,4},{8,9},{9,10},{10,1... | collective-permute-start | bytes 3145736 | tf_op jit(solution)/shard_map/student_ring/ppermute | solution.py:307
  52.8 26.0 %collective-permute-start.7 = (bf16[64,64,128]{2,1,0:T(8,128)(2,1)S(1)}, bf16[64,64,128]{2,1,0:T(8,128)(2,1)}, u32[]{:S(2)}, u32[]{:S(2)}) collective-permute-start(bf16[64,64,128]{2,1,0:T(8,128)(2,1)S(1)} %slice.89.x0), channel_id=1, source_target_pairs={{0,3},{1,0},{2,1},{3,2},{4,7},{5,4},{6,5},{7,6},{8,11},{9,8},{10,9... | collective-permute-start | bytes 3145736 | tf_op jit(solution)/shard_map/student_ring/ppermute | solution.py:307
  81.1 16.8 %collective-permute-start.8 = (bf16[32,64,128]{2,1,0:T(8,128)(2,1)S(1)}, bf16[32,64,128]{2,1,0:T(8,128)(2,1)}, u32[]{:S(2)}, u32[]{:S(2)}) collective-permute-start(bf16[32,64,128]{2,1,0:T(8,128)(2,1)S(1)} %slice.91), channel_id=1, source_target_pairs={{0,1},{1,2},{2,3},{3,0},{4,5},{5,6},{6,7},{7,4},{8,9},{9,10},{10,1... | collective-permute-start | bytes 1572872 | tf_op jit(solution)/shard_map/student_ring/ppermute | solution.py:307
  84.7 13.8 %collective-permute-start.9 = (bf16[32,64,128]{2,1,0:T(8,128)(2,1)}, bf16[32,64,128]{2,1,0:T(8,128)(2,1)}, u32[]{:S(2)}, u32[]{:S(2)}) collective-permute-start(bf16[32,64,128]{2,1,0:T(8,128)(2,1)} %slice.92), channel_id=1, source_target_pairs={{0,3},{1,0},{2,1},{3,2},{4,7},{5,4},{6,5},{7,6},{8,11},{9,8},{10,9... | collective-permute-start | bytes 1572872 | tf_op jit(solution)/shard_map/student_ring/ppermute | solution.py:307
  118.1 6.0 %collective-permute-start.10 = (f32[512,1536]{1,0:T(8,128)}, f32[512,1536]{1,0:T(8,128)}, u32[]{:S(2)}, u32[]{:S(2)}) collective-permute-start(f32[512,1536]{1,0:T(8,128)} %get-tuple-element.37), channel_id=1, source_target_pairs={{0,4},{4,0},{8,12},{12,8},{16,20},{20,16},{24,28},{28,24},{32,36},... | collective-permute-start | bytes 9437192 | tf_op jit(solution)/shard_map/grad_core/ppermute | solution.py:316
  118.1 5.2 %collective-permute-start.11 = (bf16[64,768]{1,0:T(8,128)(2,1)S(1)}, bf16[64,768]{1,0:T(8,128)(2,1)S(1)}, u32[]{:S(2)}, u32[]{:S(2)}) collective-permute-start(bf16[64,768]{1,0:T(8,128)(2,1)S(1)} %pad_maximum_fusion.2), channel_id=1, source_target_pairs={{0,8},{4,12},{8,0},{12,4},{16,24},{20,28},{24,16},{28,20},{32,40},... | collective-permute-start | bytes 294920 | tf_op jit(solution)/shard_map/ppermute | solution.py:316
  129.0 41.1 %all-to-all-start.1 = ((s16[32,16,1408]{2,1,0:T(8,128)(2,1)}), s16[32,16,1408]{2,1,0:T(8,128)(2,1)S(1)}, u32[]{:S(2)}, u32[]{:S(2)}) async-start(s16[32,16,1408]{2,1,0:T(8,128)(2,1)} %bitcast.28), calls=%async_computation.1 | async-start | bytes 2883584 | tf_op jit(solution)/shard_map/grad_xz/all_to_all | solution.py:416
  135.6 17.8 %collective-permute-start.12 = (bf16[128,768]{1,0:T(8,128)(2,1)S(1)}, bf16[128,768]{1,0:T(8,128)(2,1)S(1)}, u32[]{:S(2)}, u32[]{:S(2)}) collective-permute-start(bf16[128,768]{1,0:T(8,128)(2,1)S(1)} %pad_maximum_fusion), channel_id=1, source_target_pairs={{0,192},{4,196},{8,200},{12,204},{16,208},{20,212},{24,216},{28,22... | collective-permute-start | bytes 589832 | tf_op jit(solution)/shard_map/ppermute | solution.py:316
  137.2 16.3 %collective-permute-start.13 = (bf16[128,768]{1,0:T(8,128)(2,1)S(1)}, bf16[128,768]{1,0:T(8,128)(2,1)S(1)}, u32[]{:S(2)}, u32[]{:S(2)}) collective-permute-start(bf16[128,768]{1,0:T(8,128)(2,1)S(1)} %pad_maximum_fusion), channel_id=1, source_target_pairs={{0,128},{4,132},{8,136},{12,140},{16,144},{20,148},{24,152},{28,15... | collective-permute-start | bytes 589832 | tf_op jit(solution)/shard_map/ppermute | solution.py:316
  138.0 16.8 %collective-permute-start.14 = (bf16[128,768]{1,0:T(8,128)(2,1)S(1)}, bf16[128,768]{1,0:T(8,128)(2,1)S(1)}, u32[]{:S(2)}, u32[]{:S(2)}) collective-permute-start(bf16[128,768]{1,0:T(8,128)(2,1)S(1)} %pad_maximum_fusion), channel_id=1, source_target_pairs={{0,64},{4,68},{8,72},{12,76},{16,80},{20,84},{24,88},{28,92},{32,9... | collective-permute-start | bytes 589832 | tf_op jit(solution)/shard_map/ppermute | solution.py:316
  173.6 8.1 %collective-permute-start.15 = (f32[8,128]{1,0:T(8,128)}, f32[8,128]{1,0:T(8,128)S(1)}, u32[]{:S(2)}, u32[]{:S(2)}) collective-permute-start(f32[8,128]{1,0:T(8,128)} %get-tuple-element.45), channel_id=1, source_target_pairs={{0,1},{1,2},{2,3},{3,0},{4,5},{5,6},{6,7},{7,4},{8,9},{9,10},{10,1... | collective-permute-start | bytes 12296 | tf_op jit(solution)/shard_map/loss_parts/ppermute | solution.py:307
  174.3 7.3 %collective-permute-start.16 = (f32[8,128]{1,0:T(8,128)}, f32[8,128]{1,0:T(8,128)S(1)}, u32[]{:S(2)}, u32[]{:S(2)}) collective-permute-start(f32[8,128]{1,0:T(8,128)} %get-tuple-element.45), channel_id=1, source_target_pairs={{0,2},{1,3},{2,0},{3,1},{4,6},{5,7},{6,4},{7,5},{8,10},{9,11},{10,... | collective-permute-start | bytes 12296 | tf_op jit(solution)/shard_map/loss_parts/ppermute | solution.py:307
  177.7 3.8 %collective-permute-start.17 = (f32[8,128]{1,0:T(8,128)}, f32[8,128]{1,0:T(8,128)S(1)}, u32[]{:S(2)}, u32[]{:S(2)}) collective-permute-start(f32[8,128]{1,0:T(8,128)} %get-tuple-element.45), channel_id=1, source_target_pairs={{0,3},{1,0},{2,1},{3,2},{4,7},{5,4},{6,5},{7,6},{8,11},{9,8},{10,9... | collective-permute-start | bytes 12296 | tf_op jit(solution)/shard_map/loss_parts/ppermute | solution.py:307
  (2 other events, 12.2 us)

commit v9 on v8

--- a/solution.py
+++ b/solution.py
@@ -234,7 +234,7 @@
 def add_and_code(keep, received):
     rows, wide = keep.shape
     cols = wide - 2 * EXT
-    block = rows // 4
+    block = rows // 8
 
     def kernel(a, b, out):
         main, extra = code(a[:, :cols] + b[:, :cols], a[:, cols : cols + EXT] + b[:, cols : cols + EXT])
@@ -263,17 +263,36 @@
 
 def sum_last(received, partial):
     n, rows, wide = received.shape
+    cols = wide - EXT
+    block = n // 4
 
     def kernel(src, partial_ref, out, parts):
-        main, extra = sum_blocks([src[k] for k in range(n)])
-        out[...] = main
-        row = lax.broadcasted_iota(jnp.int32, partial.shape, 0)
-        parts[...] = jnp.where(row == 3, extra[:1], partial_ref[...])
+        main, extra = sum_blocks([src[k] for k in range(block)])
+        regress = lax.broadcasted_iota(jnp.int32, partial.shape, 0) == 3
+
+        @pl.when(pl.program_id(0) == 0)
+        def _():
+            out[...] = main
+            parts[...] = jnp.where(regress, extra[:1], partial_ref[...])
+
+        @pl.when(pl.program_id(0) > 0)
+        def _():
+            out[...] += main
+            parts[...] += jnp.where(regress, extra[:1], 0.0)
 
     return pl.pallas_call(
         kernel,
+        grid=(n // block,),
+        in_specs=[
+            pl.BlockSpec((block, rows, wide), lambda i: (i, 0, 0)),
+            pl.BlockSpec(partial.shape, lambda i: (0, 0)),
+        ],
+        out_specs=[
+            pl.BlockSpec((rows, cols), lambda i: (0, 0)),
+            pl.BlockSpec(partial.shape, lambda i: (0, 0)),
+        ],
         out_shape=[
-            jax.ShapeDtypeStruct((rows, wide - EXT), jnp.float32),
+            jax.ShapeDtypeStruct((rows, cols), jnp.float32),
             jax.ShapeDtypeStruct(partial.shape, jnp.float32),
         ],
         compiler_params=params(),
@@ -327,7 +346,7 @@
             blocks = [jnp.where(upper, blocks[k ^ 2**n], blocks[k]) for k in range(2**count)]
         return jnp.concatenate(blocks)
 
-    outgoing, texts = lax.optimization_barrier((outgoing, both(text_embed, N_Z)))
+    outgoing, texts = lax.optimization_barrier((outgoing, text_embed))
     texts, teacher_in = lax.optimization_barrier((both(texts, 1), teacher_cache))
 
     with jax.named_scope("student_exchange"):
@@ -349,7 +368,8 @@
         n_sum = sums.size // EXT
         sums = sum(p[:n_sum] for p in packed).reshape(sums.shape)
         images = jnp.concatenate([p[n_sum:] for p in packed]).reshape(img_dev, embed + EXT)
-    texts = both(texts, 4)
+    texts, sums, images = lax.optimization_barrier((texts, sums, images))
+    texts = spread(texts, 4, 2)
     mine, sums, images, texts = lax.optimization_barrier((mine, sums, images, texts))
     with jax.named_scope("student_ring"):
         counts_sent, mine = mine[:, -COUNT_ROWS:], mine[:, :-COUNT_ROWS]
@@ -405,7 +425,7 @@
         ) * (embed ** (-0.5))
         column = jnp.arange(texts.shape[0], dtype=jnp.int32)
         text_dp = column // (16 * shard_rows) * 16
-        for n, bit in enumerate((N_Z, 1, 4, 2)):
+        for n, bit in enumerate((1, 4, 8, 2)):
             text_dp = text_dp + column // (shard_rows * 2**n) % 2 * bit
         text_id = text_dp * img_dev + cache_pos * shard_rows + column % shard_rows
         best = jnp.max(logits, axis=1)

time: 185 us -> 185 us (level)
  waiting for transfers between devices: 77.6 us -> 73.8 us
  Pallas kernels: 40.2 us -> 42.9 us
    ppermute x8 -> x9, waiting for transfers between devices: 37.2 us -> 31.2 us  [swap(): return lax.ppermute(x, 'dp', [(i, i ^ bit) for i in range(n_dp)])]
    all_to_all x1, starting transfers between devices: 8.82 us -> 12.1 us  [local(): lax.all_to_all(outgoing, 'dp', split_axis=0, concat_axis=0, tiled=True)]
    ppermute x10, waiting for transfers between devices: 26.4 us -> 28.7 us  [ring(): lax.ppermute(x, 'cache', [(i, (i + step) % n_cache) for i in range(n_cach...]
    ppermute x10, starting transfers between devices: 17.7 us -> 15.6 us  [ring(): lax.ppermute(x, 'cache', [(i, (i + step) % n_cache) for i in range(n_cach...]
    pallas_call x1, Pallas kernels: 4.85 us -> 6.89 us  [add_and_code(): pl.pallas_call(kernel, grid=(rows // block,), in_specs=[spec, spec], out_...]
    ppermute x8 -> x9, starting transfers between devices: 14.1 us -> 12.6 us  [swap(): return lax.ppermute(x, 'dp', [(i, i ^ bit) for i in range(n_dp)])]
  transfers between devices with their start and end apart: 20 -> 21, of which waited for: 13 -> 12; matrix products, arithmetic and copies ran while one was open for 7% -> 6% of each run, Pallas kernels for 7% -> 6%
where the time goes in v9:
time: 185 us; the launch traced here: 182 us
  waiting for transfers between devices  73.8 us (40%)
  starting transfers between devices  47.3 us (26%)
  Pallas kernels  42.9 us (23%)
  other arithmetic  8.85 us (5%)
  local copies, waits for them, and re-layouts  7.79 us (4%)
    ppermute x9, waiting for transfers between devices, swap(): return lax.ppermute(x, 'dp', [(i, i ^ bit) for i in range(n_dp)])  31.2 us
    ppermute x10, waiting for transfers between devices, ring(): lax.ppermute(x, 'cache', [(i, (i + step) % n_cache) for i in range(n_cach...  28.7 us
    pallas_call x1, Pallas kernels, head_terms(): pl.pallas_call(kernel, grid_spec=pltpu.PrefetchScalarGridSpec(num_scalar_...  19.6 us
    ppermute x10, starting transfers between devices, ring(): lax.ppermute(x, 'cache', [(i, (i + step) % n_cache) for i in range(n_cach...  15.6 us
    all_to_all x1, waiting for transfers between devices, local(): lax.all_to_all(codes.reshape(N_X * N_Z, -1, local_cols + EXT), 'dp', 0, 0...  13.9 us
    ppermute x9, starting transfers between devices, swap(): return lax.ppermute(x, 'dp', [(i, i ^ bit) for i in range(n_dp)])  12.6 us
    all_to_all x1, starting transfers between devices, local(): lax.all_to_all(outgoing, 'dp', split_axis=0, concat_axis=0, tiled=True)  12.1 us
    pallas_call x1, Pallas kernels, near_terms(): pl.pallas_call(kernel, grid_spec=pltpu.PrefetchScalarGridSpec(num_scalar_...  10.1 us
  transfers between devices with their start and end apart: 21, of which 12 were waited for; matrix products, arithmetic and copies ran while one was open for 6% of the time, Pallas kernels for 6%

profile of v9, /device:TPU:2, one launch (start us, length us, event | category | flops | bytes accessed | tf_op | source)
XLA Modules:
  0.0 182.0 jit_solution(17133385515604130545)
XLA Ops:
  1.2 3.2 %dispatch_rows.1 = bf16[64,72,128]{2,1,0:T(8,128)(2,1)} custom-call(s32[2]{0:T(128)} %pad_add_fusion.1.place, s32[2048]{0:T(1024)} %holders.1, s32[32]{0:T(128)} %counts.1, bf16[32,32,1024]{2,1,0:T(8,128)(2,1)} %feats.1), custom_call_target="tpu_custom_call" | custom-call | tf_op jit(solution)/shard_map/dispatch_rows/pallas_call | solution.py:41
  4.5 12.1 %all-to-all-start = ((bf16[64,72,128]{2,1,0:T(8,128)(2,1)}), bf16[64,72,128]{2,1,0:T(8,128)(2,1)S(1)}, u32[]{:S(2)}, u32[]{:S(2)}) async-start(bf16[64,72,128]{2,1,0:T(8,128)(2,1)} %dispatch_rows.1), calls=%async_computation | async-start | bytes 2359296 | tf_op jit(solution)/shard_map/student_exchange/all_to_all | solution.py:353
  17.0 4.3 %convert_reduce_fusion = (f32[64,32]{1,0:T(8,128)S(1)}, f32[64,32]{1,0:T(8,128)S(1)}) fusion(bf16[64,32,1280]{2,1,0:T(8,128)(2,1)} %param.10), kind=kLoop, calls=%fused_computation.1 | loop fusion | flops 10481664 | bytes 5259264 | tf_op jit(solution)/shard_map/teacher_sums/reduce_sum | solution.py:356
  23.1 2.9 %collective-permute-start.2 = (f32[88,128]{1,0:T(8,128)S(1)}, f32[88,128]{1,0:T(8,128)S(1)}, u32[]{:S(2)}, u32[]{:S(2)}) collective-permute-start(f32[88,128]{1,0:T(8,128)S(1)} %constant_dynamic-update-slice_fusion), channel_id=1, source_target_pairs={{0,2},{1,3},{2,0},{3,1},{4,6},{5,7},{6,4},{7,5},{8,10},{9,11},{10,... | collective-permute-start | bytes 135176 | tf_op jit(solution)/shard_map/teacher_sums/ppermute | solution.py:326
  30.2 3.7 %collective-permute-start.4 = (bf16[16,768]{1,0:T(8,128)(2,1)S(1)}, bf16[16,768]{1,0:T(8,128)(2,1)S(1)}, u32[]{:S(2)}, u32[]{:S(2)}) collective-permute-start(bf16[16,768]{1,0:T(8,128)(2,1)S(1)} %pad_maximum_fusion.6), channel_id=1, source_target_pairs={{0,48},{4,52},{8,56},{12,60},{16,32},{20,36},{24,40},{28,44},{32,1... | collective-permute-start | bytes 73736 | tf_op jit(solution)/shard_map/ppermute | solution.py:335
  33.9 2.3 %collective-permute-start.5 = (bf16[16,768]{1,0:T(8,128)(2,1)S(1)}, bf16[16,768]{1,0:T(8,128)(2,1)S(1)}, u32[]{:S(2)}, u32[]{:S(2)}) collective-permute-start(bf16[16,768]{1,0:T(8,128)(2,1)S(1)} %pad_maximum_fusion.6), channel_id=1, source_target_pairs={{0,32},{4,36},{8,40},{12,44},{16,48},{20,52},{24,56},{28,60},{32,0... | collective-permute-start | bytes 73736 | tf_op jit(solution)/shard_map/ppermute | solution.py:335
  36.7 10.8 %collective-permute-done.4 = bf16[16,768]{1,0:T(8,128)(2,1)S(1)} collective-permute-done((bf16[16,768]{1,0:T(8,128)(2,1)S(1)}, bf16[16,768]{1,0:T(8,128)(2,1)S(1)}, u32[]{:S(2)}, u32[]{:S(2)}) %collective-permute-start.4) | collective-permute-done | bytes 24608 | tf_op jit(solution)/shard_map/ppermute | solution.py:335
  50.8 1.7 collective-permute-start.8
  53.4 21.8 %collective-permute-done.7.x1 = bf16[64,64,128]{2,1,0:T(8,128)(2,1)} collective-permute-done((bf16[64,64,128]{2,1,0:T(8,128)(2,1)S(1)}, bf16[64,64,128]{2,1,0:T(8,128)(2,1)}, u32[]{:S(2)}, u32[]{:S(2)}) %collective-permute-start.7) | collective-permute-done | bytes 1048608 | tf_op jit(solution)/shard_map/student_ring/ppermute | solution.py:326
  77.6 3.1 %collective-permute-start.10 = (bf16[32,64,128]{2,1,0:T(8,128)(2,1)S(1)}, bf16[32,64,128]{2,1,0:T(8,128)(2,1)}, u32[]{:S(2)}, u32[]{:S(2)}) collective-permute-start(bf16[32,64,128]{2,1,0:T(8,128)(2,1)S(1)} %slice.92), channel_id=1, source_target_pairs={{0,3},{1,0},{2,1},{3,2},{4,7},{5,4},{6,5},{7,6},{8,11},{9,8},{10,9... | collective-permute-start | bytes 1572872 | tf_op jit(solution)/shard_map/student_ring/ppermute | solution.py:326
  80.7 1.9 %slice.91 = bf16[32,64,128]{2,1,0:T(8,128)(2,1)} slice(bf16[64,64,128]{2,1,0:T(8,128)(2,1)} %collective-permute-done.7.x1), slice={[0:32], [0:64], [0:128]} | slice | bytes 1048576 | tf_op jit(solution)/shard_map/student_ring/slice | solution.py:381
  84.0 10.1 %near_terms.1 = (f32[2048,1280]{1,0:T(8,128)}, bf16[1024,2048]{1,0:T(8,128)(2,1)}) custom-call(s32[1]{0:T(128)} %bitcast.sc, bf16[64,64,128]{2,1,0:T(8,128)(2,1)} %copy-done.1, bf16[64,64,128]{2,1,0:T(8,128)(2,1)} %collective-permute-done.7.x1, bf16[64,64,128]{2,1,0:T(8,128)(2,1)} %collective-permute-done.8.x2, bf16[1024,1280]{1,0:T(8,128)(2,1)} %w_ref.3), custom_call_target="tpu_custom_call" | custom-call | flops 4026531840 | bytes 20971520 | tf_op jit(solution)/shard_map/near_terms/pallas_call | solution.py:83
  94.1 2.0 %collective-permute-done.9.fa = bf16[32,64,128]{2,1,0:T(8,128)(2,1)} collective-permute-done((bf16[32,64,128]{2,1,0:T(8,128)(2,1)}, bf16[32,64,128]{2,1,0:T(8,128)(2,1)}, u32[]{:S(2)}, u32[]{:S(2)}) %collective-permute-start.9) | collective-permute-done | bytes 524320 | tf_op jit(solution)/shard_map/student_ring/ppermute | solution.py:326
  96.1 19.6 %head_terms.1 = (f32[512,1536]{1,0:T(8,128)}, f32[512,1536]{1,0:T(8,128)}) custom-call(s32[66]{0:T(128)} %pad_add_fusion.sc, f32[2048,1280]{1,0:T(8,128)} %get-tuple-element.38.pred_ref, bf16[1024,2048]{1,0:T(8,128)(2,1)} %get-tuple-element.39.xt_ref, bf16[32,64,128]{2,1,0:T(8,128)(2,1)} %collective-permute-done.9.fa, ...), custom_call_target="tpu_custom_call" | custom-call | flops 8053063680 | bytes 31457280 | tf_op jit(solution)/shard_map/head_terms/pallas_call | solution.py:177
  115.7 1.8 %collective-permute-start.12 = (bf16[64,768]{1,0:T(8,128)(2,1)S(1)}, bf16[64,768]{1,0:T(8,128)(2,1)S(1)}, u32[]{:S(2)}, u32[]{:S(2)}) collective-permute-start(bf16[64,768]{1,0:T(8,128)(2,1)S(1)} %pad_maximum_fusion.2), channel_id=1, source_target_pairs={{0,8},{4,12},{8,0},{12,4},{16,24},{20,28},{24,16},{28,20},{32,40},... | collective-permute-start | bytes 294920 | tf_op jit(solution)/shard_map/ppermute | solution.py:335
  117.6 3.4 %collective-permute-done.12 = bf16[64,768]{1,0:T(8,128)(2,1)S(1)} collective-permute-done((bf16[64,768]{1,0:T(8,128)(2,1)S(1)}, bf16[64,768]{1,0:T(8,128)(2,1)S(1)}, u32[]{:S(2)}, u32[]{:S(2)}) %collective-permute-start.12) | collective-permute-done | bytes 98336 | tf_op jit(solution)/shard_map/ppermute | solution.py:335
  121.7 6.9 %add_and_code.1 = s16[512,1408]{1,0:T(8,128)(2,1)} custom-call(f32[512,1536]{1,0:T(8,128)} %get-tuple-element.42.a, f32[512,1536]{1,0:T(8,128)} %collective-permute-done.11.b), custom_call_target="tpu_custom_call" | custom-call | tf_op jit(solution)/shard_map/add_and_code/pallas_call | solution.py:245
  128.6 7.1 %all-to-all-start.1 = ((s16[32,16,1408]{2,1,0:T(8,128)(2,1)}), s16[32,16,1408]{2,1,0:T(8,128)(2,1)S(1)}, u32[]{:S(2)}, u32[]{:S(2)}) async-start(s16[32,16,1408]{2,1,0:T(8,128)(2,1)} %bitcast.28), calls=%async_computation.1 | async-start | bytes 2883584 | tf_op jit(solution)/shard_map/grad_xz/all_to_all | solution.py:436
  138.1 1.8 collective-permute-start.15
  140.1 13.4 %collective-permute-done.13 = bf16[128,768]{1,0:T(8,128)(2,1)S(1)} collective-permute-done((bf16[128,768]{1,0:T(8,128)(2,1)S(1)}, bf16[128,768]{1,0:T(8,128)(2,1)S(1)}, u32[]{:S(2)}, u32[]{:S(2)}) %collective-permute-start.13) | collective-permute-done | bytes 196640 | tf_op jit(solution)/shard_map/ppermute | solution.py:335
  156.3 13.9 %all-to-all-done.1.src = s16[32,16,1408]{2,1,0:T(8,128)(2,1)S(1)} async-done(((s16[32,16,1408]{2,1,0:T(8,128)(2,1)}), s16[32,16,1408]{2,1,0:T(8,128)(2,1)S(1)}, u32[]{:S(2)}, u32[]{:S(2)}) %all-to-all-start.1) | async-done | bytes 1441824 | tf_op jit(solution)/shard_map/grad_xz/all_to_all | solution.py:436
  171.3 3.1 %sum_last.1 = (f32[16,1280]{1,0:T(8,128)}, f32[8,128]{1,0:T(8,128)}) custom-call(s16[32,16,1408]{2,1,0:T(8,128)(2,1)} %copy-done, f32[8,128]{1,0:T(8,128)} %select_maximum_fusion.partial_ref), custom_call_target="tpu_custom_call" | custom-call | tf_op jit(solution)/shard_map/sum_last/pallas_call | solution.py:283
  174.3 2.3 %collective-permute-start.17 = (f32[8,128]{1,0:T(8,128)}, f32[8,128]{1,0:T(8,128)S(1)}, u32[]{:S(2)}, u32[]{:S(2)}) collective-permute-start(f32[8,128]{1,0:T(8,128)} %get-tuple-element.51), channel_id=1, source_target_pairs={{0,2},{1,3},{2,0},{3,1},{4,6},{5,7},{6,4},{7,5},{8,10},{9,11},{10,... | collective-permute-start | bytes 12296 | tf_op jit(solution)/shard_map/loss_parts/ppermute | solution.py:326
  178.3 2.2 %collective-permute-done.18 = f32[8,128]{1,0:T(8,128)S(1)} collective-permute-done((f32[8,128]{1,0:T(8,128)}, f32[8,128]{1,0:T(8,128)S(1)}, u32[]{:S(2)}, u32[]{:S(2)}) %collective-permute-start.18) | collective-permute-done | bytes 4128 | tf_op jit(solution)/shard_map/loss_parts/ppermute | solution.py:326
  (103 shorter events, 25.7 us)
Async XLA Ops:
  1.2 15.7 %copy-start.3 = (bf16[8,768]{1,0:T(8,128)(2,1)S(1)}, bf16[8,768]{1,0:T(8,128)(2,1)}, u32[]{:S(2)}) copy-start(bf16[8,768]{1,0:T(8,128)(2,1)} %param.13) | copy-start | bytes 36868
  4.5 12.5 %collective-permute-start = (bf16[8,768]{1,0:T(8,128)(2,1)S(1)}, bf16[8,768]{1,0:T(8,128)(2,1)S(1)}, u32[]{:S(2)}, u32[]{:S(2)}) collective-permute-start(bf16[8,768]{1,0:T(8,128)(2,1)S(1)} %copy-done.4), channel_id=1, source_target_pairs={{0,4},{4,0},{8,12},{12,8},{16,20},{20,16},{24,28},{28,24},{32,36},... | collective-permute-start | bytes 36872 | tf_op jit(solution)/shard_map/ppermute | solution.py:335
  4.5 44.5 %all-to-all-start = ((bf16[64,72,128]{2,1,0:T(8,128)(2,1)}), bf16[64,72,128]{2,1,0:T(8,128)(2,1)S(1)}, u32[]{:S(2)}, u32[]{:S(2)}) async-start(bf16[64,72,128]{2,1,0:T(8,128)(2,1)} %dispatch_rows.1), calls=%async_computation | async-start | bytes 2359296 | tf_op jit(solution)/shard_map/student_exchange/all_to_all | solution.py:353
  21.3 31.2 %copy-start.2 = (s32[2048]{0:T(1024)S(1)}, s32[2048]{0:T(1024)}, u32[]{:S(2)}) copy-start(s32[2048]{0:T(1024)} %holders.1) | copy-start | bytes 24580
  21.5 5.9 %collective-permute-start.1 = (f32[88,128]{1,0:T(8,128)S(1)}, f32[88,128]{1,0:T(8,128)S(1)}, u32[]{:S(2)}, u32[]{:S(2)}) collective-permute-start(f32[88,128]{1,0:T(8,128)S(1)} %constant_dynamic-update-slice_fusion), channel_id=1, source_target_pairs={{0,1},{1,2},{2,3},{3,0},{4,5},{5,6},{6,7},{7,4},{8,9},{9,10},{10,1... | collective-permute-start | bytes 135176 | tf_op jit(solution)/shard_map/teacher_sums/ppermute | solution.py:326
  23.1 5.6 %collective-permute-start.2 = (f32[88,128]{1,0:T(8,128)S(1)}, f32[88,128]{1,0:T(8,128)S(1)}, u32[]{:S(2)}, u32[]{:S(2)}) collective-permute-start(f32[88,128]{1,0:T(8,128)S(1)} %constant_dynamic-update-slice_fusion), channel_id=1, source_target_pairs={{0,2},{1,3},{2,0},{3,1},{4,6},{5,7},{6,4},{7,5},{8,10},{9,11},{10,... | collective-permute-start | bytes 135176 | tf_op jit(solution)/shard_map/teacher_sums/ppermute | solution.py:326
  26.0 4.0 %collective-permute-start.3 = (f32[88,128]{1,0:T(8,128)S(1)}, f32[88,128]{1,0:T(8,128)S(1)}, u32[]{:S(2)}, u32[]{:S(2)}) collective-permute-start(f32[88,128]{1,0:T(8,128)S(1)} %constant_dynamic-update-slice_fusion), channel_id=1, source_target_pairs={{0,3},{1,0},{2,1},{3,2},{4,7},{5,4},{6,5},{7,6},{8,11},{9,8},{10,9... | collective-permute-start | bytes 135176 | tf_op jit(solution)/shard_map/teacher_sums/ppermute | solution.py:326
  30.2 17.3 %collective-permute-start.4 = (bf16[16,768]{1,0:T(8,128)(2,1)S(1)}, bf16[16,768]{1,0:T(8,128)(2,1)S(1)}, u32[]{:S(2)}, u32[]{:S(2)}) collective-permute-start(bf16[16,768]{1,0:T(8,128)(2,1)S(1)} %pad_maximum_fusion.6), channel_id=1, source_target_pairs={{0,48},{4,52},{8,56},{12,60},{16,32},{20,36},{24,40},{28,44},{32,1... | collective-permute-start | bytes 73736 | tf_op jit(solution)/shard_map/ppermute | solution.py:335
  33.9 15.1 %collective-permute-start.5 = (bf16[16,768]{1,0:T(8,128)(2,1)S(1)}, bf16[16,768]{1,0:T(8,128)(2,1)S(1)}, u32[]{:S(2)}, u32[]{:S(2)}) collective-permute-start(bf16[16,768]{1,0:T(8,128)(2,1)S(1)} %pad_maximum_fusion.6), channel_id=1, source_target_pairs={{0,32},{4,36},{8,40},{12,44},{16,48},{20,52},{24,56},{28,60},{32,0... | collective-permute-start | bytes 73736 | tf_op jit(solution)/shard_map/ppermute | solution.py:335
  36.2 12.8 %collective-permute-start.6 = (bf16[16,768]{1,0:T(8,128)(2,1)S(1)}, bf16[16,768]{1,0:T(8,128)(2,1)S(1)}, u32[]{:S(2)}, u32[]{:S(2)}) collective-permute-start(bf16[16,768]{1,0:T(8,128)(2,1)S(1)} %pad_maximum_fusion.6), channel_id=1, source_target_pairs={{0,16},{4,20},{8,24},{12,28},{16,0},{20,4},{24,8},{28,12},{32,48},... | collective-permute-start | bytes 73736 | tf_op jit(solution)/shard_map/ppermute | solution.py:335
  49.2 34.8 %copy-start.1 = (bf16[64,64,128]{2,1,0:T(8,128)(2,1)}, bf16[64,64,128]{2,1,0:T(8,128)(2,1)S(1)}, u32[]{:S(2)}) copy-start(bf16[64,64,128]{2,1,0:T(8,128)(2,1)S(1)} %slice.89.x0) | copy-start | bytes 3145732
  49.2 26.0 %collective-permute-start.7 = (bf16[64,64,128]{2,1,0:T(8,128)(2,1)S(1)}, bf16[64,64,128]{2,1,0:T(8,128)(2,1)}, u32[]{:S(2)}, u32[]{:S(2)}) collective-permute-start(bf16[64,64,128]{2,1,0:T(8,128)(2,1)S(1)} %slice.89.x0), channel_id=1, source_target_pairs={{0,1},{1,2},{2,3},{3,0},{4,5},{5,6},{6,7},{7,4},{8,9},{9,10},{10,1... | collective-permute-start | bytes 3145736 | tf_op jit(solution)/shard_map/student_ring/ppermute | solution.py:326
  50.8 24.4 %collective-permute-start.8 = (bf16[64,64,128]{2,1,0:T(8,128)(2,1)S(1)}, bf16[64,64,128]{2,1,0:T(8,128)(2,1)}, u32[]{:S(2)}, u32[]{:S(2)}) collective-permute-start(bf16[64,64,128]{2,1,0:T(8,128)(2,1)S(1)} %slice.89.x0), channel_id=1, source_target_pairs={{0,3},{1,0},{2,1},{3,2},{4,7},{5,4},{6,5},{7,6},{8,11},{9,8},{10,9... | collective-permute-start | bytes 3145736 | tf_op jit(solution)/shard_map/student_ring/ppermute | solution.py:326
  77.6 16.5 %collective-permute-start.10 = (bf16[32,64,128]{2,1,0:T(8,128)(2,1)S(1)}, bf16[32,64,128]{2,1,0:T(8,128)(2,1)}, u32[]{:S(2)}, u32[]{:S(2)}) collective-permute-start(bf16[32,64,128]{2,1,0:T(8,128)(2,1)S(1)} %slice.92), channel_id=1, source_target_pairs={{0,3},{1,0},{2,1},{3,2},{4,7},{5,4},{6,5},{7,6},{8,11},{9,8},{10,9... | collective-permute-start | bytes 1572872 | tf_op jit(solution)/shard_map/student_ring/ppermute | solution.py:326
  82.6 13.5 %collective-permute-start.9 = (bf16[32,64,128]{2,1,0:T(8,128)(2,1)}, bf16[32,64,128]{2,1,0:T(8,128)(2,1)}, u32[]{:S(2)}, u32[]{:S(2)}) collective-permute-start(bf16[32,64,128]{2,1,0:T(8,128)(2,1)} %slice.91), channel_id=1, source_target_pairs={{0,1},{1,2},{2,3},{3,0},{4,5},{5,6},{6,7},{7,4},{8,9},{9,10},{10,1... | collective-permute-start | bytes 1572872 | tf_op jit(solution)/shard_map/student_ring/ppermute | solution.py:326
  115.7 6.0 %collective-permute-start.11 = (f32[512,1536]{1,0:T(8,128)}, f32[512,1536]{1,0:T(8,128)}, u32[]{:S(2)}, u32[]{:S(2)}) collective-permute-start(f32[512,1536]{1,0:T(8,128)} %get-tuple-element.43), channel_id=1, source_target_pairs={{0,4},{4,0},{8,12},{12,8},{16,20},{20,16},{24,28},{28,24},{32,36},... | collective-permute-start | bytes 9437192 | tf_op jit(solution)/shard_map/grad_core/ppermute | solution.py:335
  115.7 5.2 %collective-permute-start.12 = (bf16[64,768]{1,0:T(8,128)(2,1)S(1)}, bf16[64,768]{1,0:T(8,128)(2,1)S(1)}, u32[]{:S(2)}, u32[]{:S(2)}) collective-permute-start(bf16[64,768]{1,0:T(8,128)(2,1)S(1)} %pad_maximum_fusion.2), channel_id=1, source_target_pairs={{0,8},{4,12},{8,0},{12,4},{16,24},{20,28},{24,16},{28,20},{32,40},... | collective-permute-start | bytes 294920 | tf_op jit(solution)/shard_map/ppermute | solution.py:335
  128.6 41.5 %all-to-all-start.1 = ((s16[32,16,1408]{2,1,0:T(8,128)(2,1)}), s16[32,16,1408]{2,1,0:T(8,128)(2,1)S(1)}, u32[]{:S(2)}, u32[]{:S(2)}) async-start(s16[32,16,1408]{2,1,0:T(8,128)(2,1)} %bitcast.28), calls=%async_computation.1 | async-start | bytes 2883584 | tf_op jit(solution)/shard_map/grad_xz/all_to_all | solution.py:436
  135.8 17.8 %collective-permute-start.13 = (bf16[128,768]{1,0:T(8,128)(2,1)S(1)}, bf16[128,768]{1,0:T(8,128)(2,1)S(1)}, u32[]{:S(2)}, u32[]{:S(2)}) collective-permute-start(bf16[128,768]{1,0:T(8,128)(2,1)S(1)} %pad_maximum_fusion), channel_id=1, source_target_pairs={{0,192},{4,196},{8,200},{12,204},{16,208},{20,212},{24,216},{28,22... | collective-permute-start | bytes 589832 | tf_op jit(solution)/shard_map/ppermute | solution.py:335
  137.3 16.3 %collective-permute-start.14 = (bf16[128,768]{1,0:T(8,128)(2,1)S(1)}, bf16[128,768]{1,0:T(8,128)(2,1)S(1)}, u32[]{:S(2)}, u32[]{:S(2)}) collective-permute-start(bf16[128,768]{1,0:T(8,128)(2,1)S(1)} %pad_maximum_fusion), channel_id=1, source_target_pairs={{0,128},{4,132},{8,136},{12,140},{16,144},{20,148},{24,152},{28,15... | collective-permute-start | bytes 589832 | tf_op jit(solution)/shard_map/ppermute | solution.py:335
  138.1 16.8 %collective-permute-start.15 = (bf16[128,768]{1,0:T(8,128)(2,1)S(1)}, bf16[128,768]{1,0:T(8,128)(2,1)S(1)}, u32[]{:S(2)}, u32[]{:S(2)}) collective-permute-start(bf16[128,768]{1,0:T(8,128)(2,1)S(1)} %pad_maximum_fusion), channel_id=1, source_target_pairs={{0,64},{4,68},{8,72},{12,76},{16,80},{20,84},{24,88},{28,92},{32,9... | collective-permute-start | bytes 589832 | tf_op jit(solution)/shard_map/ppermute | solution.py:335
  174.3 6.3 %collective-permute-start.16 = (f32[8,128]{1,0:T(8,128)}, f32[8,128]{1,0:T(8,128)S(1)}, u32[]{:S(2)}, u32[]{:S(2)}) collective-permute-start(f32[8,128]{1,0:T(8,128)} %get-tuple-element.51), channel_id=1, source_target_pairs={{0,1},{1,2},{2,3},{3,0},{4,5},{5,6},{6,7},{7,4},{8,9},{9,10},{10,1... | collective-permute-start | bytes 12296 | tf_op jit(solution)/shard_map/loss_parts/ppermute | solution.py:326
  174.3 6.2 %collective-permute-start.17 = (f32[8,128]{1,0:T(8,128)}, f32[8,128]{1,0:T(8,128)S(1)}, u32[]{:S(2)}, u32[]{:S(2)}) collective-permute-start(f32[8,128]{1,0:T(8,128)} %get-tuple-element.51), channel_id=1, source_target_pairs={{0,2},{1,3},{2,0},{3,1},{4,6},{5,7},{6,4},{7,5},{8,10},{9,11},{10,... | collective-permute-start | bytes 12296 | tf_op jit(solution)/shard_map/loss_parts/ppermute | solution.py:326
  176.6 3.8 %collective-permute-start.18 = (f32[8,128]{1,0:T(8,128)}, f32[8,128]{1,0:T(8,128)S(1)}, u32[]{:S(2)}, u32[]{:S(2)}) collective-permute-start(f32[8,128]{1,0:T(8,128)} %get-tuple-element.51), channel_id=1, source_target_pairs={{0,3},{1,0},{2,1},{3,2},{4,7},{5,4},{6,5},{7,6},{8,11},{9,8},{10,9... | collective-permute-start | bytes 12296 | tf_op jit(solution)/shard_map/loss_parts/ppermute | solution.py:326
  (3 other events, 20.4 us)

commit v10 on v8

--- a/solution.py
+++ b/solution.py
@@ -234,7 +234,7 @@
 def add_and_code(keep, received):
     rows, wide = keep.shape
     cols = wide - 2 * EXT
-    block = rows // 4
+    block = rows // 2
 
     def kernel(a, b, out):
         main, extra = code(a[:, :cols] + b[:, :cols], a[:, cols : cols + EXT] + b[:, cols : cols + EXT])
@@ -327,7 +327,7 @@
             blocks = [jnp.where(upper, blocks[k ^ 2**n], blocks[k]) for k in range(2**count)]
         return jnp.concatenate(blocks)
 
-    outgoing, texts = lax.optimization_barrier((outgoing, both(text_embed, N_Z)))
+    outgoing, texts = lax.optimization_barrier((outgoing, text_embed))
     texts, teacher_in = lax.optimization_barrier((both(texts, 1), teacher_cache))
 
     with jax.named_scope("student_exchange"):
@@ -349,7 +349,8 @@
         n_sum = sums.size // EXT
         sums = sum(p[:n_sum] for p in packed).reshape(sums.shape)
         images = jnp.concatenate([p[n_sum:] for p in packed]).reshape(img_dev, embed + EXT)
-    texts = both(texts, 4)
+    texts, sums, images = lax.optimization_barrier((texts, sums, images))
+    texts = spread(texts, 4, 2)
     mine, sums, images, texts = lax.optimization_barrier((mine, sums, images, texts))
     with jax.named_scope("student_ring"):
         counts_sent, mine = mine[:, -COUNT_ROWS:], mine[:, :-COUNT_ROWS]
@@ -405,7 +406,7 @@
         ) * (embed ** (-0.5))
         column = jnp.arange(texts.shape[0], dtype=jnp.int32)
         text_dp = column // (16 * shard_rows) * 16
-        for n, bit in enumerate((N_Z, 1, 4, 2)):
+        for n, bit in enumerate((1, 4, 8, 2)):
             text_dp = text_dp + column // (shard_rows * 2**n) % 2 * bit
         text_id = text_dp * img_dev + cache_pos * shard_rows + column % shard_rows
         best = jnp.max(logits, axis=1)

time: 185 us -> 182 us (0.984)
  waiting for transfers between devices: 77.6 us -> 73.8 us
    ppermute x8 -> x9, waiting for transfers between devices: 37.2 us -> 31.2 us  [swap(): return lax.ppermute(x, 'dp', [(i, i ^ bit) for i in range(n_dp)])]
    all_to_all x1, starting transfers between devices: 8.82 us -> 12.1 us  [local(): lax.all_to_all(outgoing, 'dp', split_axis=0, concat_axis=0, tiled=True)]
    ppermute x10, waiting for transfers between devices: 26.4 us -> 28.7 us  [ring(): lax.ppermute(x, 'cache', [(i, (i + step) % n_cache) for i in range(n_cach...]
    ppermute x10, starting transfers between devices: 17.7 us -> 15.6 us  [ring(): lax.ppermute(x, 'cache', [(i, (i + step) % n_cache) for i in range(n_cach...]
    ppermute x8 -> x9, starting transfers between devices: 14.1 us -> 12.6 us  [swap(): return lax.ppermute(x, 'dp', [(i, i ^ bit) for i in range(n_dp)])]
  transfers between devices with their start and end apart: 20 -> 21, of which waited for: 13 -> 12; matrix products, arithmetic and copies ran while one was open for 7% -> 6% of each run, Pallas kernels for 7% -> 6%
where the time goes in v10:
time: 182 us; the launch traced here: 179 us
  waiting for transfers between devices  73.8 us (41%)
  starting transfers between devices  47.3 us (26%)
  Pallas kernels  39.5 us (22%)
  other arithmetic  8.85 us (5%)
  local copies, waits for them, and re-layouts  7.79 us (4%)
    ppermute x9, waiting for transfers between devices, swap(): return lax.ppermute(x, 'dp', [(i, i ^ bit) for i in range(n_dp)])  31.2 us
    ppermute x10, waiting for transfers between devices, ring(): lax.ppermute(x, 'cache', [(i, (i + step) % n_cache) for i in range(n_cach...  28.7 us
    pallas_call x1, Pallas kernels, head_terms(): pl.pallas_call(kernel, grid_spec=pltpu.PrefetchScalarGridSpec(num_scalar_...  19.6 us
    ppermute x10, starting transfers between devices, ring(): lax.ppermute(x, 'cache', [(i, (i + step) % n_cache) for i in range(n_cach...  15.6 us
    all_to_all x1, waiting for transfers between devices, local(): lax.all_to_all(codes.reshape(N_X * N_Z, -1, local_cols + EXT), 'dp', 0, 0...  13.9 us
    ppermute x9, starting transfers between devices, swap(): return lax.ppermute(x, 'dp', [(i, i ^ bit) for i in range(n_dp)])  12.6 us
    all_to_all x1, starting transfers between devices, local(): lax.all_to_all(outgoing, 'dp', split_axis=0, concat_axis=0, tiled=True)  12.1 us
    pallas_call x1, Pallas kernels, near_terms(): pl.pallas_call(kernel, grid_spec=pltpu.PrefetchScalarGridSpec(num_scalar_...  10.1 us
  transfers between devices with their start and end apart: 21, of which 12 were waited for; matrix products, arithmetic and copies ran while one was open for 6% of the time, Pallas kernels for 6%

profile of v10, /device:TPU:2, one launch (start us, length us, event | category | flops | bytes accessed | tf_op | source)
XLA Modules:
  0.0 178.7 jit_solution(5396749300717523102)
XLA Ops:
  1.2 3.2 %dispatch_rows.1 = bf16[64,72,128]{2,1,0:T(8,128)(2,1)} custom-call(s32[2]{0:T(128)} %pad_add_fusion.1.place, s32[2048]{0:T(1024)} %holders.1, s32[32]{0:T(128)} %counts.1, bf16[32,32,1024]{2,1,0:T(8,128)(2,1)} %feats.1), custom_call_target="tpu_custom_call" | custom-call | tf_op jit(solution)/shard_map/dispatch_rows/pallas_call | solution.py:41
  4.5 12.1 %all-to-all-start = ((bf16[64,72,128]{2,1,0:T(8,128)(2,1)}), bf16[64,72,128]{2,1,0:T(8,128)(2,1)S(1)}, u32[]{:S(2)}, u32[]{:S(2)}) async-start(bf16[64,72,128]{2,1,0:T(8,128)(2,1)} %dispatch_rows.1), calls=%async_computation | async-start | bytes 2359296 | tf_op jit(solution)/shard_map/student_exchange/all_to_all | solution.py:334
  17.0 4.3 %convert_reduce_fusion = (f32[64,32]{1,0:T(8,128)S(1)}, f32[64,32]{1,0:T(8,128)S(1)}) fusion(bf16[64,32,1280]{2,1,0:T(8,128)(2,1)} %param.10), kind=kLoop, calls=%fused_computation.1 | loop fusion | flops 10481664 | bytes 5259264 | tf_op jit(solution)/shard_map/teacher_sums/reduce_sum | solution.py:337
  23.1 2.9 %collective-permute-start.2 = (f32[88,128]{1,0:T(8,128)S(1)}, f32[88,128]{1,0:T(8,128)S(1)}, u32[]{:S(2)}, u32[]{:S(2)}) collective-permute-start(f32[88,128]{1,0:T(8,128)S(1)} %constant_dynamic-update-slice_fusion), channel_id=1, source_target_pairs={{0,2},{1,3},{2,0},{3,1},{4,6},{5,7},{6,4},{7,5},{8,10},{9,11},{10,... | collective-permute-start | bytes 135176 | tf_op jit(solution)/shard_map/teacher_sums/ppermute | solution.py:307
  30.2 3.7 %collective-permute-start.4 = (bf16[16,768]{1,0:T(8,128)(2,1)S(1)}, bf16[16,768]{1,0:T(8,128)(2,1)S(1)}, u32[]{:S(2)}, u32[]{:S(2)}) collective-permute-start(bf16[16,768]{1,0:T(8,128)(2,1)S(1)} %pad_maximum_fusion.6), channel_id=1, source_target_pairs={{0,48},{4,52},{8,56},{12,60},{16,32},{20,36},{24,40},{28,44},{32,1... | collective-permute-start | bytes 73736 | tf_op jit(solution)/shard_map/ppermute | solution.py:316
  33.9 2.3 %collective-permute-start.5 = (bf16[16,768]{1,0:T(8,128)(2,1)S(1)}, bf16[16,768]{1,0:T(8,128)(2,1)S(1)}, u32[]{:S(2)}, u32[]{:S(2)}) collective-permute-start(bf16[16,768]{1,0:T(8,128)(2,1)S(1)} %pad_maximum_fusion.6), channel_id=1, source_target_pairs={{0,32},{4,36},{8,40},{12,44},{16,48},{20,52},{24,56},{28,60},{32,0... | collective-permute-start | bytes 73736 | tf_op jit(solution)/shard_map/ppermute | solution.py:316
  36.7 10.8 %collective-permute-done.4 = bf16[16,768]{1,0:T(8,128)(2,1)S(1)} collective-permute-done((bf16[16,768]{1,0:T(8,128)(2,1)S(1)}, bf16[16,768]{1,0:T(8,128)(2,1)S(1)}, u32[]{:S(2)}, u32[]{:S(2)}) %collective-permute-start.4) | collective-permute-done | bytes 24608 | tf_op jit(solution)/shard_map/ppermute | solution.py:316
  50.8 1.7 collective-permute-start.8
  53.4 21.8 %collective-permute-done.7.x1 = bf16[64,64,128]{2,1,0:T(8,128)(2,1)} collective-permute-done((bf16[64,64,128]{2,1,0:T(8,128)(2,1)S(1)}, bf16[64,64,128]{2,1,0:T(8,128)(2,1)}, u32[]{:S(2)}, u32[]{:S(2)}) %collective-permute-start.7) | collective-permute-done | bytes 1048608 | tf_op jit(solution)/shard_map/student_ring/ppermute | solution.py:307
  77.6 3.1 %collective-permute-start.10 = (bf16[32,64,128]{2,1,0:T(8,128)(2,1)S(1)}, bf16[32,64,128]{2,1,0:T(8,128)(2,1)}, u32[]{:S(2)}, u32[]{:S(2)}) collective-permute-start(bf16[32,64,128]{2,1,0:T(8,128)(2,1)S(1)} %slice.92), channel_id=1, source_target_pairs={{0,3},{1,0},{2,1},{3,2},{4,7},{5,4},{6,5},{7,6},{8,11},{9,8},{10,9... | collective-permute-start | bytes 1572872 | tf_op jit(solution)/shard_map/student_ring/ppermute | solution.py:307
  80.7 1.9 %slice.91 = bf16[32,64,128]{2,1,0:T(8,128)(2,1)} slice(bf16[64,64,128]{2,1,0:T(8,128)(2,1)} %collective-permute-done.7.x1), slice={[0:32], [0:64], [0:128]} | slice | bytes 1048576 | tf_op jit(solution)/shard_map/student_ring/slice | solution.py:362
  84.0 10.1 %near_terms.1 = (f32[2048,1280]{1,0:T(8,128)}, bf16[1024,2048]{1,0:T(8,128)(2,1)}) custom-call(s32[1]{0:T(128)} %bitcast.sc, bf16[64,64,128]{2,1,0:T(8,128)(2,1)} %copy-done.1, bf16[64,64,128]{2,1,0:T(8,128)(2,1)} %collective-permute-done.7.x1, bf16[64,64,128]{2,1,0:T(8,128)(2,1)} %collective-permute-done.8.x2, bf16[1024,1280]{1,0:T(8,128)(2,1)} %w_ref.3), custom_call_target="tpu_custom_call" | custom-call | flops 4026531840 | bytes 20971520 | tf_op jit(solution)/shard_map/near_terms/pallas_call | solution.py:83
  94.1 2.0 %collective-permute-done.9.fa = bf16[32,64,128]{2,1,0:T(8,128)(2,1)} collective-permute-done((bf16[32,64,128]{2,1,0:T(8,128)(2,1)}, bf16[32,64,128]{2,1,0:T(8,128)(2,1)}, u32[]{:S(2)}, u32[]{:S(2)}) %collective-permute-start.9) | collective-permute-done | bytes 524320 | tf_op jit(solution)/shard_map/student_ring/ppermute | solution.py:307
  96.1 19.6 %head_terms.1 = (f32[512,1536]{1,0:T(8,128)}, f32[512,1536]{1,0:T(8,128)}) custom-call(s32[66]{0:T(128)} %pad_add_fusion.sc, f32[2048,1280]{1,0:T(8,128)} %get-tuple-element.38.pred_ref, bf16[1024,2048]{1,0:T(8,128)(2,1)} %get-tuple-element.39.xt_ref, bf16[32,64,128]{2,1,0:T(8,128)(2,1)} %collective-permute-done.9.fa, ...), custom_call_target="tpu_custom_call" | custom-call | flops 8053063680 | bytes 31457280 | tf_op jit(solution)/shard_map/head_terms/pallas_call | solution.py:177
  115.7 1.8 %collective-permute-start.12 = (bf16[64,768]{1,0:T(8,128)(2,1)S(1)}, bf16[64,768]{1,0:T(8,128)(2,1)S(1)}, u32[]{:S(2)}, u32[]{:S(2)}) collective-permute-start(bf16[64,768]{1,0:T(8,128)(2,1)S(1)} %pad_maximum_fusion.2), channel_id=1, source_target_pairs={{0,8},{4,12},{8,0},{12,4},{16,24},{20,28},{24,16},{28,20},{32,40},... | collective-permute-start | bytes 294920 | tf_op jit(solution)/shard_map/ppermute | solution.py:316
  117.6 3.4 %collective-permute-done.12 = bf16[64,768]{1,0:T(8,128)(2,1)S(1)} collective-permute-done((bf16[64,768]{1,0:T(8,128)(2,1)S(1)}, bf16[64,768]{1,0:T(8,128)(2,1)S(1)}, u32[]{:S(2)}, u32[]{:S(2)}) %collective-permute-start.12) | collective-permute-done | bytes 98336 | tf_op jit(solution)/shard_map/ppermute | solution.py:316
  121.7 4.2 %add_and_code.1 = s16[512,1408]{1,0:T(8,128)(2,1)} custom-call(f32[512,1536]{1,0:T(8,128)} %get-tuple-element.42.a, f32[512,1536]{1,0:T(8,128)} %collective-permute-done.11.b), custom_call_target="tpu_custom_call" | custom-call | tf_op jit(solution)/shard_map/add_and_code/pallas_call | solution.py:245
  125.9 7.1 %all-to-all-start.1 = ((s16[32,16,1408]{2,1,0:T(8,128)(2,1)}), s16[32,16,1408]{2,1,0:T(8,128)(2,1)S(1)}, u32[]{:S(2)}, u32[]{:S(2)}) async-start(s16[32,16,1408]{2,1,0:T(8,128)(2,1)} %bitcast.28), calls=%async_computation.1 | async-start | bytes 2883584 | tf_op jit(solution)/shard_map/grad_xz/all_to_all | solution.py:417
  135.4 1.8 %collective-permute-start.15 = (bf16[128,768]{1,0:T(8,128)(2,1)S(1)}, bf16[128,768]{1,0:T(8,128)(2,1)S(1)}, u32[]{:S(2)}, u32[]{:S(2)}) collective-permute-start(bf16[128,768]{1,0:T(8,128)(2,1)S(1)} %pad_maximum_fusion), channel_id=1, source_target_pairs={{0,64},{4,68},{8,72},{12,76},{16,80},{20,84},{24,88},{28,92},{32,9... | collective-permute-start | bytes 589832 | tf_op jit(solution)/shard_map/ppermute | solution.py:316
  137.4 13.4 %collective-permute-done.13 = bf16[128,768]{1,0:T(8,128)(2,1)S(1)} collective-permute-done((bf16[128,768]{1,0:T(8,128)(2,1)S(1)}, bf16[128,768]{1,0:T(8,128)(2,1)S(1)}, u32[]{:S(2)}, u32[]{:S(2)}) %collective-permute-start.13) | collective-permute-done | bytes 196640 | tf_op jit(solution)/shard_map/ppermute | solution.py:316
  153.6 13.9 %all-to-all-done.1.src = s16[32,16,1408]{2,1,0:T(8,128)(2,1)S(1)} async-done(((s16[32,16,1408]{2,1,0:T(8,128)(2,1)}), s16[32,16,1408]{2,1,0:T(8,128)(2,1)S(1)}, u32[]{:S(2)}, u32[]{:S(2)}) %all-to-all-start.1) | async-done | bytes 1441824 | tf_op jit(solution)/shard_map/grad_xz/all_to_all | solution.py:417
  168.5 2.4 %sum_last.1 = (f32[16,1280]{1,0:T(8,128)}, f32[8,128]{1,0:T(8,128)}) custom-call(s16[32,16,1408]{2,1,0:T(8,128)(2,1)} %copy-done, f32[8,128]{1,0:T(8,128)} %select_maximum_fusion.partial_ref), custom_call_target="tpu_custom_call" | custom-call | tf_op jit(solution)/shard_map/sum_last/pallas_call | solution.py:273
  170.9 2.3 %collective-permute-start.17 = (f32[8,128]{1,0:T(8,128)}, f32[8,128]{1,0:T(8,128)S(1)}, u32[]{:S(2)}, u32[]{:S(2)}) collective-permute-start(f32[8,128]{1,0:T(8,128)} %get-tuple-element.51), channel_id=1, source_target_pairs={{0,2},{1,3},{2,0},{3,1},{4,6},{5,7},{6,4},{7,5},{8,10},{9,11},{10,... | collective-permute-start | bytes 12296 | tf_op jit(solution)/shard_map/loss_parts/ppermute | solution.py:307
  174.9 2.2 %collective-permute-done.18 = f32[8,128]{1,0:T(8,128)S(1)} collective-permute-done((f32[8,128]{1,0:T(8,128)}, f32[8,128]{1,0:T(8,128)S(1)}, u32[]{:S(2)}, u32[]{:S(2)}) %collective-permute-start.18) | collective-permute-done | bytes 4128 | tf_op jit(solution)/shard_map/loss_parts/ppermute | solution.py:307
  (103 shorter events, 25.7 us)
Async XLA Ops:
  1.2 15.7 %copy-start.3 = (bf16[8,768]{1,0:T(8,128)(2,1)S(1)}, bf16[8,768]{1,0:T(8,128)(2,1)}, u32[]{:S(2)}) copy-start(bf16[8,768]{1,0:T(8,128)(2,1)} %param.13) | copy-start | bytes 36868
  4.5 12.5 %collective-permute-start = (bf16[8,768]{1,0:T(8,128)(2,1)S(1)}, bf16[8,768]{1,0:T(8,128)(2,1)S(1)}, u32[]{:S(2)}, u32[]{:S(2)}) collective-permute-start(bf16[8,768]{1,0:T(8,128)(2,1)S(1)} %copy-done.4), channel_id=1, source_target_pairs={{0,4},{4,0},{8,12},{12,8},{16,20},{20,16},{24,28},{28,24},{32,36},... | collective-permute-start | bytes 36872 | tf_op jit(solution)/shard_map/ppermute | solution.py:316
  4.5 44.5 %all-to-all-start = ((bf16[64,72,128]{2,1,0:T(8,128)(2,1)}), bf16[64,72,128]{2,1,0:T(8,128)(2,1)S(1)}, u32[]{:S(2)}, u32[]{:S(2)}) async-start(bf16[64,72,128]{2,1,0:T(8,128)(2,1)} %dispatch_rows.1), calls=%async_computation | async-start | bytes 2359296 | tf_op jit(solution)/shard_map/student_exchange/all_to_all | solution.py:334
  21.3 31.2 %copy-start.2 = (s32[2048]{0:T(1024)S(1)}, s32[2048]{0:T(1024)}, u32[]{:S(2)}) copy-start(s32[2048]{0:T(1024)} %holders.1) | copy-start | bytes 24580
  21.5 5.9 %collective-permute-start.1 = (f32[88,128]{1,0:T(8,128)S(1)}, f32[88,128]{1,0:T(8,128)S(1)}, u32[]{:S(2)}, u32[]{:S(2)}) collective-permute-start(f32[88,128]{1,0:T(8,128)S(1)} %constant_dynamic-update-slice_fusion), channel_id=1, source_target_pairs={{0,1},{1,2},{2,3},{3,0},{4,5},{5,6},{6,7},{7,4},{8,9},{9,10},{10,1... | collective-permute-start | bytes 135176 | tf_op jit(solution)/shard_map/teacher_sums/ppermute | solution.py:307
  23.1 5.6 %collective-permute-start.2 = (f32[88,128]{1,0:T(8,128)S(1)}, f32[88,128]{1,0:T(8,128)S(1)}, u32[]{:S(2)}, u32[]{:S(2)}) collective-permute-start(f32[88,128]{1,0:T(8,128)S(1)} %constant_dynamic-update-slice_fusion), channel_id=1, source_target_pairs={{0,2},{1,3},{2,0},{3,1},{4,6},{5,7},{6,4},{7,5},{8,10},{9,11},{10,... | collective-permute-start | bytes 135176 | tf_op jit(solution)/shard_map/teacher_sums/ppermute | solution.py:307
  26.0 4.0 %collective-permute-start.3 = (f32[88,128]{1,0:T(8,128)S(1)}, f32[88,128]{1,0:T(8,128)S(1)}, u32[]{:S(2)}, u32[]{:S(2)}) collective-permute-start(f32[88,128]{1,0:T(8,128)S(1)} %constant_dynamic-update-slice_fusion), channel_id=1, source_target_pairs={{0,3},{1,0},{2,1},{3,2},{4,7},{5,4},{6,5},{7,6},{8,11},{9,8},{10,9... | collective-permute-start | bytes 135176 | tf_op jit(solution)/shard_map/teacher_sums/ppermute | solution.py:307
  30.2 17.3 %collective-permute-start.4 = (bf16[16,768]{1,0:T(8,128)(2,1)S(1)}, bf16[16,768]{1,0:T(8,128)(2,1)S(1)}, u32[]{:S(2)}, u32[]{:S(2)}) collective-permute-start(bf16[16,768]{1,0:T(8,128)(2,1)S(1)} %pad_maximum_fusion.6), channel_id=1, source_target_pairs={{0,48},{4,52},{8,56},{12,60},{16,32},{20,36},{24,40},{28,44},{32,1... | collective-permute-start | bytes 73736 | tf_op jit(solution)/shard_map/ppermute | solution.py:316
  33.9 15.1 %collective-permute-start.5 = (bf16[16,768]{1,0:T(8,128)(2,1)S(1)}, bf16[16,768]{1,0:T(8,128)(2,1)S(1)}, u32[]{:S(2)}, u32[]{:S(2)}) collective-permute-start(bf16[16,768]{1,0:T(8,128)(2,1)S(1)} %pad_maximum_fusion.6), channel_id=1, source_target_pairs={{0,32},{4,36},{8,40},{12,44},{16,48},{20,52},{24,56},{28,60},{32,0... | collective-permute-start | bytes 73736 | tf_op jit(solution)/shard_map/ppermute | solution.py:316
  36.2 12.8 %collective-permute-start.6 = (bf16[16,768]{1,0:T(8,128)(2,1)S(1)}, bf16[16,768]{1,0:T(8,128)(2,1)S(1)}, u32[]{:S(2)}, u32[]{:S(2)}) collective-permute-start(bf16[16,768]{1,0:T(8,128)(2,1)S(1)} %pad_maximum_fusion.6), channel_id=1, source_target_pairs={{0,16},{4,20},{8,24},{12,28},{16,0},{20,4},{24,8},{28,12},{32,48},... | collective-permute-start | bytes 73736 | tf_op jit(solution)/shard_map/ppermute | solution.py:316
  49.2 34.8 %copy-start.1 = (bf16[64,64,128]{2,1,0:T(8,128)(2,1)}, bf16[64,64,128]{2,1,0:T(8,128)(2,1)S(1)}, u32[]{:S(2)}) copy-start(bf16[64,64,128]{2,1,0:T(8,128)(2,1)S(1)} %slice.89.x0) | copy-start | bytes 3145732
  49.2 26.0 %collective-permute-start.7 = (bf16[64,64,128]{2,1,0:T(8,128)(2,1)S(1)}, bf16[64,64,128]{2,1,0:T(8,128)(2,1)}, u32[]{:S(2)}, u32[]{:S(2)}) collective-permute-start(bf16[64,64,128]{2,1,0:T(8,128)(2,1)S(1)} %slice.89.x0), channel_id=1, source_target_pairs={{0,1},{1,2},{2,3},{3,0},{4,5},{5,6},{6,7},{7,4},{8,9},{9,10},{10,1... | collective-permute-start | bytes 3145736 | tf_op jit(solution)/shard_map/student_ring/ppermute | solution.py:307
  50.8 24.4 %collective-permute-start.8 = (bf16[64,64,128]{2,1,0:T(8,128)(2,1)S(1)}, bf16[64,64,128]{2,1,0:T(8,128)(2,1)}, u32[]{:S(2)}, u32[]{:S(2)}) collective-permute-start(bf16[64,64,128]{2,1,0:T(8,128)(2,1)S(1)} %slice.89.x0), channel_id=1, source_target_pairs={{0,3},{1,0},{2,1},{3,2},{4,7},{5,4},{6,5},{7,6},{8,11},{9,8},{10,9... | collective-permute-start | bytes 3145736 | tf_op jit(solution)/shard_map/student_ring/ppermute | solution.py:307
  77.6 16.5 %collective-permute-start.10 = (bf16[32,64,128]{2,1,0:T(8,128)(2,1)S(1)}, bf16[32,64,128]{2,1,0:T(8,128)(2,1)}, u32[]{:S(2)}, u32[]{:S(2)}) collective-permute-start(bf16[32,64,128]{2,1,0:T(8,128)(2,1)S(1)} %slice.92), channel_id=1, source_target_pairs={{0,3},{1,0},{2,1},{3,2},{4,7},{5,4},{6,5},{7,6},{8,11},{9,8},{10,9... | collective-permute-start | bytes 1572872 | tf_op jit(solution)/shard_map/student_ring/ppermute | solution.py:307
  82.6 13.5 %collective-permute-start.9 = (bf16[32,64,128]{2,1,0:T(8,128)(2,1)}, bf16[32,64,128]{2,1,0:T(8,128)(2,1)}, u32[]{:S(2)}, u32[]{:S(2)}) collective-permute-start(bf16[32,64,128]{2,1,0:T(8,128)(2,1)} %slice.91), channel_id=1, source_target_pairs={{0,1},{1,2},{2,3},{3,0},{4,5},{5,6},{6,7},{7,4},{8,9},{9,10},{10,1... | collective-permute-start | bytes 1572872 | tf_op jit(solution)/shard_map/student_ring/ppermute | solution.py:307
  115.7 6.0 %collective-permute-start.11 = (f32[512,1536]{1,0:T(8,128)}, f32[512,1536]{1,0:T(8,128)}, u32[]{:S(2)}, u32[]{:S(2)}) collective-permute-start(f32[512,1536]{1,0:T(8,128)} %get-tuple-element.43), channel_id=1, source_target_pairs={{0,4},{4,0},{8,12},{12,8},{16,20},{20,16},{24,28},{28,24},{32,36},... | collective-permute-start | bytes 9437192 | tf_op jit(solution)/shard_map/grad_core/ppermute | solution.py:316
  115.7 5.2 %collective-permute-start.12 = (bf16[64,768]{1,0:T(8,128)(2,1)S(1)}, bf16[64,768]{1,0:T(8,128)(2,1)S(1)}, u32[]{:S(2)}, u32[]{:S(2)}) collective-permute-start(bf16[64,768]{1,0:T(8,128)(2,1)S(1)} %pad_maximum_fusion.2), channel_id=1, source_target_pairs={{0,8},{4,12},{8,0},{12,4},{16,24},{20,28},{24,16},{28,20},{32,40},... | collective-permute-start | bytes 294920 | tf_op jit(solution)/shard_map/ppermute | solution.py:316
  125.9 41.5 %all-to-all-start.1 = ((s16[32,16,1408]{2,1,0:T(8,128)(2,1)}), s16[32,16,1408]{2,1,0:T(8,128)(2,1)S(1)}, u32[]{:S(2)}, u32[]{:S(2)}) async-start(s16[32,16,1408]{2,1,0:T(8,128)(2,1)} %bitcast.28), calls=%async_computation.1 | async-start | bytes 2883584 | tf_op jit(solution)/shard_map/grad_xz/all_to_all | solution.py:417
  133.0 17.8 %collective-permute-start.13 = (bf16[128,768]{1,0:T(8,128)(2,1)S(1)}, bf16[128,768]{1,0:T(8,128)(2,1)S(1)}, u32[]{:S(2)}, u32[]{:S(2)}) collective-permute-start(bf16[128,768]{1,0:T(8,128)(2,1)S(1)} %pad_maximum_fusion), channel_id=1, source_target_pairs={{0,192},{4,196},{8,200},{12,204},{16,208},{20,212},{24,216},{28,22... | collective-permute-start | bytes 589832 | tf_op jit(solution)/shard_map/ppermute | solution.py:316
  134.6 16.3 %collective-permute-start.14 = (bf16[128,768]{1,0:T(8,128)(2,1)S(1)}, bf16[128,768]{1,0:T(8,128)(2,1)S(1)}, u32[]{:S(2)}, u32[]{:S(2)}) collective-permute-start(bf16[128,768]{1,0:T(8,128)(2,1)S(1)} %pad_maximum_fusion), channel_id=1, source_target_pairs={{0,128},{4,132},{8,136},{12,140},{16,144},{20,148},{24,152},{28,15... | collective-permute-start | bytes 589832 | tf_op jit(solution)/shard_map/ppermute | solution.py:316
  135.4 16.8 %collective-permute-start.15 = (bf16[128,768]{1,0:T(8,128)(2,1)S(1)}, bf16[128,768]{1,0:T(8,128)(2,1)S(1)}, u32[]{:S(2)}, u32[]{:S(2)}) collective-permute-start(bf16[128,768]{1,0:T(8,128)(2,1)S(1)} %pad_maximum_fusion), channel_id=1, source_target_pairs={{0,64},{4,68},{8,72},{12,76},{16,80},{20,84},{24,88},{28,92},{32,9... | collective-permute-start | bytes 589832 | tf_op jit(solution)/shard_map/ppermute | solution.py:316
  170.9 6.3 %collective-permute-start.16 = (f32[8,128]{1,0:T(8,128)}, f32[8,128]{1,0:T(8,128)S(1)}, u32[]{:S(2)}, u32[]{:S(2)}) collective-permute-start(f32[8,128]{1,0:T(8,128)} %get-tuple-element.51), channel_id=1, source_target_pairs={{0,1},{1,2},{2,3},{3,0},{4,5},{5,6},{6,7},{7,4},{8,9},{9,10},{10,1... | collective-permute-start | bytes 12296 | tf_op jit(solution)/shard_map/loss_parts/ppermute | solution.py:307
  170.9 6.2 %collective-permute-start.17 = (f32[8,128]{1,0:T(8,128)}, f32[8,128]{1,0:T(8,128)S(1)}, u32[]{:S(2)}, u32[]{:S(2)}) collective-permute-start(f32[8,128]{1,0:T(8,128)} %get-tuple-element.51), channel_id=1, source_target_pairs={{0,2},{1,3},{2,0},{3,1},{4,6},{5,7},{6,4},{7,5},{8,10},{9,11},{10,... | collective-permute-start | bytes 12296 | tf_op jit(solution)/shard_map/loss_parts/ppermute | solution.py:307
  173.3 3.8 %collective-permute-start.18 = (f32[8,128]{1,0:T(8,128)}, f32[8,128]{1,0:T(8,128)S(1)}, u32[]{:S(2)}, u32[]{:S(2)}) collective-permute-start(f32[8,128]{1,0:T(8,128)} %get-tuple-element.51), channel_id=1, source_target_pairs={{0,3},{1,0},{2,1},{3,2},{4,7},{5,4},{6,5},{7,6},{8,11},{9,8},{10,9... | collective-permute-start | bytes 12296 | tf_op jit(solution)/shard_map/loss_parts/ppermute | solution.py:307
  (3 other events, 20.4 us)

commit v11 on v10

--- a/solution.py
+++ b/solution.py
@@ -53,7 +53,8 @@
 
 
 def near_terms(cache_pos, near, head_weight):
-    n_img, split_rows, lanes = near[0].shape
+    half_img, split_rows, lanes = near[0][0].shape
+    n_img = 2 * half_img
     width, cols = head_weight.shape
     block, patch = 512, 32
     splits = split_rows // patch
@@ -62,14 +63,16 @@
     rows = n_img * patch
     img_block = block // patch
 
-    def kernel(sc, x0, x1, x2, w_ref, pred_out, xt_out):
+    half = rows // block // 2
+
+    def kernel(sc, x0a, x0b, x1a, x1b, x2a, x2b, w_ref, pred_out, xt_out):
         xt_out[...] = jnp.zeros_like(xt_out)
+        lower = pl.program_id(0) < half
         pred = jnp.zeros((block, cols), jnp.float32)
-        for ref, off in ((x0, 0), (x1, n_part - 1), (x2, 1)):
+        for a, b, off in ((x0a, x0b, 0), (x1a, x1b, n_part - 1), (x2a, x2b, 1)):
             first = lax.rem(sc[0] + off, n_part) * part
-            pieces = [
-                ref[:, k * patch : (k + 1) * patch, :].reshape(block, lanes) for k in range(splits)
-            ]
+            x = jnp.where(lower, a[...], b[...])
+            pieces = [x[:, k * patch : (k + 1) * patch, :].reshape(block, lanes) for k in range(splits)]
             for k, piece in enumerate(pieces):
                 xt_out[pl.ds(pl.multiple_of(first + k * lanes, lanes), lanes), :] = piece.T
             pred = pred + jnp.dot(
@@ -79,13 +82,16 @@
             )
         pred_out[...] = pred
 
-    img_spec = pl.BlockSpec((img_block, split_rows, lanes), lambda i, s: (i, 0, 0))
+    img_spec = lambda f: pl.BlockSpec(
+        (img_block, split_rows, lanes), lambda i, s: (jnp.clip(f(i), 0, half - 1), 0, 0)
+    )
+    halves = [img_spec(lambda i: i), img_spec(lambda i: i - half)]
     return pl.pallas_call(
         kernel,
         grid_spec=pltpu.PrefetchScalarGridSpec(
             num_scalar_prefetch=1,
             grid=(rows // block,),
-            in_specs=[img_spec] * 3 + [pl.BlockSpec((width, cols), lambda i, s: (0, 0))],
+            in_specs=halves * 3 + [pl.BlockSpec((width, cols), lambda i, s: (0, 0))],
             out_specs=[
                 pl.BlockSpec((block, cols), lambda i, s: (i, 0)),
                 pl.BlockSpec((width, block), lambda i, s: (0, i)),
@@ -93,14 +99,14 @@
         ),
         out_shape=[
             jax.ShapeDtypeStruct((rows, cols), jnp.float32),
-            jax.ShapeDtypeStruct((width, rows), near[0].dtype),
+            jax.ShapeDtypeStruct((width, rows), near[0][0].dtype),
         ],
         compiler_params=params(),
         cost_estimate=pl.CostEstimate(
             flops=2 * rows * 3 * part * cols, bytes_accessed=20 * 2**20, transcendentals=0
         ),
         name="near_terms",
-    )(cache_pos[None].astype(jnp.int32), *near, head_weight)
+    )(cache_pos[None].astype(jnp.int32), *[x for pair in near for x in pair], head_weight)
 
 
 def head_terms(scalars, near_pred, near_cols, far_a, far_b, head_weight, teacher, row_info, full_cols):
@@ -353,15 +359,16 @@
     texts = spread(texts, 4, 2)
     mine, sums, images, texts = lax.optimization_barrier((mine, sums, images, texts))
     with jax.named_scope("student_ring"):
-        counts_sent, mine = mine[:, -COUNT_ROWS:], mine[:, :-COUNT_ROWS]
-        from_prev = ring(mine, 1)
-        from_next = ring(mine, -1)
+        counts_sent = mine[:, -COUNT_ROWS:]
+        own = [mine[: n_dp // 2, :-COUNT_ROWS], mine[n_dp // 2 :, :-COUNT_ROWS]]
+        from_prev = [ring(x, 1) for x in own]
+        from_next = [ring(x, -1) for x in own]
         from_prev, from_next, sums, counts_sent = lax.optimization_barrier(
             (from_prev, from_next, sums, counts_sent)
         )
-        far_a = ring(from_prev[: n_dp // 2], 1)
-        far_b = ring(from_next[n_dp // 2 :], -1)
-    near_pred, near_cols = near_terms(cache_pos, [mine, from_prev, from_next], head_weight)
+        far_a = ring(from_prev[0], 1)
+        far_b = ring(from_next[1], -1)
+    near_pred, near_cols = near_terms(cache_pos, [own, from_prev, from_next], head_weight)
     with jax.named_scope("teacher_sums"):
         row_mean = sums[0] / full_cols
         inv_scale = lax.rsqrt(sums[1] / full_cols - row_mean * row_mean + eps)

time: 182 us -> 180 us (0.989)
  starting transfers between devices: 47.3 us -> 50.5 us
  local copies, waits for them, and re-layouts: 7.79 us -> 4.85 us
    ppermute x10 -> x12, starting transfers between devices: 15.6 us -> 19 us  [ring(): lax.ppermute(x, 'cache', [(i, (i + step) % n_cache) for i in range(n_cach...]
    slice x4 -> x2, local copies, waits for them, and re-layouts: 3.12 us -> 0.14 us  [the longest x1 0.13 us: local(): own = [mine[:n_dp // 2, :-COUNT_ROWS], mine[n_dp // 2:, :-COUNT_ROWS]]]
    ppermute x10 -> x12, waiting for transfers between devices: 28.7 us -> 27.2 us  [ring(): lax.ppermute(x, 'cache', [(i, (i + step) % n_cache) for i in range(n_cach...]
  transfers between devices with their start and end apart: 21 -> 23, of which waited for: 12 -> 12; matrix products, arithmetic and copies ran while one was open for 6% -> 5% of each run, Pallas kernels for 6% -> 6%
where the time goes in v11:
time: 180 us; the launch traced here: 177 us
  waiting for transfers between devices  72.2 us (40%)
  starting transfers between devices  50.5 us (28%)
  Pallas kernels  39.7 us (22%)
  other arithmetic  8.85 us (5%)
  local copies, waits for them, and re-layouts  4.85 us (3%)
    ppermute x9, waiting for transfers between devices, swap(): return lax.ppermute(x, 'dp', [(i, i ^ bit) for i in range(n_dp)])  31.1 us
    ppermute x12, waiting for transfers between devices, ring(): lax.ppermute(x, 'cache', [(i, (i + step) % n_cache) for i in range(n_cach...  27.2 us
    pallas_call x1, Pallas kernels, head_terms(): pl.pallas_call(kernel, grid_spec=pltpu.PrefetchScalarGridSpec(num_scalar_...  19.6 us
    ppermute x12, starting transfers between devices, ring(): lax.ppermute(x, 'cache', [(i, (i + step) % n_cache) for i in range(n_cach...  19 us
    all_to_all x1, waiting for transfers between devices, local(): lax.all_to_all(codes.reshape(N_X * N_Z, -1, local_cols + EXT), 'dp', 0, 0...  13.8 us
    ppermute x9, starting transfers between devices, swap(): return lax.ppermute(x, 'dp', [(i, i ^ bit) for i in range(n_dp)])  12.6 us
    all_to_all x1, starting transfers between devices, local(): lax.all_to_all(outgoing, 'dp', split_axis=0, concat_axis=0, tiled=True)  12.2 us
    pallas_call x1, Pallas kernels, near_terms(): pl.pallas_call(kernel, grid_spec=pltpu.PrefetchScalarGridSpec(num_scalar_...  10.3 us
  transfers between devices with their start and end apart: 23, of which 12 were waited for; matrix products, arithmetic and copies ran while one was open for 5% of the time, Pallas kernels for 6%

profile of v11, /device:TPU:2, one launch (start us, length us, event | category | flops | bytes accessed | tf_op | source)
XLA Modules:
  0.0 177.5 jit_solution(12654180249089834443)
XLA Ops:
  1.2 3.3 %dispatch_rows.1 = bf16[64,72,128]{2,1,0:T(8,128)(2,1)} custom-call(s32[2]{0:T(128)} %pad_add_fusion.1.place, s32[2048]{0:T(1024)} %holders.1, s32[32]{0:T(128)} %counts.1, bf16[32,32,1024]{2,1,0:T(8,128)(2,1)} %feats.1), custom_call_target="tpu_custom_call" | custom-call | tf_op jit(solution)/shard_map/dispatch_rows/pallas_call | solution.py:41
  4.5 12.2 %all-to-all-start = ((bf16[64,72,128]{2,1,0:T(8,128)(2,1)}), bf16[64,72,128]{2,1,0:T(8,128)(2,1)S(1)}, u32[]{:S(2)}, u32[]{:S(2)}) async-start(bf16[64,72,128]{2,1,0:T(8,128)(2,1)} %dispatch_rows.1), calls=%async_computation | async-start | bytes 2359296 | tf_op jit(solution)/shard_map/student_exchange/all_to_all | solution.py:340
  17.1 4.3 %convert_reduce_fusion = (f32[64,32]{1,0:T(8,128)S(1)}, f32[64,32]{1,0:T(8,128)S(1)}) fusion(bf16[64,32,1280]{2,1,0:T(8,128)(2,1)} %param.10), kind=kLoop, calls=%fused_computation.1 | loop fusion | flops 10481664 | bytes 5259264 | tf_op jit(solution)/shard_map/teacher_sums/reduce_sum | solution.py:343
  23.2 2.9 %collective-permute-start.2 = (f32[88,128]{1,0:T(8,128)S(1)}, f32[88,128]{1,0:T(8,128)S(1)}, u32[]{:S(2)}, u32[]{:S(2)}) collective-permute-start(f32[88,128]{1,0:T(8,128)S(1)} %constant_dynamic-update-slice_fusion), channel_id=1, source_target_pairs={{0,2},{1,3},{2,0},{3,1},{4,6},{5,7},{6,4},{7,5},{8,10},{9,11},{10,... | collective-permute-start | bytes 135176 | tf_op jit(solution)/shard_map/teacher_sums/ppermute | solution.py:313
  30.2 3.7 %collective-permute-start.4 = (bf16[16,768]{1,0:T(8,128)(2,1)S(1)}, bf16[16,768]{1,0:T(8,128)(2,1)S(1)}, u32[]{:S(2)}, u32[]{:S(2)}) collective-permute-start(bf16[16,768]{1,0:T(8,128)(2,1)S(1)} %pad_maximum_fusion.6), channel_id=1, source_target_pairs={{0,48},{4,52},{8,56},{12,60},{16,32},{20,36},{24,40},{28,44},{32,1... | collective-permute-start | bytes 73736 | tf_op jit(solution)/shard_map/ppermute | solution.py:322
  33.9 2.3 %collective-permute-start.5 = (bf16[16,768]{1,0:T(8,128)(2,1)S(1)}, bf16[16,768]{1,0:T(8,128)(2,1)S(1)}, u32[]{:S(2)}, u32[]{:S(2)}) collective-permute-start(bf16[16,768]{1,0:T(8,128)(2,1)S(1)} %pad_maximum_fusion.6), channel_id=1, source_target_pairs={{0,32},{4,36},{8,40},{12,44},{16,48},{20,52},{24,56},{28,60},{32,0... | collective-permute-start | bytes 73736 | tf_op jit(solution)/shard_map/ppermute | solution.py:322
  36.8 10.8 %collective-permute-done.4 = bf16[16,768]{1,0:T(8,128)(2,1)S(1)} collective-permute-done((bf16[16,768]{1,0:T(8,128)(2,1)S(1)}, bf16[16,768]{1,0:T(8,128)(2,1)S(1)}, u32[]{:S(2)}, u32[]{:S(2)}) %collective-permute-start.4) | collective-permute-done | bytes 24608 | tf_op jit(solution)/shard_map/ppermute | solution.py:322
  49.2 3.1 %collective-permute-start.10 = (bf16[32,64,128]{2,1,0:T(8,128)(2,1)S(1)}, bf16[32,64,128]{2,1,0:T(8,128)(2,1)S(1)}, u32[]{:S(2)}, u32[]{:S(2)}) collective-permute-start(bf16[32,64,128]{2,1,0:T(8,128)(2,1)S(1)} %get-tuple-element.68.x0b), channel_id=1, source_target_pairs={{0,3},{1,0},{2,1},{3,2},{4,7},{5,4},{6,5},{7,6},{8,11},{9,8},{10,9... | collective-permute-start | bytes 1572872 | tf_op jit(solution)/shard_map/student_ring/ppermute | solution.py:313
  52.9 2.7 %collective-permute-start.9 = (bf16[32,64,128]{2,1,0:T(8,128)(2,1)S(1)}, bf16[32,64,128]{2,1,0:T(8,128)(2,1)}, u32[]{:S(2)}, u32[]{:S(2)}) collective-permute-start(bf16[32,64,128]{2,1,0:T(8,128)(2,1)S(1)} %get-tuple-element.69.x0a), channel_id=1, source_target_pairs={{0,3},{1,0},{2,1},{3,2},{4,7},{5,4},{6,5},{7,6},{8,11},{9,8},{10,9... | collective-permute-start | bytes 1572872 | tf_op jit(solution)/shard_map/student_ring/ppermute | solution.py:313
  56.5 8.2 %collective-permute-done.10.x2b = bf16[32,64,128]{2,1,0:T(8,128)(2,1)S(1)} collective-permute-done((bf16[32,64,128]{2,1,0:T(8,128)(2,1)S(1)}, bf16[32,64,128]{2,1,0:T(8,128)(2,1)S(1)}, u32[]{:S(2)}, u32[]{:S(2)}) %collective-permute-start.10) | collective-permute-done | bytes 524320 | tf_op jit(solution)/shard_map/student_ring/ppermute | solution.py:313
  64.7 13.2 %collective-permute-done.7.x1a = bf16[32,64,128]{2,1,0:T(8,128)(2,1)} collective-permute-done((bf16[32,64,128]{2,1,0:T(8,128)(2,1)S(1)}, bf16[32,64,128]{2,1,0:T(8,128)(2,1)}, u32[]{:S(2)}, u32[]{:S(2)}) %collective-permute-start.7) | collective-permute-done | bytes 524320 | tf_op jit(solution)/shard_map/student_ring/ppermute | solution.py:313
  79.5 3.2 %collective-permute-start.12 = (bf16[32,64,128]{2,1,0:T(8,128)(2,1)S(1)}, bf16[32,64,128]{2,1,0:T(8,128)(2,1)}, u32[]{:S(2)}, u32[]{:S(2)}) collective-permute-start(bf16[32,64,128]{2,1,0:T(8,128)(2,1)S(1)} %collective-permute-done.10.x2b), channel_id=1, source_target_pairs={{0,3},{1,0},{2,1},{3,2},{4,7},{5,4},{6,5},{7,6},{8,11},{9,8},{10,9... | collective-permute-start | bytes 1572872 | tf_op jit(solution)/shard_map/student_ring/ppermute | solution.py:313
  84.1 10.3 %near_terms.1 = (f32[2048,1280]{1,0:T(8,128)}, bf16[1024,2048]{1,0:T(8,128)(2,1)}) custom-call(s32[1]{0:T(128)} %bitcast.sc, bf16[32,64,128]{2,1,0:T(8,128)(2,1)} %copy-done.2, bf16[32,64,128]{2,1,0:T(8,128)(2,1)} %copy-done.1, bf16[32,64,128]{2,1,0:T(8,128)(2,1)} %collective-permute-done.7.x1a, bf16[32,64,128]{2,1,0:T(8,128)(2,1)} %collective-permute-done.8.x1b, ...), custom_call_target="tpu_custom_call" | custom-call | flops 4026531840 | bytes 20971520 | tf_op jit(solution)/shard_map/near_terms/pallas_call | solution.py:89
  94.4 19.6 %head_terms.1 = (f32[512,1536]{1,0:T(8,128)}, f32[512,1536]{1,0:T(8,128)}) custom-call(s32[66]{0:T(128)} %pad_add_fusion.sc, f32[2048,1280]{1,0:T(8,128)} %get-tuple-element.42.pred_ref, bf16[1024,2048]{1,0:T(8,128)(2,1)} %get-tuple-element.43.xt_ref, bf16[32,64,128]{2,1,0:T(8,128)(2,1)} %collective-permute-done.11.fa, ...), custom_call_target="tpu_custom_call" | custom-call | flops 8053063680 | bytes 31457280 | tf_op jit(solution)/shard_map/head_terms/pallas_call | solution.py:183
  114.0 1.9 %collective-permute-start.14 = (bf16[64,768]{1,0:T(8,128)(2,1)S(1)}, bf16[64,768]{1,0:T(8,128)(2,1)S(1)}, u32[]{:S(2)}, u32[]{:S(2)}) collective-permute-start(bf16[64,768]{1,0:T(8,128)(2,1)S(1)} %pad_maximum_fusion.2), channel_id=1, source_target_pairs={{0,8},{4,12},{8,0},{12,4},{16,24},{20,28},{24,16},{28,20},{32,40},... | collective-permute-start | bytes 294920 | tf_op jit(solution)/shard_map/ppermute | solution.py:322
  115.9 3.4 %collective-permute-done.14 = bf16[64,768]{1,0:T(8,128)(2,1)S(1)} collective-permute-done((bf16[64,768]{1,0:T(8,128)(2,1)S(1)}, bf16[64,768]{1,0:T(8,128)(2,1)S(1)}, u32[]{:S(2)}, u32[]{:S(2)}) %collective-permute-start.14) | collective-permute-done | bytes 98336 | tf_op jit(solution)/shard_map/ppermute | solution.py:322
  120.0 4.2 %add_and_code.1 = s16[512,1408]{1,0:T(8,128)(2,1)} custom-call(f32[512,1536]{1,0:T(8,128)} %get-tuple-element.46.a, f32[512,1536]{1,0:T(8,128)} %collective-permute-done.13.b), custom_call_target="tpu_custom_call" | custom-call | tf_op jit(solution)/shard_map/add_and_code/pallas_call | solution.py:251
  124.2 6.7 %all-to-all-start.1 = ((s16[32,16,1408]{2,1,0:T(8,128)(2,1)}), s16[32,16,1408]{2,1,0:T(8,128)(2,1)S(1)}, u32[]{:S(2)}, u32[]{:S(2)}) async-start(s16[32,16,1408]{2,1,0:T(8,128)(2,1)} %bitcast.28), calls=%async_computation.1 | async-start | bytes 2883584 | tf_op jit(solution)/shard_map/grad_xz/all_to_all | solution.py:424
  133.3 1.8 %collective-permute-start.17 = (bf16[128,768]{1,0:T(8,128)(2,1)S(1)}, bf16[128,768]{1,0:T(8,128)(2,1)S(1)}, u32[]{:S(2)}, u32[]{:S(2)}) collective-permute-start(bf16[128,768]{1,0:T(8,128)(2,1)S(1)} %pad_maximum_fusion), channel_id=1, source_target_pairs={{0,64},{4,68},{8,72},{12,76},{16,80},{20,84},{24,88},{28,92},{32,9... | collective-permute-start | bytes 589832 | tf_op jit(solution)/shard_map/ppermute | solution.py:322
  135.3 13.4 %collective-permute-done.15 = bf16[128,768]{1,0:T(8,128)(2,1)S(1)} collective-permute-done((bf16[128,768]{1,0:T(8,128)(2,1)S(1)}, bf16[128,768]{1,0:T(8,128)(2,1)S(1)}, u32[]{:S(2)}, u32[]{:S(2)}) %collective-permute-start.15) | collective-permute-done | bytes 196640 | tf_op jit(solution)/shard_map/ppermute | solution.py:322
  151.5 13.8 %all-to-all-done.1.src = s16[32,16,1408]{2,1,0:T(8,128)(2,1)S(1)} async-done(((s16[32,16,1408]{2,1,0:T(8,128)(2,1)}), s16[32,16,1408]{2,1,0:T(8,128)(2,1)S(1)}, u32[]{:S(2)}, u32[]{:S(2)}) %all-to-all-start.1) | async-done | bytes 1441824 | tf_op jit(solution)/shard_map/grad_xz/all_to_all | solution.py:424
  166.5 2.4 %sum_last.1 = (f32[16,1280]{1,0:T(8,128)}, f32[8,128]{1,0:T(8,128)}) custom-call(s16[32,16,1408]{2,1,0:T(8,128)(2,1)} %copy-done, f32[8,128]{1,0:T(8,128)} %select_maximum_fusion.partial_ref), custom_call_target="tpu_custom_call" | custom-call | tf_op jit(solution)/shard_map/sum_last/pallas_call | solution.py:279
  168.9 3.3 %collective-permute-start.19 = (f32[8,128]{1,0:T(8,128)}, f32[8,128]{1,0:T(8,128)S(1)}, u32[]{:S(2)}, u32[]{:S(2)}) collective-permute-start(f32[8,128]{1,0:T(8,128)} %get-tuple-element.55), channel_id=1, source_target_pairs={{0,2},{1,3},{2,0},{3,1},{4,6},{5,7},{6,4},{7,5},{8,10},{9,11},{10,... | collective-permute-start | bytes 12296 | tf_op jit(solution)/shard_map/loss_parts/ppermute | solution.py:313
  172.9 3.1 %collective-permute-done.20 = f32[8,128]{1,0:T(8,128)S(1)} collective-permute-done((f32[8,128]{1,0:T(8,128)}, f32[8,128]{1,0:T(8,128)S(1)}, u32[]{:S(2)}, u32[]{:S(2)}) %collective-permute-start.20) | collective-permute-done | bytes 4128 | tf_op jit(solution)/shard_map/loss_parts/ppermute | solution.py:313
  (109 shorter events, 22.9 us)
Async XLA Ops:
  4.5 12.6 %collective-permute-start = (bf16[8,768]{1,0:T(8,128)(2,1)S(1)}, bf16[8,768]{1,0:T(8,128)(2,1)S(1)}, u32[]{:S(2)}, u32[]{:S(2)}) collective-permute-start(bf16[8,768]{1,0:T(8,128)(2,1)S(1)} %copy-done.5), channel_id=1, source_target_pairs={{0,4},{4,0},{8,12},{12,8},{16,20},{20,16},{24,28},{28,24},{32,36},... | collective-permute-start | bytes 36872 | tf_op jit(solution)/shard_map/ppermute | solution.py:322
  4.5 44.6 %all-to-all-start = ((bf16[64,72,128]{2,1,0:T(8,128)(2,1)}), bf16[64,72,128]{2,1,0:T(8,128)(2,1)S(1)}, u32[]{:S(2)}, u32[]{:S(2)}) async-start(bf16[64,72,128]{2,1,0:T(8,128)(2,1)} %dispatch_rows.1), calls=%async_computation | async-start | bytes 2359296 | tf_op jit(solution)/shard_map/student_exchange/all_to_all | solution.py:340
  21.5 5.9 %collective-permute-start.1 = (f32[88,128]{1,0:T(8,128)S(1)}, f32[88,128]{1,0:T(8,128)S(1)}, u32[]{:S(2)}, u32[]{:S(2)}) collective-permute-start(f32[88,128]{1,0:T(8,128)S(1)} %constant_dynamic-update-slice_fusion), channel_id=1, source_target_pairs={{0,1},{1,2},{2,3},{3,0},{4,5},{5,6},{6,7},{7,4},{8,9},{9,10},{10,1... | collective-permute-start | bytes 135176 | tf_op jit(solution)/shard_map/teacher_sums/ppermute | solution.py:313
  23.2 5.6 %collective-permute-start.2 = (f32[88,128]{1,0:T(8,128)S(1)}, f32[88,128]{1,0:T(8,128)S(1)}, u32[]{:S(2)}, u32[]{:S(2)}) collective-permute-start(f32[88,128]{1,0:T(8,128)S(1)} %constant_dynamic-update-slice_fusion), channel_id=1, source_target_pairs={{0,2},{1,3},{2,0},{3,1},{4,6},{5,7},{6,4},{7,5},{8,10},{9,11},{10,... | collective-permute-start | bytes 135176 | tf_op jit(solution)/shard_map/teacher_sums/ppermute | solution.py:313
  26.1 4.0 %collective-permute-start.3 = (f32[88,128]{1,0:T(8,128)S(1)}, f32[88,128]{1,0:T(8,128)S(1)}, u32[]{:S(2)}, u32[]{:S(2)}) collective-permute-start(f32[88,128]{1,0:T(8,128)S(1)} %constant_dynamic-update-slice_fusion), channel_id=1, source_target_pairs={{0,3},{1,0},{2,1},{3,2},{4,7},{5,4},{6,5},{7,6},{8,11},{9,8},{10,9... | collective-permute-start | bytes 135176 | tf_op jit(solution)/shard_map/teacher_sums/ppermute | solution.py:313
  30.2 17.3 %collective-permute-start.4 = (bf16[16,768]{1,0:T(8,128)(2,1)S(1)}, bf16[16,768]{1,0:T(8,128)(2,1)S(1)}, u32[]{:S(2)}, u32[]{:S(2)}) collective-permute-start(bf16[16,768]{1,0:T(8,128)(2,1)S(1)} %pad_maximum_fusion.6), channel_id=1, source_target_pairs={{0,48},{4,52},{8,56},{12,60},{16,32},{20,36},{24,40},{28,44},{32,1... | collective-permute-start | bytes 73736 | tf_op jit(solution)/shard_map/ppermute | solution.py:322
  33.9 15.1 %collective-permute-start.5 = (bf16[16,768]{1,0:T(8,128)(2,1)S(1)}, bf16[16,768]{1,0:T(8,128)(2,1)S(1)}, u32[]{:S(2)}, u32[]{:S(2)}) collective-permute-start(bf16[16,768]{1,0:T(8,128)(2,1)S(1)} %pad_maximum_fusion.6), channel_id=1, source_target_pairs={{0,32},{4,36},{8,40},{12,44},{16,48},{20,52},{24,56},{28,60},{32,0... | collective-permute-start | bytes 73736 | tf_op jit(solution)/shard_map/ppermute | solution.py:322
  36.2 12.8 %collective-permute-start.6 = (bf16[16,768]{1,0:T(8,128)(2,1)S(1)}, bf16[16,768]{1,0:T(8,128)(2,1)S(1)}, u32[]{:S(2)}, u32[]{:S(2)}) collective-permute-start(bf16[16,768]{1,0:T(8,128)(2,1)S(1)} %pad_maximum_fusion.6), channel_id=1, source_target_pairs={{0,16},{4,20},{8,24},{12,28},{16,0},{20,4},{24,8},{28,12},{32,48},... | collective-permute-start | bytes 73736 | tf_op jit(solution)/shard_map/ppermute | solution.py:322
  49.2 34.9 %copy-start.1 = (bf16[32,64,128]{2,1,0:T(8,128)(2,1)}, bf16[32,64,128]{2,1,0:T(8,128)(2,1)S(1)}, u32[]{:S(2)}) copy-start(bf16[32,64,128]{2,1,0:T(8,128)(2,1)S(1)} %get-tuple-element.68.x0b) | copy-start | bytes 1572868
  49.2 15.5 %collective-permute-start.10 = (bf16[32,64,128]{2,1,0:T(8,128)(2,1)S(1)}, bf16[32,64,128]{2,1,0:T(8,128)(2,1)S(1)}, u32[]{:S(2)}, u32[]{:S(2)}) collective-permute-start(bf16[32,64,128]{2,1,0:T(8,128)(2,1)S(1)} %get-tuple-element.68.x0b), channel_id=1, source_target_pairs={{0,3},{1,0},{2,1},{3,2},{4,7},{5,4},{6,5},{7,6},{8,11},{9,8},{10,9... | collective-permute-start | bytes 1572872 | tf_op jit(solution)/shard_map/student_ring/ppermute | solution.py:313
  52.3 25.6 %collective-permute-start.8 = (bf16[32,64,128]{2,1,0:T(8,128)(2,1)S(1)}, bf16[32,64,128]{2,1,0:T(8,128)(2,1)}, u32[]{:S(2)}, u32[]{:S(2)}) collective-permute-start(bf16[32,64,128]{2,1,0:T(8,128)(2,1)S(1)} %get-tuple-element.68.x0b), channel_id=1, source_target_pairs={{0,1},{1,2},{2,3},{3,0},{4,5},{5,6},{6,7},{7,4},{8,9},{9,10},{10,1... | collective-permute-start | bytes 1572872 | tf_op jit(solution)/shard_map/student_ring/ppermute | solution.py:313
  52.3 25.6 %collective-permute-start.7 = (bf16[32,64,128]{2,1,0:T(8,128)(2,1)S(1)}, bf16[32,64,128]{2,1,0:T(8,128)(2,1)}, u32[]{:S(2)}, u32[]{:S(2)}) collective-permute-start(bf16[32,64,128]{2,1,0:T(8,128)(2,1)S(1)} %get-tuple-element.69.x0a), channel_id=1, source_target_pairs={{0,1},{1,2},{2,3},{3,0},{4,5},{5,6},{6,7},{7,4},{8,9},{9,10},{10,1... | collective-permute-start | bytes 1572872 | tf_op jit(solution)/shard_map/student_ring/ppermute | solution.py:313
  52.9 25.0 %collective-permute-start.9 = (bf16[32,64,128]{2,1,0:T(8,128)(2,1)S(1)}, bf16[32,64,128]{2,1,0:T(8,128)(2,1)}, u32[]{:S(2)}, u32[]{:S(2)}) collective-permute-start(bf16[32,64,128]{2,1,0:T(8,128)(2,1)S(1)} %get-tuple-element.69.x0a), channel_id=1, source_target_pairs={{0,3},{1,0},{2,1},{3,2},{4,7},{5,4},{6,5},{7,6},{8,11},{9,8},{10,9... | collective-permute-start | bytes 1572872 | tf_op jit(solution)/shard_map/student_ring/ppermute | solution.py:313
  79.2 15.2 %collective-permute-start.11 = (bf16[32,64,128]{2,1,0:T(8,128)(2,1)}, bf16[32,64,128]{2,1,0:T(8,128)(2,1)}, u32[]{:S(2)}, u32[]{:S(2)}) collective-permute-start(bf16[32,64,128]{2,1,0:T(8,128)(2,1)} %collective-permute-done.7.x1a), channel_id=1, source_target_pairs={{0,1},{1,2},{2,3},{3,0},{4,5},{5,6},{6,7},{7,4},{8,9},{9,10},{10,1... | collective-permute-start | bytes 1572872 | tf_op jit(solution)/shard_map/student_ring/ppermute | solution.py:313
  79.5 15.0 %collective-permute-start.12 = (bf16[32,64,128]{2,1,0:T(8,128)(2,1)S(1)}, bf16[32,64,128]{2,1,0:T(8,128)(2,1)}, u32[]{:S(2)}, u32[]{:S(2)}) collective-permute-start(bf16[32,64,128]{2,1,0:T(8,128)(2,1)S(1)} %collective-permute-done.10.x2b), channel_id=1, source_target_pairs={{0,3},{1,0},{2,1},{3,2},{4,7},{5,4},{6,5},{7,6},{8,11},{9,8},{10,9... | collective-permute-start | bytes 1572872 | tf_op jit(solution)/shard_map/student_ring/ppermute | solution.py:313
  114.0 6.0 %collective-permute-start.13 = (f32[512,1536]{1,0:T(8,128)}, f32[512,1536]{1,0:T(8,128)}, u32[]{:S(2)}, u32[]{:S(2)}) collective-permute-start(f32[512,1536]{1,0:T(8,128)} %get-tuple-element.47), channel_id=1, source_target_pairs={{0,4},{4,0},{8,12},{12,8},{16,20},{20,16},{24,28},{28,24},{32,36},... | collective-permute-start | bytes 9437192 | tf_op jit(solution)/shard_map/grad_core/ppermute | solution.py:322
  114.0 5.3 %collective-permute-start.14 = (bf16[64,768]{1,0:T(8,128)(2,1)S(1)}, bf16[64,768]{1,0:T(8,128)(2,1)S(1)}, u32[]{:S(2)}, u32[]{:S(2)}) collective-permute-start(bf16[64,768]{1,0:T(8,128)(2,1)S(1)} %pad_maximum_fusion.2), channel_id=1, source_target_pairs={{0,8},{4,12},{8,0},{12,4},{16,24},{20,28},{24,16},{28,20},{32,40},... | collective-permute-start | bytes 294920 | tf_op jit(solution)/shard_map/ppermute | solution.py:322
  124.2 41.1 %all-to-all-start.1 = ((s16[32,16,1408]{2,1,0:T(8,128)(2,1)}), s16[32,16,1408]{2,1,0:T(8,128)(2,1)S(1)}, u32[]{:S(2)}, u32[]{:S(2)}) async-start(s16[32,16,1408]{2,1,0:T(8,128)(2,1)} %bitcast.28), calls=%async_computation.1 | async-start | bytes 2883584 | tf_op jit(solution)/shard_map/grad_xz/all_to_all | solution.py:424
  131.0 17.8 %collective-permute-start.15 = (bf16[128,768]{1,0:T(8,128)(2,1)S(1)}, bf16[128,768]{1,0:T(8,128)(2,1)S(1)}, u32[]{:S(2)}, u32[]{:S(2)}) collective-permute-start(bf16[128,768]{1,0:T(8,128)(2,1)S(1)} %pad_maximum_fusion), channel_id=1, source_target_pairs={{0,192},{4,196},{8,200},{12,204},{16,208},{20,212},{24,216},{28,22... | collective-permute-start | bytes 589832 | tf_op jit(solution)/shard_map/ppermute | solution.py:322
  132.5 16.3 %collective-permute-start.16 = (bf16[128,768]{1,0:T(8,128)(2,1)S(1)}, bf16[128,768]{1,0:T(8,128)(2,1)S(1)}, u32[]{:S(2)}, u32[]{:S(2)}) collective-permute-start(bf16[128,768]{1,0:T(8,128)(2,1)S(1)} %pad_maximum_fusion), channel_id=1, source_target_pairs={{0,128},{4,132},{8,136},{12,140},{16,144},{20,148},{24,152},{28,15... | collective-permute-start | bytes 589832 | tf_op jit(solution)/shard_map/ppermute | solution.py:322
  133.3 16.8 %collective-permute-start.17 = (bf16[128,768]{1,0:T(8,128)(2,1)S(1)}, bf16[128,768]{1,0:T(8,128)(2,1)S(1)}, u32[]{:S(2)}, u32[]{:S(2)}) collective-permute-start(bf16[128,768]{1,0:T(8,128)(2,1)S(1)} %pad_maximum_fusion), channel_id=1, source_target_pairs={{0,64},{4,68},{8,72},{12,76},{16,80},{20,84},{24,88},{28,92},{32,9... | collective-permute-start | bytes 589832 | tf_op jit(solution)/shard_map/ppermute | solution.py:322
  168.9 7.2 %collective-permute-start.18 = (f32[8,128]{1,0:T(8,128)}, f32[8,128]{1,0:T(8,128)S(1)}, u32[]{:S(2)}, u32[]{:S(2)}) collective-permute-start(f32[8,128]{1,0:T(8,128)} %get-tuple-element.55), channel_id=1, source_target_pairs={{0,1},{1,2},{2,3},{3,0},{4,5},{5,6},{6,7},{7,4},{8,9},{9,10},{10,1... | collective-permute-start | bytes 12296 | tf_op jit(solution)/shard_map/loss_parts/ppermute | solution.py:313
  168.9 7.1 %collective-permute-start.19 = (f32[8,128]{1,0:T(8,128)}, f32[8,128]{1,0:T(8,128)S(1)}, u32[]{:S(2)}, u32[]{:S(2)}) collective-permute-start(f32[8,128]{1,0:T(8,128)} %get-tuple-element.55), channel_id=1, source_target_pairs={{0,2},{1,3},{2,0},{3,1},{4,6},{5,7},{6,4},{7,5},{8,10},{9,11},{10,... | collective-permute-start | bytes 12296 | tf_op jit(solution)/shard_map/loss_parts/ppermute | solution.py:313
  172.1 3.8 %collective-permute-start.20 = (f32[8,128]{1,0:T(8,128)}, f32[8,128]{1,0:T(8,128)S(1)}, u32[]{:S(2)}, u32[]{:S(2)}) collective-permute-start(f32[8,128]{1,0:T(8,128)} %get-tuple-element.55), channel_id=1, source_target_pairs={{0,3},{1,0},{2,1},{3,2},{4,7},{5,4},{6,5},{7,6},{8,11},{9,8},{10,9... | collective-permute-start | bytes 12296 | tf_op jit(solution)/shard_map/loss_parts/ppermute | solution.py:313
  (7 other events, 108.9 us)
